TPU v7x, 32 devices: a whole 2x2x4 slice. The times are simulated.
32 devices in a mesh: rows: 8 (over z, x), heads: 4 (over y, core).
Axes of the slice: x: 2, y: 2, z: 4, core: 2. Of those that a mesh axis runs over, the one named last changes fastest.
Arguments:
- inputs: bfloat16 [4096, 512], P('rows'), may hold values from -6 to 6
- key_weight: bfloat16 [512, 1024], P(None, 'heads'), may hold values from -0.25 to 0.25
- value_weight: bfloat16 [512, 1024], P(None, 'heads'), may hold values from -0.25 to 0.25
- queries: bfloat16 [2, 1024, 1024], P(None, None, 'heads'), may hold values from -100 to 100
- out_grad: bfloat16 [2, 1024, 1024], P(None, None, 'heads'), may hold values from -3072 to 3072
Outputs:
- query_grad: float32 [2, 1024, 1024], P(None, 'rows', 'heads')
- key_weight_grad: float32 [512, 1024], P(None, 'heads')
- value_weight_grad: float32 [512, 1024], P(None, 'heads')
- input_grad: float32 [4096, 512], P('rows', 'heads')
All inputs are finite; a program needn't handle non-finite values.
Results may differ from a plain program's by a relative error of at most 0.003.
The roundings to bfloat16 on the way count: a program that leaves them out, or rounds other values in their place, can miss the bound.
Values sent between devices are 32-bit elements; how exact they have to be, the bound alone decides.
No kernel may reach another device: no remote copies, remote signals or barrier semaphores. Data moves between devices by JAX's collectives and lax.ppermute only.
A program may use at most 64 MiB of HBM per device.

v0:
```python
import jax
import jax.numpy as jnp
from jax import lax
from jax.sharding import PartitionSpec as P

HD = 128


def last_contract(left, right):
    return lax.dot_general(
        left, right, (((1,), (1,)), ((), ())), preferred_element_type=jnp.float32
    )


def rows_contract(left, right):
    return lax.dot_general(
        left, right, (((0,), (0,)), ((), ())), preferred_element_type=jnp.float32
    )


def on_device(inputs, key_weight, value_weight, queries, out_grad):
    keys = jnp.dot(inputs, key_weight, preferred_element_type=jnp.float32).astype(jnp.bfloat16)
    values = jnp.dot(inputs, value_weight, preferred_element_type=jnp.float32).astype(jnp.bfloat16)
    head_count = key_weight.shape[1] // HD
    read_count = queries.shape[0]
    factor = HD ** (-0.5)

    def block_terms(read_index, head_index):
        lower = head_index * HD
        upper = lower + HD
        query_block = queries[read_index, :, lower:upper]
        grad_block = out_grad[read_index, :, lower:upper]
        key_block = keys[:, lower:upper]
        scores = last_contract(query_block, key_block) * factor
        weighted = last_contract(grad_block, values[:, lower:upper])
        return (query_block, grad_block, key_block, scores, weighted)

    top_list = []
    total_list = []
    accum_list = []
    for read_index in range(read_count):
        for head_index in range(head_count):
            terms = block_terms(read_index, head_index)
            scores = terms[3]
            local_top = jnp.max(scores, axis=1)
            expos = jnp.exp(scores - local_top[:, None])
            top_list.append(local_top)
            total_list.append(jnp.sum(expos, axis=1))
            accum_list.append(jnp.sum(expos * terms[4], axis=1))
    tops = jnp.stack(top_list)
    totals = jnp.stack(total_list)
    accums = jnp.stack(accum_list)
    global_top = lax.pmax(tops, "rows")
    rescale = jnp.exp(tops - global_top)
    global_total, global_accum = lax.psum((totals * rescale, accums * rescale), "rows")
    inverse = 1.0 / global_total
    delta = global_accum * inverse
    row_count = inputs.shape[0]
    key_accs = [jnp.zeros((row_count, HD), jnp.float32) for head_index in range(head_count)]
    value_accs = [jnp.zeros((row_count, HD), jnp.float32) for head_index in range(head_count)]
    pieces = []
    for read_index in range(read_count):
        latent_cols = []
        for head_index in range(head_count):
            position = read_index * head_count + head_index
            query_block, grad_block, key_block, scores, weighted = block_terms(
                read_index, head_index
            )
            probs = jnp.exp(scores - global_top[position][:, None]) * inverse[position][:, None]
            score_grad = (probs * (weighted - delta[position][:, None]) * factor).astype(
                jnp.bfloat16
            )
            latent_cols.append(jnp.dot(score_grad, key_block, preferred_element_type=jnp.float32))
            key_accs[head_index] = key_accs[head_index] + rows_contract(score_grad, query_block)
            value_accs[head_index] = value_accs[head_index] + rows_contract(
                probs.astype(jnp.bfloat16), grad_block
            )
        latent_grad = jnp.concatenate(latent_cols, axis=1)
        pieces.append(latent_grad)
    query_grad = lax.psum_scatter(jnp.stack(pieces), "rows", scatter_dimension=1, tiled=True)
    key_grad = jnp.concatenate(key_accs, axis=1).astype(jnp.bfloat16)
    value_grad = jnp.concatenate(value_accs, axis=1).astype(jnp.bfloat16)
    key_weight_grad, value_weight_grad = lax.psum(
        (rows_contract(inputs, key_grad), rows_contract(inputs, value_grad)), "rows"
    )
    partial_input = last_contract(key_grad, key_weight) + last_contract(value_grad, value_weight)
    input_grad = lax.psum_scatter(partial_input, "heads", scatter_dimension=1, tiled=True)
    return (query_grad, key_weight_grad, value_weight_grad, input_grad)


def solution(mesh):
    in_specs = (
        P("rows", None),
        P(None, "heads"),
        P(None, "heads"),
        P(None, None, "heads"),
        P(None, None, "heads"),
    )
    out_specs = (P(None, "rows", "heads"), P(None, "heads"), P(None, "heads"), P("rows", "heads"))
    return jax.shard_map(
        on_device, mesh=mesh, in_specs=in_specs, out_specs=out_specs, check_vma=False
    )
```

profile of v0, /device:TPU:0, one launch (start us, length us, event | category | flops | bytes accessed | tf_op | source)
XLA Modules:
  0.0 295.0 jit_solution(7583211702279549888)
XLA Ops:
  8.2 1.3 convolution_convert_fusion.1
  9.6 1.4 fusion.90
  11.0 1.8 fusion.89
  12.8 1.8 fusion.91
  14.5 1.7 fusion.92
  16.6 38.8 %pmax.7 = f32[4,1024]{1,0:T(4,128)S(1)} all-reduce(f32[4,1024]{1,0:T(4,128)S(1)} %pad_maximum_fusion.7), channel_id=1, replica_groups=mesh['rows'=8,'heads'=4] {'rows'}, use_global_device_ids=true, to_apply=%region_4.0 | all-reduce | flops 4096 | bytes 32768 | tf_op jit(solution)/shard_map/pmax | solution.py:53
  55.5 3.6 %fusion = (f32[1024]{0:T(1024)S(1)}, f32[1024]{0:T(1024)S(1)}, f32[512,1024]{1,0:T(8,128)}) fusion(f32[512,1024]{1,0:T(8,128)} %get-tuple-element.46, f32[1024]{0:T(1024)S(1)} %get-tuple-element.45, bf16[2,1024,256]{2,1,0:T(8,128)(2,1)} %param.9, bf16[512,256]{1,0:T(8,128)(2,1)S(1)} %convolution_convert_fusion), kind=kOutput, calls=%fused_computation.17 | convolution fusion | flops 136312832 | bytes 4599808 | tf_op jit(solution)/shard_map/dot_general | solution.py:10
  59.1 1.9 fusion.1
  61.1 1.8 fusion.3
  62.9 1.7 fusion.2
  64.7 33.1 %all-reduce = (f32[4,1024]{1,0:T(4,128)S(1)}, f32[4,1024]{1,0:T(4,128)S(1)}) all-reduce(f32[4,1024]{1,0:T(4,128)S(1)} %get-tuple-element.21, f32[4,1024]{1,0:T(4,128)S(1)} %get-tuple-element.20), channel_id=1, replica_groups=mesh['rows'=8,'heads'=4] {'rows'}, use_global_device_ids=true, to_apply=%region_14.0 | all-reduce | flops 8192 | bytes 65536 | tf_op jit(solution)/shard_map/psum | solution.py:55
  97.8 2.3 fusion.16
  100.1 2.3 multiply_convert_fusion.3
  108.4 1.4 copy-done.13
  111.4 1.1 convolution_bitcast_fusion.1
  113.8 1.6 fusion.75
  117.7 1.6 pad_maximum_fusion
  120.6 1.3 convolution_add_fusion
  121.9 67.6 %all-reduce.4.cloned.1.call-done = (f32[512,256]{0,1:T(8,128)}, f32[512,256]{0,1:T(8,128)}) async-done(((f32[512,256]{0,1:T(8,128)}, f32[512,256]{0,1:T(8,128)}), (f32[512,256]{0,1:T(8,128)}, f32[512,256]{0,1:T(8,128)})) %all-reduce.4.cloned.1.call-update) | async-done | bytes 1048592 | tf_op jit(solution)/shard_map/psum | solution.py:83
  189.5 2.0 copy.10
  191.5 2.0 copy.11
  193.6 67.7 %reduce-scatter.3.cloned.1.call-done = f32[2,128,256]{1,2,0:T(8,128)} async-done(((f32[2,1024,256]{1,2,0:T(8,128)}), f32[2,128,256]{1,2,0:T(8,128)}) %reduce-scatter.3.cloned.1.call-update) | async-done | bytes 262160 | tf_op jit(solution)/shard_map/reduce_scatter | solution.py:80
  261.3 1.8 copy.9
  263.1 25.4 %reduce-scatter.5.cloned.1.call-done = f32[512,128]{1,0:T(8,128)} async-done(((f32[512,512]{1,0:T(8,128)}), f32[512,128]{1,0:T(8,128)}) %reduce-scatter.5.cloned.1.call-update) | async-done | bytes 262160 | tf_op jit(solution)/shard_map/reduce_scatter | solution.py:87
  (74 shorter events, 13.9 us)
Async XLA Ops:
  7.2 182.3 %all-reduce.4.cloned.1.call-start = ((), (), s32[]{:S(2)}) async-start(), calls=%async_computation.4 | async-start | bytes 2097152 | tf_op jit(solution)/shard_map/psum | solution.py:83
  8.2 2.7 copy-start.16
  12.8 3.5 %copy-start.20 = (bf16[512,256]{1,0:T(8,128)(2,1)S(1)}, bf16[512,256]{1,0:T(8,128)(2,1)}, u32[]{:S(2)}) copy-start(bf16[512,256]{1,0:T(8,128)(2,1)} %param.7) | copy-start | bytes 786436
  55.4 3.7 %copy-start.3 = (f32[512,1024]{1,0:T(8,128)S(1)}, f32[512,1024]{1,0:T(8,128)}, u32[]{:S(2)}) copy-start(f32[512,1024]{1,0:T(8,128)} %get-tuple-element.43) | copy-start | bytes 6291460
  55.5 3.6 %copy-start.18 = (bf16[2,1024,256]{2,1,0:T(8,128)(2,1)S(1)}, bf16[2,1024,256]{2,1,0:T(8,128)(2,1)}, u32[]{:S(2)}) copy-start(bf16[2,1024,256]{2,1,0:T(8,128)(2,1)} %param.9) | copy-start | bytes 3145732
  59.1 2.0 copy-start.1
  97.7 2.4 copy-start.5
  100.1 2.3 copy-start.17
  100.1 2.8 copy-start.4
  100.1 2.8 copy-start.19
  102.4 1.1 copy-start.6
  102.4 2.1 copy-start.15
  104.5 1.7 copy-start.2
  105.1 1.6 copy-start.8
  105.1 2.1 copy-start.14
  107.8 3.1 %copy-start.10 = (bf16[512,1024]{1,0:T(8,128)(2,1)}, bf16[512,1024]{1,0:T(8,128)(2,1)S(1)}, u32[]{:S(2)}) copy-start(bf16[512,1024]{1,0:T(8,128)(2,1)S(1)} %multiply_convert_fusion) | copy-start | bytes 3145732
  107.9 2.0 copy-start.13
  110.4 2.1 copy-start.12
  112.5 2.9 copy-start.11
  113.6 147.7 %reduce-scatter.3.cloned.1.call-start = ((), (), s32[]{:S(2)}) async-start(), calls=%async_computation.2 | async-start | bytes 2359296 | tf_op jit(solution)/shard_map/reduce_scatter | solution.py:80
  115.4 1.3 copy-start.7
  115.8 1.5 copy-start.9
  119.3 1.3 copy-start.21
  119.3 169.2 %reduce-scatter.5.cloned.1.call-start = ((), (), s32[]{:S(2)}) async-start(), calls=%async_computation.3 | async-start | bytes 1310720 | tf_op jit(solution)/shard_map/reduce_scatter | solution.py:87
  (2 other events, 2.0 us)
Sparse Core Ops, SparseCore 0:
  113.7 75.7 all-reduce.3
  193.5 67.7 reduce-scatter.2
  264.5 23.8 reduce-scatter.4
where the time goes:
time: 296 us; the launch traced here: 295 us
  waiting for transfers between devices  161 us (54%)
  blocking collectives  71.9 us (24%)
  matrix products  29.7 us (10%)
  between operations  14.1 us (5%)
  local copies, waits for them, and re-layouts  12.4 us (4%)
  other arithmetic  5.86 us (2%)
    reduce_scatter x1, waiting for transfers between devices, on_device(): lax.psum_scatter(jnp.stack(pieces), 'rows', scatter_dimension=1, tiled=True)  67.7 us
    psum x1, waiting for transfers between devices, on_device(): lax.psum((rows_contract(inputs, key_grad), rows_contract(inputs, value_gr...  67.6 us
    pmax x1, blocking collectives, on_device(): global_top = lax.pmax(tops, 'rows')  38.8 us
    psum x1, blocking collectives, on_device(): lax.psum((totals * rescale, accums * rescale), 'rows')  33.1 us
    reduce_scatter x1, waiting for transfers between devices, on_device(): lax.psum_scatter(partial_input, 'heads', scatter_dimension=1, tiled=True)  25.4 us
    dot_general x10, matrix products, last_contract(): lax.dot_general(left, right, (((1,), (1,)), ((), ())), preferred_element_...  17.4 us
    unnamed x49, local copies, waits for them, and re-layouts  12.4 us
    dot_general x10, matrix products, rows_contract(): lax.dot_general(left, right, (((0,), (0,)), ((), ())), preferred_element_...  8.04 us
  transfers between devices with their start and end apart: 3, of which 3 were waited for; matrix products, arithmetic and copies ran while one was open for 4% of the time, Pallas kernels for 0%

commit v1 on v0

--- a/solution.py
+++ b/solution.py
@@ -18,11 +18,48 @@
     )
 
 
-def on_device(inputs, key_weight, value_weight, queries, out_grad):
+def swap(array, axis, count, bit):
+    pairs = [(device, device ^ bit) for device in range(count)]
+    return lax.ppermute(array, axis, pairs)
+
+
+def bits_of(count):
+    bit = 1
+    while bit < count:
+        yield bit
+        bit *= 2
+
+
+def scatter_sum(array, axis, count):
+    for bit in bits_of(count):
+        halves = array.reshape((array.shape[0] // 2, 2) + array.shape[1:])
+        array = halves[:, 0] + swap(halves[:, 1], axis, count, bit)
+    return array[0]
+
+
+def gather_all(array, axis, count):
+    array = array[None]
+    for bit in reversed(list(bits_of(count))):
+        theirs = swap(array, axis, count, bit)
+        array = jnp.stack([array, theirs], axis=1).reshape((-1,) + array.shape[1:])
+    return array
+
+
+def on_device(row_devices, head_devices, inputs, key_weight, value_weight, queries, out_grad):
+    me = lax.axis_index("rows")
+    order = me ^ jnp.arange(row_devices, dtype=jnp.int32)
+    reads, latents, columns = queries.shape
+    piece = latents // row_devices
+
+    def reorder(array):
+        blocks = array.reshape(reads, row_devices, piece, columns)
+        return jnp.take(blocks, order, axis=1).reshape(array.shape)
+
+    queries = reorder(queries)
+    out_grad = reorder(out_grad)
     keys = jnp.dot(inputs, key_weight, preferred_element_type=jnp.float32).astype(jnp.bfloat16)
     values = jnp.dot(inputs, value_weight, preferred_element_type=jnp.float32).astype(jnp.bfloat16)
-    head_count = key_weight.shape[1] // HD
-    read_count = queries.shape[0]
+    head_count = columns // HD
     factor = HD ** (-0.5)
 
     def block_terms(read_index, head_index):
@@ -38,7 +75,7 @@
     top_list = []
     total_list = []
     accum_list = []
-    for read_index in range(read_count):
+    for read_index in range(reads):
         for head_index in range(head_count):
             terms = block_terms(read_index, head_index)
             scores = terms[3]
@@ -47,19 +84,27 @@
             top_list.append(local_top)
             total_list.append(jnp.sum(expos, axis=1))
             accum_list.append(jnp.sum(expos * terms[4], axis=1))
-    tops = jnp.stack(top_list)
-    totals = jnp.stack(total_list)
-    accums = jnp.stack(accum_list)
-    global_top = lax.pmax(tops, "rows")
-    rescale = jnp.exp(tops - global_top)
-    global_total, global_accum = lax.psum((totals * rescale, accums * rescale), "rows")
-    inverse = 1.0 / global_total
-    delta = global_accum * inverse
+    stats = jnp.stack([jnp.stack(top_list), jnp.stack(total_list), jnp.stack(accum_list)])
+    for bit in bits_of(row_devices):
+        shape = (3, reads * head_count, row_devices // (2 * bit), 2, bit * piece)
+        theirs = swap(stats, "rows", row_devices, bit).reshape(shape)
+        theirs = jnp.flip(theirs, axis=3).reshape(stats.shape)
+        top = jnp.maximum(stats[0], theirs[0])
+        mine_scale = jnp.exp(stats[0] - top)
+        their_scale = jnp.exp(theirs[0] - top)
+        stats = jnp.stack([
+            top,
+            stats[1] * mine_scale + theirs[1] * their_scale,
+            stats[2] * mine_scale + theirs[2] * their_scale,
+        ])
+    global_top = stats[0]
+    inverse = 1.0 / stats[1]
+    delta = stats[2] * inverse
     row_count = inputs.shape[0]
     key_accs = [jnp.zeros((row_count, HD), jnp.float32) for head_index in range(head_count)]
     value_accs = [jnp.zeros((row_count, HD), jnp.float32) for head_index in range(head_count)]
     pieces = []
-    for read_index in range(read_count):
+    for read_index in range(reads):
         latent_cols = []
         for head_index in range(head_count):
             position = read_index * head_count + head_index
@@ -76,16 +121,27 @@
                 probs.astype(jnp.bfloat16), grad_block
             )
         latent_grad = jnp.concatenate(latent_cols, axis=1)
-        pieces.append(latent_grad)
-    query_grad = lax.psum_scatter(jnp.stack(pieces), "rows", scatter_dimension=1, tiled=True)
+        pieces.append(scatter_sum(latent_grad.reshape(row_devices, piece, columns), "rows", row_devices))
+    query_grad = jnp.stack(pieces)
     key_grad = jnp.concatenate(key_accs, axis=1).astype(jnp.bfloat16)
     value_grad = jnp.concatenate(value_accs, axis=1).astype(jnp.bfloat16)
-    key_weight_grad, value_weight_grad = lax.psum(
-        (rows_contract(inputs, key_grad), rows_contract(inputs, value_grad)), "rows"
+
+    weights = jnp.concatenate(
+        [rows_contract(inputs, key_grad), rows_contract(inputs, value_grad)], axis=1
     )
+    features = inputs.shape[1]
+    blocks = weights.reshape(row_devices, features // row_devices, 2 * columns)
+    mine = scatter_sum(jnp.take(blocks, order, axis=0), "rows", row_devices)
+    gathered = jnp.take(gather_all(mine, "rows", row_devices), order, axis=0)
+    gathered = gathered.reshape(features, 2 * columns)
+
     partial_input = last_contract(key_grad, key_weight) + last_contract(value_grad, value_weight)
-    input_grad = lax.psum_scatter(partial_input, "heads", scatter_dimension=1, tiled=True)
-    return (query_grad, key_weight_grad, value_weight_grad, input_grad)
+    place = lax.axis_index("heads")
+    head_order = place ^ jnp.arange(head_devices, dtype=jnp.int32)
+    parts = partial_input.reshape(row_count, head_devices, features // head_devices)
+    parts = jnp.take(parts.transpose(1, 0, 2), head_order, axis=0)
+    input_grad = scatter_sum(parts, "heads", head_devices)
+    return (query_grad, gathered[:, :columns], gathered[:, columns:], input_grad)
 
 
 def solution(mesh):
@@ -97,6 +153,8 @@
         P(None, None, "heads"),
     )
     out_specs = (P(None, "rows", "heads"), P(None, "heads"), P(None, "heads"), P("rows", "heads"))
-    return jax.shard_map(
-        on_device, mesh=mesh, in_specs=in_specs, out_specs=out_specs, check_vma=False
-    )
+
+    def body(*args):
+        return on_device(mesh.shape["rows"], mesh.shape["heads"], *args)
+
+    return jax.shard_map(body, mesh=mesh, in_specs=in_specs, out_specs=out_specs, check_vma=False)

time: 296 us -> 159 us (0.54)
  waiting for transfers between devices: 161 us -> 39.7 us
  blocking collectives: 71.9 us -> 0 us
  starting transfers between devices: 0.3 us -> 30 us
  local copies, waits for them, and re-layouts: 12.4 us -> 41.8 us
  other arithmetic: 5.86 us -> 22.1 us
  between operations: 14.1 us -> 1.54 us
  matrix products: 29.7 us -> 22.8 us
    reduce_scatter x2 -> x0, waiting for transfers between devices: 93.1 us -> none  [the longest x1 67.7 us: on_device(): lax.psum_scatter(jnp.stack(pieces), 'rows', scatter_dimension=1, tiled=True)]
    psum x1 -> x0, waiting for transfers between devices: 67.6 us -> none  [on_device(): lax.psum((rows_contract(inputs, key_grad), rows_contract(inputs, value_gr...]
    ppermute x0 -> x17, waiting for transfers between devices: none -> 39.7 us  [swap(): return lax.ppermute(array, axis, pairs)]
    pmax x1 -> x0, blocking collectives: 38.8 us -> none  [on_device(): global_top = lax.pmax(tops, 'rows')]
    psum x1 -> x0, blocking collectives: 33.1 us -> none  [on_device(): lax.psum((totals * rescale, accums * rescale), 'rows')]
    ppermute x0 -> x17, starting transfers between devices: none -> 30 us  [swap(): return lax.ppermute(array, axis, pairs)]
    slice x0 -> x25, local copies, waits for them, and re-layouts: none -> 13.6 us  [the longest x6 4.22 us: on_device(): theirs[2] * their_scale]
    dot_general x10, matrix products: 17.4 us -> 9.58 us  [last_contract(): lax.dot_general(left, right, (((1,), (1,)), ((), ())), preferred_element_...]
  transfers between devices with their start and end apart: 3 -> 17, of which waited for: 3 -> 8; matrix products, arithmetic and copies ran while one was open for 4% -> 18% of each run, Pallas kernels for 0% -> 0%
where the time goes in v1:
time: 159 us; the launch traced here: 158 us
  local copies, waits for them, and re-layouts  41.8 us (26%)
  waiting for transfers between devices  39.7 us (25%)
  starting transfers between devices  30 us (19%)
  matrix products  22.8 us (14%)
  other arithmetic  22.1 us (14%)
    ppermute x17, waiting for transfers between devices, swap(): return lax.ppermute(array, axis, pairs)  39.7 us
    ppermute x17, starting transfers between devices, swap(): return lax.ppermute(array, axis, pairs)  30 us
    unnamed x91, local copies, waits for them, and re-layouts  14.9 us
    dot_general x10, matrix products, last_contract(): lax.dot_general(left, right, (((1,), (1,)), ((), ())), preferred_element_...  9.58 us
    dot_general x10, matrix products, rows_contract(): lax.dot_general(left, right, (((0,), (0,)), ((), ())), preferred_element_...  7.96 us
    dot_general x4, matrix products, on_device(): jnp.dot(score_grad, key_block, preferred_element_type=jnp.float32)  4.64 us
    another operation x2, local copies, waits for them, and re-layouts, scatter_sum(): halves = array.reshape((array.shape[0] // 2, 2) + array.shape[1:])  4.22 us
    slice x6, local copies, waits for them, and re-layouts, on_device(): theirs[2] * their_scale  4.22 us
  transfers between devices with their start and end apart: 17, of which 8 were waited for; matrix products, arithmetic and copies ran while one was open for 18% of the time, Pallas kernels for 0%

profile of v1, /device:TPU:0, one launch (start us, length us, event | category | flops | bytes accessed | tf_op | source)
XLA Modules:
  0.0 157.8 jit_solution(10682742663733197093)
XLA Ops:
  9.4 1.8 %fusion.1 = (f32[1024]{0:T(1024)S(1)}, f32[1024]{0:T(1024)S(1)}, f32[1024,512]{0,1:T(8,128)}) fusion(f32[1024,512]{0,1:T(8,128)S(1)} %get-tuple-element.58, f32[1024]{0:T(1024)S(1)} %get-tuple-element.57, bf16[512,256]{1,0:T(8,128)(2,1)S(1)} %convolution_convert_fusion, bf16[2,1024,256]{2,1,0:T(8,128)(2,1)S(1)} %bitcast.260), kind=kOutput, calls=%fused_computation.22 | convolution fusion | flops 136312832 | bytes 4599808 | tf_op jit(solution)/shard_map/dot_general | solution.py:10
  13.0 1.9 %fusion.3 = (f32[1024]{0:T(1024)S(1)}, f32[1024]{0:T(1024)S(1)}, f32[1024,512]{0,1:T(8,128)}) fusion(f32[1024,512]{0,1:T(8,128)S(1)} %get-tuple-element.52, f32[1024]{0:T(1024)S(1)} %get-tuple-element.51, bf16[512,256]{1,0:T(8,128)(2,1)S(1)} %convolution_convert_fusion, bf16[2,1024,256]{2,1,0:T(8,128)(2,1)S(1)} %bitcast.262), kind=kOutput, calls=%fused_computation.24 | convolution fusion | flops 136312832 | bytes 4599808 | tf_op jit(solution)/shard_map/dot_general | solution.py:10
  15.6 2.9 %collective-permute-start = (f32[3,4,1024]{2,1,0:T(4,128)}, f32[3,4,1024]{2,1,0:T(4,128)S(1)}, u32[]{:S(2)}, u32[]{:S(2)}) collective-permute-start(f32[3,4,1024]{2,1,0:T(4,128)} %pad_maximum_fusion.13), channel_id=1, source_target_pairs={{0,4},{4,0},{8,12},{12,8},{16,20},{20,16},{24,28},{28,24},{1,5},{5... | collective-permute-start | bytes 147464 | tf_op jit(solution)/shard_map/ppermute | solution.py:23
  23.3 2.2 %collective-permute-start.1 = (f32[3,4,1024]{2,1,0:T(4,128)S(1)}, f32[3,4,1024]{2,1,0:T(4,128)S(1)}, u32[]{:S(2)}, u32[]{:S(2)}) collective-permute-start(f32[3,4,1024]{2,1,0:T(4,128)S(1)} %pad_maximum_fusion.14), channel_id=1, source_target_pairs={{0,8},{4,12},{8,0},{12,4},{16,24},{20,28},{24,16},{28,20},{1,9},{5... | collective-permute-start | bytes 147464 | tf_op jit(solution)/shard_map/ppermute | solution.py:23
  34.9 3.0 %collective-permute-start.2 = (f32[3,4,1024]{2,1,0:T(4,128)}, f32[3,4,1024]{2,1,0:T(4,128)}, u32[]{:S(2)}, u32[]{:S(2)}) collective-permute-start(f32[3,4,1024]{2,1,0:T(4,128)} %pad_maximum_fusion.15), channel_id=1, source_target_pairs={{0,16},{4,20},{8,24},{12,28},{16,0},{20,4},{24,8},{28,12},{1,17},{... | collective-permute-start | bytes 147464 | tf_op jit(solution)/shard_map/ppermute | solution.py:23
  48.4 2.2 %fusion.16 = f32[512,128]{0,1:T(8,128)S(1)} fusion(f32[1024,512]{0,1:T(8,128)} %copy-done.2, f32[1024]{0:T(1024)S(1)} %bitcast.353, f32[1024]{0:T(1024)} %bitcast.347, bf16[2,1024,256]{2,1,0:T(8,128)(2,1)} %bitcast.263), kind=kOutput, calls=%fused_computation.47 | convolution fusion | flops 135790592 | bytes 2629632 | tf_op jit(solution)/shard_map/dot_general | solution.py:16
  50.6 2.2 %multiply_convert_fusion.3 = bf16[1024,512]{0,1:T(8,128)(2,1)S(1)} fusion(f32[1024,512]{0,1:T(8,128)} %get-tuple-element.62, f32[1024,512]{0,1:T(8,128)S(1)} %copy-done.3, f32[1024]{0:T(1024)S(1)} %bitcast.358, f32[1024]{0:T(1024)S(1)} %bitcast.354, f32[1024]{0:T(1024)S(1)} %bitcast.348), kind=kLoop, calls=%fused_computation.11 | loop fusion | flops 3145728 | bytes 5255168 | tf_op jit(solution)/shard_map/convert_element_type | solution.py:115
  73.5 1.8 %collective-permute-start.9 = (f32[4,64,512]{2,1,0:T(8,128)}, f32[4,64,512]{2,1,0:T(8,128)}, u32[]{:S(2)}, u32[]{:S(2)}) collective-permute-start(f32[4,64,512]{2,1,0:T(8,128)} %slice_bitcast_fusion.2), channel_id=1, source_target_pairs={{0,4},{4,0},{8,12},{12,8},{16,20},{20,16},{24,28},{28,24},{1,5},{5... | collective-permute-start | bytes 1572872 | tf_op jit(solution)/shard_map/ppermute | solution.py:23
  76.5 2.1 %reshape_reshape.6 = f32[4,2,128,256]{2,1,0,3:T(2,128)S(1)} reshape(f32[1024,256]{0,1:T(8,128)} %pad_maximum_fusion) | data formatting | bytes 2097152 | tf_op jit(solution)/shard_map/reshape;reshape | solution.py:35
  78.6 1.8 %fusion.81 = (f32[4,1,128,256]{2,1,0,3:T(1,128)}, f32[4,1,128,256]{2,1,0,3:T(1,128)}) fusion(f32[4,2,128,256]{2,1,0,3:T(2,128)S(1)} %reshape_reshape.6), kind=kLoop, calls=%fused_computation.182 | loop fusion | bytes 2097152 | tf_op jit(solution)/shard_map/slice | solution.py:36
  80.4 1.9 %copy.44 = f32[4,1,128,256]{3,2,0,1:T(8,128)} copy(f32[4,1,128,256]{2,1,0,3:T(1,128)} %get-tuple-element.23) | data formatting | bytes 1048576
  82.5 2.3 %pad_maximum_fusion.1 = f32[1024,256]{0,1:T(8,128)} fusion(f32[1024,128]{0,1:T(8,128)} %fusion.53, f32[1024,128]{0,1:T(8,128)} %fusion.59), kind=kLoop, calls=%fused_computation.49 | loop fusion | flops 262144 | bytes 2097152 | tf_op jit(solution)/shard_map/concatenate | solution.py:123
  84.8 2.1 %reshape_reshape.7 = f32[4,2,128,256]{2,1,0,3:T(2,128)S(1)} reshape(f32[1024,256]{0,1:T(8,128)} %pad_maximum_fusion.1) | data formatting | bytes 2097152 | tf_op jit(solution)/shard_map/reshape;reshape | solution.py:35
  89.9 2.0 %copy.47 = f32[4,1,128,256]{3,2,0,1:T(8,128)} copy(f32[4,1,128,256]{2,1,0,3:T(1,128)} %get-tuple-element.25) | data formatting | bytes 1048576
  91.9 1.8 %collective-permute-start.6 = (f32[4,128,256]{2,1,0:T(8,128)}, f32[4,128,256]{2,1,0:T(8,128)}, u32[]{:S(2)}, u32[]{:S(2)}) collective-permute-start(f32[4,128,256]{2,1,0:T(8,128)} %bitcast.62), channel_id=1, source_target_pairs={{0,4},{4,0},{8,12},{12,8},{16,20},{20,16},{24,28},{28,24},{1,5},{5... | collective-permute-start | bytes 1572872 | tf_op jit(solution)/shard_map/ppermute | solution.py:23
  103.0 7.4 %collective-permute-done.6 = f32[4,128,256]{2,1,0:T(8,128)} collective-permute-done((f32[4,128,256]{2,1,0:T(8,128)}, f32[4,128,256]{2,1,0:T(8,128)}, u32[]{:S(2)}, u32[]{:S(2)}) %collective-permute-start.6) | collective-permute-done | bytes 524320 | tf_op jit(solution)/shard_map/ppermute | solution.py:23
  111.5 1.9 %collective-permute-start.7 = (f32[2,128,256]{2,1,0:T(8,128)S(1)}, f32[2,128,256]{2,1,0:T(8,128)S(1)}, u32[]{:S(2)}, u32[]{:S(2)}) collective-permute-start(f32[2,128,256]{2,1,0:T(8,128)S(1)} %slice_bitcast_fusion.8), channel_id=1, source_target_pairs={{0,8},{4,12},{8,0},{12,4},{16,24},{20,28},{24,16},{28,20},{1,9},{5... | collective-permute-start | bytes 786440 | tf_op jit(solution)/shard_map/ppermute | solution.py:23
  113.5 3.1 %collective-permute-start.11 = (f32[1,64,512]{2,1,0:T(8,128)S(1)}, f32[1,64,512]{2,1,0:T(8,128)S(1)}, u32[]{:S(2)}, u32[]{:S(2)}) collective-permute-start(f32[1,64,512]{2,1,0:T(8,128)S(1)} %slice_bitcast_fusion.36), channel_id=1, source_target_pairs={{0,16},{4,20},{8,24},{12,28},{16,0},{20,4},{24,8},{28,12},{1,17},{... | collective-permute-start | bytes 393224 | tf_op jit(solution)/shard_map/ppermute | solution.py:23
  116.7 6.0 %collective-permute-done.11 = f32[1,64,512]{2,1,0:T(8,128)S(1)} collective-permute-done((f32[1,64,512]{2,1,0:T(8,128)S(1)}, f32[1,64,512]{2,1,0:T(8,128)S(1)}, u32[]{:S(2)}, u32[]{:S(2)}) %collective-permute-start.11) | collective-permute-done | bytes 131104 | tf_op jit(solution)/shard_map/ppermute | solution.py:23
  122.7 3.5 %collective-permute-start.12 = (f32[1,64,512]{2,1,0:T(8,128)S(1)}, f32[1,64,512]{2,1,0:T(8,128)S(1)}, u32[]{:S(2)}, u32[]{:S(2)}) collective-permute-start(f32[1,64,512]{2,1,0:T(8,128)S(1)} %fusion.46), channel_id=1, source_target_pairs={{0,16},{4,20},{8,24},{12,28},{16,0},{20,4},{24,8},{28,12},{1,17},{... | collective-permute-start | bytes 393224 | tf_op jit(solution)/shard_map/ppermute | solution.py:23
  126.3 7.3 %collective-permute-done.12 = f32[1,64,512]{2,1,0:T(8,128)S(1)} collective-permute-done((f32[1,64,512]{2,1,0:T(8,128)S(1)}, f32[1,64,512]{2,1,0:T(8,128)S(1)}, u32[]{:S(2)}, u32[]{:S(2)}) %collective-permute-start.12) | collective-permute-done | bytes 131104 | tf_op jit(solution)/shard_map/ppermute | solution.py:23
  134.1 2.9 %collective-permute-start.8 = (f32[1,128,256]{2,1,0:T(8,128)S(1)}, f32[1,128,256]{2,1,0:T(8,128)S(1)}, u32[]{:S(2)}, u32[]{:S(2)}) collective-permute-start(f32[1,128,256]{2,1,0:T(8,128)S(1)} %slice_bitcast_fusion.38), channel_id=1, source_target_pairs={{0,16},{4,20},{8,24},{12,28},{16,0},{20,4},{24,8},{28,12},{1,17},{... | collective-permute-start | bytes 393224 | tf_op jit(solution)/shard_map/ppermute | solution.py:23
  137.7 5.2 %collective-permute-done.13 = f32[2,64,512]{2,1,0:T(8,128)S(1)} collective-permute-done((f32[2,64,512]{2,1,0:T(8,128)S(1)}, f32[2,64,512]{2,1,0:T(8,128)S(1)}, u32[]{:S(2)}, u32[]{:S(2)}) %collective-permute-start.13) | collective-permute-done | bytes 262176 | tf_op jit(solution)/shard_map/ppermute | solution.py:23
  145.3 10.2 %collective-permute-done.14 = f32[4,64,512]{2,1,0:T(8,128)S(1)} collective-permute-done((f32[4,64,512]{2,1,0:T(8,128)S(1)}, f32[4,64,512]{2,1,0:T(8,128)S(1)}, u32[]{:S(2)}, u32[]{:S(2)}) %collective-permute-start.14) | collective-permute-done | bytes 524320 | tf_op jit(solution)/shard_map/ppermute | solution.py:23
  (231 shorter events, 76.8 us)
Async XLA Ops:
  6.2 5.1 %copy-start.6 = (f32[1024,512]{0,1:T(8,128)}, f32[1024,512]{0,1:T(8,128)S(1)}, u32[]{:S(2)}) copy-start(f32[1024,512]{0,1:T(8,128)S(1)} %get-tuple-element.55) | copy-start | bytes 6291460
  6.6 6.4 %copy-start.4 = (f32[1024,512]{0,1:T(8,128)}, f32[1024,512]{0,1:T(8,128)S(1)}, u32[]{:S(2)}) copy-start(f32[1024,512]{0,1:T(8,128)S(1)} %get-tuple-element.52) | copy-start | bytes 6291460
  7.3 5.7 %copy-start.8 = (bf16[2,8,128,256]{3,2,1,0:T(8,128)(2,1)}, bf16[2,8,128,256]{3,2,1,0:T(8,128)(2,1)S(1)}, u32[]{:S(2)}) copy-start(bf16[2,8,128,256]{3,2,1,0:T(8,128)(2,1)S(1)} %copy.26) | copy-start | bytes 3145732
  9.4 11.7 %copy-start.26 = (f32[1024]{0:T(1024)}, f32[1024]{0:T(1024)S(1)}, u32[]{:S(2)}) copy-start(f32[1024]{0:T(1024)S(1)} %get-tuple-element.6) | copy-start | bytes 12292
  9.4 12.5 %copy-start.27 = (f32[1024]{0:T(1024)}, f32[1024]{0:T(1024)S(1)}, u32[]{:S(2)}) copy-start(f32[1024]{0:T(1024)S(1)} %get-tuple-element.7) | copy-start | bytes 12292
  11.3 9.9 %copy-start.28 = (f32[1024]{0:T(1024)}, f32[1024]{0:T(1024)S(1)}, u32[]{:S(2)}) copy-start(f32[1024]{0:T(1024)S(1)} %get-tuple-element.8) | copy-start | bytes 12292
  11.3 10.6 %copy-start.29 = (f32[1024]{0:T(1024)}, f32[1024]{0:T(1024)S(1)}, u32[]{:S(2)}) copy-start(f32[1024]{0:T(1024)S(1)} %get-tuple-element.9) | copy-start | bytes 12292
  15.6 5.2 %collective-permute-start = (f32[3,4,1024]{2,1,0:T(4,128)}, f32[3,4,1024]{2,1,0:T(4,128)S(1)}, u32[]{:S(2)}, u32[]{:S(2)}) collective-permute-start(f32[3,4,1024]{2,1,0:T(4,128)} %pad_maximum_fusion.13), channel_id=1, source_target_pairs={{0,4},{4,0},{8,12},{12,8},{16,20},{20,16},{24,28},{28,24},{1,5},{5... | collective-permute-start | bytes 147464 | tf_op jit(solution)/shard_map/ppermute | solution.py:23
  23.3 4.2 %collective-permute-start.1 = (f32[3,4,1024]{2,1,0:T(4,128)S(1)}, f32[3,4,1024]{2,1,0:T(4,128)S(1)}, u32[]{:S(2)}, u32[]{:S(2)}) collective-permute-start(f32[3,4,1024]{2,1,0:T(4,128)S(1)} %pad_maximum_fusion.14), channel_id=1, source_target_pairs={{0,8},{4,12},{8,0},{12,4},{16,24},{20,28},{24,16},{28,20},{1,9},{5... | collective-permute-start | bytes 147464 | tf_op jit(solution)/shard_map/ppermute | solution.py:23
  34.9 5.4 %collective-permute-start.2 = (f32[3,4,1024]{2,1,0:T(4,128)}, f32[3,4,1024]{2,1,0:T(4,128)}, u32[]{:S(2)}, u32[]{:S(2)}) collective-permute-start(f32[3,4,1024]{2,1,0:T(4,128)} %pad_maximum_fusion.15), channel_id=1, source_target_pairs={{0,16},{4,20},{8,24},{12,28},{16,0},{20,4},{24,8},{28,12},{1,17},{... | collective-permute-start | bytes 147464 | tf_op jit(solution)/shard_map/ppermute | solution.py:23
  70.9 24.1 %collective-permute-start.15 = (f32[2,512,128]{2,1,0:T(8,128)}, f32[2,512,128]{2,1,0:T(8,128)}, u32[]{:S(2)}, u32[]{:S(2)}) collective-permute-start(f32[2,512,128]{2,1,0:T(8,128)} %slice_bitcast_fusion), channel_id=1, source_target_pairs={{0,1},{1,0},{2,3},{3,2},{4,5},{5,4},{6,7},{7,6},{8,9},{9,8},{10,11... | collective-permute-start | bytes 1572872 | tf_op jit(solution)/shard_map/ppermute | solution.py:23
  73.5 24.2 %collective-permute-start.9 = (f32[4,64,512]{2,1,0:T(8,128)}, f32[4,64,512]{2,1,0:T(8,128)}, u32[]{:S(2)}, u32[]{:S(2)}) collective-permute-start(f32[4,64,512]{2,1,0:T(8,128)} %slice_bitcast_fusion.2), channel_id=1, source_target_pairs={{0,4},{4,0},{8,12},{12,8},{16,20},{20,16},{24,28},{28,24},{1,5},{5... | collective-permute-start | bytes 1572872 | tf_op jit(solution)/shard_map/ppermute | solution.py:23
  82.3 18.2 %collective-permute-start.3 = (f32[4,128,256]{2,1,0:T(8,128)}, f32[4,128,256]{2,1,0:T(8,128)}, u32[]{:S(2)}, u32[]{:S(2)}) collective-permute-start(f32[4,128,256]{2,1,0:T(8,128)} %bitcast.48), channel_id=1, source_target_pairs={{0,4},{4,0},{8,12},{12,8},{16,20},{20,16},{24,28},{28,24},{1,5},{5... | collective-permute-start | bytes 1572872 | tf_op jit(solution)/shard_map/ppermute | solution.py:23
  91.9 18.5 %collective-permute-start.6 = (f32[4,128,256]{2,1,0:T(8,128)}, f32[4,128,256]{2,1,0:T(8,128)}, u32[]{:S(2)}, u32[]{:S(2)}) collective-permute-start(f32[4,128,256]{2,1,0:T(8,128)} %bitcast.62), channel_id=1, source_target_pairs={{0,4},{4,0},{8,12},{12,8},{16,20},{20,16},{24,28},{28,24},{1,5},{5... | collective-permute-start | bytes 1572872 | tf_op jit(solution)/shard_map/ppermute | solution.py:23
  96.1 40.8 %collective-permute-start.16 = (f32[1,512,128]{2,1,0:T(8,128)S(1)}, f32[1,512,128]{2,1,0:T(8,128)S(1)}, u32[]{:S(2)}, u32[]{:S(2)}) collective-permute-start(f32[1,512,128]{2,1,0:T(8,128)S(1)} %slice_bitcast_fusion.4), channel_id=1, source_target_pairs={{0,2},{1,3},{2,0},{3,1},{4,6},{5,7},{6,4},{7,5},{8,10},{9,11},{10,... | collective-permute-start | bytes 786440 | tf_op jit(solution)/shard_map/ppermute | solution.py:23
  98.9 14.5 %collective-permute-start.10 = (f32[2,64,512]{2,1,0:T(8,128)S(1)}, f32[2,64,512]{2,1,0:T(8,128)S(1)}, u32[]{:S(2)}, u32[]{:S(2)}) collective-permute-start(f32[2,64,512]{2,1,0:T(8,128)S(1)} %slice_bitcast_fusion.6), channel_id=1, source_target_pairs={{0,8},{4,12},{8,0},{12,4},{16,24},{20,28},{24,16},{28,20},{1,9},{5... | collective-permute-start | bytes 786440 | tf_op jit(solution)/shard_map/ppermute | solution.py:23
  101.7 14.9 %collective-permute-start.4 = (f32[2,128,256]{2,1,0:T(8,128)S(1)}, f32[2,128,256]{2,1,0:T(8,128)S(1)}, u32[]{:S(2)}, u32[]{:S(2)}) collective-permute-start(f32[2,128,256]{2,1,0:T(8,128)S(1)} %slice_bitcast_fusion.10), channel_id=1, source_target_pairs={{0,8},{4,12},{8,0},{12,4},{16,24},{20,28},{24,16},{28,20},{1,9},{5... | collective-permute-start | bytes 786440 | tf_op jit(solution)/shard_map/ppermute | solution.py:23
  111.5 14.7 %collective-permute-start.7 = (f32[2,128,256]{2,1,0:T(8,128)S(1)}, f32[2,128,256]{2,1,0:T(8,128)S(1)}, u32[]{:S(2)}, u32[]{:S(2)}) collective-permute-start(f32[2,128,256]{2,1,0:T(8,128)S(1)} %slice_bitcast_fusion.8), channel_id=1, source_target_pairs={{0,8},{4,12},{8,0},{12,4},{16,24},{20,28},{24,16},{28,20},{1,9},{5... | collective-permute-start | bytes 786440 | tf_op jit(solution)/shard_map/ppermute | solution.py:23
  113.5 9.2 %collective-permute-start.11 = (f32[1,64,512]{2,1,0:T(8,128)S(1)}, f32[1,64,512]{2,1,0:T(8,128)S(1)}, u32[]{:S(2)}, u32[]{:S(2)}) collective-permute-start(f32[1,64,512]{2,1,0:T(8,128)S(1)} %slice_bitcast_fusion.36), channel_id=1, source_target_pairs={{0,16},{4,20},{8,24},{12,28},{16,0},{20,4},{24,8},{28,12},{1,17},{... | collective-permute-start | bytes 393224 | tf_op jit(solution)/shard_map/ppermute | solution.py:23
  116.6 27.9 %collective-permute-start.5 = (f32[1,128,256]{2,1,0:T(8,128)S(1)}, f32[1,128,256]{2,1,0:T(8,128)S(1)}, u32[]{:S(2)}, u32[]{:S(2)}) collective-permute-start(f32[1,128,256]{2,1,0:T(8,128)S(1)} %slice_bitcast_fusion.40), channel_id=1, source_target_pairs={{0,16},{4,20},{8,24},{12,28},{16,0},{20,4},{24,8},{28,12},{1,17},{... | collective-permute-start | bytes 393224 | tf_op jit(solution)/shard_map/ppermute | solution.py:23
  122.7 10.8 %collective-permute-start.12 = (f32[1,64,512]{2,1,0:T(8,128)S(1)}, f32[1,64,512]{2,1,0:T(8,128)S(1)}, u32[]{:S(2)}, u32[]{:S(2)}) collective-permute-start(f32[1,64,512]{2,1,0:T(8,128)S(1)} %fusion.46), channel_id=1, source_target_pairs={{0,16},{4,20},{8,24},{12,28},{16,0},{20,4},{24,8},{28,12},{1,17},{... | collective-permute-start | bytes 393224 | tf_op jit(solution)/shard_map/ppermute | solution.py:23
  133.6 9.3 %collective-permute-start.13 = (f32[2,64,512]{2,1,0:T(8,128)S(1)}, f32[2,64,512]{2,1,0:T(8,128)S(1)}, u32[]{:S(2)}, u32[]{:S(2)}) collective-permute-start(f32[2,64,512]{2,1,0:T(8,128)S(1)} %get-tuple-element.27), channel_id=1, source_target_pairs={{0,8},{4,12},{8,0},{12,4},{16,24},{20,28},{24,16},{28,20},{1,9},{5... | collective-permute-start | bytes 786440 | tf_op jit(solution)/shard_map/ppermute | solution.py:23
  134.1 10.5 %collective-permute-start.8 = (f32[1,128,256]{2,1,0:T(8,128)S(1)}, f32[1,128,256]{2,1,0:T(8,128)S(1)}, u32[]{:S(2)}, u32[]{:S(2)}) collective-permute-start(f32[1,128,256]{2,1,0:T(8,128)S(1)} %slice_bitcast_fusion.38), channel_id=1, source_target_pairs={{0,16},{4,20},{8,24},{12,28},{16,0},{20,4},{24,8},{28,12},{1,17},{... | collective-permute-start | bytes 393224 | tf_op jit(solution)/shard_map/ppermute | solution.py:23
  142.9 12.6 %collective-permute-start.14 = (f32[4,64,512]{2,1,0:T(8,128)S(1)}, f32[4,64,512]{2,1,0:T(8,128)S(1)}, u32[]{:S(2)}, u32[]{:S(2)}) collective-permute-start(f32[4,64,512]{2,1,0:T(8,128)S(1)} %bitcast.281), channel_id=1, source_target_pairs={{0,4},{4,0},{8,12},{12,8},{16,20},{20,16},{24,28},{28,24},{1,5},{5... | collective-permute-start | bytes 1572872 | tf_op jit(solution)/shard_map/ppermute | solution.py:23
  (35 other events, 70.1 us)

commit v2 on v0

v2 whole, which is shorter than its diff:
```python
import functools

import jax
import jax.numpy as jnp
from jax import lax
from jax.experimental import pallas as pl
from jax.experimental.pallas import tpu as pltpu
from jax.sharding import PartitionSpec as P

HD = 128
GROUPS = 8
FACTOR = HD ** (-0.5)
LOG2_E = 1.4426950408889634
VMEM = pl.BlockSpec(memory_space=pltpu.VMEM)
PARAMS = pltpu.CompilerParams(vmem_limit_bytes=48 * 1024 * 1024)


def last_contract(left, right):
    return lax.dot_general(
        left, right, (((1,), (1,)), ((), ())), preferred_element_type=jnp.float32
    )


def rows_contract(left, right):
    return lax.dot_general(
        left, right, (((0,), (0,)), ((), ())), preferred_element_type=jnp.float32
    )


def plain_dot(left, right):
    return jnp.dot(left, right, preferred_element_type=jnp.float32)


def swap(array, axis, count, bit):
    pairs = [(device, device ^ bit) for device in range(count)]
    return lax.ppermute(array, axis, pairs)


def bits_of(count):
    return [1 << place for place in range(count.bit_length() - 1)]


def project_kernel(tile, inputs, key_weight, value_weight, queries, out_grad, keys, values, stats):
    reads, latents, columns = queries.shape
    head_count = columns // HD
    rows = inputs[...]
    keys[...] = plain_dot(rows, key_weight[...]).astype(jnp.bfloat16)
    values[...] = plain_dot(rows, value_weight[...]).astype(jnp.bfloat16)
    for read_index in range(reads):
        for head_index in range(head_count):
            cols = slice(head_index * HD, (head_index + 1) * HD)
            position = read_index * head_count + head_index

            @pl.loop(0, latents // tile)
            def _(step):
                at = pl.ds(pl.multiple_of(step * tile, tile), tile)
                scores = last_contract(keys[:, cols], queries[read_index, at, cols])
                scores = scores * (FACTOR * LOG2_E)
                weighted = last_contract(values[:, cols], out_grad[read_index, at, cols])
                top = jnp.max(scores, axis=0, keepdims=True)
                expos = jnp.exp2(scores - top)
                total = jnp.sum(expos, axis=0, keepdims=True)
                accum = jnp.sum(expos * weighted, axis=0, keepdims=True)
                stats[position : position + 1, at] = top + jnp.log2(total)
                lower = reads * head_count + position
                stats[lower : lower + 1, at] = accum / total


def merge_kernel(mine, theirs, merged):
    blocks = mine.shape[0] // 2
    own, other = mine[:blocks], theirs[:blocks]
    top = jnp.maximum(own, other)
    own_share = jnp.exp2(own - top)
    other_share = jnp.exp2(other - top)
    total = own_share + other_share
    merged[:blocks] = top + jnp.log2(total)
    merged[blocks:] = (mine[blocks:] * own_share + theirs[blocks:] * other_share) / total


def head_kernel(head_index, row_axis, head_axis, low, last, *refs):
    (inputs, keys, values, queries, out_grad, stats) = refs[:6]
    if last:
        (key_weight, value_weight, other_grads) = refs[6:9]
        (grads, query_keep, query_send, weight_keep, weight_send, input_keep, input_send) = refs[9:16]
        key_acc, value_acc, tile_ref, weights_ref, input_ref = refs[16:]
    else:
        (grads, query_keep, query_send, weight_keep, weight_send) = refs[6:11]
        key_acc, value_acc, tile_ref, weights_ref = refs[11:]
    reads, latents, _ = queries.shape
    head_count = stats.shape[0] // (2 * reads)
    pairs = GROUPS // 2
    tile = latents // pairs
    half = tile // 2
    me = lax.axis_index(row_axis) // low
    side = lax.rem(me, 2)
    mine = pl.ds(pl.multiple_of(side * half, half), half)
    yours = pl.ds(pl.multiple_of((1 - side) * half, half), half)
    key_acc[...] = jnp.zeros_like(key_acc)
    value_acc[...] = jnp.zeros_like(value_acc)
    for read_index in range(reads):
        position = read_index * head_count + head_index
        lower = reads * head_count + position

        @pl.loop(0, pairs)
        def _(slot):
            relative = (slot // (pairs // 2)) + 2 * lax.rem(slot, pairs // 2)
            pair = (me // 2) ^ relative
            at = pl.ds(pl.multiple_of(pair * tile, tile), tile)
            query_block = queries[read_index, at, :]
            grad_block = out_grad[read_index, at, :]
            scores = last_contract(keys[...], query_block) * (FACTOR * LOG2_E)
            weighted = last_contract(values[...], grad_block)
            probs = jnp.exp2(scores - stats[position : position + 1, at])
            score_grad = (probs * (weighted - stats[lower : lower + 1, at]) * FACTOR).astype(
                jnp.bfloat16
            )
            key_acc[...] += plain_dot(score_grad, query_block)
            value_acc[...] += plain_dot(probs.astype(jnp.bfloat16), grad_block)
            tile_ref[...] = rows_contract(score_grad, keys[...])
            query_keep[slot, read_index] = tile_ref[mine, :]
            query_send[slot, read_index] = tile_ref[yours, :]

    grads[:, :HD] = key_acc[...].astype(jnp.bfloat16)
    grads[:, HD:] = value_acc[...].astype(jnp.bfloat16)
    weights_ref[...] = rows_contract(inputs[...], grads[...])
    features = inputs.shape[1]
    piece = features // GROUPS
    for slot in range(pairs):
        relative = (slot // (pairs // 2)) + 2 * (slot % (pairs // 2))
        base = 2 * ((me // 2) ^ relative)
        weight_keep[slot] = weights_ref[pl.ds(pl.multiple_of((base + side) * piece, piece), piece), :]
        weight_send[slot] = weights_ref[
            pl.ds(pl.multiple_of((base + 1 - side) * piece, piece), piece), :
        ]
    if last:
        total = last_contract(grads[:, :HD], key_weight[:, HD:])
        total += last_contract(grads[:, HD:], value_weight[:, HD:])
        total += last_contract(other_grads[:, :HD], key_weight[:, :HD])
        total += last_contract(other_grads[:, HD:], value_weight[:, :HD])
        input_ref[...] = total
        place = lax.axis_index(head_axis)
        width = features // (2 * input_keep.shape[0])
        for relative in range(2 * input_keep.shape[0]):
            ref = input_send if relative % 2 else input_keep
            start = pl.multiple_of((place ^ relative) * width, width)
            ref[relative // 2] = input_ref[:, pl.ds(start, width)]


def assemble_kernel(row_axis, low, *refs):
    key_out, value_out = refs[-2:]
    piece = key_out.shape[0] // GROUPS
    me = lax.axis_index(row_axis) // low
    for head_index in range((len(refs) - 2) // 2):
        near, far = refs[2 * head_index : 2 * head_index + 2]
        cols = slice(head_index * HD, (head_index + 1) * HD)
        for slot in range(GROUPS // 2):
            relative = 2 * (slot // (GROUPS // 4) + 2 * (slot % (GROUPS // 4)))
            start = pl.multiple_of((me ^ relative) * piece, piece)
            key_out[pl.ds(start, piece), cols] = near[slot, :, :HD]
            value_out[pl.ds(start, piece), cols] = near[slot, :, HD:]
            start = pl.multiple_of((me ^ (relative + 1)) * piece, piece)
            key_out[pl.ds(start, piece), cols] = far[slot, :, :HD]
            value_out[pl.ds(start, piece), cols] = far[slot, :, HD:]


def shape_of(shape, dtype=jnp.float32):
    return jax.ShapeDtypeStruct(shape, dtype)


def reduce_bits(keep, send, count, bits):
    for index, bit in enumerate(bits):
        theirs = swap(send, "rows", count, bit)
        if index + 1 == len(bits):
            return keep + theirs
        middle = keep.shape[0] // 2
        send = keep[middle:] + theirs[middle:]
        keep = keep[:middle] + theirs[:middle]


def on_device(row_devices, head_devices, inputs, key_weight, value_weight, queries, out_grad):
    reads, latents, columns = queries.shape
    head_count = columns // HD
    row_count, features = inputs.shape
    blocks = reads * head_count
    low = row_devices // GROUPS
    group_bits = [bit * low for bit in bits_of(GROUPS)]
    tile = latents // (GROUPS // 2)

    keys, values, stats = pl.pallas_call(
        functools.partial(project_kernel, tile),
        out_shape=(
            shape_of((row_count, columns), jnp.bfloat16),
            shape_of((row_count, columns), jnp.bfloat16),
            shape_of((2 * blocks, latents)),
        ),
        in_specs=[VMEM] * 5,
        out_specs=(VMEM,) * 3,
        compiler_params=PARAMS,
        name="project",
    )(inputs, key_weight, value_weight, queries, out_grad)

    for bit in bits_of(row_devices):
        theirs = swap(stats, "rows", row_devices, bit)
        stats = pl.pallas_call(
            merge_kernel,
            out_shape=shape_of(stats.shape),
            in_specs=[VMEM] * 2,
            out_specs=VMEM,
            name="merge",
        )(stats, theirs)

    half = GROUPS // 2
    piece = features // GROUPS
    heads_out = []
    other_grads = None
    for head_index in range(head_count):
        last = head_index + 1 == head_count
        column = pl.BlockSpec((row_count, HD), lambda _, at=head_index: (0, at))
        stack = pl.BlockSpec((reads, latents, HD), lambda _, at=head_index: (0, 0, at))
        whole = lambda shape: pl.BlockSpec(shape, lambda _, rank=len(shape): (0,) * rank)
        operands = [inputs, keys, values, queries, out_grad, stats]
        in_specs = [whole(inputs.shape), column, column, stack, stack, whole(stats.shape)]
        out_shape = [
            shape_of((row_count, 2 * HD), jnp.bfloat16),
            shape_of((half, reads, latents // GROUPS, HD)),
            shape_of((half, reads, latents // GROUPS, HD)),
            shape_of((half, piece, 2 * HD)),
            shape_of((half, piece, 2 * HD)),
        ]
        scratch = [
            pltpu.VMEM((row_count, HD), jnp.float32),
            pltpu.VMEM((row_count, HD), jnp.float32),
            pltpu.VMEM((tile, HD), jnp.float32),
            pltpu.VMEM((features, 2 * HD), jnp.float32),
        ]
        if last:
            operands += [key_weight, value_weight, other_grads]
            in_specs += [whole(key_weight.shape), whole(value_weight.shape), whole(other_grads.shape)]
            share = (head_devices // 2, row_count, features // head_devices)
            out_shape += [shape_of(share), shape_of(share)]
            scratch += [pltpu.VMEM((row_count, features), jnp.float32)]
        results = pl.pallas_call(
            functools.partial(head_kernel, head_index, "rows", "heads", low, last),
            grid=(1,),
            out_shape=out_shape,
            in_specs=in_specs,
            out_specs=[whole(item.shape) for item in out_shape],
            scratch_shapes=scratch,
            compiler_params=PARAMS,
            name="head",
        )(*operands)
        other_grads = results[0]
        heads_out.append(results[1:])

    input_keep, input_send = heads_out[-1][4:]
    order_low = (lax.axis_index("rows") % low) ^ jnp.arange(low, dtype=jnp.int32)
    low_bits = [bit for bit in bits_of(row_devices) if bit < low]

    def scatter_low(block, axis):
        if low == 1:
            return block
        parts = jnp.moveaxis(
            block.reshape(block.shape[:axis] + (low, -1) + block.shape[axis + 1 :]), axis, 0
        )
        parts = jnp.take(parts, order_low, axis=0)
        for bit in low_bits:
            parts = parts.reshape((-1, 2) + parts.shape[1:])
            parts = parts[:, 0] + swap(parts[:, 1], "rows", row_devices, bit)
        return parts[0]

    def gather_low(block):
        if low == 1:
            return block
        parts = block[None]
        for bit in reversed(low_bits):
            theirs = swap(parts, "rows", row_devices, bit)
            parts = jnp.stack([parts, theirs], axis=1).reshape((-1,) + parts.shape[1:])
        parts = jnp.take(parts, order_low, axis=0)
        return parts.reshape((low * block.shape[0],) + block.shape[1:])

    query_parts = []
    assembled = []
    for head_index in range(head_count):
        query_keep, query_send, weight_keep, weight_send = heads_out[head_index][:4]
        mine = reduce_bits(weight_keep, weight_send, row_devices, group_bits)
        block = gather_low(scatter_low(mine[0], 0))[None]
        for bit in reversed(group_bits[1:]):
            block = jnp.concatenate([block, swap(block, "rows", row_devices, bit)], axis=0)
        assembled += [block, swap(block, "rows", row_devices, group_bits[0])]
        mine = reduce_bits(query_keep, query_send, row_devices, group_bits)
        query_parts.append(scatter_low(mine[0], 1))
    query_grad = jnp.concatenate(query_parts, axis=2)

    key_weight_grad, value_weight_grad = pl.pallas_call(
        functools.partial(assemble_kernel, "rows", low),
        out_shape=(shape_of((features, columns)),) * 2,
        in_specs=[VMEM] * len(assembled),
        out_specs=(VMEM,) * 2,
        compiler_params=PARAMS,
        name="assemble",
    )(*assembled)

    total = input_keep + swap(input_send, "heads", head_devices, 1)
    for bit in bits_of(head_devices)[1:]:
        pairs = total.reshape((-1, 2) + total.shape[1:])
        total = pairs[:, 0] + swap(pairs[:, 1], "heads", head_devices, bit)
    return (query_grad, key_weight_grad, value_weight_grad, total[0])


def solution(mesh):
    in_specs = (
        P("rows", None),
        P(None, "heads"),
        P(None, "heads"),
        P(None, None, "heads"),
        P(None, None, "heads"),
    )
    out_specs = (P(None, "rows", "heads"), P(None, "heads"), P(None, "heads"), P("rows", "heads"))

    def body(*args):
        return on_device(mesh.shape["rows"], mesh.shape["heads"], *args)

    return jax.shard_map(body, mesh=mesh, in_specs=in_specs, out_specs=out_specs, check_vma=False)
```

time: 296 us -> 101 us (0.34)
  waiting for transfers between devices: 161 us -> 23 us
  blocking collectives: 71.9 us -> 0 us
  starting transfers between devices: 0.3 us -> 41.7 us
  matrix products: 29.7 us -> 0 us
  Pallas kernels: 0 us -> 25.3 us
  between operations: 14.1 us -> 0.78 us
  local copies, waits for them, and re-layouts: 12.4 us -> 8.03 us
  other arithmetic: 5.86 us -> 1.95 us
    reduce_scatter x2 -> x0, waiting for transfers between devices: 93.1 us -> none  [the longest x1 67.7 us: on_device(): lax.psum_scatter(jnp.stack(pieces), 'rows', scatter_dimension=1, tiled=True)]
    psum x1 -> x0, waiting for transfers between devices: 67.6 us -> none  [on_device(): lax.psum((rows_contract(inputs, key_grad), rows_contract(inputs, value_gr...]
    ppermute x0 -> x23, starting transfers between devices: none -> 41.7 us  [swap(): return lax.ppermute(array, axis, pairs)]
    pmax x1 -> x0, blocking collectives: 38.8 us -> none  [on_device(): global_top = lax.pmax(tops, 'rows')]
    psum x1 -> x0, blocking collectives: 33.1 us -> none  [on_device(): lax.psum((totals * rescale, accums * rescale), 'rows')]
    dot_general x26 -> x0, matrix products: 29.7 us -> none  [the longest x10 17.4 us: last_contract(): lax.dot_general(left, right, (((1,), (1,)), ((), ())), preferred_element_...]
    pallas_call x0 -> x7, Pallas kernels: none -> 25.3 us  [the longest x2 12.6 us: on_device(): pl.pallas_call(functools.partial(head_kernel, head_index, 'rows', 'heads'...]
    ppermute x0 -> x23, waiting for transfers between devices: none -> 23 us  [swap(): return lax.ppermute(array, axis, pairs)]
  transfers between devices with their start and end apart: 3 -> 23, of which waited for: 3 -> 12; matrix products, arithmetic and copies ran while one was open for 4% -> 2% of each run, Pallas kernels for 0% -> 7%
where the time goes in v2:
time: 101 us
  starting transfers between devices  41.7 us (41%)
  Pallas kernels  25.3 us (25%)
  waiting for transfers between devices  23 us (23%)
  local copies, waits for them, and re-layouts  8.03 us (8%)
  other arithmetic  1.95 us (2%)
    ppermute x23, starting transfers between devices, swap(): return lax.ppermute(array, axis, pairs)  41.7 us
    ppermute x23, waiting for transfers between devices, swap(): return lax.ppermute(array, axis, pairs)  23 us
    pallas_call x2, Pallas kernels, on_device(): pl.pallas_call(functools.partial(head_kernel, head_index, 'rows', 'heads'...  12.6 us
    unnamed x32, local copies, waits for them, and re-layouts  8.01 us
    pallas_call x1, Pallas kernels, on_device(): pl.pallas_call(functools.partial(project_kernel, tile), out_shape=(shape_...  7.43 us
    pallas_call x3, Pallas kernels, on_device(): pl.pallas_call(merge_kernel, out_shape=shape_of(stats.shape), in_specs=[V...  4.25 us
  transfers between devices with their start and end apart: 23, of which 12 were waited for; matrix products, arithmetic and copies ran while one was open for 2% of the time, Pallas kernels for 7%

profile of v2, /device:TPU:0, one launch (start us, length us, event | category | flops | bytes accessed | tf_op | source)
XLA Modules:
  0.0 100.8 jit_solution(6966472394549258272)
XLA Ops:
  6.0 7.4 %project.1 = (bf16[512,256]{1,0:T(8,128)(2,1)S(1)}, bf16[512,256]{1,0:T(8,128)(2,1)S(1)}, f32[8,1024]{1,0:T(8,128)S(1)}) custom-call(bf16[512,512]{1,0:T(8,128)(2,1)S(1)} %copy-done.4, bf16[512,256]{1,0:T(8,128)(2,1)S(1)} %copy-done.6, bf16[512,256]{1,0:T(8,128)(2,1)S(1)} %copy-done.8, bf16[2,1024,256]{2,1,0:T(8,128)(2,1)S(1)} %copy-done, ...), custom_call_target="tpu_custom_call" | custom-call | tf_op jit(solution)/shard_map/project/pallas_call | solution.py:189
  13.5 3.0 %collective-permute-start = (f32[8,1024]{1,0:T(8,128)S(1)}, f32[8,1024]{1,0:T(8,128)S(1)}, u32[]{:S(2)}, u32[]{:S(2)}) collective-permute-start(f32[8,1024]{1,0:T(8,128)S(1)} %get-tuple-element.22.mine), channel_id=1, source_target_pairs={{0,4},{4,0},{8,12},{12,8},{16,20},{20,16},{24,28},{28,24},{1,5},{5... | collective-permute-start | bytes 98312 | tf_op jit(solution)/shard_map/ppermute | solution.py:36
  16.5 1.9 %collective-permute-done.theirs = f32[8,1024]{1,0:T(8,128)S(1)} collective-permute-done((f32[8,1024]{1,0:T(8,128)S(1)}, f32[8,1024]{1,0:T(8,128)S(1)}, u32[]{:S(2)}, u32[]{:S(2)}) %collective-permute-start) | collective-permute-done | bytes 32800 | tf_op jit(solution)/shard_map/ppermute | solution.py:36
  20.4 2.1 %collective-permute-start.1 = (f32[8,1024]{1,0:T(8,128)}, f32[8,1024]{1,0:T(8,128)S(1)}, u32[]{:S(2)}, u32[]{:S(2)}) collective-permute-start(f32[8,1024]{1,0:T(8,128)} %merge.3.mine), channel_id=1, source_target_pairs={{0,8},{4,12},{8,0},{12,4},{16,24},{20,28},{24,16},{28,20},{1,9},{5... | collective-permute-start | bytes 98312 | tf_op jit(solution)/shard_map/ppermute | solution.py:36
  22.5 2.1 %collective-permute-done.1.theirs = f32[8,1024]{1,0:T(8,128)S(1)} collective-permute-done((f32[8,1024]{1,0:T(8,128)}, f32[8,1024]{1,0:T(8,128)S(1)}, u32[]{:S(2)}, u32[]{:S(2)}) %collective-permute-start.1) | collective-permute-done | bytes 32800 | tf_op jit(solution)/shard_map/ppermute | solution.py:36
  26.7 3.0 %collective-permute-start.2 = (f32[8,1024]{1,0:T(8,128)}, f32[8,1024]{1,0:T(8,128)S(1)}, u32[]{:S(2)}, u32[]{:S(2)}) collective-permute-start(f32[8,1024]{1,0:T(8,128)} %merge.4.mine), channel_id=1, source_target_pairs={{0,16},{4,20},{8,24},{12,28},{16,0},{20,4},{24,8},{28,12},{1,17},{... | collective-permute-start | bytes 98312 | tf_op jit(solution)/shard_map/ppermute | solution.py:36
  29.7 2.1 %collective-permute-done.2.theirs = f32[8,1024]{1,0:T(8,128)S(1)} collective-permute-done((f32[8,1024]{1,0:T(8,128)}, f32[8,1024]{1,0:T(8,128)S(1)}, u32[]{:S(2)}, u32[]{:S(2)}) %collective-permute-start.2) | collective-permute-done | bytes 32800 | tf_op jit(solution)/shard_map/ppermute | solution.py:36
  34.6 5.4 %head.2 = (bf16[512,256]{1,0:T(8,128)(2,1)S(1)}, f32[4,2,128,128]{3,2,1,0:T(8,128)S(1)}, f32[4,2,128,128]{3,2,1,0:T(8,128)S(1)}, f32[4,64,256]{2,1,0:T(8,128)S(1)}, f32[4,64,256]{2,1,0:T(8,128)S(1)}) custom-call(bf16[512,512]{1,0:T(8,128)(2,1)S(1)} %copy-done.5, bf16[512,256]{1,0:T(8,128)(2,1)S(1)} %get-tuple-element.20.refs_1_, ...), custom_call_target="tpu_custom_call" | custom-call | tf_op jit(solution)/shard_map/head/pallas_call | solution.py:242
  40.0 1.9 %collective-permute-start.9 = (f32[4,64,256]{2,1,0:T(8,128)S(1)}, f32[4,64,256]{2,1,0:T(8,128)S(1)}, u32[]{:S(2)}, u32[]{:S(2)}) collective-permute-start(f32[4,64,256]{2,1,0:T(8,128)S(1)} %get-tuple-element.29), channel_id=1, source_target_pairs={{0,4},{4,0},{8,12},{12,8},{16,20},{20,16},{24,28},{28,24},{1,5},{5... | collective-permute-start | bytes 786440 | tf_op jit(solution)/shard_map/ppermute | solution.py:36
  41.9 7.2 %head.3 = (bf16[512,256]{1,0:T(8,128)(2,1)}, f32[4,2,128,128]{3,2,1,0:T(8,128)S(1)}, f32[4,2,128,128]{3,2,1,0:T(8,128)S(1)}, f32[4,64,256]{2,1,0:T(8,128)S(1)}, ...) custom-call(bf16[512,512]{1,0:T(8,128)(2,1)S(1)} %copy-done.5, ...), custom_call_target="tpu_custom_call" | custom-call | tf_op jit(solution)/shard_map/head/pallas_call | solution.py:242
  49.3 1.8 %collective-permute-start.3 = (f32[4,2,128,128]{3,2,1,0:T(8,128)S(1)}, f32[4,2,128,128]{3,2,1,0:T(8,128)S(1)}, u32[]{:S(2)}, u32[]{:S(2)}) collective-permute-start(f32[4,2,128,128]{3,2,1,0:T(8,128)S(1)} %get-tuple-element.24), channel_id=1, source_target_pairs={{0,4},{4,0},{8,12},{12,8},{16,20},{20,16},{24,28},{28,24},{1,5},{5... | collective-permute-start | bytes 1572872 | tf_op jit(solution)/shard_map/ppermute | solution.py:36
  51.4 2.0 %collective-permute-start.10 = (f32[2,64,256]{2,1,0:T(8,128)S(1)}, f32[2,64,256]{2,1,0:T(8,128)S(1)}, u32[]{:S(2)}, u32[]{:S(2)}) collective-permute-start(f32[2,64,256]{2,1,0:T(8,128)S(1)} %get-tuple-element.43), channel_id=1, source_target_pairs={{0,8},{4,12},{8,0},{12,4},{16,24},{20,28},{24,16},{28,20},{1,9},{5... | collective-permute-start | bytes 393224 | tf_op jit(solution)/shard_map/ppermute | solution.py:36
  53.4 5.0 %collective-permute-done.15 = f32[4,64,256]{2,1,0:T(8,128)S(1)} collective-permute-done((f32[4,64,256]{2,1,0:T(8,128)S(1)}, f32[4,64,256]{2,1,0:T(8,128)S(1)}, u32[]{:S(2)}, u32[]{:S(2)}) %collective-permute-start.15) | collective-permute-done | bytes 262176 | tf_op jit(solution)/shard_map/ppermute | solution.py:36
  58.4 1.7 %collective-permute-start.16 = (f32[2,64,256]{2,1,0:T(8,128)S(1)}, f32[2,64,256]{2,1,0:T(8,128)S(1)}, u32[]{:S(2)}, u32[]{:S(2)}) collective-permute-start(f32[2,64,256]{2,1,0:T(8,128)S(1)} %get-tuple-element.41), channel_id=1, source_target_pairs={{0,8},{4,12},{8,0},{12,4},{16,24},{20,28},{24,16},{28,20},{1,9},{5... | collective-permute-start | bytes 393224 | tf_op jit(solution)/shard_map/ppermute | solution.py:36
  60.1 2.9 %collective-permute-start.11 = (f32[1,64,256]{2,1,0:T(8,128)S(1)}, f32[1,64,256]{2,1,0:T(8,128)S(1)}, u32[]{:S(2)}, u32[]{:S(2)}) collective-permute-start(f32[1,64,256]{2,1,0:T(8,128)S(1)} %slice_add_fusion.14), channel_id=1, source_target_pairs={{0,16},{4,20},{8,24},{12,28},{16,0},{20,4},{24,8},{28,12},{1,17},{... | collective-permute-start | bytes 196616 | tf_op jit(solution)/shard_map/ppermute | solution.py:36
  63.4 3.4 %collective-permute-start.17 = (f32[1,64,256]{2,1,0:T(8,128)S(1)}, f32[1,64,256]{2,1,0:T(8,128)S(1)}, u32[]{:S(2)}, u32[]{:S(2)}) collective-permute-start(f32[1,64,256]{2,1,0:T(8,128)S(1)} %slice_add_fusion.12), channel_id=1, source_target_pairs={{0,16},{4,20},{8,24},{12,28},{16,0},{20,4},{24,8},{28,12},{1,17},{... | collective-permute-start | bytes 196616 | tf_op jit(solution)/shard_map/ppermute | solution.py:36
  69.5 2.6 %collective-permute-start.18 = (f32[1,64,256]{2,1,0:T(8,128)S(1)}, f32[1,64,256]{2,1,0:T(8,128)S(1)}, u32[]{:S(2)}, u32[]{:S(2)}) collective-permute-start(f32[1,64,256]{2,1,0:T(8,128)S(1)} %fusion.6), channel_id=1, source_target_pairs={{0,16},{4,20},{8,24},{12,28},{16,0},{20,4},{24,8},{28,12},{1,17},{... | collective-permute-start | bytes 196616 | tf_op jit(solution)/shard_map/ppermute | solution.py:36
  73.2 2.0 %collective-permute-start.13 = (f32[2,64,256]{2,1,0:T(8,128)S(1)}, f32[2,64,256]{2,1,0:T(8,128)S(1)}, u32[]{:S(2)}, u32[]{:S(2)}) collective-permute-start(f32[2,64,256]{2,1,0:T(8,128)S(1)} %pad_maximum_fusion.3), channel_id=1, source_target_pairs={{0,8},{4,12},{8,0},{12,4},{16,24},{20,28},{24,16},{28,20},{1,9},{5... | collective-permute-start | bytes 393224 | tf_op jit(solution)/shard_map/ppermute | solution.py:36
  75.1 2.9 %collective-permute-start.19 = (f32[2,64,256]{2,1,0:T(8,128)S(1)}, f32[2,64,256]{2,1,0:T(8,128)S(1)}, u32[]{:S(2)}, u32[]{:S(2)}) collective-permute-start(f32[2,64,256]{2,1,0:T(8,128)S(1)} %pad_maximum_fusion.4), channel_id=1, source_target_pairs={{0,8},{4,12},{8,0},{12,4},{16,24},{20,28},{24,16},{28,20},{1,9},{5... | collective-permute-start | bytes 393224 | tf_op jit(solution)/shard_map/ppermute | solution.py:36
  78.3 2.1 %collective-permute-start.7 = (f32[2,2,128,128]{3,2,1,0:T(8,128)S(1)}, f32[2,2,128,128]{3,2,1,0:T(8,128)S(1)}, u32[]{:S(2)}, u32[]{:S(2)}) collective-permute-start(f32[2,2,128,128]{3,2,1,0:T(8,128)S(1)} %get-tuple-element.39), channel_id=1, source_target_pairs={{0,8},{4,12},{8,0},{12,4},{16,24},{20,28},{24,16},{28,20},{1,9},{5... | collective-permute-start | bytes 786440 | tf_op jit(solution)/shard_map/ppermute | solution.py:36
  84.3 3.2 %collective-permute-done.4 = f32[2,2,128,128]{3,2,1,0:T(8,128)S(1)} collective-permute-done((f32[2,2,128,128]{3,2,1,0:T(8,128)S(1)}, f32[2,2,128,128]{3,2,1,0:T(8,128)S(1)}, u32[]{:S(2)}, u32[]{:S(2)}) %collective-permute-start.4) | collective-permute-done | bytes 262176 | tf_op jit(solution)/shard_map/ppermute | solution.py:36
  87.5 2.7 %collective-permute-start.5 = (f32[1,2,128,128]{3,2,1,0:T(8,128)S(1)}, f32[1,2,128,128]{3,2,1,0:T(8,128)S(1)}, u32[]{:S(2)}, u32[]{:S(2)}) collective-permute-start(f32[1,2,128,128]{3,2,1,0:T(8,128)S(1)} %slice_add_fusion.10), channel_id=1, source_target_pairs={{0,16},{4,20},{8,24},{12,28},{16,0},{20,4},{24,8},{28,12},{1,17},{... | collective-permute-start | bytes 393224 | tf_op jit(solution)/shard_map/ppermute | solution.py:36
  91.7 2.7 %collective-permute-start.8 = (f32[1,2,128,128]{3,2,1,0:T(8,128)S(1)}, f32[1,2,128,128]{3,2,1,0:T(8,128)S(1)}, u32[]{:S(2)}, u32[]{:S(2)}) collective-permute-start(f32[1,2,128,128]{3,2,1,0:T(8,128)S(1)} %slice_add_fusion.8), channel_id=1, source_target_pairs={{0,16},{4,20},{8,24},{12,28},{16,0},{20,4},{24,8},{28,12},{1,17},{... | collective-permute-start | bytes 393224 | tf_op jit(solution)/shard_map/ppermute | solution.py:36
  95.4 3.6 %collective-permute-done.8 = f32[1,2,128,128]{3,2,1,0:T(8,128)S(1)} collective-permute-done((f32[1,2,128,128]{3,2,1,0:T(8,128)S(1)}, f32[1,2,128,128]{3,2,1,0:T(8,128)S(1)}, u32[]{:S(2)}, u32[]{:S(2)}) %collective-permute-start.8) | collective-permute-done | bytes 131104 | tf_op jit(solution)/shard_map/ppermute | solution.py:36
  (81 shorter events, 25.5 us)
Async XLA Ops:
  6.0 27.8 %copy-start.5 = (bf16[512,512]{1,0:T(8,128)(2,1)S(1)}, bf16[512,512]{1,0:T(8,128)(2,1)}, u32[]{:S(2)}) copy-start(bf16[512,512]{1,0:T(8,128)(2,1)} %refs_0_.3) | copy-start | bytes 1572868
  13.5 4.9 %collective-permute-start = (f32[8,1024]{1,0:T(8,128)S(1)}, f32[8,1024]{1,0:T(8,128)S(1)}, u32[]{:S(2)}, u32[]{:S(2)}) collective-permute-start(f32[8,1024]{1,0:T(8,128)S(1)} %get-tuple-element.22.mine), channel_id=1, source_target_pairs={{0,4},{4,0},{8,12},{12,8},{16,20},{20,16},{24,28},{28,24},{1,5},{5... | collective-permute-start | bytes 98312 | tf_op jit(solution)/shard_map/ppermute | solution.py:36
  20.4 4.2 %collective-permute-start.1 = (f32[8,1024]{1,0:T(8,128)}, f32[8,1024]{1,0:T(8,128)S(1)}, u32[]{:S(2)}, u32[]{:S(2)}) collective-permute-start(f32[8,1024]{1,0:T(8,128)} %merge.3.mine), channel_id=1, source_target_pairs={{0,8},{4,12},{8,0},{12,4},{16,24},{20,28},{24,16},{28,20},{1,9},{5... | collective-permute-start | bytes 98312 | tf_op jit(solution)/shard_map/ppermute | solution.py:36
  26.7 5.1 %collective-permute-start.2 = (f32[8,1024]{1,0:T(8,128)}, f32[8,1024]{1,0:T(8,128)S(1)}, u32[]{:S(2)}, u32[]{:S(2)}) collective-permute-start(f32[8,1024]{1,0:T(8,128)} %merge.4.mine), channel_id=1, source_target_pairs={{0,16},{4,20},{8,24},{12,28},{16,0},{20,4},{24,8},{28,12},{1,17},{... | collective-permute-start | bytes 98312 | tf_op jit(solution)/shard_map/ppermute | solution.py:36
  40.0 11.3 %collective-permute-start.9 = (f32[4,64,256]{2,1,0:T(8,128)S(1)}, f32[4,64,256]{2,1,0:T(8,128)S(1)}, u32[]{:S(2)}, u32[]{:S(2)}) collective-permute-start(f32[4,64,256]{2,1,0:T(8,128)S(1)} %get-tuple-element.29), channel_id=1, source_target_pairs={{0,4},{4,0},{8,12},{12,8},{16,20},{20,16},{24,28},{28,24},{1,5},{5... | collective-permute-start | bytes 786440 | tf_op jit(solution)/shard_map/ppermute | solution.py:36
  49.1 9.2 %collective-permute-start.15 = (f32[4,64,256]{2,1,0:T(8,128)S(1)}, f32[4,64,256]{2,1,0:T(8,128)S(1)}, u32[]{:S(2)}, u32[]{:S(2)}) collective-permute-start(f32[4,64,256]{2,1,0:T(8,128)S(1)} %get-tuple-element.31), channel_id=1, source_target_pairs={{0,4},{4,0},{8,12},{12,8},{16,20},{20,16},{24,28},{28,24},{1,5},{5... | collective-permute-start | bytes 786440 | tf_op jit(solution)/shard_map/ppermute | solution.py:36
  49.3 28.7 %collective-permute-start.3 = (f32[4,2,128,128]{3,2,1,0:T(8,128)S(1)}, f32[4,2,128,128]{3,2,1,0:T(8,128)S(1)}, u32[]{:S(2)}, u32[]{:S(2)}) collective-permute-start(f32[4,2,128,128]{3,2,1,0:T(8,128)S(1)} %get-tuple-element.24), channel_id=1, source_target_pairs={{0,4},{4,0},{8,12},{12,8},{16,20},{20,16},{24,28},{28,24},{1,5},{5... | collective-permute-start | bytes 1572872 | tf_op jit(solution)/shard_map/ppermute | solution.py:36
  51.1 27.1 %collective-permute-start.6 = (f32[4,2,128,128]{3,2,1,0:T(8,128)S(1)}, f32[4,2,128,128]{3,2,1,0:T(8,128)S(1)}, u32[]{:S(2)}, u32[]{:S(2)}) collective-permute-start(f32[4,2,128,128]{3,2,1,0:T(8,128)S(1)} %get-tuple-element.27), channel_id=1, source_target_pairs={{0,4},{4,0},{8,12},{12,8},{16,20},{20,16},{24,28},{28,24},{1,5},{5... | collective-permute-start | bytes 1572872 | tf_op jit(solution)/shard_map/ppermute | solution.py:36
  51.4 29.0 %collective-permute-start.21 = (f32[2,512,128]{2,1,0:T(8,128)S(1)}, f32[2,512,128]{2,1,0:T(8,128)S(1)}, u32[]{:S(2)}, u32[]{:S(2)}) collective-permute-start(f32[2,512,128]{2,1,0:T(8,128)S(1)} %get-tuple-element.35), channel_id=1, source_target_pairs={{0,1},{1,0},{2,3},{3,2},{4,5},{5,4},{6,7},{7,6},{8,9},{9,8},{10,11... | collective-permute-start | bytes 1572872 | tf_op jit(solution)/shard_map/ppermute | solution.py:36
  51.4 8.7 %collective-permute-start.10 = (f32[2,64,256]{2,1,0:T(8,128)S(1)}, f32[2,64,256]{2,1,0:T(8,128)S(1)}, u32[]{:S(2)}, u32[]{:S(2)}) collective-permute-start(f32[2,64,256]{2,1,0:T(8,128)S(1)} %get-tuple-element.43), channel_id=1, source_target_pairs={{0,8},{4,12},{8,0},{12,4},{16,24},{20,28},{24,16},{28,20},{1,9},{5... | collective-permute-start | bytes 393224 | tf_op jit(solution)/shard_map/ppermute | solution.py:36
  58.4 5.0 %collective-permute-start.16 = (f32[2,64,256]{2,1,0:T(8,128)S(1)}, f32[2,64,256]{2,1,0:T(8,128)S(1)}, u32[]{:S(2)}, u32[]{:S(2)}) collective-permute-start(f32[2,64,256]{2,1,0:T(8,128)S(1)} %get-tuple-element.41), channel_id=1, source_target_pairs={{0,8},{4,12},{8,0},{12,4},{16,24},{20,28},{24,16},{28,20},{1,9},{5... | collective-permute-start | bytes 393224 | tf_op jit(solution)/shard_map/ppermute | solution.py:36
  60.1 7.7 %collective-permute-start.11 = (f32[1,64,256]{2,1,0:T(8,128)S(1)}, f32[1,64,256]{2,1,0:T(8,128)S(1)}, u32[]{:S(2)}, u32[]{:S(2)}) collective-permute-start(f32[1,64,256]{2,1,0:T(8,128)S(1)} %slice_add_fusion.14), channel_id=1, source_target_pairs={{0,16},{4,20},{8,24},{12,28},{16,0},{20,4},{24,8},{28,12},{1,17},{... | collective-permute-start | bytes 196616 | tf_op jit(solution)/shard_map/ppermute | solution.py:36
  63.4 6.1 %collective-permute-start.17 = (f32[1,64,256]{2,1,0:T(8,128)S(1)}, f32[1,64,256]{2,1,0:T(8,128)S(1)}, u32[]{:S(2)}, u32[]{:S(2)}) collective-permute-start(f32[1,64,256]{2,1,0:T(8,128)S(1)} %slice_add_fusion.12), channel_id=1, source_target_pairs={{0,16},{4,20},{8,24},{12,28},{16,0},{20,4},{24,8},{28,12},{1,17},{... | collective-permute-start | bytes 196616 | tf_op jit(solution)/shard_map/ppermute | solution.py:36
  67.8 5.3 %collective-permute-start.12 = (f32[1,64,256]{2,1,0:T(8,128)S(1)}, f32[1,64,256]{2,1,0:T(8,128)S(1)}, u32[]{:S(2)}, u32[]{:S(2)}) collective-permute-start(f32[1,64,256]{2,1,0:T(8,128)S(1)} %fusion.7), channel_id=1, source_target_pairs={{0,16},{4,20},{8,24},{12,28},{16,0},{20,4},{24,8},{28,12},{1,17},{... | collective-permute-start | bytes 196616 | tf_op jit(solution)/shard_map/ppermute | solution.py:36
  69.5 5.6 %collective-permute-start.18 = (f32[1,64,256]{2,1,0:T(8,128)S(1)}, f32[1,64,256]{2,1,0:T(8,128)S(1)}, u32[]{:S(2)}, u32[]{:S(2)}) collective-permute-start(f32[1,64,256]{2,1,0:T(8,128)S(1)} %fusion.6), channel_id=1, source_target_pairs={{0,16},{4,20},{8,24},{12,28},{16,0},{20,4},{24,8},{28,12},{1,17},{... | collective-permute-start | bytes 196616 | tf_op jit(solution)/shard_map/ppermute | solution.py:36
  73.2 8.9 %collective-permute-start.13 = (f32[2,64,256]{2,1,0:T(8,128)S(1)}, f32[2,64,256]{2,1,0:T(8,128)S(1)}, u32[]{:S(2)}, u32[]{:S(2)}) collective-permute-start(f32[2,64,256]{2,1,0:T(8,128)S(1)} %pad_maximum_fusion.3), channel_id=1, source_target_pairs={{0,8},{4,12},{8,0},{12,4},{16,24},{20,28},{24,16},{28,20},{1,9},{5... | collective-permute-start | bytes 393224 | tf_op jit(solution)/shard_map/ppermute | solution.py:36
  75.1 7.9 %collective-permute-start.19 = (f32[2,64,256]{2,1,0:T(8,128)S(1)}, f32[2,64,256]{2,1,0:T(8,128)S(1)}, u32[]{:S(2)}, u32[]{:S(2)}) collective-permute-start(f32[2,64,256]{2,1,0:T(8,128)S(1)} %pad_maximum_fusion.4), channel_id=1, source_target_pairs={{0,8},{4,12},{8,0},{12,4},{16,24},{20,28},{24,16},{28,20},{1,9},{5... | collective-permute-start | bytes 393224 | tf_op jit(solution)/shard_map/ppermute | solution.py:36
  78.1 9.4 %collective-permute-start.4 = (f32[2,2,128,128]{3,2,1,0:T(8,128)S(1)}, f32[2,2,128,128]{3,2,1,0:T(8,128)S(1)}, u32[]{:S(2)}, u32[]{:S(2)}) collective-permute-start(f32[2,2,128,128]{3,2,1,0:T(8,128)S(1)} %get-tuple-element.37), channel_id=1, source_target_pairs={{0,8},{4,12},{8,0},{12,4},{16,24},{20,28},{24,16},{28,20},{1,9},{5... | collective-permute-start | bytes 786440 | tf_op jit(solution)/shard_map/ppermute | solution.py:36
  78.3 13.4 %collective-permute-start.7 = (f32[2,2,128,128]{3,2,1,0:T(8,128)S(1)}, f32[2,2,128,128]{3,2,1,0:T(8,128)S(1)}, u32[]{:S(2)}, u32[]{:S(2)}) collective-permute-start(f32[2,2,128,128]{3,2,1,0:T(8,128)S(1)} %get-tuple-element.39), channel_id=1, source_target_pairs={{0,8},{4,12},{8,0},{12,4},{16,24},{20,28},{24,16},{28,20},{1,9},{5... | collective-permute-start | bytes 786440 | tf_op jit(solution)/shard_map/ppermute | solution.py:36
  80.5 13.9 %collective-permute-start.22 = (f32[1,512,128]{2,1,0:T(8,128)S(1)}, f32[1,512,128]{2,1,0:T(8,128)S(1)}, u32[]{:S(2)}, u32[]{:S(2)}) collective-permute-start(f32[1,512,128]{2,1,0:T(8,128)S(1)} %slice_bitcast_fusion), channel_id=1, source_target_pairs={{0,2},{1,3},{2,0},{3,1},{4,6},{5,7},{6,4},{7,5},{8,10},{9,11},{10,... | collective-permute-start | bytes 786440 | tf_op jit(solution)/shard_map/ppermute | solution.py:36
  82.1 17.7 %collective-permute-start.14 = (f32[4,64,256]{2,1,0:T(8,128)S(1)}, f32[4,64,256]{2,1,0:T(8,128)S(1)}, u32[]{:S(2)}, u32[]{:S(2)}) collective-permute-start(f32[4,64,256]{2,1,0:T(8,128)S(1)} %pad_maximum_fusion.1.refs_0_), channel_id=1, source_target_pairs={{0,4},{4,0},{8,12},{12,8},{16,20},{20,16},{24,28},{28,24},{1,5},{5... | collective-permute-start | bytes 786440 | tf_op jit(solution)/shard_map/ppermute | solution.py:36
  83.1 16.7 %collective-permute-start.20 = (f32[4,64,256]{2,1,0:T(8,128)S(1)}, f32[4,64,256]{2,1,0:T(8,128)S(1)}, u32[]{:S(2)}, u32[]{:S(2)}) collective-permute-start(f32[4,64,256]{2,1,0:T(8,128)S(1)} %pad_maximum_fusion.2.refs_2_), channel_id=1, source_target_pairs={{0,4},{4,0},{8,12},{12,8},{16,20},{20,16},{24,28},{28,24},{1,5},{5... | collective-permute-start | bytes 786440 | tf_op jit(solution)/shard_map/ppermute | solution.py:36
  87.5 7.9 %collective-permute-start.5 = (f32[1,2,128,128]{3,2,1,0:T(8,128)S(1)}, f32[1,2,128,128]{3,2,1,0:T(8,128)S(1)}, u32[]{:S(2)}, u32[]{:S(2)}) collective-permute-start(f32[1,2,128,128]{3,2,1,0:T(8,128)S(1)} %slice_add_fusion.10), channel_id=1, source_target_pairs={{0,16},{4,20},{8,24},{12,28},{16,0},{20,4},{24,8},{28,12},{1,17},{... | collective-permute-start | bytes 393224 | tf_op jit(solution)/shard_map/ppermute | solution.py:36
  91.7 7.3 %collective-permute-start.8 = (f32[1,2,128,128]{3,2,1,0:T(8,128)S(1)}, f32[1,2,128,128]{3,2,1,0:T(8,128)S(1)}, u32[]{:S(2)}, u32[]{:S(2)}) collective-permute-start(f32[1,2,128,128]{3,2,1,0:T(8,128)S(1)} %slice_add_fusion.8), channel_id=1, source_target_pairs={{0,16},{4,20},{8,24},{12,28},{16,0},{20,4},{24,8},{28,12},{1,17},{... | collective-permute-start | bytes 393224 | tf_op jit(solution)/shard_map/ppermute | solution.py:36
  (15 other events, 90.4 us)

commit v3 on v2

--- a/solution.py
+++ b/solution.py
@@ -12,7 +12,8 @@
 FACTOR = HD ** (-0.5)
 LOG2_E = 1.4426950408889634
 VMEM = pl.BlockSpec(memory_space=pltpu.VMEM)
-PARAMS = pltpu.CompilerParams(vmem_limit_bytes=48 * 1024 * 1024)
+HBM = pl.BlockSpec(memory_space=pltpu.HBM)
+PARAMS = pltpu.CompilerParams(vmem_limit_bytes=24 * 1024 * 1024)
 
 
 def last_contract(left, right):
@@ -40,20 +41,39 @@
     return [1 << place for place in range(count.bit_length() - 1)]
 
 
-def project_kernel(tile, inputs, key_weight, value_weight, queries, out_grad, keys, values, stats):
+def project_kernel(
+    tile, inputs_hbm, key_weight_hbm, value_weight_hbm, queries_hbm, out_grad_hbm,
+    keys, values, stats, inputs, key_weight, value_weight, queries, out_grad, local, sems
+):
+    loads = [
+        pltpu.make_async_copy(source, target, sems.at[index])
+        for index, (source, target) in enumerate([
+            (inputs_hbm, inputs),
+            (key_weight_hbm, key_weight),
+            (value_weight_hbm, value_weight),
+            (queries_hbm, queries),
+            (out_grad_hbm, out_grad),
+        ])
+    ]
+    for load in loads:
+        load.start()
     reads, latents, columns = queries.shape
     head_count = columns // HD
-    rows = inputs[...]
-    keys[...] = plain_dot(rows, key_weight[...]).astype(jnp.bfloat16)
-    values[...] = plain_dot(rows, value_weight[...]).astype(jnp.bfloat16)
-    for read_index in range(reads):
-        for head_index in range(head_count):
-            cols = slice(head_index * HD, (head_index + 1) * HD)
-            position = read_index * head_count + head_index
-
-            @pl.loop(0, latents // tile)
-            def _(step):
-                at = pl.ds(pl.multiple_of(step * tile, tile), tile)
+    for load in loads[:2]:
+        load.wait()
+    keys[...] = plain_dot(inputs[...], key_weight[...]).astype(jnp.bfloat16)
+    loads[2].wait()
+    values[...] = plain_dot(inputs[...], value_weight[...]).astype(jnp.bfloat16)
+    for load in loads[3:]:
+        load.wait()
+
+    @pl.loop(0, latents // tile)
+    def _(step):
+        at = pl.ds(pl.multiple_of(step * tile, tile), tile)
+        for read_index in range(reads):
+            for head_index in range(head_count):
+                cols = slice(head_index * HD, (head_index + 1) * HD)
+                position = read_index * head_count + head_index
                 scores = last_contract(keys[:, cols], queries[read_index, at, cols])
                 scores = scores * (FACTOR * LOG2_E)
                 weighted = last_contract(values[:, cols], out_grad[read_index, at, cols])
@@ -61,33 +81,36 @@
                 expos = jnp.exp2(scores - top)
                 total = jnp.sum(expos, axis=0, keepdims=True)
                 accum = jnp.sum(expos * weighted, axis=0, keepdims=True)
-                stats[position : position + 1, at] = top + jnp.log2(total)
+                local[position : position + 1, at] = top + jnp.log2(total)
                 lower = reads * head_count + position
-                stats[lower : lower + 1, at] = accum / total
-
-
-def merge_kernel(mine, theirs, merged):
-    blocks = mine.shape[0] // 2
-    own, other = mine[:blocks], theirs[:blocks]
-    top = jnp.maximum(own, other)
-    own_share = jnp.exp2(own - top)
-    other_share = jnp.exp2(other - top)
-    total = own_share + other_share
-    merged[:blocks] = top + jnp.log2(total)
-    merged[blocks:] = (mine[blocks:] * own_share + theirs[blocks:] * other_share) / total
+                local[lower : lower + 1, at] = accum / total
+
+    for device in range(stats.shape[0]):
+        stats[device] = local[...]
+
+
+def merge(gathered):
+    blocks = gathered.shape[1] // 2
+    sums = gathered[:, :blocks]
+    top = jnp.max(sums, axis=0)
+    shares = jnp.exp2(sums - top)
+    total = jnp.sum(shares, axis=0)
+    return top + jnp.log2(total), jnp.sum(gathered[:, blocks:] * shares, axis=0) / total
 
 
 def head_kernel(head_index, row_axis, head_axis, low, last, *refs):
-    (inputs, keys, values, queries, out_grad, stats) = refs[:6]
+    (inputs, keys, values, queries, out_grad, gathered) = refs[:6]
     if last:
         (key_weight, value_weight, other_grads) = refs[6:9]
         (grads, query_keep, query_send, weight_keep, weight_send, input_keep, input_send) = refs[9:16]
-        key_acc, value_acc, tile_ref, weights_ref, input_ref = refs[16:]
+        key_acc, value_acc, tile_ref, weights_ref, stats, input_ref = refs[16:]
     else:
         (grads, query_keep, query_send, weight_keep, weight_send) = refs[6:11]
-        key_acc, value_acc, tile_ref, weights_ref = refs[11:]
+        key_acc, value_acc, tile_ref, weights_ref, stats = refs[11:]
     reads, latents, _ = queries.shape
-    head_count = stats.shape[0] // (2 * reads)
+    blocks = gathered.shape[1] // 2
+    head_count = blocks // reads
+    stats[:blocks], stats[blocks:] = merge(gathered)
     pairs = GROUPS // 2
     tile = latents // pairs
     half = tile // 2
@@ -95,30 +118,31 @@
     side = lax.rem(me, 2)
     mine = pl.ds(pl.multiple_of(side * half, half), half)
     yours = pl.ds(pl.multiple_of((1 - side) * half, half), half)
+    cols = slice(head_index * HD, (head_index + 1) * HD)
     key_acc[...] = jnp.zeros_like(key_acc)
     value_acc[...] = jnp.zeros_like(value_acc)
-    for read_index in range(reads):
-        position = read_index * head_count + head_index
-        lower = reads * head_count + position
-
-        @pl.loop(0, pairs)
-        def _(slot):
-            relative = (slot // (pairs // 2)) + 2 * lax.rem(slot, pairs // 2)
-            pair = (me // 2) ^ relative
-            at = pl.ds(pl.multiple_of(pair * tile, tile), tile)
-            query_block = queries[read_index, at, :]
-            grad_block = out_grad[read_index, at, :]
-            scores = last_contract(keys[...], query_block) * (FACTOR * LOG2_E)
-            weighted = last_contract(values[...], grad_block)
+
+    @pl.loop(0, pairs)
+    def _(slot):
+        relative = (slot // (pairs // 2)) + 2 * lax.rem(slot, pairs // 2)
+        pair = (me // 2) ^ relative
+        at = pl.ds(pl.multiple_of(pair * tile, tile), tile)
+        for read_index in range(reads):
+            position = read_index * head_count + head_index
+            lower = blocks + position
+            query_block = queries[read_index, at, cols]
+            grad_block = out_grad[read_index, at, cols]
+            scores = last_contract(keys[:, cols], query_block) * (FACTOR * LOG2_E)
+            weighted = last_contract(values[:, cols], grad_block)
             probs = jnp.exp2(scores - stats[position : position + 1, at])
             score_grad = (probs * (weighted - stats[lower : lower + 1, at]) * FACTOR).astype(
                 jnp.bfloat16
             )
             key_acc[...] += plain_dot(score_grad, query_block)
             value_acc[...] += plain_dot(probs.astype(jnp.bfloat16), grad_block)
-            tile_ref[...] = rows_contract(score_grad, keys[...])
-            query_keep[slot, read_index] = tile_ref[mine, :]
-            query_send[slot, read_index] = tile_ref[yours, :]
+            tile_ref[read_index] = rows_contract(score_grad, keys[:, cols])
+            query_keep[slot, read_index] = tile_ref[read_index, mine, :]
+            query_send[slot, read_index] = tile_ref[read_index, yours, :]
 
     grads[:, :HD] = key_acc[...].astype(jnp.bfloat16)
     grads[:, HD:] = value_acc[...].astype(jnp.bfloat16)
@@ -186,28 +210,31 @@
     group_bits = [bit * low for bit in bits_of(GROUPS)]
     tile = latents // (GROUPS // 2)
 
+    operands = (inputs, key_weight, value_weight, queries, out_grad)
     keys, values, stats = pl.pallas_call(
         functools.partial(project_kernel, tile),
         out_shape=(
             shape_of((row_count, columns), jnp.bfloat16),
             shape_of((row_count, columns), jnp.bfloat16),
-            shape_of((2 * blocks, latents)),
+            shape_of((row_devices, 2 * blocks, latents)),
         ),
-        in_specs=[VMEM] * 5,
+        in_specs=[HBM] * 5,
         out_specs=(VMEM,) * 3,
-        compiler_params=PARAMS,
+        scratch_shapes=[pltpu.VMEM(item.shape, item.dtype) for item in operands]
+        + [
+            pltpu.VMEM((2 * blocks, latents), jnp.float32),
+            pltpu.SemaphoreType.DMA((5,)),
+        ],
+        compiler_params=pltpu.CompilerParams(vmem_limit_bytes=57 * 1024 * 1024),
+        cost_estimate=pl.CostEstimate(
+            flops=4 * row_count * columns * (features + reads * latents),
+            bytes_accessed=8 * 2**20,
+            transcendentals=blocks * row_count * latents,
+        ),
         name="project",
-    )(inputs, key_weight, value_weight, queries, out_grad)
-
-    for bit in bits_of(row_devices):
-        theirs = swap(stats, "rows", row_devices, bit)
-        stats = pl.pallas_call(
-            merge_kernel,
-            out_shape=shape_of(stats.shape),
-            in_specs=[VMEM] * 2,
-            out_specs=VMEM,
-            name="merge",
-        )(stats, theirs)
+    )(*operands)
+
+    gathered = lax.all_to_all(stats, "rows", 0, 0, tiled=True)
 
     half = GROUPS // 2
     piece = features // GROUPS
@@ -215,11 +242,7 @@
     other_grads = None
     for head_index in range(head_count):
         last = head_index + 1 == head_count
-        column = pl.BlockSpec((row_count, HD), lambda _, at=head_index: (0, at))
-        stack = pl.BlockSpec((reads, latents, HD), lambda _, at=head_index: (0, 0, at))
-        whole = lambda shape: pl.BlockSpec(shape, lambda _, rank=len(shape): (0,) * rank)
-        operands = [inputs, keys, values, queries, out_grad, stats]
-        in_specs = [whole(inputs.shape), column, column, stack, stack, whole(stats.shape)]
+        operands = [inputs, keys, values, queries, out_grad, gathered]
         out_shape = [
             shape_of((row_count, 2 * HD), jnp.bfloat16),
             shape_of((half, reads, latents // GROUPS, HD)),
@@ -230,23 +253,27 @@
         scratch = [
             pltpu.VMEM((row_count, HD), jnp.float32),
             pltpu.VMEM((row_count, HD), jnp.float32),
-            pltpu.VMEM((tile, HD), jnp.float32),
+            pltpu.VMEM((reads, tile, HD), jnp.float32),
             pltpu.VMEM((features, 2 * HD), jnp.float32),
+            pltpu.VMEM((2 * blocks, latents), jnp.float32),
         ]
         if last:
             operands += [key_weight, value_weight, other_grads]
-            in_specs += [whole(key_weight.shape), whole(value_weight.shape), whole(other_grads.shape)]
             share = (head_devices // 2, row_count, features // head_devices)
             out_shape += [shape_of(share), shape_of(share)]
             scratch += [pltpu.VMEM((row_count, features), jnp.float32)]
         results = pl.pallas_call(
             functools.partial(head_kernel, head_index, "rows", "heads", low, last),
-            grid=(1,),
             out_shape=out_shape,
-            in_specs=in_specs,
-            out_specs=[whole(item.shape) for item in out_shape],
+            in_specs=[VMEM] * len(operands),
+            out_specs=[VMEM] * len(out_shape),
             scratch_shapes=scratch,
             compiler_params=PARAMS,
+            cost_estimate=pl.CostEstimate(
+                flops=20 * reads * row_count * latents * HD,
+                bytes_accessed=8 * 2**20,
+                transcendentals=reads * row_count * latents,
+            ),
             name="head",
         )(*operands)
         other_grads = results[0]

time: 101 us -> 88.1 us (0.87)
  starting transfers between devices: 41.7 us -> 17.6 us
  blocking collectives: 0 us -> 16.3 us
  waiting for transfers between devices: 23 us -> 31.5 us
  Pallas kernels: 25.3 us -> 17.8 us
  local copies, waits for them, and re-layouts: 8.03 us -> 1.94 us
    ppermute x23 -> x20, starting transfers between devices: 41.7 us -> 17.6 us  [swap(): return lax.ppermute(array, axis, pairs)]
    all_to_all x0 -> x1, blocking collectives: none -> 16.3 us  [on_device(): gathered = lax.all_to_all(stats, 'rows', 0, 0, tiled=True)]
    ppermute x23 -> x20, waiting for transfers between devices: 23 us -> 31.5 us  [swap(): return lax.ppermute(array, axis, pairs)]
    unnamed x32 -> x16, local copies, waits for them, and re-layouts: 8.01 us -> 1.92 us
    pallas_call x3 -> x0, Pallas kernels: 4.25 us -> none  [on_device(): pl.pallas_call(merge_kernel, out_shape=shape_of(stats.shape), in_specs=[V...]
    pallas_call x2, Pallas kernels: 12.6 us -> 10 us  [on_device(): pl.pallas_call(functools.partial(head_kernel, head_index, 'rows', 'heads'...]
  transfers between devices with their start and end apart: 23 -> 20, of which waited for: 12 -> 11; matrix products, arithmetic and copies ran while one was open for 2% -> 2% of each run, Pallas kernels for 7% -> 6%
where the time goes in v3:
time: 88.1 us; the launch traced here: 87.8 us
  waiting for transfers between devices  31.5 us (36%)
  Pallas kernels  17.8 us (20%)
  starting transfers between devices  17.6 us (20%)
  blocking collectives  16.3 us (19%)
  local copies, waits for them, and re-layouts  1.94 us (2%)
  other arithmetic  1.86 us (2%)
    ppermute x20, waiting for transfers between devices, swap(): return lax.ppermute(array, axis, pairs)  31.5 us
    ppermute x20, starting transfers between devices, swap(): return lax.ppermute(array, axis, pairs)  17.6 us
    all_to_all x1, blocking collectives, on_device(): gathered = lax.all_to_all(stats, 'rows', 0, 0, tiled=True)  16.3 us
    pallas_call x2, Pallas kernels, on_device(): pl.pallas_call(functools.partial(head_kernel, head_index, 'rows', 'heads'...  10 us
    pallas_call x1, Pallas kernels, on_device(): pl.pallas_call(functools.partial(project_kernel, tile), out_shape=(shape_...  6.78 us
    unnamed x16, local copies, waits for them, and re-layouts  1.92 us
  transfers between devices with their start and end apart: 20, of which 11 were waited for; matrix products, arithmetic and copies ran while one was open for 2% of the time, Pallas kernels for 6%

profile of v3, /device:TPU:0, one launch (start us, length us, event | category | flops | bytes accessed | tf_op | source)
XLA Modules:
  0.0 87.8 jit_solution(8075798692965002818)
XLA Ops:
  0.7 6.8 %project.1 = (bf16[512,256]{1,0:T(8,128)(2,1)}, bf16[512,256]{1,0:T(8,128)(2,1)}, f32[8,8,1024]{2,1,0:T(8,128)}) custom-call(bf16[512,512]{1,0:T(8,128)(2,1)} %refs_0_.3, bf16[512,256]{1,0:T(8,128)(2,1)} %refs_6_.1, bf16[512,256]{1,0:T(8,128)(2,1)} %refs_7_.1, bf16[2,1024,256]{2,1,0:T(8,128)(2,1)} %refs_3_.3, bf16[2,1024,256]{2,1,0:T(8,128)(2,1)} %refs_4_.3), custom_call_target="tpu_custom_call" | custom-call | flops 1342177280 | bytes 8388608 | tf_op jit(solution)/shard_map/project/pallas_call | solution.py:214
  7.4 16.3 %all_to_all.5.refs_5_ = f32[8,8,1024]{2,1,0:T(8,128)S(1)} all-to-all(f32[8,8,1024]{2,1,0:T(8,128)} %get-tuple-element.22), channel_id=1, replica_groups=mesh['rows'=8,'heads'=4] {'rows'}, dimensions={0} | all-to-all | bytes 524288 | tf_op jit(solution)/shard_map/all_to_all | solution.py:237
  25.7 4.6 %head.2 = (bf16[512,256]{1,0:T(8,128)(2,1)S(1)}, f32[4,2,128,128]{3,2,1,0:T(8,128)S(1)}, f32[4,2,128,128]{3,2,1,0:T(8,128)S(1)}, f32[4,64,256]{2,1,0:T(8,128)S(1)}, f32[4,64,256]{2,1,0:T(8,128)S(1)}) custom-call(bf16[512,512]{1,0:T(8,128)(2,1)S(1)} %copy-done.2, bf16[512,256]{1,0:T(8,128)(2,1)S(1)} %copy-done.5, bf16[512,256]{1,0:T(8,128)(2,1)S(1)} %copy-done.6, ...), custom_call_target="tpu_custom_call" | custom-call | flops 2684354560 | bytes 8388608 | tf_op jit(solution)/shard_map/head/pallas_call | solution.py:265
  30.3 1.5 %collective-permute-start.6 = (f32[4,64,256]{2,1,0:T(8,128)S(1)}, f32[4,64,256]{2,1,0:T(8,128)S(1)}, u32[]{:S(2)}, u32[]{:S(2)}) collective-permute-start(f32[4,64,256]{2,1,0:T(8,128)S(1)} %get-tuple-element.29), channel_id=1, source_target_pairs={{0,4},{4,0},{8,12},{12,8},{16,20},{20,16},{24,28},{28,24},{1,5},{5... | collective-permute-start | bytes 786440 | tf_op jit(solution)/shard_map/ppermute | solution.py:37
  31.8 5.4 %head.3 = (bf16[512,256]{1,0:T(8,128)(2,1)}, f32[4,2,128,128]{3,2,1,0:T(8,128)S(1)}, f32[4,2,128,128]{3,2,1,0:T(8,128)S(1)}, f32[4,64,256]{2,1,0:T(8,128)S(1)}, ...) custom-call(bf16[512,512]{1,0:T(8,128)(2,1)S(1)} %copy-done.2, ...), custom_call_target="tpu_custom_call" | custom-call | flops 2684354560 | bytes 8388608 | tf_op jit(solution)/shard_map/head/pallas_call | solution.py:265
  37.8 1.4 %collective-permute-start = (f32[4,2,128,128]{3,2,1,0:T(8,128)S(1)}, f32[4,2,128,128]{3,2,1,0:T(8,128)S(1)}, u32[]{:S(2)}, u32[]{:S(2)}) collective-permute-start(f32[4,2,128,128]{3,2,1,0:T(8,128)S(1)} %get-tuple-element.24), channel_id=1, source_target_pairs={{0,4},{4,0},{8,12},{12,8},{16,20},{20,16},{24,28},{28,24},{1,5},{5... | collective-permute-start | bytes 1572872 | tf_op jit(solution)/shard_map/ppermute | solution.py:37
  39.9 1.1 %collective-permute-start.7 = (f32[2,64,256]{2,1,0:T(8,128)S(1)}, f32[2,64,256]{2,1,0:T(8,128)S(1)}, u32[]{:S(2)}, u32[]{:S(2)}) collective-permute-start(f32[2,64,256]{2,1,0:T(8,128)S(1)} %get-tuple-element.43), channel_id=1, source_target_pairs={{0,8},{4,12},{8,0},{12,4},{16,24},{20,28},{24,16},{28,20},{1,9},{5... | collective-permute-start | bytes 393224 | tf_op jit(solution)/shard_map/ppermute | solution.py:37
  41.0 5.4 %collective-permute-done.12 = f32[4,64,256]{2,1,0:T(8,128)S(1)} collective-permute-done((f32[4,64,256]{2,1,0:T(8,128)S(1)}, f32[4,64,256]{2,1,0:T(8,128)S(1)}, u32[]{:S(2)}, u32[]{:S(2)}) %collective-permute-start.12) | collective-permute-done | bytes 262176 | tf_op jit(solution)/shard_map/ppermute | solution.py:37
  46.6 2.0 %collective-permute-start.8 = (f32[1,64,256]{2,1,0:T(8,128)S(1)}, f32[1,64,256]{2,1,0:T(8,128)S(1)}, u32[]{:S(2)}, u32[]{:S(2)}) collective-permute-start(f32[1,64,256]{2,1,0:T(8,128)S(1)} %slice_add_fusion.14), channel_id=1, source_target_pairs={{0,16},{4,20},{8,24},{12,28},{16,0},{20,4},{24,8},{28,12},{1,17},{... | collective-permute-start | bytes 196616 | tf_op jit(solution)/shard_map/ppermute | solution.py:37
  48.6 3.6 %collective-permute-done.13 = f32[2,64,256]{2,1,0:T(8,128)S(1)} collective-permute-done((f32[2,64,256]{2,1,0:T(8,128)S(1)}, f32[2,64,256]{2,1,0:T(8,128)S(1)}, u32[]{:S(2)}, u32[]{:S(2)}) %collective-permute-start.13) | collective-permute-done | bytes 131104 | tf_op jit(solution)/shard_map/ppermute | solution.py:37
  52.4 1.5 %collective-permute-done.8 = f32[1,64,256]{2,1,0:T(8,128)S(1)} collective-permute-done((f32[1,64,256]{2,1,0:T(8,128)S(1)}, f32[1,64,256]{2,1,0:T(8,128)S(1)}, u32[]{:S(2)}, u32[]{:S(2)}) %collective-permute-start.8) | collective-permute-done | bytes 65568 | tf_op jit(solution)/shard_map/ppermute | solution.py:37
  54.0 1.4 %collective-permute-start.9 = (f32[1,64,256]{2,1,0:T(8,128)S(1)}, f32[1,64,256]{2,1,0:T(8,128)S(1)}, u32[]{:S(2)}, u32[]{:S(2)}) collective-permute-start(f32[1,64,256]{2,1,0:T(8,128)S(1)} %fusion.7), channel_id=1, source_target_pairs={{0,16},{4,20},{8,24},{12,28},{16,0},{20,4},{24,8},{28,12},{1,17},{... | collective-permute-start | bytes 196616 | tf_op jit(solution)/shard_map/ppermute | solution.py:37
  55.3 3.7 %collective-permute-done.14 = f32[1,64,256]{2,1,0:T(8,128)S(1)} collective-permute-done((f32[1,64,256]{2,1,0:T(8,128)S(1)}, f32[1,64,256]{2,1,0:T(8,128)S(1)}, u32[]{:S(2)}, u32[]{:S(2)}) %collective-permute-start.14) | collective-permute-done | bytes 65568 | tf_op jit(solution)/shard_map/ppermute | solution.py:37
  59.1 1.2 %collective-permute-done.9 = f32[1,64,256]{2,1,0:T(8,128)S(1)} collective-permute-done((f32[1,64,256]{2,1,0:T(8,128)S(1)}, f32[1,64,256]{2,1,0:T(8,128)S(1)}, u32[]{:S(2)}, u32[]{:S(2)}) %collective-permute-start.9) | collective-permute-done | bytes 65568 | tf_op jit(solution)/shard_map/ppermute | solution.py:37
  61.4 1.1 %collective-permute-start.1 = (f32[2,2,128,128]{3,2,1,0:T(8,128)S(1)}, f32[2,2,128,128]{3,2,1,0:T(8,128)S(1)}, u32[]{:S(2)}, u32[]{:S(2)}) collective-permute-start(f32[2,2,128,128]{3,2,1,0:T(8,128)S(1)} %get-tuple-element.37), channel_id=1, source_target_pairs={{0,8},{4,12},{8,0},{12,4},{16,24},{20,28},{24,16},{28,20},{1,9},{5... | collective-permute-start | bytes 786440 | tf_op jit(solution)/shard_map/ppermute | solution.py:37
  62.5 1.9 %collective-permute-done.15 = f32[1,64,256]{2,1,0:T(8,128)S(1)} collective-permute-done((f32[1,64,256]{2,1,0:T(8,128)S(1)}, f32[1,64,256]{2,1,0:T(8,128)S(1)}, u32[]{:S(2)}, u32[]{:S(2)}) %collective-permute-start.15) | collective-permute-done | bytes 65568 | tf_op jit(solution)/shard_map/ppermute | solution.py:37
  65.4 1.3 %collective-permute-start.4 = (f32[2,2,128,128]{3,2,1,0:T(8,128)S(1)}, f32[2,2,128,128]{3,2,1,0:T(8,128)S(1)}, u32[]{:S(2)}, u32[]{:S(2)}) collective-permute-start(f32[2,2,128,128]{3,2,1,0:T(8,128)S(1)} %get-tuple-element.39), channel_id=1, source_target_pairs={{0,8},{4,12},{8,0},{12,4},{16,24},{20,28},{24,16},{28,20},{1,9},{5... | collective-permute-start | bytes 786440 | tf_op jit(solution)/shard_map/ppermute | solution.py:37
  66.8 1.6 %collective-permute-start.19 = (f32[1,512,128]{2,1,0:T(8,128)S(1)}, f32[1,512,128]{2,1,0:T(8,128)S(1)}, u32[]{:S(2)}, u32[]{:S(2)}) collective-permute-start(f32[1,512,128]{2,1,0:T(8,128)S(1)} %slice_bitcast_fusion), channel_id=1, source_target_pairs={{0,2},{1,3},{2,0},{3,1},{4,6},{5,7},{6,4},{7,5},{8,10},{9,11},{10,... | collective-permute-start | bytes 786440 | tf_op jit(solution)/shard_map/ppermute | solution.py:37
  68.4 1.2 %collective-permute-start.11 = (f32[4,64,256]{2,1,0:T(8,128)S(1)}, f32[4,64,256]{2,1,0:T(8,128)S(1)}, u32[]{:S(2)}, u32[]{:S(2)}) collective-permute-start(f32[4,64,256]{2,1,0:T(8,128)S(1)} %pad_maximum_fusion.1.refs_0_), channel_id=1, source_target_pairs={{0,4},{4,0},{8,12},{12,8},{16,20},{20,16},{24,28},{28,24},{1,5},{5... | collective-permute-start | bytes 786440 | tf_op jit(solution)/shard_map/ppermute | solution.py:37
  69.6 5.7 %collective-permute-done.16 = f32[2,64,256]{2,1,0:T(8,128)S(1)} collective-permute-done((f32[2,64,256]{2,1,0:T(8,128)S(1)}, f32[2,64,256]{2,1,0:T(8,128)S(1)}, u32[]{:S(2)}, u32[]{:S(2)}) %collective-permute-start.16) | collective-permute-done | bytes 131104 | tf_op jit(solution)/shard_map/ppermute | solution.py:37
  75.3 1.6 %collective-permute-start.17 = (f32[4,64,256]{2,1,0:T(8,128)S(1)}, f32[4,64,256]{2,1,0:T(8,128)S(1)}, u32[]{:S(2)}, u32[]{:S(2)}) collective-permute-start(f32[4,64,256]{2,1,0:T(8,128)S(1)} %pad_maximum_fusion.2.refs_2_), channel_id=1, source_target_pairs={{0,4},{4,0},{8,12},{12,8},{16,20},{20,16},{24,28},{28,24},{1,5},{5... | collective-permute-start | bytes 786440 | tf_op jit(solution)/shard_map/ppermute | solution.py:37
  77.0 2.5 %collective-permute-done.4 = f32[2,2,128,128]{3,2,1,0:T(8,128)S(1)} collective-permute-done((f32[2,2,128,128]{3,2,1,0:T(8,128)S(1)}, f32[2,2,128,128]{3,2,1,0:T(8,128)S(1)}, u32[]{:S(2)}, u32[]{:S(2)}) %collective-permute-start.4) | collective-permute-done | bytes 262176 | tf_op jit(solution)/shard_map/ppermute | solution.py:37
  80.7 3.9 %collective-permute-done.2 = f32[1,2,128,128]{3,2,1,0:T(8,128)S(1)} collective-permute-done((f32[1,2,128,128]{3,2,1,0:T(8,128)S(1)}, f32[1,2,128,128]{3,2,1,0:T(8,128)S(1)}, u32[]{:S(2)}, u32[]{:S(2)}) %collective-permute-start.2) | collective-permute-done | bytes 131104 | tf_op jit(solution)/shard_map/ppermute | solution.py:37
  84.7 1.4 %collective-permute-done.5 = f32[1,2,128,128]{3,2,1,0:T(8,128)S(1)} collective-permute-done((f32[1,2,128,128]{3,2,1,0:T(8,128)S(1)}, f32[1,2,128,128]{3,2,1,0:T(8,128)S(1)}, u32[]{:S(2)}, u32[]{:S(2)}) %collective-permute-start.5) | collective-permute-done | bytes 131104 | tf_op jit(solution)/shard_map/ppermute | solution.py:37
  (57 shorter events, 8.9 us)
Async XLA Ops:
  0.6 23.1 %copy-start.1 = (bf16[2,1024,256]{2,1,0:T(8,128)(2,1)S(1)}, bf16[2,1024,256]{2,1,0:T(8,128)(2,1)}, u32[]{:S(2)}) copy-start(bf16[2,1024,256]{2,1,0:T(8,128)(2,1)} %refs_4_.3) | copy-start | bytes 3145732
  0.6 23.1 %copy-start = (bf16[2,1024,256]{2,1,0:T(8,128)(2,1)S(1)}, bf16[2,1024,256]{2,1,0:T(8,128)(2,1)}, u32[]{:S(2)}) copy-start(bf16[2,1024,256]{2,1,0:T(8,128)(2,1)} %refs_3_.3) | copy-start | bytes 3145732
  7.4 16.3 %copy-start.2 = (bf16[512,512]{1,0:T(8,128)(2,1)S(1)}, bf16[512,512]{1,0:T(8,128)(2,1)}, u32[]{:S(2)}) copy-start(bf16[512,512]{1,0:T(8,128)(2,1)} %refs_0_.3) | copy-start | bytes 1572868
  25.7 6.1 %copy-start.7 = (bf16[512,256]{1,0:T(8,128)(2,1)S(1)}, bf16[512,256]{1,0:T(8,128)(2,1)}, u32[]{:S(2)}) copy-start(bf16[512,256]{1,0:T(8,128)(2,1)} %get-tuple-element.21.refs_2_) | copy-start | bytes 786436
  30.3 9.6 %collective-permute-start.6 = (f32[4,64,256]{2,1,0:T(8,128)S(1)}, f32[4,64,256]{2,1,0:T(8,128)S(1)}, u32[]{:S(2)}, u32[]{:S(2)}) collective-permute-start(f32[4,64,256]{2,1,0:T(8,128)S(1)} %get-tuple-element.29), channel_id=1, source_target_pairs={{0,4},{4,0},{8,12},{12,8},{16,20},{20,16},{24,28},{28,24},{1,5},{5... | collective-permute-start | bytes 786440 | tf_op jit(solution)/shard_map/ppermute | solution.py:37
  37.2 9.2 %collective-permute-start.12 = (f32[4,64,256]{2,1,0:T(8,128)S(1)}, f32[4,64,256]{2,1,0:T(8,128)S(1)}, u32[]{:S(2)}, u32[]{:S(2)}) collective-permute-start(f32[4,64,256]{2,1,0:T(8,128)S(1)} %get-tuple-element.31), channel_id=1, source_target_pairs={{0,4},{4,0},{8,12},{12,8},{16,20},{20,16},{24,28},{28,24},{1,5},{5... | collective-permute-start | bytes 786440 | tf_op jit(solution)/shard_map/ppermute | solution.py:37
  37.8 23.5 %collective-permute-start = (f32[4,2,128,128]{3,2,1,0:T(8,128)S(1)}, f32[4,2,128,128]{3,2,1,0:T(8,128)S(1)}, u32[]{:S(2)}, u32[]{:S(2)}) collective-permute-start(f32[4,2,128,128]{3,2,1,0:T(8,128)S(1)} %get-tuple-element.24), channel_id=1, source_target_pairs={{0,4},{4,0},{8,12},{12,8},{16,20},{20,16},{24,28},{28,24},{1,5},{5... | collective-permute-start | bytes 1572872 | tf_op jit(solution)/shard_map/ppermute | solution.py:37
  39.2 26.1 %collective-permute-start.3 = (f32[4,2,128,128]{3,2,1,0:T(8,128)S(1)}, f32[4,2,128,128]{3,2,1,0:T(8,128)S(1)}, u32[]{:S(2)}, u32[]{:S(2)}) collective-permute-start(f32[4,2,128,128]{3,2,1,0:T(8,128)S(1)} %get-tuple-element.27), channel_id=1, source_target_pairs={{0,4},{4,0},{8,12},{12,8},{16,20},{20,16},{24,28},{28,24},{1,5},{5... | collective-permute-start | bytes 1572872 | tf_op jit(solution)/shard_map/ppermute | solution.py:37
  39.8 26.9 %collective-permute-start.18 = (f32[2,512,128]{2,1,0:T(8,128)S(1)}, f32[2,512,128]{2,1,0:T(8,128)S(1)}, u32[]{:S(2)}, u32[]{:S(2)}) collective-permute-start(f32[2,512,128]{2,1,0:T(8,128)S(1)} %get-tuple-element.35), channel_id=1, source_target_pairs={{0,1},{1,0},{2,3},{3,2},{4,5},{5,4},{6,7},{7,6},{8,9},{9,8},{10,11... | collective-permute-start | bytes 1572872 | tf_op jit(solution)/shard_map/ppermute | solution.py:37
  39.9 6.7 %collective-permute-start.7 = (f32[2,64,256]{2,1,0:T(8,128)S(1)}, f32[2,64,256]{2,1,0:T(8,128)S(1)}, u32[]{:S(2)}, u32[]{:S(2)}) collective-permute-start(f32[2,64,256]{2,1,0:T(8,128)S(1)} %get-tuple-element.43), channel_id=1, source_target_pairs={{0,8},{4,12},{8,0},{12,4},{16,24},{20,28},{24,16},{28,20},{1,9},{5... | collective-permute-start | bytes 393224 | tf_op jit(solution)/shard_map/ppermute | solution.py:37
  46.5 5.8 %collective-permute-start.13 = (f32[2,64,256]{2,1,0:T(8,128)S(1)}, f32[2,64,256]{2,1,0:T(8,128)S(1)}, u32[]{:S(2)}, u32[]{:S(2)}) collective-permute-start(f32[2,64,256]{2,1,0:T(8,128)S(1)} %get-tuple-element.41), channel_id=1, source_target_pairs={{0,8},{4,12},{8,0},{12,4},{16,24},{20,28},{24,16},{28,20},{1,9},{5... | collective-permute-start | bytes 393224 | tf_op jit(solution)/shard_map/ppermute | solution.py:37
  46.6 7.3 %collective-permute-start.8 = (f32[1,64,256]{2,1,0:T(8,128)S(1)}, f32[1,64,256]{2,1,0:T(8,128)S(1)}, u32[]{:S(2)}, u32[]{:S(2)}) collective-permute-start(f32[1,64,256]{2,1,0:T(8,128)S(1)} %slice_add_fusion.14), channel_id=1, source_target_pairs={{0,16},{4,20},{8,24},{12,28},{16,0},{20,4},{24,8},{28,12},{1,17},{... | collective-permute-start | bytes 196616 | tf_op jit(solution)/shard_map/ppermute | solution.py:37
  52.3 6.8 %collective-permute-start.14 = (f32[1,64,256]{2,1,0:T(8,128)S(1)}, f32[1,64,256]{2,1,0:T(8,128)S(1)}, u32[]{:S(2)}, u32[]{:S(2)}) collective-permute-start(f32[1,64,256]{2,1,0:T(8,128)S(1)} %slice_add_fusion.12), channel_id=1, source_target_pairs={{0,16},{4,20},{8,24},{12,28},{16,0},{20,4},{24,8},{28,12},{1,17},{... | collective-permute-start | bytes 196616 | tf_op jit(solution)/shard_map/ppermute | solution.py:37
  54.0 6.3 %collective-permute-start.9 = (f32[1,64,256]{2,1,0:T(8,128)S(1)}, f32[1,64,256]{2,1,0:T(8,128)S(1)}, u32[]{:S(2)}, u32[]{:S(2)}) collective-permute-start(f32[1,64,256]{2,1,0:T(8,128)S(1)} %fusion.7), channel_id=1, source_target_pairs={{0,16},{4,20},{8,24},{12,28},{16,0},{20,4},{24,8},{28,12},{1,17},{... | collective-permute-start | bytes 196616 | tf_op jit(solution)/shard_map/ppermute | solution.py:37
  59.1 5.4 %collective-permute-start.15 = (f32[1,64,256]{2,1,0:T(8,128)S(1)}, f32[1,64,256]{2,1,0:T(8,128)S(1)}, u32[]{:S(2)}, u32[]{:S(2)}) collective-permute-start(f32[1,64,256]{2,1,0:T(8,128)S(1)} %fusion.6), channel_id=1, source_target_pairs={{0,16},{4,20},{8,24},{12,28},{16,0},{20,4},{24,8},{28,12},{1,17},{... | collective-permute-start | bytes 196616 | tf_op jit(solution)/shard_map/ppermute | solution.py:37
  60.3 8.0 %collective-permute-start.10 = (f32[2,64,256]{2,1,0:T(8,128)S(1)}, f32[2,64,256]{2,1,0:T(8,128)S(1)}, u32[]{:S(2)}, u32[]{:S(2)}) collective-permute-start(f32[2,64,256]{2,1,0:T(8,128)S(1)} %pad_maximum_fusion.3), channel_id=1, source_target_pairs={{0,8},{4,12},{8,0},{12,4},{16,24},{20,28},{24,16},{28,20},{1,9},{5... | collective-permute-start | bytes 393224 | tf_op jit(solution)/shard_map/ppermute | solution.py:37
  61.4 15.5 %collective-permute-start.1 = (f32[2,2,128,128]{3,2,1,0:T(8,128)S(1)}, f32[2,2,128,128]{3,2,1,0:T(8,128)S(1)}, u32[]{:S(2)}, u32[]{:S(2)}) collective-permute-start(f32[2,2,128,128]{3,2,1,0:T(8,128)S(1)} %get-tuple-element.37), channel_id=1, source_target_pairs={{0,8},{4,12},{8,0},{12,4},{16,24},{20,28},{24,16},{28,20},{1,9},{5... | collective-permute-start | bytes 786440 | tf_op jit(solution)/shard_map/ppermute | solution.py:37
  64.5 10.8 %collective-permute-start.16 = (f32[2,64,256]{2,1,0:T(8,128)S(1)}, f32[2,64,256]{2,1,0:T(8,128)S(1)}, u32[]{:S(2)}, u32[]{:S(2)}) collective-permute-start(f32[2,64,256]{2,1,0:T(8,128)S(1)} %pad_maximum_fusion.4), channel_id=1, source_target_pairs={{0,8},{4,12},{8,0},{12,4},{16,24},{20,28},{24,16},{28,20},{1,9},{5... | collective-permute-start | bytes 393224 | tf_op jit(solution)/shard_map/ppermute | solution.py:37
  65.4 14.1 %collective-permute-start.4 = (f32[2,2,128,128]{3,2,1,0:T(8,128)S(1)}, f32[2,2,128,128]{3,2,1,0:T(8,128)S(1)}, u32[]{:S(2)}, u32[]{:S(2)}) collective-permute-start(f32[2,2,128,128]{3,2,1,0:T(8,128)S(1)} %get-tuple-element.39), channel_id=1, source_target_pairs={{0,8},{4,12},{8,0},{12,4},{16,24},{20,28},{24,16},{28,20},{1,9},{5... | collective-permute-start | bytes 786440 | tf_op jit(solution)/shard_map/ppermute | solution.py:37
  66.8 13.2 %collective-permute-start.19 = (f32[1,512,128]{2,1,0:T(8,128)S(1)}, f32[1,512,128]{2,1,0:T(8,128)S(1)}, u32[]{:S(2)}, u32[]{:S(2)}) collective-permute-start(f32[1,512,128]{2,1,0:T(8,128)S(1)} %slice_bitcast_fusion), channel_id=1, source_target_pairs={{0,2},{1,3},{2,0},{3,1},{4,6},{5,7},{6,4},{7,5},{8,10},{9,11},{10,... | collective-permute-start | bytes 786440 | tf_op jit(solution)/shard_map/ppermute | solution.py:37
  68.4 18.4 %collective-permute-start.11 = (f32[4,64,256]{2,1,0:T(8,128)S(1)}, f32[4,64,256]{2,1,0:T(8,128)S(1)}, u32[]{:S(2)}, u32[]{:S(2)}) collective-permute-start(f32[4,64,256]{2,1,0:T(8,128)S(1)} %pad_maximum_fusion.1.refs_0_), channel_id=1, source_target_pairs={{0,4},{4,0},{8,12},{12,8},{16,20},{20,16},{24,28},{28,24},{1,5},{5... | collective-permute-start | bytes 786440 | tf_op jit(solution)/shard_map/ppermute | solution.py:37
  75.3 11.5 %collective-permute-start.17 = (f32[4,64,256]{2,1,0:T(8,128)S(1)}, f32[4,64,256]{2,1,0:T(8,128)S(1)}, u32[]{:S(2)}, u32[]{:S(2)}) collective-permute-start(f32[4,64,256]{2,1,0:T(8,128)S(1)} %pad_maximum_fusion.2.refs_2_), channel_id=1, source_target_pairs={{0,4},{4,0},{8,12},{12,8},{16,20},{20,16},{24,28},{28,24},{1,5},{5... | collective-permute-start | bytes 786440 | tf_op jit(solution)/shard_map/ppermute | solution.py:37
  76.9 7.7 %collective-permute-start.2 = (f32[1,2,128,128]{3,2,1,0:T(8,128)S(1)}, f32[1,2,128,128]{3,2,1,0:T(8,128)S(1)}, u32[]{:S(2)}, u32[]{:S(2)}) collective-permute-start(f32[1,2,128,128]{3,2,1,0:T(8,128)S(1)} %slice_add_fusion.10), channel_id=1, source_target_pairs={{0,16},{4,20},{8,24},{12,28},{16,0},{20,4},{24,8},{28,12},{1,17},{... | collective-permute-start | bytes 393224 | tf_op jit(solution)/shard_map/ppermute | solution.py:37
  79.5 6.6 %collective-permute-start.5 = (f32[1,2,128,128]{3,2,1,0:T(8,128)S(1)}, f32[1,2,128,128]{3,2,1,0:T(8,128)S(1)}, u32[]{:S(2)}, u32[]{:S(2)}) collective-permute-start(f32[1,2,128,128]{3,2,1,0:T(8,128)S(1)} %slice_add_fusion.8), channel_id=1, source_target_pairs={{0,16},{4,20},{8,24},{12,28},{16,0},{20,4},{24,8},{28,12},{1,17},{... | collective-permute-start | bytes 393224 | tf_op jit(solution)/shard_map/ppermute | solution.py:37
  (4 other events, 14.1 us)

commit v4 on v2

v4 whole, which is shorter than its diff:
```python
import functools

import jax
import jax.numpy as jnp
from jax import lax
from jax.experimental import pallas as pl
from jax.experimental.pallas import tpu as pltpu
from jax.sharding import PartitionSpec as P

HD = 128
GROUPS = 8
FACTOR = HD ** (-0.5)
LOG2_E = 1.4426950408889634
VMEM = pl.BlockSpec(memory_space=pltpu.VMEM)
HBM = pl.BlockSpec(memory_space=pltpu.HBM)


def params(mebibytes):
    return pltpu.CompilerParams(vmem_limit_bytes=mebibytes * 1024 * 1024)


def last_contract(left, right):
    return lax.dot_general(
        left, right, (((1,), (1,)), ((), ())), preferred_element_type=jnp.float32
    )


def rows_contract(left, right):
    return lax.dot_general(
        left, right, (((0,), (0,)), ((), ())), preferred_element_type=jnp.float32
    )


def plain_dot(left, right):
    return jnp.dot(left, right, preferred_element_type=jnp.float32)


def swap(array, axis, count, bit):
    pairs = [(device, device ^ bit) for device in range(count)]
    return lax.ppermute(array, axis, pairs)


def bits_of(count):
    return [1 << place for place in range(count.bit_length() - 1)]


def head_statistics(tile, cols, inputs, key_weight, value_weight, queries, out_grad, keys, values, stats):
    reads, latents, _ = queries.shape
    keys[...] = plain_dot(inputs[...], key_weight[:, cols]).astype(jnp.bfloat16)
    values[...] = plain_dot(inputs[...], value_weight[:, cols]).astype(jnp.bfloat16)

    @pl.loop(0, latents // tile)
    def _(step):
        at = pl.ds(pl.multiple_of(step * tile, tile), tile)
        for read_index in range(reads):
            scores = last_contract(keys[...], queries[read_index, at, cols])
            scores = scores * (FACTOR * LOG2_E)
            weighted = last_contract(values[...], out_grad[read_index, at, cols])
            top = jnp.max(scores, axis=0, keepdims=True)
            expos = jnp.exp2(scores - top)
            total = jnp.sum(expos, axis=0, keepdims=True)
            accum = jnp.sum(expos * weighted, axis=0, keepdims=True)
            stats[read_index : read_index + 1, at] = top + jnp.log2(total)
            stats[reads + read_index : reads + read_index + 1, at] = accum / total


def first_kernel(tile, *refs):
    sources, results, targets, sems = refs[:5], refs[5:8], refs[8:13], refs[13]
    loads = []
    for index, (source, target) in enumerate(zip(sources, targets)):
        if index:
            source = source.at[..., :HD]
        loads.append(pltpu.make_async_copy(source, target, sems.at[index]))
    for load in loads:
        load.start()
    for load in loads:
        load.wait()
    head_statistics(tile, slice(0, HD), *targets, *results)


def later_kernel(tile, head_index, *refs):
    head_statistics(tile, slice(head_index * HD, (head_index + 1) * HD), *refs)


def merged(mine, theirs):
    reads = mine.shape[0] // 2
    own, other = mine[:reads], theirs[:reads]
    top = jnp.maximum(own, other)
    own_share = jnp.exp2(own - top)
    other_share = jnp.exp2(other - top)
    total = own_share + other_share
    delta = (mine[reads:] * own_share + theirs[reads:] * other_share) / total
    return top + jnp.log2(total), delta


def merge_kernel(mine, theirs, result):
    reads = mine.shape[0] // 2
    result[:reads], result[reads:] = merged(mine, theirs)


def group_at(bits, relative, me):
    low = me % GROUPS
    group = 0
    for bit, flip in zip(bits, relative):
        group = group + ((low // bit) % 2 ^ flip) * bit
    return group


WEIGHT_BITS = (1, 2)
LAST_BIT = 4
QUERY_BITS = ((1, 2, 4), (2, 1, 4))


def grads_kernel(head_index, row_axis, head_axis, low, last, *refs):
    (inputs, keys, values, queries, out_grad, mine, theirs) = refs[:7]
    if last:
        (key_weight, value_weight, other_grads) = refs[7:10]
        refs = refs[10:]
        input_keep, input_send, input_ref = refs[4], refs[5], refs[-1]
    else:
        refs = refs[7:]
    grads, score_grads = refs[:2]
    weight_parts = refs[2:4]
    scratch = refs[6:] if last else refs[4:]
    key_acc, value_acc, weights_ref, stats = scratch[:4]
    reads, latents, _ = queries.shape
    tile = latents // (GROUPS // 2)
    cols = slice(head_index * HD, (head_index + 1) * HD)
    stats[:reads], stats[reads:] = merged(mine, theirs)
    key_acc[...] = jnp.zeros_like(key_acc)
    value_acc[...] = jnp.zeros_like(value_acc)

    @pl.loop(0, latents // tile)
    def _(step):
        at = pl.ds(pl.multiple_of(step * tile, tile), tile)
        for read_index in range(reads):
            query_block = queries[read_index, at, cols]
            grad_block = out_grad[read_index, at, cols]
            scores = last_contract(keys[...], query_block) * (FACTOR * LOG2_E)
            weighted = last_contract(values[...], grad_block)
            probs = jnp.exp2(scores - stats[read_index : read_index + 1, at])
            delta = stats[reads + read_index : reads + read_index + 1, at]
            score_grad = (probs * (weighted - delta) * FACTOR).astype(jnp.bfloat16)
            score_grads[read_index, :, at] = score_grad
            key_acc[...] += plain_dot(score_grad, query_block)
            value_acc[...] += plain_dot(probs.astype(jnp.bfloat16), grad_block)

    grads[:, :HD] = key_acc[...].astype(jnp.bfloat16)
    grads[:, HD:] = value_acc[...].astype(jnp.bfloat16)
    weights_ref[...] = rows_contract(inputs[...], grads[...])
    features = inputs.shape[1]
    piece = features // GROUPS
    me = lax.axis_index(row_axis) // low
    for first in range(2):
        for second in range(2):
            base = group_at(WEIGHT_BITS, (first, second), me)
            for high in range(2):
                start = pl.multiple_of((base + LAST_BIT * high) * piece, piece)
                weight_parts[first][second, high] = weights_ref[pl.ds(start, piece), :]
    if last:
        total = last_contract(grads[:, :HD], key_weight[:, HD:])
        total += last_contract(grads[:, HD:], value_weight[:, HD:])
        total += last_contract(other_grads[:, :HD], key_weight[:, :HD])
        total += last_contract(other_grads[:, HD:], value_weight[:, :HD])
        input_ref[...] = total
        place = lax.axis_index(head_axis)
        width = features // (2 * input_keep.shape[0])
        for relative in range(2 * input_keep.shape[0]):
            ref = input_send if relative % 2 else input_keep
            start = pl.multiple_of((place ^ relative) * width, width)
            ref[relative // 2] = input_ref[:, pl.ds(start, width)]


def query_kernel(bits, row_axis, low, score_grads, keys, query_keep, query_send, tile_ref):
    reads, _, latents = score_grads.shape
    piece = latents // GROUPS
    me = lax.axis_index(row_axis) // low
    side = lax.rem(me, 2)
    for upper in range(GROUPS // 2):
        pair = (me // 2) ^ upper
        at = pl.ds(pl.multiple_of(pair * 2 * piece, 2 * piece), 2 * piece)
        for read_index in range(reads):
            slot = upper * reads + read_index
            tile_ref[slot] = rows_contract(score_grads[read_index, :, at], keys[...])
            for flip in range(2):
                half = pl.ds(pl.multiple_of((side ^ flip) * piece, piece), piece)
                relative = 2 * upper + flip
                ref = query_send if relative & bits[0] else query_keep
                index = 2 * ((relative & bits[1]) // bits[1]) + (relative & bits[2]) // bits[2]
                ref[index, read_index] = tile_ref[slot, half, :]


def assemble_kernel(row_axis, low, *refs):
    key_out, value_out = refs[-2:]
    piece = key_out.shape[0] // GROUPS
    me = lax.axis_index(row_axis) // low
    for head_index in range(len(refs) // 2 - 1):
        cols = slice(head_index * HD, (head_index + 1) * HD)
        for first in range(2):
            source = refs[2 * head_index + first]
            for second in range(2):
                base = group_at(WEIGHT_BITS, (first, second), me)
                for high in range(2):
                    start = pl.multiple_of((base + LAST_BIT * high) * piece, piece)
                    key_out[pl.ds(start, piece), cols] = source[second, high, :, :HD]
                    value_out[pl.ds(start, piece), cols] = source[second, high, :, HD:]


def shape_of(shape, dtype=jnp.float32):
    return jax.ShapeDtypeStruct(shape, dtype)


def scatter_steps(keep, send, count, bits):
    for index, bit in enumerate(bits):
        theirs = swap(send, "rows", count, bit)
        if index + 1 == len(bits):
            return keep + theirs
        middle = keep.shape[0] // 2
        send = keep[middle:] + theirs[middle:]
        keep = keep[:middle] + theirs[:middle]


def on_device(row_devices, head_devices, inputs, key_weight, value_weight, queries, out_grad):
    reads, latents, columns = queries.shape
    head_count = columns // HD
    row_count, features = inputs.shape
    low = row_devices // GROUPS
    tile = latents // (GROUPS // 2)
    piece = features // GROUPS
    operands = (inputs, key_weight, value_weight, queries, out_grad)
    block_work = pl.CostEstimate(
        flops=8 * reads * row_count * latents * HD,
        bytes_accessed=4 * 2**20,
        transcendentals=reads * row_count * latents,
    )

    projected = []
    for head_index in range(head_count):
        first = head_index == 0
        loaded = [
            pltpu.VMEM(item.shape[:-1] + ((HD,) if place else item.shape[-1:]), item.dtype)
            for place, item in enumerate(operands)
        ]
        projected.append(
            pl.pallas_call(
                functools.partial(first_kernel, tile)
                if first
                else functools.partial(later_kernel, tile, head_index),
                out_shape=(
                    shape_of((row_count, HD), jnp.bfloat16),
                    shape_of((row_count, HD), jnp.bfloat16),
                    shape_of((2 * reads, latents)),
                ),
                in_specs=[HBM if first else VMEM] * 5,
                out_specs=(VMEM,) * 3,
                scratch_shapes=loaded + [pltpu.SemaphoreType.DMA((5,))] if first else [],
                compiler_params=params(57 if first else 16),
                cost_estimate=block_work,
                name="project",
            )(*operands)
        )

    stats_parts = []
    for head_index in range(head_count):
        stats = projected[head_index][2]
        for bit in bits_of(row_devices)[:-1]:
            theirs = swap(stats, "rows", row_devices, bit)
            stats = pl.pallas_call(
                merge_kernel,
                out_shape=shape_of(stats.shape),
                in_specs=[VMEM] * 2,
                out_specs=VMEM,
                compiler_params=params(2),
                name="merge",
            )(stats, theirs)
        stats_parts.append((stats, swap(stats, "rows", row_devices, bits_of(row_devices)[-1])))

    grads_out = []
    for head_index in range(head_count):
        last = head_index + 1 == head_count
        keys, values, _ = projected[head_index]
        operands = [inputs, keys, values, queries, out_grad, *stats_parts[head_index]]
        out_shape = [
            shape_of((row_count, 2 * HD), jnp.bfloat16),
            shape_of((reads, row_count, latents), jnp.bfloat16),
        ] + [shape_of((2, 2, piece, 2 * HD))] * 2
        scratch = [
            pltpu.VMEM((row_count, HD), jnp.float32),
            pltpu.VMEM((row_count, HD), jnp.float32),
            pltpu.VMEM((features, 2 * HD), jnp.float32),
            pltpu.VMEM((2 * reads, latents), jnp.float32),
        ]
        if last:
            operands += [key_weight, value_weight, grads_out[0][0]]
            share = (head_devices // 2, row_count, features // head_devices)
            out_shape += [shape_of(share), shape_of(share)]
            scratch += [pltpu.VMEM((row_count, features), jnp.float32)]
        grads_out.append(
            pl.pallas_call(
                functools.partial(grads_kernel, head_index, "rows", "heads", low, last),
                out_shape=out_shape,
                in_specs=[VMEM] * len(operands),
                out_specs=[VMEM] * len(out_shape),
                scratch_shapes=scratch,
                compiler_params=params(20),
                cost_estimate=block_work,
                name="grads",
            )(*operands)
        )

    query_out = []
    for head_index in range(head_count):
        share = (GROUPS // 2, reads, latents // GROUPS, HD)
        query_out.append(
            pl.pallas_call(
                functools.partial(query_kernel, QUERY_BITS[head_index % 2], "rows", low),
                out_shape=(shape_of(share), shape_of(share)),
                in_specs=[VMEM] * 2,
                out_specs=(VMEM,) * 2,
                scratch_shapes=[pltpu.VMEM((GROUPS // 2 * reads, tile, HD), jnp.float32)],
                compiler_params=params(16),
                cost_estimate=block_work,
                name="query",
            )(grads_out[head_index][1], projected[head_index][0])
        )

    order_low = (lax.axis_index("rows") % low) ^ jnp.arange(low, dtype=jnp.int32)
    low_bits = [bit for bit in bits_of(row_devices) if bit < low]

    def scatter_low(block, axis):
        if low == 1:
            return block
        parts = jnp.moveaxis(
            block.reshape(block.shape[:axis] + (low, -1) + block.shape[axis + 1 :]), axis, 0
        )
        parts = jnp.take(parts, order_low, axis=0)
        for bit in low_bits:
            parts = parts.reshape((-1, 2) + parts.shape[1:])
            parts = parts[:, 0] + swap(parts[:, 1], "rows", row_devices, bit)
        return parts[0]

    def sum_low(block):
        for bit in low_bits:
            block = block + swap(block, "rows", row_devices, bit)
        return block

    query_parts = []
    assembled = []
    for head_index in range(head_count):
        keep, send = grads_out[head_index][2:4]
        mine = scatter_steps(keep, send, row_devices, [bit * low for bit in WEIGHT_BITS])
        mine = mine + swap(mine, "rows", row_devices, LAST_BIT * low)
        mine = sum_low(mine)
        near = jnp.concatenate([mine, swap(mine, "rows", row_devices, WEIGHT_BITS[1] * low)], axis=0)
        assembled += [near, swap(near, "rows", row_devices, WEIGHT_BITS[0] * low)]
        keep, send = query_out[head_index]
        bits = [bit * low for bit in QUERY_BITS[head_index % 2]]
        mine = scatter_steps(keep, send, row_devices, bits)
        query_parts.append(scatter_low(mine[0], 1))
    query_grad = jnp.concatenate(query_parts, axis=2)

    key_weight_grad, value_weight_grad = pl.pallas_call(
        functools.partial(assemble_kernel, "rows", low),
        out_shape=(shape_of((features, columns)),) * 2,
        in_specs=[VMEM] * len(assembled),
        out_specs=(VMEM,) * 2,
        compiler_params=params(8),
        name="assemble",
    )(*assembled)

    input_keep, input_send = grads_out[-1][4:]
    total = input_keep + swap(input_send, "heads", head_devices, 1)
    for bit in bits_of(head_devices)[1:]:
        pairs = total.reshape((-1, 2) + total.shape[1:])
        total = pairs[:, 0] + swap(pairs[:, 1], "heads", head_devices, bit)
    return (query_grad, key_weight_grad, value_weight_grad, total[0])


def solution(mesh):
    in_specs = (
        P("rows", None),
        P(None, "heads"),
        P(None, "heads"),
        P(None, None, "heads"),
        P(None, None, "heads"),
    )
    out_specs = (P(None, "rows", "heads"), P(None, "heads"), P(None, "heads"), P("rows", "heads"))

    def body(*args):
        return on_device(mesh.shape["rows"], mesh.shape["heads"], *args)

    return jax.shard_map(body, mesh=mesh, in_specs=in_specs, out_specs=out_specs, check_vma=False)
```

time: 101 us -> 83.5 us (0.83)
  local copies, waits for them, and re-layouts: 8.03 us -> 0.06 us
  starting transfers between devices: 41.7 us -> 33.8 us
  Pallas kernels: 25.3 us -> 18.8 us
  waiting for transfers between devices: 23 us -> 28 us
    unnamed x32 -> x16, local copies, waits for them, and re-layouts: 8.01 us -> 0.04 us
    ppermute x23 -> x24, starting transfers between devices: 41.7 us -> 33.8 us  [swap(): return lax.ppermute(array, axis, pairs)]
    ppermute x23 -> x24, waiting for transfers between devices: 23 us -> 28 us  [swap(): return lax.ppermute(array, axis, pairs)]
    pallas_call x3 -> x4, Pallas kernels: 4.25 us -> 0.08 us  [on_device(): pl.pallas_call(merge_kernel, out_shape=shape_of(stats.shape), in_specs=[V...]
    pallas_call x3 -> x6, Pallas kernels: 20 us -> 17.6 us  [the longest x2 8.03 us: on_device(): pl.pallas_call(functools.partial(first_kernel, tile) if first else functo...]
  transfers between devices with their start and end apart: 23 -> 24, of which waited for: 12 -> 8; matrix products, arithmetic and copies ran while one was open for 2% -> 2% of each run, Pallas kernels for 7% -> 15%
where the time goes in v4:
time: 83.5 us; the launch traced here: 83.4 us
  starting transfers between devices  33.8 us (40%)
  waiting for transfers between devices  28 us (34%)
  Pallas kernels  18.8 us (23%)
  other arithmetic  1.85 us (2%)
  between operations  0.86 us (1%)
    ppermute x24, starting transfers between devices, swap(): return lax.ppermute(array, axis, pairs)  33.8 us
    ppermute x24, waiting for transfers between devices, swap(): return lax.ppermute(array, axis, pairs)  28 us
    pallas_call x2, Pallas kernels, on_device(): pl.pallas_call(functools.partial(first_kernel, tile) if first else functo...  8.03 us
    pallas_call x2, Pallas kernels, on_device(): pl.pallas_call(functools.partial(grads_kernel, head_index, 'rows', 'heads...  7.37 us
    pallas_call x2, Pallas kernels, on_device(): pl.pallas_call(functools.partial(query_kernel, QUERY_BITS[head_index % 2]...  2.23 us
  transfers between devices with their start and end apart: 24, of which 8 were waited for; matrix products, arithmetic and copies ran while one was open for 2% of the time, Pallas kernels for 15%

profile of v4, /device:TPU:0, one launch (start us, length us, event | category | flops | bytes accessed | tf_op | source)
XLA Modules:
  0.0 83.4 jit_solution(6845726484826011251)
XLA Ops:
  0.7 5.1 %project.2 = (bf16[512,128]{1,0:T(8,128)(2,1)}, bf16[512,128]{1,0:T(8,128)(2,1)}, f32[4,1024]{1,0:T(4,128)}) custom-call(bf16[512,512]{1,0:T(8,128)(2,1)} %refs_0_.7, bf16[512,256]{1,0:T(8,128)(2,1)} %refs_7_.1, bf16[512,256]{1,0:T(8,128)(2,1)} %refs_8_.1, bf16[2,1024,256]{2,1,0:T(8,128)(2,1)} %refs_3_.7, bf16[2,1024,256]{2,1,0:T(8,128)(2,1)} %refs_4_.7), custom_call_target="tpu_custom_call" | custom-call | flops 1073741824 | bytes 4194304 | tf_op jit(solution)/shard_map/project/pallas_call | solution.py:245
  5.9 3.0 %collective-permute-start = (f32[4,1024]{1,0:T(4,128)}, f32[4,1024]{1,0:T(4,128)S(1)}, u32[]{:S(2)}, u32[]{:S(2)}) collective-permute-start(f32[4,1024]{1,0:T(4,128)} %get-tuple-element.27.mine), channel_id=1, source_target_pairs={{0,4},{4,0},{8,12},{12,8},{16,20},{20,16},{24,28},{28,24},{1,5},{5... | collective-permute-start | bytes 49160 | tf_op jit(solution)/shard_map/ppermute | solution.py:40
  8.9 2.9 %project.3 = (bf16[512,128]{1,0:T(8,128)(2,1)S(1)}, bf16[512,128]{1,0:T(8,128)(2,1)S(1)}, f32[4,1024]{1,0:T(4,128)S(1)}) custom-call(bf16[512,512]{1,0:T(8,128)(2,1)S(1)} %copy-done.3, bf16[512,256]{1,0:T(8,128)(2,1)S(1)} %copy-done.4, bf16[512,256]{1,0:T(8,128)(2,1)S(1)} %copy-done.5, bf16[2,1024,256]{2,1,0:T(8,128)(2,1)S(1)} %copy-done.1, ...), custom_call_target="tpu_custom_call" | custom-call | flops 1073741824 | bytes 4194304 | tf_op jit(solution)/shard_map/project/pallas_call | solution.py:245
  11.9 2.1 %collective-permute-start.1 = (f32[4,1024]{1,0:T(4,128)S(1)}, f32[4,1024]{1,0:T(4,128)S(1)}, u32[]{:S(2)}, u32[]{:S(2)}) collective-permute-start(f32[4,1024]{1,0:T(4,128)S(1)} %merge.4.mine), channel_id=1, source_target_pairs={{0,8},{4,12},{8,0},{12,4},{16,24},{20,28},{24,16},{28,20},{1,9},{5... | collective-permute-start | bytes 49160 | tf_op jit(solution)/shard_map/ppermute | solution.py:40
  14.1 1.5 %collective-permute-done.6.theirs = f32[4,1024]{1,0:T(4,128)S(1)} collective-permute-done((f32[4,1024]{1,0:T(4,128)S(1)}, f32[4,1024]{1,0:T(4,128)S(1)}, u32[]{:S(2)}, u32[]{:S(2)}) %collective-permute-start.6) | collective-permute-done | bytes 16416 | tf_op jit(solution)/shard_map/ppermute | solution.py:40
  15.6 1.6 %collective-permute-start.7 = (f32[4,1024]{1,0:T(4,128)S(1)}, f32[4,1024]{1,0:T(4,128)S(1)}, u32[]{:S(2)}, u32[]{:S(2)}) collective-permute-start(f32[4,1024]{1,0:T(4,128)S(1)} %merge.6.mine), channel_id=1, source_target_pairs={{0,8},{4,12},{8,0},{12,4},{16,24},{20,28},{24,16},{28,20},{1,9},{5... | collective-permute-start | bytes 49160 | tf_op jit(solution)/shard_map/ppermute | solution.py:40
  17.3 2.7 %collective-permute-start.2 = (f32[4,1024]{1,0:T(4,128)S(1)}, f32[4,1024]{1,0:T(4,128)S(1)}, u32[]{:S(2)}, u32[]{:S(2)}) collective-permute-start(f32[4,1024]{1,0:T(4,128)S(1)} %merge.5.refs_5_), channel_id=1, source_target_pairs={{0,16},{4,20},{8,24},{12,28},{16,0},{20,4},{24,8},{28,12},{1,17},{... | collective-permute-start | bytes 49160 | tf_op jit(solution)/shard_map/ppermute | solution.py:40
  20.0 2.2 %collective-permute-start.8 = (f32[4,1024]{1,0:T(4,128)S(1)}, f32[4,1024]{1,0:T(4,128)S(1)}, u32[]{:S(2)}, u32[]{:S(2)}) collective-permute-start(f32[4,1024]{1,0:T(4,128)S(1)} %merge.7.refs_5_), channel_id=1, source_target_pairs={{0,16},{4,20},{8,24},{12,28},{16,0},{20,4},{24,8},{28,12},{1,17},{... | collective-permute-start | bytes 49160 | tf_op jit(solution)/shard_map/ppermute | solution.py:40
  22.2 3.3 %grads.2 = (bf16[512,256]{1,0:T(8,128)(2,1)S(1)}, bf16[2,512,1024]{2,1,0:T(8,128)(2,1)S(1)}, f32[2,2,64,256]{3,2,1,0:T(8,128)S(1)}, f32[2,2,64,256]{3,2,1,0:T(8,128)S(1)}) custom-call(bf16[512,512]{1,0:T(8,128)(2,1)S(1)} %copy-done.3, bf16[512,128]{1,0:T(8,128)(2,1)S(1)} %copy-done.6, bf16[512,128]{1,0:T(8,128)(2,1)S(1)} %copy-done.7, ...), custom_call_target="tpu_custom_call" | custom-call | flops 1073741824 | bytes 4194304 | tf_op jit(solution)/shard_map/grads/pallas_call | solution.py:299
  27.1 1.7 %collective-permute-start.3 = (f32[4,2,128,128]{3,2,1,0:T(8,128)S(1)}, f32[4,2,128,128]{3,2,1,0:T(8,128)S(1)}, u32[]{:S(2)}, u32[]{:S(2)}) collective-permute-start(f32[4,2,128,128]{3,2,1,0:T(8,128)S(1)} %get-tuple-element.30), channel_id=1, source_target_pairs={{0,4},{4,0},{8,12},{12,8},{16,20},{20,16},{24,28},{28,24},{1,5},{5... | collective-permute-start | bytes 1572872 | tf_op jit(solution)/shard_map/ppermute | solution.py:40
  28.8 4.1 %grads.3 = (bf16[512,256]{1,0:T(8,128)(2,1)}, bf16[2,512,1024]{2,1,0:T(8,128)(2,1)S(1)}, f32[2,2,64,256]{3,2,1,0:T(8,128)S(1)}, f32[2,2,64,256]{3,2,1,0:T(8,128)...) custom-call(bf16[512,512]{1,0:T(8,128)(2,1)S(1)} %copy-done.3, ...), custom_call_target="tpu_custom_call" | custom-call | flops 1073741824 | bytes 4194304 | tf_op jit(solution)/shard_map/grads/pallas_call | solution.py:299
  34.4 1.8 %collective-permute-start.9 = (f32[4,2,128,128]{3,2,1,0:T(8,128)S(1)}, f32[4,2,128,128]{3,2,1,0:T(8,128)S(1)}, u32[]{:S(2)}, u32[]{:S(2)}) collective-permute-start(f32[4,2,128,128]{3,2,1,0:T(8,128)S(1)} %get-tuple-element.37), channel_id=1, source_target_pairs={{0,8},{4,12},{8,0},{12,4},{16,24},{20,28},{24,16},{28,20},{1,9},{5... | collective-permute-start | bytes 1572872 | tf_op jit(solution)/shard_map/ppermute | solution.py:40
  36.6 10.9 %collective-permute-done.17 = f32[2,2,64,256]{3,2,1,0:T(8,128)S(1)} collective-permute-done((f32[2,2,64,256]{3,2,1,0:T(8,128)S(1)}, f32[2,2,64,256]{3,2,1,0:T(8,128)S(1)}, u32[]{:S(2)}, u32[]{:S(2)}) %collective-permute-start.17) | collective-permute-done | bytes 262176 | tf_op jit(solution)/shard_map/ppermute | solution.py:40
  47.6 1.6 %collective-permute-start.18 = (f32[1,2,64,256]{3,2,1,0:T(8,128)S(1)}, f32[1,2,64,256]{3,2,1,0:T(8,128)S(1)}, u32[]{:S(2)}, u32[]{:S(2)}) collective-permute-start(f32[1,2,64,256]{3,2,1,0:T(8,128)S(1)} %slice_add_fusion.4), channel_id=1, source_target_pairs={{0,8},{4,12},{8,0},{12,4},{16,24},{20,28},{24,16},{28,20},{1,9},{5... | collective-permute-start | bytes 393224 | tf_op jit(solution)/shard_map/ppermute | solution.py:40
  49.2 2.8 %collective-permute-start.14 = (f32[1,2,64,256]{3,2,1,0:T(8,128)S(1)}, f32[1,2,64,256]{3,2,1,0:T(8,128)S(1)}, u32[]{:S(2)}, u32[]{:S(2)}) collective-permute-start(f32[1,2,64,256]{3,2,1,0:T(8,128)S(1)} %fusion.3), channel_id=1, source_target_pairs={{0,16},{4,20},{8,24},{12,28},{16,0},{20,4},{24,8},{28,12},{1,17},{... | collective-permute-start | bytes 393224 | tf_op jit(solution)/shard_map/ppermute | solution.py:40
  52.6 2.7 %collective-permute-start.19 = (f32[1,2,64,256]{3,2,1,0:T(8,128)S(1)}, f32[1,2,64,256]{3,2,1,0:T(8,128)S(1)}, u32[]{:S(2)}, u32[]{:S(2)}) collective-permute-start(f32[1,2,64,256]{3,2,1,0:T(8,128)S(1)} %fusion.2), channel_id=1, source_target_pairs={{0,16},{4,20},{8,24},{12,28},{16,0},{20,4},{24,8},{28,12},{1,17},{... | collective-permute-start | bytes 393224 | tf_op jit(solution)/shard_map/ppermute | solution.py:40
  56.2 1.7 %collective-permute-start.10 = (f32[2,2,128,128]{3,2,1,0:T(8,128)S(1)}, f32[2,2,128,128]{3,2,1,0:T(8,128)S(1)}, u32[]{:S(2)}, u32[]{:S(2)}) collective-permute-start(f32[2,2,128,128]{3,2,1,0:T(8,128)S(1)} %get-tuple-element.49), channel_id=1, source_target_pairs={{0,4},{4,0},{8,12},{12,8},{16,20},{20,16},{24,28},{28,24},{1,5},{5... | collective-permute-start | bytes 786440 | tf_op jit(solution)/shard_map/ppermute | solution.py:40
  58.0 1.6 %collective-permute-done.14 = f32[1,2,64,256]{3,2,1,0:T(8,128)S(1)} collective-permute-done((f32[1,2,64,256]{3,2,1,0:T(8,128)S(1)}, f32[1,2,64,256]{3,2,1,0:T(8,128)S(1)}, u32[]{:S(2)}, u32[]{:S(2)}) %collective-permute-start.14) | collective-permute-done | bytes 131104 | tf_op jit(solution)/shard_map/ppermute | solution.py:40
  59.7 2.3 %collective-permute-done.19 = f32[1,2,64,256]{3,2,1,0:T(8,128)S(1)} collective-permute-done((f32[1,2,64,256]{3,2,1,0:T(8,128)S(1)}, f32[1,2,64,256]{3,2,1,0:T(8,128)S(1)}, u32[]{:S(2)}, u32[]{:S(2)}) %collective-permute-start.19) | collective-permute-done | bytes 131104 | tf_op jit(solution)/shard_map/ppermute | solution.py:40
  62.1 1.6 %collective-permute-start.23 = (f32[1,512,128]{2,1,0:T(8,128)S(1)}, f32[1,512,128]{2,1,0:T(8,128)S(1)}, u32[]{:S(2)}, u32[]{:S(2)}) collective-permute-start(f32[1,512,128]{2,1,0:T(8,128)S(1)} %slice_bitcast_fusion), channel_id=1, source_target_pairs={{0,2},{1,3},{2,0},{3,1},{4,6},{5,7},{6,4},{7,5},{8,10},{9,11},{10,... | collective-permute-start | bytes 786440 | tf_op jit(solution)/shard_map/ppermute | solution.py:40
  63.8 3.9 %collective-permute-done.15 = f32[1,2,64,256]{3,2,1,0:T(8,128)S(1)} collective-permute-done((f32[1,2,64,256]{3,2,1,0:T(8,128)S(1)}, f32[1,2,64,256]{3,2,1,0:T(8,128)S(1)}, u32[]{:S(2)}, u32[]{:S(2)}) %collective-permute-start.15) | collective-permute-done | bytes 131104 | tf_op jit(solution)/shard_map/ppermute | solution.py:40
  67.7 1.4 %collective-permute-start.16 = (f32[2,2,64,256]{3,2,1,0:T(8,128)S(1)}, f32[2,2,64,256]{3,2,1,0:T(8,128)S(1)}, u32[]{:S(2)}, u32[]{:S(2)}) collective-permute-start(f32[2,2,64,256]{3,2,1,0:T(8,128)S(1)} %pad_maximum_fusion.1.refs_0_), channel_id=1, source_target_pairs={{0,4},{4,0},{8,12},{12,8},{16,20},{20,16},{24,28},{28,24},{1,5},{5... | collective-permute-start | bytes 786440 | tf_op jit(solution)/shard_map/ppermute | solution.py:40
  71.6 2.0 %collective-permute-start.11 = (f32[1,2,128,128]{3,2,1,0:T(8,128)S(1)}, f32[1,2,128,128]{3,2,1,0:T(8,128)S(1)}, u32[]{:S(2)}, u32[]{:S(2)}) collective-permute-start(f32[1,2,128,128]{3,2,1,0:T(8,128)S(1)} %slice_add_fusion.8), channel_id=1, source_target_pairs={{0,16},{4,20},{8,24},{12,28},{16,0},{20,4},{24,8},{28,12},{1,17},{... | collective-permute-start | bytes 393224 | tf_op jit(solution)/shard_map/ppermute | solution.py:40
  74.4 5.7 %collective-permute-done.5 = f32[1,2,128,128]{3,2,1,0:T(8,128)S(1)} collective-permute-done((f32[1,2,128,128]{3,2,1,0:T(8,128)S(1)}, f32[1,2,128,128]{3,2,1,0:T(8,128)S(1)}, u32[]{:S(2)}, u32[]{:S(2)}) %collective-permute-start.5) | collective-permute-done | bytes 131104 | tf_op jit(solution)/shard_map/ppermute | solution.py:40
  (69 shorter events, 12.1 us)
Async XLA Ops:
  5.9 6.0 %collective-permute-start = (f32[4,1024]{1,0:T(4,128)}, f32[4,1024]{1,0:T(4,128)S(1)}, u32[]{:S(2)}, u32[]{:S(2)}) collective-permute-start(f32[4,1024]{1,0:T(4,128)} %get-tuple-element.27.mine), channel_id=1, source_target_pairs={{0,4},{4,0},{8,12},{12,8},{16,20},{20,16},{24,28},{28,24},{1,5},{5... | collective-permute-start | bytes 49160 | tf_op jit(solution)/shard_map/ppermute | solution.py:40
  11.8 3.8 %collective-permute-start.6 = (f32[4,1024]{1,0:T(4,128)S(1)}, f32[4,1024]{1,0:T(4,128)S(1)}, u32[]{:S(2)}, u32[]{:S(2)}) collective-permute-start(f32[4,1024]{1,0:T(4,128)S(1)} %get-tuple-element.33.mine), channel_id=1, source_target_pairs={{0,4},{4,0},{8,12},{12,8},{16,20},{20,16},{24,28},{28,24},{1,5},{5... | collective-permute-start | bytes 49160 | tf_op jit(solution)/shard_map/ppermute | solution.py:40
  11.9 5.3 %collective-permute-start.1 = (f32[4,1024]{1,0:T(4,128)S(1)}, f32[4,1024]{1,0:T(4,128)S(1)}, u32[]{:S(2)}, u32[]{:S(2)}) collective-permute-start(f32[4,1024]{1,0:T(4,128)S(1)} %merge.4.mine), channel_id=1, source_target_pairs={{0,8},{4,12},{8,0},{12,4},{16,24},{20,28},{24,16},{28,20},{1,9},{5... | collective-permute-start | bytes 49160 | tf_op jit(solution)/shard_map/ppermute | solution.py:40
  15.6 4.3 %collective-permute-start.7 = (f32[4,1024]{1,0:T(4,128)S(1)}, f32[4,1024]{1,0:T(4,128)S(1)}, u32[]{:S(2)}, u32[]{:S(2)}) collective-permute-start(f32[4,1024]{1,0:T(4,128)S(1)} %merge.6.mine), channel_id=1, source_target_pairs={{0,8},{4,12},{8,0},{12,4},{16,24},{20,28},{24,16},{28,20},{1,9},{5... | collective-permute-start | bytes 49160 | tf_op jit(solution)/shard_map/ppermute | solution.py:40
  17.3 4.9 %collective-permute-start.2 = (f32[4,1024]{1,0:T(4,128)S(1)}, f32[4,1024]{1,0:T(4,128)S(1)}, u32[]{:S(2)}, u32[]{:S(2)}) collective-permute-start(f32[4,1024]{1,0:T(4,128)S(1)} %merge.5.refs_5_), channel_id=1, source_target_pairs={{0,16},{4,20},{8,24},{12,28},{16,0},{20,4},{24,8},{28,12},{1,17},{... | collective-permute-start | bytes 49160 | tf_op jit(solution)/shard_map/ppermute | solution.py:40
  20.0 8.8 %collective-permute-start.8 = (f32[4,1024]{1,0:T(4,128)S(1)}, f32[4,1024]{1,0:T(4,128)S(1)}, u32[]{:S(2)}, u32[]{:S(2)}) collective-permute-start(f32[4,1024]{1,0:T(4,128)S(1)} %merge.7.refs_5_), channel_id=1, source_target_pairs={{0,16},{4,20},{8,24},{12,28},{16,0},{20,4},{24,8},{28,12},{1,17},{... | collective-permute-start | bytes 49160 | tf_op jit(solution)/shard_map/ppermute | solution.py:40
  25.5 10.7 %collective-permute-start.12 = (f32[2,2,64,256]{3,2,1,0:T(8,128)S(1)}, f32[2,2,64,256]{3,2,1,0:T(8,128)S(1)}, u32[]{:S(2)}, u32[]{:S(2)}) collective-permute-start(f32[2,2,64,256]{3,2,1,0:T(8,128)S(1)} %get-tuple-element.39), channel_id=1, source_target_pairs={{0,4},{4,0},{8,12},{12,8},{16,20},{20,16},{24,28},{28,24},{1,5},{5... | collective-permute-start | bytes 786440 | tf_op jit(solution)/shard_map/ppermute | solution.py:40
  27.1 28.2 %collective-permute-start.3 = (f32[4,2,128,128]{3,2,1,0:T(8,128)S(1)}, f32[4,2,128,128]{3,2,1,0:T(8,128)S(1)}, u32[]{:S(2)}, u32[]{:S(2)}) collective-permute-start(f32[4,2,128,128]{3,2,1,0:T(8,128)S(1)} %get-tuple-element.30), channel_id=1, source_target_pairs={{0,4},{4,0},{8,12},{12,8},{16,20},{20,16},{24,28},{28,24},{1,5},{5... | collective-permute-start | bytes 1572872 | tf_op jit(solution)/shard_map/ppermute | solution.py:40
  32.9 14.6 %collective-permute-start.17 = (f32[2,2,64,256]{3,2,1,0:T(8,128)S(1)}, f32[2,2,64,256]{3,2,1,0:T(8,128)S(1)}, u32[]{:S(2)}, u32[]{:S(2)}) collective-permute-start(f32[2,2,64,256]{3,2,1,0:T(8,128)S(1)} %get-tuple-element.41), channel_id=1, source_target_pairs={{0,4},{4,0},{8,12},{12,8},{16,20},{20,16},{24,28},{28,24},{1,5},{5... | collective-permute-start | bytes 786440 | tf_op jit(solution)/shard_map/ppermute | solution.py:40
  34.4 21.7 %collective-permute-start.9 = (f32[4,2,128,128]{3,2,1,0:T(8,128)S(1)}, f32[4,2,128,128]{3,2,1,0:T(8,128)S(1)}, u32[]{:S(2)}, u32[]{:S(2)}) collective-permute-start(f32[4,2,128,128]{3,2,1,0:T(8,128)S(1)} %get-tuple-element.37), channel_id=1, source_target_pairs={{0,8},{4,12},{8,0},{12,4},{16,24},{20,28},{24,16},{28,20},{1,9},{5... | collective-permute-start | bytes 1572872 | tf_op jit(solution)/shard_map/ppermute | solution.py:40
  36.2 21.7 %collective-permute-start.22 = (f32[2,512,128]{2,1,0:T(8,128)S(1)}, f32[2,512,128]{2,1,0:T(8,128)S(1)}, u32[]{:S(2)}, u32[]{:S(2)}) collective-permute-start(f32[2,512,128]{2,1,0:T(8,128)S(1)} %get-tuple-element.45), channel_id=1, source_target_pairs={{0,1},{1,0},{2,3},{3,2},{4,5},{5,4},{6,7},{7,6},{8,9},{9,8},{10,11... | collective-permute-start | bytes 1572872 | tf_op jit(solution)/shard_map/ppermute | solution.py:40
  36.2 12.9 %collective-permute-start.13 = (f32[1,2,64,256]{3,2,1,0:T(8,128)S(1)}, f32[1,2,64,256]{3,2,1,0:T(8,128)S(1)}, u32[]{:S(2)}, u32[]{:S(2)}) collective-permute-start(f32[1,2,64,256]{3,2,1,0:T(8,128)S(1)} %slice_add_fusion.6), channel_id=1, source_target_pairs={{0,8},{4,12},{8,0},{12,4},{16,24},{20,28},{24,16},{28,20},{1,9},{5... | collective-permute-start | bytes 393224 | tf_op jit(solution)/shard_map/ppermute | solution.py:40
  47.6 5.0 %collective-permute-start.18 = (f32[1,2,64,256]{3,2,1,0:T(8,128)S(1)}, f32[1,2,64,256]{3,2,1,0:T(8,128)S(1)}, u32[]{:S(2)}, u32[]{:S(2)}) collective-permute-start(f32[1,2,64,256]{3,2,1,0:T(8,128)S(1)} %slice_add_fusion.4), channel_id=1, source_target_pairs={{0,8},{4,12},{8,0},{12,4},{16,24},{20,28},{24,16},{28,20},{1,9},{5... | collective-permute-start | bytes 393224 | tf_op jit(solution)/shard_map/ppermute | solution.py:40
  49.2 10.4 %collective-permute-start.14 = (f32[1,2,64,256]{3,2,1,0:T(8,128)S(1)}, f32[1,2,64,256]{3,2,1,0:T(8,128)S(1)}, u32[]{:S(2)}, u32[]{:S(2)}) collective-permute-start(f32[1,2,64,256]{3,2,1,0:T(8,128)S(1)} %fusion.3), channel_id=1, source_target_pairs={{0,16},{4,20},{8,24},{12,28},{16,0},{20,4},{24,8},{28,12},{1,17},{... | collective-permute-start | bytes 393224 | tf_op jit(solution)/shard_map/ppermute | solution.py:40
  52.6 9.4 %collective-permute-start.19 = (f32[1,2,64,256]{3,2,1,0:T(8,128)S(1)}, f32[1,2,64,256]{3,2,1,0:T(8,128)S(1)}, u32[]{:S(2)}, u32[]{:S(2)}) collective-permute-start(f32[1,2,64,256]{3,2,1,0:T(8,128)S(1)} %fusion.2), channel_id=1, source_target_pairs={{0,16},{4,20},{8,24},{12,28},{16,0},{20,4},{24,8},{28,12},{1,17},{... | collective-permute-start | bytes 393224 | tf_op jit(solution)/shard_map/ppermute | solution.py:40
  55.3 15.3 %collective-permute-start.4 = (f32[2,2,128,128]{3,2,1,0:T(8,128)S(1)}, f32[2,2,128,128]{3,2,1,0:T(8,128)S(1)}, u32[]{:S(2)}, u32[]{:S(2)}) collective-permute-start(f32[2,2,128,128]{3,2,1,0:T(8,128)S(1)} %get-tuple-element.47), channel_id=1, source_target_pairs={{0,8},{4,12},{8,0},{12,4},{16,24},{20,28},{24,16},{28,20},{1,9},{5... | collective-permute-start | bytes 786440 | tf_op jit(solution)/shard_map/ppermute | solution.py:40
  56.2 15.4 %collective-permute-start.10 = (f32[2,2,128,128]{3,2,1,0:T(8,128)S(1)}, f32[2,2,128,128]{3,2,1,0:T(8,128)S(1)}, u32[]{:S(2)}, u32[]{:S(2)}) collective-permute-start(f32[2,2,128,128]{3,2,1,0:T(8,128)S(1)} %get-tuple-element.49), channel_id=1, source_target_pairs={{0,4},{4,0},{8,12},{12,8},{16,20},{20,16},{24,28},{28,24},{1,5},{5... | collective-permute-start | bytes 786440 | tf_op jit(solution)/shard_map/ppermute | solution.py:40
  59.6 8.1 %collective-permute-start.15 = (f32[1,2,64,256]{3,2,1,0:T(8,128)S(1)}, f32[1,2,64,256]{3,2,1,0:T(8,128)S(1)}, u32[]{:S(2)}, u32[]{:S(2)}) collective-permute-start(f32[1,2,64,256]{3,2,1,0:T(8,128)S(1)} %add.73), channel_id=1, source_target_pairs={{0,8},{4,12},{8,0},{12,4},{16,24},{20,28},{24,16},{28,20},{1,9},{5... | collective-permute-start | bytes 393224 | tf_op jit(solution)/shard_map/ppermute | solution.py:40
  62.0 7.2 %collective-permute-start.20 = (f32[1,2,64,256]{3,2,1,0:T(8,128)S(1)}, f32[1,2,64,256]{3,2,1,0:T(8,128)S(1)}, u32[]{:S(2)}, u32[]{:S(2)}) collective-permute-start(f32[1,2,64,256]{3,2,1,0:T(8,128)S(1)} %add.77), channel_id=1, source_target_pairs={{0,8},{4,12},{8,0},{12,4},{16,24},{20,28},{24,16},{28,20},{1,9},{5... | collective-permute-start | bytes 393224 | tf_op jit(solution)/shard_map/ppermute | solution.py:40
  62.1 11.5 %collective-permute-start.23 = (f32[1,512,128]{2,1,0:T(8,128)S(1)}, f32[1,512,128]{2,1,0:T(8,128)S(1)}, u32[]{:S(2)}, u32[]{:S(2)}) collective-permute-start(f32[1,512,128]{2,1,0:T(8,128)S(1)} %slice_bitcast_fusion), channel_id=1, source_target_pairs={{0,2},{1,3},{2,0},{3,1},{4,6},{5,7},{6,4},{7,5},{8,10},{9,11},{10,... | collective-permute-start | bytes 786440 | tf_op jit(solution)/shard_map/ppermute | solution.py:40
  67.7 14.6 %collective-permute-start.16 = (f32[2,2,64,256]{3,2,1,0:T(8,128)S(1)}, f32[2,2,64,256]{3,2,1,0:T(8,128)S(1)}, u32[]{:S(2)}, u32[]{:S(2)}) collective-permute-start(f32[2,2,64,256]{3,2,1,0:T(8,128)S(1)} %pad_maximum_fusion.1.refs_0_), channel_id=1, source_target_pairs={{0,4},{4,0},{8,12},{12,8},{16,20},{20,16},{24,28},{28,24},{1,5},{5... | collective-permute-start | bytes 786440 | tf_op jit(solution)/shard_map/ppermute | solution.py:40
  69.2 13.1 %collective-permute-start.21 = (f32[2,2,64,256]{3,2,1,0:T(8,128)S(1)}, f32[2,2,64,256]{3,2,1,0:T(8,128)S(1)}, u32[]{:S(2)}, u32[]{:S(2)}) collective-permute-start(f32[2,2,64,256]{3,2,1,0:T(8,128)S(1)} %pad_maximum_fusion.2.refs_2_), channel_id=1, source_target_pairs={{0,4},{4,0},{8,12},{12,8},{16,20},{20,16},{24,28},{28,24},{1,5},{5... | collective-permute-start | bytes 786440 | tf_op jit(solution)/shard_map/ppermute | solution.py:40
  70.6 9.6 %collective-permute-start.5 = (f32[1,2,128,128]{3,2,1,0:T(8,128)S(1)}, f32[1,2,128,128]{3,2,1,0:T(8,128)S(1)}, u32[]{:S(2)}, u32[]{:S(2)}) collective-permute-start(f32[1,2,128,128]{3,2,1,0:T(8,128)S(1)} %slice_add_fusion.10), channel_id=1, source_target_pairs={{0,16},{4,20},{8,24},{12,28},{16,0},{20,4},{24,8},{28,12},{1,17},{... | collective-permute-start | bytes 393224 | tf_op jit(solution)/shard_map/ppermute | solution.py:40
  71.6 9.9 %collective-permute-start.11 = (f32[1,2,128,128]{3,2,1,0:T(8,128)S(1)}, f32[1,2,128,128]{3,2,1,0:T(8,128)S(1)}, u32[]{:S(2)}, u32[]{:S(2)}) collective-permute-start(f32[1,2,128,128]{3,2,1,0:T(8,128)S(1)} %slice_add_fusion.8), channel_id=1, source_target_pairs={{0,16},{4,20},{8,24},{12,28},{16,0},{20,4},{24,8},{28,12},{1,17},{... | collective-permute-start | bytes 393224 | tf_op jit(solution)/shard_map/ppermute | solution.py:40
  (8 other events, 79.9 us)

commit v5 on v4

--- a/solution.py
+++ b/solution.py
@@ -49,7 +49,7 @@
     keys[...] = plain_dot(inputs[...], key_weight[:, cols]).astype(jnp.bfloat16)
     values[...] = plain_dot(inputs[...], value_weight[:, cols]).astype(jnp.bfloat16)
 
-    @pl.loop(0, latents // tile)
+    @pl.loop(0, latents // tile, unroll=True)
     def _(step):
         at = pl.ds(pl.multiple_of(step * tile, tile), tile)
         for read_index in range(reads):
@@ -108,7 +108,7 @@
 
 WEIGHT_BITS = (1, 2)
 LAST_BIT = 4
-QUERY_BITS = ((1, 2, 4), (2, 1, 4))
+QUERY_BITS = ((2, 1, 4), (1, 2, 4))
 
 
 def grads_kernel(head_index, row_axis, head_axis, low, last, *refs):
@@ -130,7 +130,7 @@
     key_acc[...] = jnp.zeros_like(key_acc)
     value_acc[...] = jnp.zeros_like(value_acc)
 
-    @pl.loop(0, latents // tile)
+    @pl.loop(0, latents // tile, unroll=True)
     def _(step):
         at = pl.ds(pl.multiple_of(step * tile, tile), tile)
         for read_index in range(reads):
@@ -190,12 +190,16 @@
                 ref[index, read_index] = tile_ref[slot, half, :]
 
 
-def assemble_kernel(row_axis, low, *refs):
-    key_out, value_out = refs[-2:]
+def assemble_kernel(head_count, row_axis, low, *refs):
+    query_out, key_out, value_out = refs[-3:]
+    query_parts = refs[2 * head_count : -3]
+    terms = len(query_parts) // head_count
     piece = key_out.shape[0] // GROUPS
     me = lax.axis_index(row_axis) // low
-    for head_index in range(len(refs) // 2 - 1):
+    for head_index in range(head_count):
         cols = slice(head_index * HD, (head_index + 1) * HD)
+        parts = query_parts[head_index * terms : (head_index + 1) * terms]
+        query_out[:, :, cols] = sum(part[0] for part in parts[1:]) + parts[0][0]
         for first in range(2):
             source = refs[2 * head_index + first]
             for second in range(2):
@@ -214,7 +218,7 @@
     for index, bit in enumerate(bits):
         theirs = swap(send, "rows", count, bit)
         if index + 1 == len(bits):
-            return keep + theirs
+            return keep, theirs
         middle = keep.shape[0] // 2
         send = keep[middle:] + theirs[middle:]
         keep = keep[:middle] + theirs[:middle]
@@ -348,25 +352,29 @@
     assembled = []
     for head_index in range(head_count):
         keep, send = grads_out[head_index][2:4]
-        mine = scatter_steps(keep, send, row_devices, [bit * low for bit in WEIGHT_BITS])
+        mine, theirs = scatter_steps(keep, send, row_devices, [bit * low for bit in WEIGHT_BITS])
+        mine = mine + theirs
         mine = mine + swap(mine, "rows", row_devices, LAST_BIT * low)
         mine = sum_low(mine)
         near = jnp.concatenate([mine, swap(mine, "rows", row_devices, WEIGHT_BITS[1] * low)], axis=0)
         assembled += [near, swap(near, "rows", row_devices, WEIGHT_BITS[0] * low)]
         keep, send = query_out[head_index]
         bits = [bit * low for bit in QUERY_BITS[head_index % 2]]
-        mine = scatter_steps(keep, send, row_devices, bits)
-        query_parts.append(scatter_low(mine[0], 1))
-    query_grad = jnp.concatenate(query_parts, axis=2)
-
-    key_weight_grad, value_weight_grad = pl.pallas_call(
-        functools.partial(assemble_kernel, "rows", low),
-        out_shape=(shape_of((features, columns)),) * 2,
-        in_specs=[VMEM] * len(assembled),
-        out_specs=(VMEM,) * 2,
+        mine, theirs = scatter_steps(keep, send, row_devices, bits)
+        if low == 1:
+            query_parts += [mine, theirs]
+        else:
+            query_parts.append(scatter_low((mine + theirs)[0], 1)[None])
+
+    query_grad, key_weight_grad, value_weight_grad = pl.pallas_call(
+        functools.partial(assemble_kernel, head_count, "rows", low),
+        out_shape=(shape_of((reads, latents // row_devices, columns)),)
+        + (shape_of((features, columns)),) * 2,
+        in_specs=[VMEM] * (len(assembled) + len(query_parts)),
+        out_specs=(VMEM,) * 3,
         compiler_params=params(8),
         name="assemble",
-    )(*assembled)
+    )(*assembled, *query_parts)
 
     input_keep, input_send = grads_out[-1][4:]
     total = input_keep + swap(input_send, "heads", head_devices, 1)

time: 83.5 us -> 77.7 us (0.931)
  waiting for transfers between devices: 28 us -> 24 us
  Pallas kernels: 18.8 us -> 17.1 us
    ppermute x24, waiting for transfers between devices: 28 us -> 24 us  [swap(): return lax.ppermute(array, axis, pairs)]
    pallas_call x2, Pallas kernels: 8.03 us -> 6.47 us  [on_device(): pl.pallas_call(functools.partial(first_kernel, tile) if first else functo...]
  transfers between devices with their start and end apart: 24 -> 24, of which waited for: 8 -> 10; matrix products, arithmetic and copies ran while one was open for 2% -> 1% of each run, Pallas kernels for 15% -> 15%
where the time goes in v5:
time: 77.7 us; the launch traced here: 77.6 us
  starting transfers between devices  34.4 us (44%)
  waiting for transfers between devices  24 us (31%)
  Pallas kernels  17.1 us (22%)
  other arithmetic  1.13 us (1%)
  between operations  0.87 us (1%)
    ppermute x24, starting transfers between devices, swap(): return lax.ppermute(array, axis, pairs)  34.4 us
    ppermute x24, waiting for transfers between devices, swap(): return lax.ppermute(array, axis, pairs)  24 us
    pallas_call x2, Pallas kernels, on_device(): pl.pallas_call(functools.partial(grads_kernel, head_index, 'rows', 'heads...  7.17 us
    pallas_call x2, Pallas kernels, on_device(): pl.pallas_call(functools.partial(first_kernel, tile) if first else functo...  6.47 us
    pallas_call x2, Pallas kernels, on_device(): pl.pallas_call(functools.partial(query_kernel, QUERY_BITS[head_index % 2]...  2.22 us
  transfers between devices with their start and end apart: 24, of which 10 were waited for; matrix products, arithmetic and copies ran while one was open for 1% of the time, Pallas kernels for 15%

profile of v5, /device:TPU:0, one launch (start us, length us, event | category | flops | bytes accessed | tf_op | source)
XLA Modules:
  0.0 77.6 jit_solution(3636058075497546485)
XLA Ops:
  0.7 4.3 %project.2 = (bf16[512,128]{1,0:T(8,128)(2,1)}, bf16[512,128]{1,0:T(8,128)(2,1)}, f32[4,1024]{1,0:T(4,128)}) custom-call(bf16[512,512]{1,0:T(8,128)(2,1)} %refs_0_.7, bf16[512,256]{1,0:T(8,128)(2,1)} %refs_7_.1, bf16[512,256]{1,0:T(8,128)(2,1)} %refs_8_.1, bf16[2,1024,256]{2,1,0:T(8,128)(2,1)} %refs_3_.7, bf16[2,1024,256]{2,1,0:T(8,128)(2,1)} %refs_4_.7), custom_call_target="tpu_custom_call" | custom-call | flops 1073741824 | bytes 4194304 | tf_op jit(solution)/shard_map/project/pallas_call | solution.py:249
  5.1 3.0 %collective-permute-start = (f32[4,1024]{1,0:T(4,128)}, f32[4,1024]{1,0:T(4,128)S(1)}, u32[]{:S(2)}, u32[]{:S(2)}) collective-permute-start(f32[4,1024]{1,0:T(4,128)} %get-tuple-element.28.mine), channel_id=1, source_target_pairs={{0,4},{4,0},{8,12},{12,8},{16,20},{20,16},{24,28},{28,24},{1,5},{5... | collective-permute-start | bytes 49160 | tf_op jit(solution)/shard_map/ppermute | solution.py:40
  8.1 2.1 %project.3 = (bf16[512,128]{1,0:T(8,128)(2,1)S(1)}, bf16[512,128]{1,0:T(8,128)(2,1)S(1)}, f32[4,1024]{1,0:T(4,128)S(1)}) custom-call(bf16[512,512]{1,0:T(8,128)(2,1)S(1)} %copy-done.3, bf16[512,256]{1,0:T(8,128)(2,1)S(1)} %copy-done.4, bf16[512,256]{1,0:T(8,128)(2,1)S(1)} %copy-done.5, bf16[2,1024,256]{2,1,0:T(8,128)(2,1)S(1)} %copy-done.1, ...), custom_call_target="tpu_custom_call" | custom-call | flops 1073741824 | bytes 4194304 | tf_op jit(solution)/shard_map/project/pallas_call | solution.py:249
  10.4 2.1 %collective-permute-start.1 = (f32[4,1024]{1,0:T(4,128)S(1)}, f32[4,1024]{1,0:T(4,128)S(1)}, u32[]{:S(2)}, u32[]{:S(2)}) collective-permute-start(f32[4,1024]{1,0:T(4,128)S(1)} %merge.4.mine), channel_id=1, source_target_pairs={{0,8},{4,12},{8,0},{12,4},{16,24},{20,28},{24,16},{28,20},{1,9},{5... | collective-permute-start | bytes 49160 | tf_op jit(solution)/shard_map/ppermute | solution.py:40
  12.5 1.5 %collective-permute-done.8.theirs = f32[4,1024]{1,0:T(4,128)S(1)} collective-permute-done((f32[4,1024]{1,0:T(4,128)S(1)}, f32[4,1024]{1,0:T(4,128)S(1)}, u32[]{:S(2)}, u32[]{:S(2)}) %collective-permute-start.8) | collective-permute-done | bytes 16416 | tf_op jit(solution)/shard_map/ppermute | solution.py:40
  14.1 1.6 %collective-permute-start.9 = (f32[4,1024]{1,0:T(4,128)S(1)}, f32[4,1024]{1,0:T(4,128)S(1)}, u32[]{:S(2)}, u32[]{:S(2)}) collective-permute-start(f32[4,1024]{1,0:T(4,128)S(1)} %merge.6.mine), channel_id=1, source_target_pairs={{0,8},{4,12},{8,0},{12,4},{16,24},{20,28},{24,16},{28,20},{1,9},{5... | collective-permute-start | bytes 49160 | tf_op jit(solution)/shard_map/ppermute | solution.py:40
  15.7 2.7 %collective-permute-start.2 = (f32[4,1024]{1,0:T(4,128)S(1)}, f32[4,1024]{1,0:T(4,128)S(1)}, u32[]{:S(2)}, u32[]{:S(2)}) collective-permute-start(f32[4,1024]{1,0:T(4,128)S(1)} %merge.5.refs_5_), channel_id=1, source_target_pairs={{0,16},{4,20},{8,24},{12,28},{16,0},{20,4},{24,8},{28,12},{1,17},{... | collective-permute-start | bytes 49160 | tf_op jit(solution)/shard_map/ppermute | solution.py:40
  18.4 2.2 %collective-permute-start.10 = (f32[4,1024]{1,0:T(4,128)S(1)}, f32[4,1024]{1,0:T(4,128)S(1)}, u32[]{:S(2)}, u32[]{:S(2)}) collective-permute-start(f32[4,1024]{1,0:T(4,128)S(1)} %merge.7.refs_5_), channel_id=1, source_target_pairs={{0,16},{4,20},{8,24},{12,28},{16,0},{20,4},{24,8},{28,12},{1,17},{... | collective-permute-start | bytes 49160 | tf_op jit(solution)/shard_map/ppermute | solution.py:40
  20.7 2.9 %grads.2 = (bf16[512,256]{1,0:T(8,128)(2,1)S(1)}, bf16[2,512,1024]{2,1,0:T(8,128)(2,1)S(1)}, f32[2,2,64,256]{3,2,1,0:T(8,128)S(1)}, f32[2,2,64,256]{3,2,1,0:T(8,128)S(1)}) custom-call(bf16[512,512]{1,0:T(8,128)(2,1)S(1)} %copy-done.3, bf16[512,128]{1,0:T(8,128)(2,1)S(1)} %copy-done.6, bf16[512,128]{1,0:T(8,128)(2,1)S(1)} %copy-done.7, ...), custom_call_target="tpu_custom_call" | custom-call | flops 1073741824 | bytes 4194304 | tf_op jit(solution)/shard_map/grads/pallas_call | solution.py:303
  25.2 1.8 %collective-permute-start.16 = (f32[4,2,128,128]{3,2,1,0:T(8,128)S(1)}, f32[4,2,128,128]{3,2,1,0:T(8,128)S(1)}, u32[]{:S(2)}, u32[]{:S(2)}) collective-permute-start(f32[4,2,128,128]{3,2,1,0:T(8,128)S(1)} %get-tuple-element.39), channel_id=1, source_target_pairs={{0,8},{4,12},{8,0},{12,4},{16,24},{20,28},{24,16},{28,20},{1,9},{5... | collective-permute-start | bytes 1572872 | tf_op jit(solution)/shard_map/ppermute | solution.py:40
  26.9 4.3 %grads.3 = (bf16[512,256]{1,0:T(8,128)(2,1)}, bf16[2,512,1024]{2,1,0:T(8,128)(2,1)S(1)}, f32[2,2,64,256]{3,2,1,0:T(8,128)S(1)}, f32[2,2,64,256]{3,2,1,0:T(8,128)...) custom-call(bf16[512,512]{1,0:T(8,128)(2,1)S(1)} %copy-done.3, ...), custom_call_target="tpu_custom_call" | custom-call | flops 1073741824 | bytes 4194304 | tf_op jit(solution)/shard_map/grads/pallas_call | solution.py:303
  34.9 3.3 %collective-permute-done.11 = f32[2,2,64,256]{3,2,1,0:T(8,128)S(1)} collective-permute-done((f32[2,2,64,256]{3,2,1,0:T(8,128)S(1)}, f32[2,2,64,256]{3,2,1,0:T(8,128)S(1)}, u32[]{:S(2)}, u32[]{:S(2)}) %collective-permute-start.11) | collective-permute-done | bytes 262176 | tf_op jit(solution)/shard_map/ppermute | solution.py:40
  38.8 2.1 %collective-permute-done.4 = f32[1,2,64,256]{3,2,1,0:T(8,128)S(1)} collective-permute-done((f32[1,2,64,256]{3,2,1,0:T(8,128)S(1)}, f32[1,2,64,256]{3,2,1,0:T(8,128)S(1)}, u32[]{:S(2)}, u32[]{:S(2)}) %collective-permute-start.4) | collective-permute-done | bytes 131104 | tf_op jit(solution)/shard_map/ppermute | solution.py:40
  40.9 2.4 %collective-permute-start.5 = (f32[1,2,64,256]{3,2,1,0:T(8,128)S(1)}, f32[1,2,64,256]{3,2,1,0:T(8,128)S(1)}, u32[]{:S(2)}, u32[]{:S(2)}) collective-permute-start(f32[1,2,64,256]{3,2,1,0:T(8,128)S(1)} %fusion.3), channel_id=1, source_target_pairs={{0,16},{4,20},{8,24},{12,28},{16,0},{20,4},{24,8},{28,12},{1,17},{... | collective-permute-start | bytes 393224 | tf_op jit(solution)/shard_map/ppermute | solution.py:40
  43.4 4.6 %collective-permute-start.13 = (f32[1,2,64,256]{3,2,1,0:T(8,128)S(1)}, f32[1,2,64,256]{3,2,1,0:T(8,128)S(1)}, u32[]{:S(2)}, u32[]{:S(2)}) collective-permute-start(f32[1,2,64,256]{3,2,1,0:T(8,128)S(1)} %fusion.2), channel_id=1, source_target_pairs={{0,16},{4,20},{8,24},{12,28},{16,0},{20,4},{24,8},{28,12},{1,17},{... | collective-permute-start | bytes 393224 | tf_op jit(solution)/shard_map/ppermute | solution.py:40
  48.2 1.6 %collective-permute-start.23 = (f32[1,512,128]{2,1,0:T(8,128)S(1)}, f32[1,512,128]{2,1,0:T(8,128)S(1)}, u32[]{:S(2)}, u32[]{:S(2)}) collective-permute-start(f32[1,512,128]{2,1,0:T(8,128)S(1)} %slice_bitcast_fusion), channel_id=1, source_target_pairs={{0,2},{1,3},{2,0},{3,1},{4,6},{5,7},{6,4},{7,5},{8,10},{9,11},{10,... | collective-permute-start | bytes 786440 | tf_op jit(solution)/shard_map/ppermute | solution.py:40
  49.7 2.7 %collective-permute-done.5 = f32[1,2,64,256]{3,2,1,0:T(8,128)S(1)} collective-permute-done((f32[1,2,64,256]{3,2,1,0:T(8,128)S(1)}, f32[1,2,64,256]{3,2,1,0:T(8,128)S(1)}, u32[]{:S(2)}, u32[]{:S(2)}) %collective-permute-start.5) | collective-permute-done | bytes 131104 | tf_op jit(solution)/shard_map/ppermute | solution.py:40
  52.5 2.0 %collective-permute-done.13 = f32[1,2,64,256]{3,2,1,0:T(8,128)S(1)} collective-permute-done((f32[1,2,64,256]{3,2,1,0:T(8,128)S(1)}, f32[1,2,64,256]{3,2,1,0:T(8,128)S(1)}, u32[]{:S(2)}, u32[]{:S(2)}) %collective-permute-start.13) | collective-permute-done | bytes 131104 | tf_op jit(solution)/shard_map/ppermute | solution.py:40
  54.7 2.0 %collective-permute-start.20 = (f32[2,2,128,128]{3,2,1,0:T(8,128)S(1)}, f32[2,2,128,128]{3,2,1,0:T(8,128)S(1)}, u32[]{:S(2)}, u32[]{:S(2)}) collective-permute-start(f32[2,2,128,128]{3,2,1,0:T(8,128)S(1)} %get-tuple-element.49), channel_id=1, source_target_pairs={{0,8},{4,12},{8,0},{12,4},{16,24},{20,28},{24,16},{28,20},{1,9},{5... | collective-permute-start | bytes 786440 | tf_op jit(solution)/shard_map/ppermute | solution.py:40
  56.7 1.9 %collective-permute-done.6 = f32[1,2,64,256]{3,2,1,0:T(8,128)S(1)} collective-permute-done((f32[1,2,64,256]{3,2,1,0:T(8,128)S(1)}, f32[1,2,64,256]{3,2,1,0:T(8,128)S(1)}, u32[]{:S(2)}, u32[]{:S(2)}) %collective-permute-start.6) | collective-permute-done | bytes 131104 | tf_op jit(solution)/shard_map/ppermute | solution.py:40
  58.7 2.1 %collective-permute-start.7 = (f32[2,2,64,256]{3,2,1,0:T(8,128)S(1)}, f32[2,2,64,256]{3,2,1,0:T(8,128)S(1)}, u32[]{:S(2)}, u32[]{:S(2)}) collective-permute-start(f32[2,2,64,256]{3,2,1,0:T(8,128)S(1)} %pad_maximum_fusion.refs_0_), channel_id=1, source_target_pairs={{0,4},{4,0},{8,12},{12,8},{16,20},{20,16},{24,28},{28,24},{1,5},{5... | collective-permute-start | bytes 786440 | tf_op jit(solution)/shard_map/ppermute | solution.py:40
  61.5 2.1 %collective-permute-start.15 = (f32[2,2,64,256]{3,2,1,0:T(8,128)S(1)}, f32[2,2,64,256]{3,2,1,0:T(8,128)S(1)}, u32[]{:S(2)}, u32[]{:S(2)}) collective-permute-start(f32[2,2,64,256]{3,2,1,0:T(8,128)S(1)} %pad_maximum_fusion.1.refs_2_), channel_id=1, source_target_pairs={{0,4},{4,0},{8,12},{12,8},{16,20},{20,16},{24,28},{28,24},{1,5},{5... | collective-permute-start | bytes 786440 | tf_op jit(solution)/shard_map/ppermute | solution.py:40
  64.6 2.7 %collective-permute-done.20 = f32[2,2,128,128]{3,2,1,0:T(8,128)S(1)} collective-permute-done((f32[2,2,128,128]{3,2,1,0:T(8,128)S(1)}, f32[2,2,128,128]{3,2,1,0:T(8,128)S(1)}, u32[]{:S(2)}, u32[]{:S(2)}) %collective-permute-start.20) | collective-permute-done | bytes 262176 | tf_op jit(solution)/shard_map/ppermute | solution.py:40
  69.3 5.5 %collective-permute-done.18.refs_5_ = f32[1,2,128,128]{3,2,1,0:T(8,128)S(1)} collective-permute-done((f32[1,2,128,128]{3,2,1,0:T(8,128)S(1)}, f32[1,2,128,128]{3,2,1,0:T(8,128)S(1)}, u32[]{:S(2)}, u32[]{:S(2)}) %collective-permute-start.18) | collective-permute-done | bytes 131104 | tf_op jit(solution)/shard_map/ppermute | solution.py:40
  (66 shorter events, 13.1 us)
Async XLA Ops:
  5.1 5.3 %collective-permute-start = (f32[4,1024]{1,0:T(4,128)}, f32[4,1024]{1,0:T(4,128)S(1)}, u32[]{:S(2)}, u32[]{:S(2)}) collective-permute-start(f32[4,1024]{1,0:T(4,128)} %get-tuple-element.28.mine), channel_id=1, source_target_pairs={{0,4},{4,0},{8,12},{12,8},{16,20},{20,16},{24,28},{28,24},{1,5},{5... | collective-permute-start | bytes 49160 | tf_op jit(solution)/shard_map/ppermute | solution.py:40
  10.2 3.8 %collective-permute-start.8 = (f32[4,1024]{1,0:T(4,128)S(1)}, f32[4,1024]{1,0:T(4,128)S(1)}, u32[]{:S(2)}, u32[]{:S(2)}) collective-permute-start(f32[4,1024]{1,0:T(4,128)S(1)} %get-tuple-element.33.mine), channel_id=1, source_target_pairs={{0,4},{4,0},{8,12},{12,8},{16,20},{20,16},{24,28},{28,24},{1,5},{5... | collective-permute-start | bytes 49160 | tf_op jit(solution)/shard_map/ppermute | solution.py:40
  10.4 5.3 %collective-permute-start.1 = (f32[4,1024]{1,0:T(4,128)S(1)}, f32[4,1024]{1,0:T(4,128)S(1)}, u32[]{:S(2)}, u32[]{:S(2)}) collective-permute-start(f32[4,1024]{1,0:T(4,128)S(1)} %merge.4.mine), channel_id=1, source_target_pairs={{0,8},{4,12},{8,0},{12,4},{16,24},{20,28},{24,16},{28,20},{1,9},{5... | collective-permute-start | bytes 49160 | tf_op jit(solution)/shard_map/ppermute | solution.py:40
  14.1 4.3 %collective-permute-start.9 = (f32[4,1024]{1,0:T(4,128)S(1)}, f32[4,1024]{1,0:T(4,128)S(1)}, u32[]{:S(2)}, u32[]{:S(2)}) collective-permute-start(f32[4,1024]{1,0:T(4,128)S(1)} %merge.6.mine), channel_id=1, source_target_pairs={{0,8},{4,12},{8,0},{12,4},{16,24},{20,28},{24,16},{28,20},{1,9},{5... | collective-permute-start | bytes 49160 | tf_op jit(solution)/shard_map/ppermute | solution.py:40
  15.7 4.9 %collective-permute-start.2 = (f32[4,1024]{1,0:T(4,128)S(1)}, f32[4,1024]{1,0:T(4,128)S(1)}, u32[]{:S(2)}, u32[]{:S(2)}) collective-permute-start(f32[4,1024]{1,0:T(4,128)S(1)} %merge.5.refs_5_), channel_id=1, source_target_pairs={{0,16},{4,20},{8,24},{12,28},{16,0},{20,4},{24,8},{28,12},{1,17},{... | collective-permute-start | bytes 49160 | tf_op jit(solution)/shard_map/ppermute | solution.py:40
  18.4 8.5 %collective-permute-start.10 = (f32[4,1024]{1,0:T(4,128)S(1)}, f32[4,1024]{1,0:T(4,128)S(1)}, u32[]{:S(2)}, u32[]{:S(2)}) collective-permute-start(f32[4,1024]{1,0:T(4,128)S(1)} %merge.7.refs_5_), channel_id=1, source_target_pairs={{0,16},{4,20},{8,24},{12,28},{16,0},{20,4},{24,8},{28,12},{1,17},{... | collective-permute-start | bytes 49160 | tf_op jit(solution)/shard_map/ppermute | solution.py:40
  23.6 10.9 %collective-permute-start.3 = (f32[2,2,64,256]{3,2,1,0:T(8,128)S(1)}, f32[2,2,64,256]{3,2,1,0:T(8,128)S(1)}, u32[]{:S(2)}, u32[]{:S(2)}) collective-permute-start(f32[2,2,64,256]{3,2,1,0:T(8,128)S(1)} %get-tuple-element.30), channel_id=1, source_target_pairs={{0,4},{4,0},{8,12},{12,8},{16,20},{20,16},{24,28},{28,24},{1,5},{5... | collective-permute-start | bytes 786440 | tf_op jit(solution)/shard_map/ppermute | solution.py:40
  25.2 22.8 %collective-permute-start.16 = (f32[4,2,128,128]{3,2,1,0:T(8,128)S(1)}, f32[4,2,128,128]{3,2,1,0:T(8,128)S(1)}, u32[]{:S(2)}, u32[]{:S(2)}) collective-permute-start(f32[4,2,128,128]{3,2,1,0:T(8,128)S(1)} %get-tuple-element.39), channel_id=1, source_target_pairs={{0,8},{4,12},{8,0},{12,4},{16,24},{20,28},{24,16},{28,20},{1,9},{5... | collective-permute-start | bytes 1572872 | tf_op jit(solution)/shard_map/ppermute | solution.py:40
  31.2 7.0 %collective-permute-start.11 = (f32[2,2,64,256]{3,2,1,0:T(8,128)S(1)}, f32[2,2,64,256]{3,2,1,0:T(8,128)S(1)}, u32[]{:S(2)}, u32[]{:S(2)}) collective-permute-start(f32[2,2,64,256]{3,2,1,0:T(8,128)S(1)} %get-tuple-element.36), channel_id=1, source_target_pairs={{0,4},{4,0},{8,12},{12,8},{16,20},{20,16},{24,28},{28,24},{1,5},{5... | collective-permute-start | bytes 786440 | tf_op jit(solution)/shard_map/ppermute | solution.py:40
  32.6 15.5 %collective-permute-start.22 = (f32[2,512,128]{2,1,0:T(8,128)S(1)}, f32[2,512,128]{2,1,0:T(8,128)S(1)}, u32[]{:S(2)}, u32[]{:S(2)}) collective-permute-start(f32[2,512,128]{2,1,0:T(8,128)S(1)} %get-tuple-element.47), channel_id=1, source_target_pairs={{0,1},{1,0},{2,3},{3,2},{4,5},{5,4},{6,7},{7,6},{8,9},{9,8},{10,11... | collective-permute-start | bytes 1572872 | tf_op jit(solution)/shard_map/ppermute | solution.py:40
  33.8 20.9 %collective-permute-start.19 = (f32[4,2,128,128]{3,2,1,0:T(8,128)S(1)}, f32[4,2,128,128]{3,2,1,0:T(8,128)S(1)}, u32[]{:S(2)}, u32[]{:S(2)}) collective-permute-start(f32[4,2,128,128]{3,2,1,0:T(8,128)S(1)} %get-tuple-element.42), channel_id=1, source_target_pairs={{0,4},{4,0},{8,12},{12,8},{16,20},{20,16},{24,28},{28,24},{1,5},{5... | collective-permute-start | bytes 1572872 | tf_op jit(solution)/shard_map/ppermute | solution.py:40
  34.5 6.4 %collective-permute-start.4 = (f32[1,2,64,256]{3,2,1,0:T(8,128)S(1)}, f32[1,2,64,256]{3,2,1,0:T(8,128)S(1)}, u32[]{:S(2)}, u32[]{:S(2)}) collective-permute-start(f32[1,2,64,256]{3,2,1,0:T(8,128)S(1)} %slice_add_fusion.10), channel_id=1, source_target_pairs={{0,8},{4,12},{8,0},{12,4},{16,24},{20,28},{24,16},{28,20},{1,9},{5... | collective-permute-start | bytes 393224 | tf_op jit(solution)/shard_map/ppermute | solution.py:40
  38.2 5.2 %collective-permute-start.12 = (f32[1,2,64,256]{3,2,1,0:T(8,128)S(1)}, f32[1,2,64,256]{3,2,1,0:T(8,128)S(1)}, u32[]{:S(2)}, u32[]{:S(2)}) collective-permute-start(f32[1,2,64,256]{3,2,1,0:T(8,128)S(1)} %slice_add_fusion.8), channel_id=1, source_target_pairs={{0,8},{4,12},{8,0},{12,4},{16,24},{20,28},{24,16},{28,20},{1,9},{5... | collective-permute-start | bytes 393224 | tf_op jit(solution)/shard_map/ppermute | solution.py:40
  40.9 11.5 %collective-permute-start.5 = (f32[1,2,64,256]{3,2,1,0:T(8,128)S(1)}, f32[1,2,64,256]{3,2,1,0:T(8,128)S(1)}, u32[]{:S(2)}, u32[]{:S(2)}) collective-permute-start(f32[1,2,64,256]{3,2,1,0:T(8,128)S(1)} %fusion.3), channel_id=1, source_target_pairs={{0,16},{4,20},{8,24},{12,28},{16,0},{20,4},{24,8},{28,12},{1,17},{... | collective-permute-start | bytes 393224 | tf_op jit(solution)/shard_map/ppermute | solution.py:40
  43.4 11.1 %collective-permute-start.13 = (f32[1,2,64,256]{3,2,1,0:T(8,128)S(1)}, f32[1,2,64,256]{3,2,1,0:T(8,128)S(1)}, u32[]{:S(2)}, u32[]{:S(2)}) collective-permute-start(f32[1,2,64,256]{3,2,1,0:T(8,128)S(1)} %fusion.2), channel_id=1, source_target_pairs={{0,16},{4,20},{8,24},{12,28},{16,0},{20,4},{24,8},{28,12},{1,17},{... | collective-permute-start | bytes 393224 | tf_op jit(solution)/shard_map/ppermute | solution.py:40
  48.0 15.5 %collective-permute-start.17 = (f32[2,2,128,128]{3,2,1,0:T(8,128)S(1)}, f32[2,2,128,128]{3,2,1,0:T(8,128)S(1)}, u32[]{:S(2)}, u32[]{:S(2)}) collective-permute-start(f32[2,2,128,128]{3,2,1,0:T(8,128)S(1)} %get-tuple-element.51), channel_id=1, source_target_pairs={{0,4},{4,0},{8,12},{12,8},{16,20},{20,16},{24,28},{28,24},{1,5},{5... | collective-permute-start | bytes 786440 | tf_op jit(solution)/shard_map/ppermute | solution.py:40
  48.2 20.4 %collective-permute-start.23 = (f32[1,512,128]{2,1,0:T(8,128)S(1)}, f32[1,512,128]{2,1,0:T(8,128)S(1)}, u32[]{:S(2)}, u32[]{:S(2)}) collective-permute-start(f32[1,512,128]{2,1,0:T(8,128)S(1)} %slice_bitcast_fusion), channel_id=1, source_target_pairs={{0,2},{1,3},{2,0},{3,1},{4,6},{5,7},{6,4},{7,5},{8,10},{9,11},{10,... | collective-permute-start | bytes 786440 | tf_op jit(solution)/shard_map/ppermute | solution.py:40
  52.5 6.2 %collective-permute-start.6 = (f32[1,2,64,256]{3,2,1,0:T(8,128)S(1)}, f32[1,2,64,256]{3,2,1,0:T(8,128)S(1)}, u32[]{:S(2)}, u32[]{:S(2)}) collective-permute-start(f32[1,2,64,256]{3,2,1,0:T(8,128)S(1)} %add.57), channel_id=1, source_target_pairs={{0,8},{4,12},{8,0},{12,4},{16,24},{20,28},{24,16},{28,20},{1,9},{5... | collective-permute-start | bytes 393224 | tf_op jit(solution)/shard_map/ppermute | solution.py:40
  54.5 6.9 %collective-permute-start.14 = (f32[1,2,64,256]{3,2,1,0:T(8,128)S(1)}, f32[1,2,64,256]{3,2,1,0:T(8,128)S(1)}, u32[]{:S(2)}, u32[]{:S(2)}) collective-permute-start(f32[1,2,64,256]{3,2,1,0:T(8,128)S(1)} %add.61), channel_id=1, source_target_pairs={{0,8},{4,12},{8,0},{12,4},{16,24},{20,28},{24,16},{28,20},{1,9},{5... | collective-permute-start | bytes 393224 | tf_op jit(solution)/shard_map/ppermute | solution.py:40
  54.7 12.6 %collective-permute-start.20 = (f32[2,2,128,128]{3,2,1,0:T(8,128)S(1)}, f32[2,2,128,128]{3,2,1,0:T(8,128)S(1)}, u32[]{:S(2)}, u32[]{:S(2)}) collective-permute-start(f32[2,2,128,128]{3,2,1,0:T(8,128)S(1)} %get-tuple-element.49), channel_id=1, source_target_pairs={{0,8},{4,12},{8,0},{12,4},{16,24},{20,28},{24,16},{28,20},{1,9},{5... | collective-permute-start | bytes 786440 | tf_op jit(solution)/shard_map/ppermute | solution.py:40
  58.7 17.7 %collective-permute-start.7 = (f32[2,2,64,256]{3,2,1,0:T(8,128)S(1)}, f32[2,2,64,256]{3,2,1,0:T(8,128)S(1)}, u32[]{:S(2)}, u32[]{:S(2)}) collective-permute-start(f32[2,2,64,256]{3,2,1,0:T(8,128)S(1)} %pad_maximum_fusion.refs_0_), channel_id=1, source_target_pairs={{0,4},{4,0},{8,12},{12,8},{16,20},{20,16},{24,28},{28,24},{1,5},{5... | collective-permute-start | bytes 786440 | tf_op jit(solution)/shard_map/ppermute | solution.py:40
  61.5 14.9 %collective-permute-start.15 = (f32[2,2,64,256]{3,2,1,0:T(8,128)S(1)}, f32[2,2,64,256]{3,2,1,0:T(8,128)S(1)}, u32[]{:S(2)}, u32[]{:S(2)}) collective-permute-start(f32[2,2,64,256]{3,2,1,0:T(8,128)S(1)} %pad_maximum_fusion.1.refs_2_), channel_id=1, source_target_pairs={{0,4},{4,0},{8,12},{12,8},{16,20},{20,16},{24,28},{28,24},{1,5},{5... | collective-permute-start | bytes 786440 | tf_op jit(solution)/shard_map/ppermute | solution.py:40
  63.6 11.3 %collective-permute-start.18 = (f32[1,2,128,128]{3,2,1,0:T(8,128)S(1)}, f32[1,2,128,128]{3,2,1,0:T(8,128)S(1)}, u32[]{:S(2)}, u32[]{:S(2)}) collective-permute-start(f32[1,2,128,128]{3,2,1,0:T(8,128)S(1)} %get-tuple-element.54), channel_id=1, source_target_pairs={{0,16},{4,20},{8,24},{12,28},{16,0},{20,4},{24,8},{28,12},{1,17},{... | collective-permute-start | bytes 393224 | tf_op jit(solution)/shard_map/ppermute | solution.py:40
  67.4 9.0 %collective-permute-start.21 = (f32[1,2,128,128]{3,2,1,0:T(8,128)S(1)}, f32[1,2,128,128]{3,2,1,0:T(8,128)S(1)}, u32[]{:S(2)}, u32[]{:S(2)}) collective-permute-start(f32[1,2,128,128]{3,2,1,0:T(8,128)S(1)} %get-tuple-element.52), channel_id=1, source_target_pairs={{0,16},{4,20},{8,24},{12,28},{16,0},{20,4},{24,8},{28,12},{1,17},{... | collective-permute-start | bytes 393224 | tf_op jit(solution)/shard_map/ppermute | solution.py:40
  (8 other events, 73.7 us)

commit v6 on v5

v6 whole, which is shorter than its diff:
```python
import functools

import jax
import jax.numpy as jnp
from jax import lax
from jax.experimental import pallas as pl
from jax.experimental.pallas import tpu as pltpu
from jax.sharding import PartitionSpec as P

HD = 128
GROUPS = 8
FACTOR = HD ** (-0.5)
LOG2_E = 1.4426950408889634
VMEM = pl.BlockSpec(memory_space=pltpu.VMEM)
HBM = pl.BlockSpec(memory_space=pltpu.HBM)
ANY = pl.BlockSpec(memory_space=pl.ANY)


def params(mebibytes):
    return pltpu.CompilerParams(vmem_limit_bytes=mebibytes * 1024 * 1024)


def last_contract(left, right):
    return lax.dot_general(
        left, right, (((1,), (1,)), ((), ())), preferred_element_type=jnp.float32
    )


def rows_contract(left, right):
    return lax.dot_general(
        left, right, (((0,), (0,)), ((), ())), preferred_element_type=jnp.float32
    )


def plain_dot(left, right):
    return jnp.dot(left, right, preferred_element_type=jnp.float32)


def swap(array, axis, count, bit):
    pairs = [(device, device ^ bit) for device in range(count)]
    return lax.ppermute(array, axis, pairs)


def bits_of(count):
    return [1 << place for place in range(count.bit_length() - 1)]


def head_statistics(tile, cols, inputs, key_weight, value_weight, queries, out_grad, keys, values, stats):
    reads, latents, _ = queries.shape
    keys[...] = plain_dot(inputs[...], key_weight[:, cols]).astype(jnp.bfloat16)
    values[...] = plain_dot(inputs[...], value_weight[:, cols]).astype(jnp.bfloat16)

    @pl.loop(0, latents // tile, unroll=True)
    def _(step):
        at = pl.ds(pl.multiple_of(step * tile, tile), tile)
        for read_index in range(reads):
            scores = last_contract(keys[...], queries[read_index, at, cols])
            scores = scores * (FACTOR * LOG2_E)
            weighted = last_contract(values[...], out_grad[read_index, at, cols])
            top = jnp.max(scores, axis=0, keepdims=True)
            expos = jnp.exp2(scores - top)
            total = jnp.sum(expos, axis=0, keepdims=True)
            accum = jnp.sum(expos * weighted, axis=0, keepdims=True)
            stats[read_index : read_index + 1, at] = top + jnp.log2(total)
            stats[reads + read_index : reads + read_index + 1, at] = accum / total


def first_kernel(tile, *refs):
    sources, results, targets, sems = refs[:5], refs[5:8], refs[8:13], refs[13]
    loads = []
    for index, (source, target) in enumerate(zip(sources, targets)):
        if index:
            source = source.at[..., :HD]
        loads.append(pltpu.make_async_copy(source, target, sems.at[index]))
    for load in loads:
        load.start()
    for load in loads:
        load.wait()
    head_statistics(tile, slice(0, HD), *targets, *results)


def later_kernel(tile, head_index, after, *refs):
    del after
    head_statistics(tile, slice(head_index * HD, (head_index + 1) * HD), *refs)


def merged(mine, theirs):
    reads = mine.shape[0] // 2
    own, other = mine[:reads], theirs[:reads]
    top = jnp.maximum(own, other)
    own_share = jnp.exp2(own - top)
    other_share = jnp.exp2(other - top)
    total = own_share + other_share
    delta = (mine[reads:] * own_share + theirs[reads:] * other_share) / total
    return top + jnp.log2(total), delta


def merge_kernel(mine, theirs, result):
    reads = mine.shape[0] // 2
    result[:reads], result[reads:] = merged(mine, theirs)


def group_at(bits, relative, me):
    low = me % GROUPS
    group = 0
    for bit, flip in zip(bits, relative):
        group = group + ((low // bit) % 2 ^ flip) * bit
    return group


LAST_BIT = 4
WEIGHT_PARTS = (((0, 256, (1, 2)),), ((0, 256, (1, 2)),))
QUERY_PARTS = (((0, 2, (2, 1, 4)),), ((0, 2, (1, 2, 4)),))


def grads_kernel(
    head_index, row_axis, low, after, inputs, keys, values, queries, out_grad, mine, theirs, *refs
):
    del after
    grads, score_grads = refs[:2]
    weight_parts = refs[2:-4]
    key_acc, value_acc, weights_ref, stats = refs[-4:]
    reads, latents, _ = queries.shape
    tile = latents // (GROUPS // 2)
    cols = slice(head_index * HD, (head_index + 1) * HD)
    stats[:reads], stats[reads:] = merged(mine, theirs)
    key_acc[...] = jnp.zeros_like(key_acc)
    value_acc[...] = jnp.zeros_like(value_acc)

    @pl.loop(0, latents // tile, unroll=True)
    def _(step):
        at = pl.ds(pl.multiple_of(step * tile, tile), tile)
        for read_index in range(reads):
            query_block = queries[read_index, at, cols]
            grad_block = out_grad[read_index, at, cols]
            scores = last_contract(keys[...], query_block) * (FACTOR * LOG2_E)
            weighted = last_contract(values[...], grad_block)
            probs = jnp.exp2(scores - stats[read_index : read_index + 1, at])
            delta = stats[reads + read_index : reads + read_index + 1, at]
            score_grad = (probs * (weighted - delta) * FACTOR).astype(jnp.bfloat16)
            score_grads[read_index, :, at] = score_grad
            key_acc[...] += plain_dot(score_grad, query_block)
            value_acc[...] += plain_dot(probs.astype(jnp.bfloat16), grad_block)

    grads[:, :HD] = key_acc[...].astype(jnp.bfloat16)
    grads[:, HD:] = value_acc[...].astype(jnp.bfloat16)
    weights_ref[...] = rows_contract(inputs[...], grads[...])
    features = inputs.shape[1]
    piece = features // GROUPS
    me = lax.axis_index(row_axis) // low
    for part, (begin, end, bits) in enumerate(WEIGHT_PARTS[head_index]):
        for first in range(2):
            ref = weight_parts[2 * part + first]
            for second in range(2):
                base = group_at(bits, (first, second), me)
                for high in range(2):
                    start = pl.multiple_of((base + LAST_BIT * high) * piece, piece)
                    ref[second, high] = weights_ref[pl.ds(start, piece), begin:end]


def input_kernel(head_axis, key_weight, value_weight, *refs):
    head_grads, (_, input_keep, input_send, total) = refs[:-4], refs[-4:]
    for head_index, grads in enumerate(head_grads):
        cols = slice(head_index * HD, (head_index + 1) * HD)
        part = last_contract(grads[:, :HD], key_weight[:, cols])
        part += last_contract(grads[:, HD:], value_weight[:, cols])
        total[...] = total[...] + part if head_index else part
    place = lax.axis_index(head_axis)
    shares = 2 * input_keep.shape[0]
    width = total.shape[1] // shares
    for relative in range(shares):
        ref = input_send if relative % 2 else input_keep
        start = pl.multiple_of((place ^ relative) * width, width)
        ref[relative // 2] = total[:, pl.ds(start, width)]


def query_kernel(parts, row_axis, low, score_grads, keys, *refs):
    tile_ref = refs[-1]
    reads, _, latents = score_grads.shape
    piece = latents // GROUPS
    me = lax.axis_index(row_axis) // low
    side = lax.rem(me, 2)
    for part, (begin, end, bits) in enumerate(parts):
        for upper in range(GROUPS // 2):
            pair = (me // 2) ^ upper
            at = pl.ds(pl.multiple_of(pair * 2 * piece, 2 * piece), 2 * piece)
            for read_index in range(begin, end):
                slot = upper * reads + read_index
                tile_ref[slot] = rows_contract(score_grads[read_index, :, at], keys[...])
                for flip in range(2):
                    half = pl.ds(pl.multiple_of((side ^ flip) * piece, piece), piece)
                    relative = 2 * upper + flip
                    ref = refs[2 * part + (1 if relative & bits[0] else 0)]
                    index = 2 * ((relative & bits[1]) // bits[1]) + (relative & bits[2]) // bits[2]
                    ref[index, read_index - begin] = tile_ref[slot, half, :]


def assemble_kernel(weight_parts, query_parts, row_axis, low, *refs):
    query_out, key_out, value_out = refs[-3:]
    refs = list(refs[:-3])
    piece = key_out.shape[0] // GROUPS
    me = lax.axis_index(row_axis) // low
    for head_index, begin, end, bits in weight_parts:
        cols = slice(head_index * HD, (head_index + 1) * HD)
        for first in range(2):
            source = refs.pop(0)
            for second in range(2):
                base = group_at(bits, (first, second), me)
                for high in range(2):
                    start = pl.multiple_of((base + LAST_BIT * high) * piece, piece)
                    at = pl.ds(start, piece)
                    if begin == 0:
                        key_out[at, cols] = source[second, high, :, :HD]
                    if end == 2 * HD:
                        value_out[at, cols] = source[second, high, :, end - begin - HD :]
    for head_index, begin, end in query_parts:
        cols = slice(head_index * HD, (head_index + 1) * HD)
        total = refs.pop(0)[0]
        if low == 1:
            total = total + refs.pop(0)[0]
        query_out[begin:end, :, cols] = total


def shape_of(shape, dtype=jnp.float32):
    return jax.ShapeDtypeStruct(shape, dtype)


def scatter_steps(keep, send, count, bits):
    for index, bit in enumerate(bits):
        theirs = swap(send, "rows", count, bit)
        if index + 1 == len(bits):
            return keep, theirs
        middle = keep.shape[0] // 2
        send = keep[middle:] + theirs[middle:]
        keep = keep[:middle] + theirs[:middle]


def on_device(row_devices, head_devices, inputs, key_weight, value_weight, queries, out_grad):
    reads, latents, columns = queries.shape
    head_count = columns // HD
    row_count, features = inputs.shape
    low = row_devices // GROUPS
    tile = latents // (GROUPS // 2)
    piece = features // GROUPS
    operands = (inputs, key_weight, value_weight, queries, out_grad)
    block_work = pl.CostEstimate(
        flops=8 * reads * row_count * latents * HD,
        bytes_accessed=4 * 2**20,
        transcendentals=reads * row_count * latents,
    )

    projected = []
    for head_index in range(head_count):
        first = head_index == 0
        loaded = [
            pltpu.VMEM(item.shape[:-1] + ((HD,) if place else item.shape[-1:]), item.dtype)
            for place, item in enumerate(operands)
        ]
        projected.append(
            pl.pallas_call(
                functools.partial(first_kernel, tile)
                if first
                else functools.partial(later_kernel, tile, head_index),
                out_shape=(
                    shape_of((row_count, HD), jnp.bfloat16),
                    shape_of((row_count, HD), jnp.bfloat16),
                    shape_of((2 * reads, latents)),
                ),
                in_specs=[HBM] * 5 if first else [ANY] + [VMEM] * 5,
                out_specs=(VMEM,) * 3,
                scratch_shapes=loaded + [pltpu.SemaphoreType.DMA((5,))] if first else [],
                compiler_params=params(57 if first else 16),
                cost_estimate=block_work,
                name="project",
            )(*([] if first else [projected[0][2]]), *operands)
        )

    stats_parts = []
    for head_index in range(head_count):
        stats = projected[head_index][2]
        for bit in bits_of(row_devices)[:-1]:
            theirs = swap(stats, "rows", row_devices, bit)
            stats = pl.pallas_call(
                merge_kernel,
                out_shape=shape_of(stats.shape),
                in_specs=[VMEM] * 2,
                out_specs=VMEM,
                compiler_params=params(2),
                name="merge",
            )(stats, theirs)
        stats_parts.append((stats, swap(stats, "rows", row_devices, bits_of(row_devices)[-1])))

    order_low = (lax.axis_index("rows") % low) ^ jnp.arange(low, dtype=jnp.int32)
    low_bits = [bit for bit in bits_of(row_devices) if bit < low]

    def scatter_low(block, axis):
        if low == 1:
            return block
        parts = jnp.moveaxis(
            block.reshape(block.shape[:axis] + (low, -1) + block.shape[axis + 1 :]), axis, 0
        )
        parts = jnp.take(parts, order_low, axis=0)
        for bit in low_bits:
            parts = parts.reshape((-1, 2) + parts.shape[1:])
            parts = parts[:, 0] + swap(parts[:, 1], "rows", row_devices, bit)
        return parts[0]

    def sum_low(block):
        for bit in low_bits:
            block = block + row_swap(block, bit=bit)
        return block

    row_swap = functools.partial(swap, axis="rows", count=row_devices)

    def kernel_call(kernel, shapes, operands, scratch, limit, name):
        return pl.pallas_call(
            kernel,
            out_shape=[shape_of(*item) for item in shapes],
            in_specs=[ANY if name == "grads" and not place else VMEM for place in range(len(operands))],
            out_specs=[VMEM] * len(shapes),
            scratch_shapes=scratch,
            compiler_params=params(limit),
            cost_estimate=block_work,
            name=name,
        )(*operands)

    grads_out, query_out = [], []
    for head_index in range(head_count):
        keys, values, _ = projected[head_index]
        results = kernel_call(
            functools.partial(grads_kernel, head_index, "rows", low),
            [((row_count, 2 * HD), jnp.bfloat16), ((reads, row_count, latents), jnp.bfloat16)]
            + [
                ((2, 2, piece, end - begin),)
                for begin, end, _ in WEIGHT_PARTS[head_index]
                for _ in range(2)
            ],
            [
                grads_out[-1][0] if grads_out else stats_parts[0][0],
                *(inputs, keys, values, queries, out_grad),
                *stats_parts[head_index],
            ],
            [
                pltpu.VMEM((row_count, HD), jnp.float32),
                pltpu.VMEM((row_count, HD), jnp.float32),
                pltpu.VMEM((features, 2 * HD), jnp.float32),
                pltpu.VMEM((2 * reads, latents), jnp.float32),
            ],
            20,
            "grads",
        )
        grads_out.append(results)
        query_out.append(
            kernel_call(
                functools.partial(query_kernel, QUERY_PARTS[head_index], "rows", low),
                [
                    ((GROUPS // 2, end - begin, latents // GROUPS, HD),)
                    for begin, end, _ in QUERY_PARTS[head_index]
                    for _ in range(2)
                ],
                [results[1], keys],
                [pltpu.VMEM((GROUPS // 2 * reads, tile, HD), jnp.float32)],
                16,
                "query",
            )
        )

    assembled, weight_list, marks = [], [], []
    for head_index in range(head_count):
        for part, (begin, end, bits) in enumerate(WEIGHT_PARTS[head_index]):
            keep, send = grads_out[head_index][2 + 2 * part : 4 + 2 * part]
            first, second = (bit * low for bit in bits)
            mine, theirs = scatter_steps(keep, send, row_devices, (first, second))
            marks.append(mine)
            mine = mine + theirs
            mine = sum_low(mine + row_swap(mine, bit=LAST_BIT * low))
            near = jnp.concatenate([mine, row_swap(mine, bit=second)], axis=0)
            assembled += [near, row_swap(near, bit=first)]
            weight_list.append((head_index, begin, end, bits))
    query_list = []
    for head_index in range(head_count):
        for part, (begin, end, bits) in enumerate(QUERY_PARTS[head_index]):
            keep, send = query_out[head_index][2 * part : 2 * part + 2]
            mine, theirs = scatter_steps(keep, send, row_devices, [bit * low for bit in bits])
            if low == 1:
                assembled += [mine, theirs]
            else:
                assembled.append(scatter_low((mine + theirs)[0], 1)[None])
            query_list.append((head_index, begin, end))

    share = ((head_devices // 2, row_count, features // head_devices),)
    after = marks[0]
    input_keep, input_send = pl.pallas_call(
        functools.partial(input_kernel, "heads"),
        out_shape=[shape_of(*share)] * 2,
        in_specs=[VMEM] * (2 + head_count) + [ANY],
        out_specs=[VMEM] * 2,
        scratch_shapes=[pltpu.VMEM((row_count, features), jnp.float32)],
        compiler_params=params(16),
        cost_estimate=block_work,
        name="input",
    )(key_weight, value_weight, *(item[0] for item in grads_out), after)
    total = input_keep + swap(input_send, "heads", head_devices, 1)
    for bit in bits_of(head_devices)[1:]:
        pairs = total.reshape((-1, 2) + total.shape[1:])
        total = pairs[:, 0] + swap(pairs[:, 1], "heads", head_devices, bit)

    query_grad, key_weight_grad, value_weight_grad = pl.pallas_call(
        functools.partial(assemble_kernel, weight_list, query_list, "rows", low),
        out_shape=(shape_of((reads, latents // row_devices, columns)),)
        + (shape_of((features, columns)),) * 2,
        in_specs=[VMEM] * len(assembled),
        out_specs=(VMEM,) * 3,
        compiler_params=params(8),
        name="assemble",
    )(*assembled)
    return (query_grad, key_weight_grad, value_weight_grad, total[0])


def solution(mesh):
    in_specs = (
        P("rows", None),
        P(None, "heads"),
        P(None, "heads"),
        P(None, None, "heads"),
        P(None, None, "heads"),
    )
    out_specs = (P(None, "rows", "heads"), P(None, "heads"), P(None, "heads"), P("rows", "heads"))

    def body(*args):
        return on_device(mesh.shape["rows"], mesh.shape["heads"], *args)

    return jax.shard_map(body, mesh=mesh, in_specs=in_specs, out_specs=out_specs, check_vma=False)
```

time: 77.7 us -> 76.5 us (0.985)
  waiting for transfers between devices: 24 us -> 23.2 us
    ppermute x24, waiting for transfers between devices: 24 us -> 23.2 us  [swap(): return lax.ppermute(array, axis, pairs)]
    pallas_call x5 -> x6, Pallas kernels: 10.6 us -> 10 us  [the longest x4 8.01 us: kernel_call(): pl.pallas_call(kernel, out_shape=[shape_of(*item) for item in shapes], in...]
  transfers between devices with their start and end apart: 24 -> 24, of which waited for: 10 -> 10; matrix products, arithmetic and copies ran while one was open for 1% -> 1% of each run, Pallas kernels for 15% -> 16%
where the time goes in v6:
time: 76.5 us; the launch traced here: 76.3 us
  starting transfers between devices  33.7 us (44%)
  waiting for transfers between devices  23.2 us (30%)
  Pallas kernels  16.6 us (22%)
  other arithmetic  1.13 us (1%)
  between operations  0.87 us (1%)
  local copies, waits for them, and re-layouts  0.77 us (1%)
    ppermute x24, starting transfers between devices, swap(): return lax.ppermute(array, axis, pairs)  33.7 us
    ppermute x24, waiting for transfers between devices, swap(): return lax.ppermute(array, axis, pairs)  23.2 us
    pallas_call x4, Pallas kernels, kernel_call(): pl.pallas_call(kernel, out_shape=[shape_of(*item) for item in shapes], in...  8.01 us
    pallas_call x2, Pallas kernels, on_device(): pl.pallas_call(functools.partial(first_kernel, tile) if first else functo...  6.47 us
  transfers between devices with their start and end apart: 24, of which 10 were waited for; matrix products, arithmetic and copies ran while one was open for 1% of the time, Pallas kernels for 16%

profile of v6, /device:TPU:0, one launch (start us, length us, event | category | flops | bytes accessed | tf_op | source)
XLA Modules:
  0.0 76.3 jit_solution(14197792738965138385)
XLA Ops:
  0.7 4.3 %project.2 = (bf16[512,128]{1,0:T(8,128)(2,1)}, bf16[512,128]{1,0:T(8,128)(2,1)}, f32[4,1024]{1,0:T(4,128)}) custom-call(bf16[512,512]{1,0:T(8,128)(2,1)} %inputs.3, bf16[512,256]{1,0:T(8,128)(2,1)} %key_weight.1, bf16[512,256]{1,0:T(8,128)(2,1)} %value_weight.1, bf16[2,1024,256]{2,1,0:T(8,128)(2,1)} %queries.3, bf16[2,1024,256]{2,1,0:T(8,128)(2,1)} %out_grad.3), custom_call_target="tpu_custom_call" | custom-call | flops 1073741824 | bytes 4194304 | tf_op jit(solution)/shard_map/project/pallas_call | solution.py:260
  5.0 3.0 %collective-permute-start = (f32[4,1024]{1,0:T(4,128)}, f32[4,1024]{1,0:T(4,128)S(1)}, u32[]{:S(2)}, u32[]{:S(2)}) collective-permute-start(f32[4,1024]{1,0:T(4,128)} %get-tuple-element.27.mine.after), channel_id=1, source_target_pairs={{0,4},{4,0},{8,12},{12,8},{16,20},{20,16},{24,28},{28,24},{1,5},{5... | collective-permute-start | bytes 49160 | tf_op jit(solution)/shard_map/ppermute | solution.py:41
  8.8 2.1 %project.3 = (bf16[512,128]{1,0:T(8,128)(2,1)S(1)}, bf16[512,128]{1,0:T(8,128)(2,1)S(1)}, f32[4,1024]{1,0:T(4,128)S(1)}) custom-call(f32[4,1024]{1,0:T(4,128)S(1)} %copy-done, bf16[512,512]{1,0:T(8,128)(2,1)S(1)} %copy-done.3, bf16[512,256]{1,0:T(8,128)(2,1)S(1)} %copy-done.4, bf16[512,256]{1,0:T(8,128)(2,1)S(1)} %copy-done.5, ...), custom_call_target="tpu_custom_call" | custom-call | flops 1073741824 | bytes 4194304 | tf_op jit(solution)/shard_map/project/pallas_call | solution.py:260
  11.1 2.1 %collective-permute-start.1 = (f32[4,1024]{1,0:T(4,128)S(1)}, f32[4,1024]{1,0:T(4,128)S(1)}, u32[]{:S(2)}, u32[]{:S(2)}) collective-permute-start(f32[4,1024]{1,0:T(4,128)S(1)} %merge.4.mine), channel_id=1, source_target_pairs={{0,8},{4,12},{8,0},{12,4},{16,24},{20,28},{24,16},{28,20},{1,9},{5... | collective-permute-start | bytes 49160 | tf_op jit(solution)/shard_map/ppermute | solution.py:41
  14.8 1.6 %collective-permute-start.9 = (f32[4,1024]{1,0:T(4,128)S(1)}, f32[4,1024]{1,0:T(4,128)S(1)}, u32[]{:S(2)}, u32[]{:S(2)}) collective-permute-start(f32[4,1024]{1,0:T(4,128)S(1)} %merge.6.mine), channel_id=1, source_target_pairs={{0,8},{4,12},{8,0},{12,4},{16,24},{20,28},{24,16},{28,20},{1,9},{5... | collective-permute-start | bytes 49160 | tf_op jit(solution)/shard_map/ppermute | solution.py:41
  16.4 2.7 %collective-permute-start.2 = (f32[4,1024]{1,0:T(4,128)S(1)}, f32[4,1024]{1,0:T(4,128)S(1)}, u32[]{:S(2)}, u32[]{:S(2)}) collective-permute-start(f32[4,1024]{1,0:T(4,128)S(1)} %merge.5.after.mine), channel_id=1, source_target_pairs={{0,16},{4,20},{8,24},{12,28},{16,0},{20,4},{24,8},{28,12},{1,17},{... | collective-permute-start | bytes 49160 | tf_op jit(solution)/shard_map/ppermute | solution.py:41
  19.1 2.2 %collective-permute-start.10 = (f32[4,1024]{1,0:T(4,128)S(1)}, f32[4,1024]{1,0:T(4,128)S(1)}, u32[]{:S(2)}, u32[]{:S(2)}) collective-permute-start(f32[4,1024]{1,0:T(4,128)S(1)} %merge.7.mine), channel_id=1, source_target_pairs={{0,16},{4,20},{8,24},{12,28},{16,0},{20,4},{24,8},{28,12},{1,17},{... | collective-permute-start | bytes 49160 | tf_op jit(solution)/shard_map/ppermute | solution.py:41
  21.4 2.9 %grads.2 = (bf16[512,256]{1,0:T(8,128)(2,1)S(1)}, bf16[2,512,1024]{2,1,0:T(8,128)(2,1)S(1)}, f32[2,2,64,256]{3,2,1,0:T(8,128)S(1)}, f32[2,2,64,256]{3,2,1,0:T(8,128)S(1)}) custom-call(f32[4,1024]{1,0:T(4,128)S(1)} %merge.5.after.mine, bf16[512,512]{1,0:T(8,128)(2,1)S(1)} %copy-done.3, bf16[512,128]{1,0:T(8,128)(2,1)S(1)} %copy-done.6, ...), custom_call_target="tpu_custom_call" | custom-call | flops 1073741824 | bytes 4194304 | tf_op jit(solution)/shard_map/grads/pallas_call | solution.py:316
  25.9 1.8 %collective-permute-start.16 = (f32[4,2,128,128]{3,2,1,0:T(8,128)S(1)}, f32[4,2,128,128]{3,2,1,0:T(8,128)S(1)}, u32[]{:S(2)}, u32[]{:S(2)}) collective-permute-start(f32[4,2,128,128]{3,2,1,0:T(8,128)S(1)} %get-tuple-element.40), channel_id=1, source_target_pairs={{0,8},{4,12},{8,0},{12,4},{16,24},{20,28},{24,16},{28,20},{1,9},{5... | collective-permute-start | bytes 1572872 | tf_op jit(solution)/shard_map/ppermute | solution.py:41
  27.7 2.9 %grads.3 = (bf16[512,256]{1,0:T(8,128)(2,1)S(1)}, bf16[2,512,1024]{2,1,0:T(8,128)(2,1)S(1)}, f32[2,2,64,256]{3,2,1,0:T(8,128)S(1)}, f32[2,2,64,256]{3,2,1,0:T(8,128)S(1)}) custom-call(bf16[512,256]{1,0:T(8,128)(2,1)S(1)} %get-tuple-element.32.after.refs_0_, bf16[512,512]{1,0:T(8,128)(2,1)S(1)} %copy-done.3, bf16[512,128]{1,0:T(8,128)(2,1)S(1)} %get-tuple-element.33.keys, ...), custom_call_target="tpu_custom_call" | custom-call | flops 1073741824 | bytes 4194304 | tf_op jit(solution)/shard_map/grads/pallas_call | solution.py:316
  34.5 5.4 %collective-permute-done.11 = f32[2,2,64,256]{3,2,1,0:T(8,128)S(1)} collective-permute-done((f32[2,2,64,256]{3,2,1,0:T(8,128)S(1)}, f32[2,2,64,256]{3,2,1,0:T(8,128)S(1)}, u32[]{:S(2)}, u32[]{:S(2)}) %collective-permute-start.11) | collective-permute-done | bytes 262176 | tf_op jit(solution)/shard_map/ppermute | solution.py:41
  40.3 1.9 %collective-permute-done.4 = f32[1,2,64,256]{3,2,1,0:T(8,128)S(1)} collective-permute-done((f32[1,2,64,256]{3,2,1,0:T(8,128)S(1)}, f32[1,2,64,256]{3,2,1,0:T(8,128)S(1)}, u32[]{:S(2)}, u32[]{:S(2)}) %collective-permute-start.4) | collective-permute-done | bytes 131104 | tf_op jit(solution)/shard_map/ppermute | solution.py:41
  42.2 3.0 %collective-permute-start.5 = (f32[1,2,64,256]{3,2,1,0:T(8,128)S(1)}, f32[1,2,64,256]{3,2,1,0:T(8,128)S(1)}, u32[]{:S(2)}, u32[]{:S(2)}) collective-permute-start(f32[1,2,64,256]{3,2,1,0:T(8,128)S(1)} %get-tuple-element.50), channel_id=1, source_target_pairs={{0,16},{4,20},{8,24},{12,28},{16,0},{20,4},{24,8},{28,12},{1,17},{... | collective-permute-start | bytes 393224 | tf_op jit(solution)/shard_map/ppermute | solution.py:41
  46.0 1.9 %collective-permute-start.13 = (f32[1,2,64,256]{3,2,1,0:T(8,128)S(1)}, f32[1,2,64,256]{3,2,1,0:T(8,128)S(1)}, u32[]{:S(2)}, u32[]{:S(2)}) collective-permute-start(f32[1,2,64,256]{3,2,1,0:T(8,128)S(1)} %fusion.2), channel_id=1, source_target_pairs={{0,16},{4,20},{8,24},{12,28},{16,0},{20,4},{24,8},{28,12},{1,17},{... | collective-permute-start | bytes 393224 | tf_op jit(solution)/shard_map/ppermute | solution.py:41
  50.1 1.6 %collective-permute-start.6 = (f32[1,2,64,256]{3,2,1,0:T(8,128)S(1)}, f32[1,2,64,256]{3,2,1,0:T(8,128)S(1)}, u32[]{:S(2)}, u32[]{:S(2)}) collective-permute-start(f32[1,2,64,256]{3,2,1,0:T(8,128)S(1)} %add.57), channel_id=1, source_target_pairs={{0,8},{4,12},{8,0},{12,4},{16,24},{20,28},{24,16},{28,20},{1,9},{5... | collective-permute-start | bytes 393224 | tf_op jit(solution)/shard_map/ppermute | solution.py:41
  51.7 1.7 %collective-permute-done.13 = f32[1,2,64,256]{3,2,1,0:T(8,128)S(1)} collective-permute-done((f32[1,2,64,256]{3,2,1,0:T(8,128)S(1)}, f32[1,2,64,256]{3,2,1,0:T(8,128)S(1)}, u32[]{:S(2)}, u32[]{:S(2)}) %collective-permute-start.13) | collective-permute-done | bytes 131104 | tf_op jit(solution)/shard_map/ppermute | solution.py:41
  53.5 2.1 %collective-permute-start.20 = (f32[2,2,128,128]{3,2,1,0:T(8,128)S(1)}, f32[2,2,128,128]{3,2,1,0:T(8,128)S(1)}, u32[]{:S(2)}, u32[]{:S(2)}) collective-permute-start(f32[2,2,128,128]{3,2,1,0:T(8,128)S(1)} %get-tuple-element.53), channel_id=1, source_target_pairs={{0,8},{4,12},{8,0},{12,4},{16,24},{20,28},{24,16},{28,20},{1,9},{5... | collective-permute-start | bytes 786440 | tf_op jit(solution)/shard_map/ppermute | solution.py:41
  56.5 1.6 %collective-permute-start.7 = (f32[2,2,64,256]{3,2,1,0:T(8,128)S(1)}, f32[2,2,64,256]{3,2,1,0:T(8,128)S(1)}, u32[]{:S(2)}, u32[]{:S(2)}) collective-permute-start(f32[2,2,64,256]{3,2,1,0:T(8,128)S(1)} %pad_maximum_fusion.refs_0_), channel_id=1, source_target_pairs={{0,4},{4,0},{8,12},{12,8},{16,20},{20,16},{24,28},{28,24},{1,5},{5... | collective-permute-start | bytes 786440 | tf_op jit(solution)/shard_map/ppermute | solution.py:41
  58.1 1.8 %collective-permute-done.14 = f32[1,2,64,256]{3,2,1,0:T(8,128)S(1)} collective-permute-done((f32[1,2,64,256]{3,2,1,0:T(8,128)S(1)}, f32[1,2,64,256]{3,2,1,0:T(8,128)S(1)}, u32[]{:S(2)}, u32[]{:S(2)}) %collective-permute-start.14) | collective-permute-done | bytes 131104 | tf_op jit(solution)/shard_map/ppermute | solution.py:41
  61.2 1.5 %collective-permute-start.18 = (f32[1,2,128,128]{3,2,1,0:T(8,128)S(1)}, f32[1,2,128,128]{3,2,1,0:T(8,128)S(1)}, u32[]{:S(2)}, u32[]{:S(2)}) collective-permute-start(f32[1,2,128,128]{3,2,1,0:T(8,128)S(1)} %get-tuple-element.58), channel_id=1, source_target_pairs={{0,16},{4,20},{8,24},{12,28},{16,0},{20,4},{24,8},{28,12},{1,17},{... | collective-permute-start | bytes 393224 | tf_op jit(solution)/shard_map/ppermute | solution.py:41
  62.8 1.6 %collective-permute-start.23 = (f32[1,512,128]{2,1,0:T(8,128)S(1)}, f32[1,512,128]{2,1,0:T(8,128)S(1)}, u32[]{:S(2)}, u32[]{:S(2)}) collective-permute-start(f32[1,512,128]{2,1,0:T(8,128)S(1)} %slice_bitcast_fusion), channel_id=1, source_target_pairs={{0,2},{1,3},{2,0},{3,1},{4,6},{5,7},{6,4},{7,5},{8,10},{9,11},{10,... | collective-permute-start | bytes 786440 | tf_op jit(solution)/shard_map/ppermute | solution.py:41
  64.4 1.7 %collective-permute-done.20 = f32[2,2,128,128]{3,2,1,0:T(8,128)S(1)} collective-permute-done((f32[2,2,128,128]{3,2,1,0:T(8,128)S(1)}, f32[2,2,128,128]{3,2,1,0:T(8,128)S(1)}, u32[]{:S(2)}, u32[]{:S(2)}) %collective-permute-start.20) | collective-permute-done | bytes 262176 | tf_op jit(solution)/shard_map/ppermute | solution.py:41
  66.8 5.2 %collective-permute-done.18.refs_5_ = f32[1,2,128,128]{3,2,1,0:T(8,128)S(1)} collective-permute-done((f32[1,2,128,128]{3,2,1,0:T(8,128)S(1)}, f32[1,2,128,128]{3,2,1,0:T(8,128)S(1)}, u32[]{:S(2)}, u32[]{:S(2)}) %collective-permute-start.18) | collective-permute-done | bytes 131104 | tf_op jit(solution)/shard_map/ppermute | solution.py:41
  72.1 2.3 %collective-permute-done.21.refs_7_ = f32[1,2,128,128]{3,2,1,0:T(8,128)S(1)} collective-permute-done((f32[1,2,128,128]{3,2,1,0:T(8,128)S(1)}, f32[1,2,128,128]{3,2,1,0:T(8,128)S(1)}, u32[]{:S(2)}, u32[]{:S(2)}) %collective-permute-start.21) | collective-permute-done | bytes 131104 | tf_op jit(solution)/shard_map/ppermute | solution.py:41
  (67 shorter events, 16.5 us)
Async XLA Ops:
  5.0 6.0 %collective-permute-start = (f32[4,1024]{1,0:T(4,128)}, f32[4,1024]{1,0:T(4,128)S(1)}, u32[]{:S(2)}, u32[]{:S(2)}) collective-permute-start(f32[4,1024]{1,0:T(4,128)} %get-tuple-element.27.mine.after), channel_id=1, source_target_pairs={{0,4},{4,0},{8,12},{12,8},{16,20},{20,16},{24,28},{28,24},{1,5},{5... | collective-permute-start | bytes 49160 | tf_op jit(solution)/shard_map/ppermute | solution.py:41
  10.9 3.8 %collective-permute-start.8 = (f32[4,1024]{1,0:T(4,128)S(1)}, f32[4,1024]{1,0:T(4,128)S(1)}, u32[]{:S(2)}, u32[]{:S(2)}) collective-permute-start(f32[4,1024]{1,0:T(4,128)S(1)} %get-tuple-element.35.mine), channel_id=1, source_target_pairs={{0,4},{4,0},{8,12},{12,8},{16,20},{20,16},{24,28},{28,24},{1,5},{5... | collective-permute-start | bytes 49160 | tf_op jit(solution)/shard_map/ppermute | solution.py:41
  11.1 5.3 %collective-permute-start.1 = (f32[4,1024]{1,0:T(4,128)S(1)}, f32[4,1024]{1,0:T(4,128)S(1)}, u32[]{:S(2)}, u32[]{:S(2)}) collective-permute-start(f32[4,1024]{1,0:T(4,128)S(1)} %merge.4.mine), channel_id=1, source_target_pairs={{0,8},{4,12},{8,0},{12,4},{16,24},{20,28},{24,16},{28,20},{1,9},{5... | collective-permute-start | bytes 49160 | tf_op jit(solution)/shard_map/ppermute | solution.py:41
  14.8 4.3 %collective-permute-start.9 = (f32[4,1024]{1,0:T(4,128)S(1)}, f32[4,1024]{1,0:T(4,128)S(1)}, u32[]{:S(2)}, u32[]{:S(2)}) collective-permute-start(f32[4,1024]{1,0:T(4,128)S(1)} %merge.6.mine), channel_id=1, source_target_pairs={{0,8},{4,12},{8,0},{12,4},{16,24},{20,28},{24,16},{28,20},{1,9},{5... | collective-permute-start | bytes 49160 | tf_op jit(solution)/shard_map/ppermute | solution.py:41
  16.4 4.9 %collective-permute-start.2 = (f32[4,1024]{1,0:T(4,128)S(1)}, f32[4,1024]{1,0:T(4,128)S(1)}, u32[]{:S(2)}, u32[]{:S(2)}) collective-permute-start(f32[4,1024]{1,0:T(4,128)S(1)} %merge.5.after.mine), channel_id=1, source_target_pairs={{0,16},{4,20},{8,24},{12,28},{16,0},{20,4},{24,8},{28,12},{1,17},{... | collective-permute-start | bytes 49160 | tf_op jit(solution)/shard_map/ppermute | solution.py:41
  19.1 8.5 %collective-permute-start.10 = (f32[4,1024]{1,0:T(4,128)S(1)}, f32[4,1024]{1,0:T(4,128)S(1)}, u32[]{:S(2)}, u32[]{:S(2)}) collective-permute-start(f32[4,1024]{1,0:T(4,128)S(1)} %merge.7.mine), channel_id=1, source_target_pairs={{0,16},{4,20},{8,24},{12,28},{16,0},{20,4},{24,8},{28,12},{1,17},{... | collective-permute-start | bytes 49160 | tf_op jit(solution)/shard_map/ppermute | solution.py:41
  24.3 9.6 %collective-permute-start.3 = (f32[2,2,64,256]{3,2,1,0:T(8,128)S(1)}, f32[2,2,64,256]{3,2,1,0:T(8,128)S(1)}, u32[]{:S(2)}, u32[]{:S(2)}) collective-permute-start(f32[2,2,64,256]{3,2,1,0:T(8,128)S(1)} %get-tuple-element.31), channel_id=1, source_target_pairs={{0,4},{4,0},{8,12},{12,8},{16,20},{20,16},{24,28},{28,24},{1,5},{5... | collective-permute-start | bytes 786440 | tf_op jit(solution)/shard_map/ppermute | solution.py:41
  25.9 22.9 %collective-permute-start.16 = (f32[4,2,128,128]{3,2,1,0:T(8,128)S(1)}, f32[4,2,128,128]{3,2,1,0:T(8,128)S(1)}, u32[]{:S(2)}, u32[]{:S(2)}) collective-permute-start(f32[4,2,128,128]{3,2,1,0:T(8,128)S(1)} %get-tuple-element.40), channel_id=1, source_target_pairs={{0,8},{4,12},{8,0},{12,4},{16,24},{20,28},{24,16},{28,20},{1,9},{5... | collective-permute-start | bytes 1572872 | tf_op jit(solution)/shard_map/ppermute | solution.py:41
  30.6 9.3 %collective-permute-start.11 = (f32[2,2,64,256]{3,2,1,0:T(8,128)S(1)}, f32[2,2,64,256]{3,2,1,0:T(8,128)S(1)}, u32[]{:S(2)}, u32[]{:S(2)}) collective-permute-start(f32[2,2,64,256]{3,2,1,0:T(8,128)S(1)} %get-tuple-element.37), channel_id=1, source_target_pairs={{0,4},{4,0},{8,12},{12,8},{16,20},{20,16},{24,28},{28,24},{1,5},{5... | collective-permute-start | bytes 786440 | tf_op jit(solution)/shard_map/ppermute | solution.py:41
  33.1 20.3 %collective-permute-start.19 = (f32[4,2,128,128]{3,2,1,0:T(8,128)S(1)}, f32[4,2,128,128]{3,2,1,0:T(8,128)S(1)}, u32[]{:S(2)}, u32[]{:S(2)}) collective-permute-start(f32[4,2,128,128]{3,2,1,0:T(8,128)S(1)} %get-tuple-element.43), channel_id=1, source_target_pairs={{0,4},{4,0},{8,12},{12,8},{16,20},{20,16},{24,28},{28,24},{1,5},{5... | collective-permute-start | bytes 1572872 | tf_op jit(solution)/shard_map/ppermute | solution.py:41
  33.9 8.2 %collective-permute-start.4 = (f32[1,2,64,256]{3,2,1,0:T(8,128)S(1)}, f32[1,2,64,256]{3,2,1,0:T(8,128)S(1)}, u32[]{:S(2)}, u32[]{:S(2)}) collective-permute-start(f32[1,2,64,256]{3,2,1,0:T(8,128)S(1)} %slice_add_fusion.10), channel_id=1, source_target_pairs={{0,8},{4,12},{8,0},{12,4},{16,24},{20,28},{24,16},{28,20},{1,9},{5... | collective-permute-start | bytes 393224 | tf_op jit(solution)/shard_map/ppermute | solution.py:41
  39.9 6.1 %collective-permute-start.12 = (f32[1,2,64,256]{3,2,1,0:T(8,128)S(1)}, f32[1,2,64,256]{3,2,1,0:T(8,128)S(1)}, u32[]{:S(2)}, u32[]{:S(2)}) collective-permute-start(f32[1,2,64,256]{3,2,1,0:T(8,128)S(1)} %slice_add_fusion.8), channel_id=1, source_target_pairs={{0,8},{4,12},{8,0},{12,4},{16,24},{20,28},{24,16},{28,20},{1,9},{5... | collective-permute-start | bytes 393224 | tf_op jit(solution)/shard_map/ppermute | solution.py:41
  42.2 7.9 %collective-permute-start.5 = (f32[1,2,64,256]{3,2,1,0:T(8,128)S(1)}, f32[1,2,64,256]{3,2,1,0:T(8,128)S(1)}, u32[]{:S(2)}, u32[]{:S(2)}) collective-permute-start(f32[1,2,64,256]{3,2,1,0:T(8,128)S(1)} %get-tuple-element.50), channel_id=1, source_target_pairs={{0,16},{4,20},{8,24},{12,28},{16,0},{20,4},{24,8},{28,12},{1,17},{... | collective-permute-start | bytes 393224 | tf_op jit(solution)/shard_map/ppermute | solution.py:41
  46.0 7.4 %collective-permute-start.13 = (f32[1,2,64,256]{3,2,1,0:T(8,128)S(1)}, f32[1,2,64,256]{3,2,1,0:T(8,128)S(1)}, u32[]{:S(2)}, u32[]{:S(2)}) collective-permute-start(f32[1,2,64,256]{3,2,1,0:T(8,128)S(1)} %fusion.2), channel_id=1, source_target_pairs={{0,16},{4,20},{8,24},{12,28},{16,0},{20,4},{24,8},{28,12},{1,17},{... | collective-permute-start | bytes 393224 | tf_op jit(solution)/shard_map/ppermute | solution.py:41
  48.7 14.0 %collective-permute-start.22 = (f32[2,512,128]{2,1,0:T(8,128)S(1)}, f32[2,512,128]{2,1,0:T(8,128)S(1)}, u32[]{:S(2)}, u32[]{:S(2)}) collective-permute-start(f32[2,512,128]{2,1,0:T(8,128)S(1)} %get-tuple-element.49), channel_id=1, source_target_pairs={{0,1},{1,0},{2,3},{3,2},{4,5},{5,4},{6,7},{7,6},{8,9},{9,8},{10,11... | collective-permute-start | bytes 1572872 | tf_op jit(solution)/shard_map/ppermute | solution.py:41
  48.9 12.3 %collective-permute-start.17 = (f32[2,2,128,128]{3,2,1,0:T(8,128)S(1)}, f32[2,2,128,128]{3,2,1,0:T(8,128)S(1)}, u32[]{:S(2)}, u32[]{:S(2)}) collective-permute-start(f32[2,2,128,128]{3,2,1,0:T(8,128)S(1)} %get-tuple-element.55), channel_id=1, source_target_pairs={{0,4},{4,0},{8,12},{12,8},{16,20},{20,16},{24,28},{28,24},{1,5},{5... | collective-permute-start | bytes 786440 | tf_op jit(solution)/shard_map/ppermute | solution.py:41
  50.1 6.4 %collective-permute-start.6 = (f32[1,2,64,256]{3,2,1,0:T(8,128)S(1)}, f32[1,2,64,256]{3,2,1,0:T(8,128)S(1)}, u32[]{:S(2)}, u32[]{:S(2)}) collective-permute-start(f32[1,2,64,256]{3,2,1,0:T(8,128)S(1)} %add.57), channel_id=1, source_target_pairs={{0,8},{4,12},{8,0},{12,4},{16,24},{20,28},{24,16},{28,20},{1,9},{5... | collective-permute-start | bytes 393224 | tf_op jit(solution)/shard_map/ppermute | solution.py:41
  53.4 6.5 %collective-permute-start.14 = (f32[1,2,64,256]{3,2,1,0:T(8,128)S(1)}, f32[1,2,64,256]{3,2,1,0:T(8,128)S(1)}, u32[]{:S(2)}, u32[]{:S(2)}) collective-permute-start(f32[1,2,64,256]{3,2,1,0:T(8,128)S(1)} %add.61), channel_id=1, source_target_pairs={{0,8},{4,12},{8,0},{12,4},{16,24},{20,28},{24,16},{28,20},{1,9},{5... | collective-permute-start | bytes 393224 | tf_op jit(solution)/shard_map/ppermute | solution.py:41
  53.5 12.6 %collective-permute-start.20 = (f32[2,2,128,128]{3,2,1,0:T(8,128)S(1)}, f32[2,2,128,128]{3,2,1,0:T(8,128)S(1)}, u32[]{:S(2)}, u32[]{:S(2)}) collective-permute-start(f32[2,2,128,128]{3,2,1,0:T(8,128)S(1)} %get-tuple-element.53), channel_id=1, source_target_pairs={{0,8},{4,12},{8,0},{12,4},{16,24},{20,28},{24,16},{28,20},{1,9},{5... | collective-permute-start | bytes 786440 | tf_op jit(solution)/shard_map/ppermute | solution.py:41
  56.5 17.9 %collective-permute-start.7 = (f32[2,2,64,256]{3,2,1,0:T(8,128)S(1)}, f32[2,2,64,256]{3,2,1,0:T(8,128)S(1)}, u32[]{:S(2)}, u32[]{:S(2)}) collective-permute-start(f32[2,2,64,256]{3,2,1,0:T(8,128)S(1)} %pad_maximum_fusion.refs_0_), channel_id=1, source_target_pairs={{0,4},{4,0},{8,12},{12,8},{16,20},{20,16},{24,28},{28,24},{1,5},{5... | collective-permute-start | bytes 786440 | tf_op jit(solution)/shard_map/ppermute | solution.py:41
  59.9 14.5 %collective-permute-start.15 = (f32[2,2,64,256]{3,2,1,0:T(8,128)S(1)}, f32[2,2,64,256]{3,2,1,0:T(8,128)S(1)}, u32[]{:S(2)}, u32[]{:S(2)}) collective-permute-start(f32[2,2,64,256]{3,2,1,0:T(8,128)S(1)} %pad_maximum_fusion.1.refs_2_), channel_id=1, source_target_pairs={{0,4},{4,0},{8,12},{12,8},{16,20},{20,16},{24,28},{28,24},{1,5},{5... | collective-permute-start | bytes 786440 | tf_op jit(solution)/shard_map/ppermute | solution.py:41
  61.2 10.9 %collective-permute-start.18 = (f32[1,2,128,128]{3,2,1,0:T(8,128)S(1)}, f32[1,2,128,128]{3,2,1,0:T(8,128)S(1)}, u32[]{:S(2)}, u32[]{:S(2)}) collective-permute-start(f32[1,2,128,128]{3,2,1,0:T(8,128)S(1)} %get-tuple-element.58), channel_id=1, source_target_pairs={{0,16},{4,20},{8,24},{12,28},{16,0},{20,4},{24,8},{28,12},{1,17},{... | collective-permute-start | bytes 393224 | tf_op jit(solution)/shard_map/ppermute | solution.py:41
  62.8 12.7 %collective-permute-start.23 = (f32[1,512,128]{2,1,0:T(8,128)S(1)}, f32[1,512,128]{2,1,0:T(8,128)S(1)}, u32[]{:S(2)}, u32[]{:S(2)}) collective-permute-start(f32[1,512,128]{2,1,0:T(8,128)S(1)} %slice_bitcast_fusion), channel_id=1, source_target_pairs={{0,2},{1,3},{2,0},{3,1},{4,6},{5,7},{6,4},{7,5},{8,10},{9,11},{10,... | collective-permute-start | bytes 786440 | tf_op jit(solution)/shard_map/ppermute | solution.py:41
  66.2 8.1 %collective-permute-start.21 = (f32[1,2,128,128]{3,2,1,0:T(8,128)S(1)}, f32[1,2,128,128]{3,2,1,0:T(8,128)S(1)}, u32[]{:S(2)}, u32[]{:S(2)}) collective-permute-start(f32[1,2,128,128]{3,2,1,0:T(8,128)S(1)} %get-tuple-element.56), channel_id=1, source_target_pairs={{0,16},{4,20},{8,24},{12,28},{16,0},{20,4},{24,8},{28,12},{1,17},{... | collective-permute-start | bytes 393224 | tf_op jit(solution)/shard_map/ppermute | solution.py:41
  (8 other events, 62.8 us)

commit v7 on v6

--- a/solution.py
+++ b/solution.py
@@ -45,10 +45,15 @@
     return [1 << place for place in range(count.bit_length() - 1)]
 
 
-def head_statistics(tile, cols, inputs, key_weight, value_weight, queries, out_grad, keys, values, stats):
+def head_statistics(
+    tile, cols, wait, inputs, key_weight, value_weight, queries, out_grad, keys, values, stats
+):
     reads, latents, _ = queries.shape
+    wait(0, 1)
     keys[...] = plain_dot(inputs[...], key_weight[:, cols]).astype(jnp.bfloat16)
+    wait(2)
     values[...] = plain_dot(inputs[...], value_weight[:, cols]).astype(jnp.bfloat16)
+    wait(3, 4)
 
     @pl.loop(0, latents // tile, unroll=True)
     def _(step):
@@ -74,14 +79,17 @@
         loads.append(pltpu.make_async_copy(source, target, sems.at[index]))
     for load in loads:
         load.start()
-    for load in loads:
-        load.wait()
-    head_statistics(tile, slice(0, HD), *targets, *results)
-
-
-def later_kernel(tile, head_index, after, *refs):
-    del after
-    head_statistics(tile, slice(head_index * HD, (head_index + 1) * HD), *refs)
+
+    def wait(*places):
+        for place in places:
+            loads[place].wait()
+
+    head_statistics(tile, slice(0, HD), wait, *targets, *results)
+
+
+def later_kernel(tile, head_index, *refs):
+    cols = slice(head_index * HD, (head_index + 1) * HD)
+    head_statistics(tile, cols, lambda *_: None, *refs)
 
 
 def merged(mine, theirs):
@@ -111,6 +119,7 @@
 LAST_BIT = 4
 WEIGHT_PARTS = (((0, 256, (1, 2)),), ((0, 256, (1, 2)),))
 QUERY_PARTS = (((0, 2, (2, 1, 4)),), ((0, 2, (1, 2, 4)),))
+DIRECT = ()
 
 
 def grads_kernel(
@@ -169,9 +178,9 @@
     shares = 2 * input_keep.shape[0]
     width = total.shape[1] // shares
     for relative in range(shares):
-        ref = input_send if relative % 2 else input_keep
+        ref = input_send if relative >= shares // 2 else input_keep
         start = pl.multiple_of((place ^ relative) * width, width)
-        ref[relative // 2] = total[:, pl.ds(start, width)]
+        ref[relative % (shares // 2)] = total[:, pl.ds(start, width)]
 
 
 def query_kernel(parts, row_axis, low, score_grads, keys, *refs):
@@ -196,8 +205,9 @@
 
 
 def assemble_kernel(weight_parts, query_parts, row_axis, low, *refs):
-    query_out, key_out, value_out = refs[-3:]
-    refs = list(refs[:-3])
+    query_out, key_out, value_out, input_out = refs[-4:]
+    refs = list(refs[:-4])
+    input_out[...] = refs.pop(0)[0] + refs.pop(0)[0]
     piece = key_out.shape[0] // GROUPS
     me = lax.axis_index(row_axis) // low
     for head_index, begin, end, bits in weight_parts:
@@ -213,10 +223,10 @@
                         key_out[at, cols] = source[second, high, :, :HD]
                     if end == 2 * HD:
                         value_out[at, cols] = source[second, high, :, end - begin - HD :]
-    for head_index, begin, end in query_parts:
+    for head_index, begin, end, terms in query_parts:
         cols = slice(head_index * HD, (head_index + 1) * HD)
         total = refs.pop(0)[0]
-        if low == 1:
+        for _ in range(terms - 1):
             total = total + refs.pop(0)[0]
         query_out[begin:end, :, cols] = total
 
@@ -266,13 +276,13 @@
                     shape_of((row_count, HD), jnp.bfloat16),
                     shape_of((2 * reads, latents)),
                 ),
-                in_specs=[HBM] * 5 if first else [ANY] + [VMEM] * 5,
+                in_specs=[HBM if first else VMEM] * 5,
                 out_specs=(VMEM,) * 3,
                 scratch_shapes=loaded + [pltpu.SemaphoreType.DMA((5,))] if first else [],
                 compiler_params=params(57 if first else 16),
                 cost_estimate=block_work,
                 name="project",
-            )(*([] if first else [projected[0][2]]), *operands)
+            )(*operands)
         )
 
     stats_parts = []
@@ -381,15 +391,22 @@
     for head_index in range(head_count):
         for part, (begin, end, bits) in enumerate(QUERY_PARTS[head_index]):
             keep, send = query_out[head_index][2 * part : 2 * part + 2]
-            mine, theirs = scatter_steps(keep, send, row_devices, [bit * low for bit in bits])
-            if low == 1:
-                assembled += [mine, theirs]
+            if (head_index, part) in DIRECT:
+                theirs = row_swap(send, bit=bits[0] * low)
+                terms = [keep[:1] + theirs[:1]]
+                for index in range(1, keep.shape[0]):
+                    bit = (index // 2) * bits[1] + (index % 2) * bits[2]
+                    block = keep[index : index + 1] + theirs[index : index + 1]
+                    terms.append(row_swap(block, bit=bit * low))
             else:
-                assembled.append(scatter_low((mine + theirs)[0], 1)[None])
-            query_list.append((head_index, begin, end))
+                terms = scatter_steps(keep, send, row_devices, [bit * low for bit in bits])
+            if low > 1:
+                terms = [scatter_low(sum(terms)[0], 1)[None]]
+            assembled += terms
+            query_list.append((head_index, begin, end, len(terms)))
 
     share = ((head_devices // 2, row_count, features // head_devices),)
-    after = marks[0]
+    after = query_out[-1][0]
     input_keep, input_send = pl.pallas_call(
         functools.partial(input_kernel, "heads"),
         out_shape=[shape_of(*share)] * 2,
@@ -400,21 +417,24 @@
         cost_estimate=block_work,
         name="input",
     )(key_weight, value_weight, *(item[0] for item in grads_out), after)
-    total = input_keep + swap(input_send, "heads", head_devices, 1)
-    for bit in bits_of(head_devices)[1:]:
-        pairs = total.reshape((-1, 2) + total.shape[1:])
-        total = pairs[:, 0] + swap(pairs[:, 1], "heads", head_devices, bit)
-
-    query_grad, key_weight_grad, value_weight_grad = pl.pallas_call(
+    head_bits = bits_of(head_devices)[::-1]
+    keep, theirs = input_keep, swap(input_send, "heads", head_devices, head_bits[0])
+    for bit in head_bits[1:]:
+        send = keep[bit:] + theirs[bit:]
+        keep, theirs = keep[:bit] + theirs[:bit], swap(send, "heads", head_devices, bit)
+    input_terms = (keep, theirs)
+
+    query_grad, key_weight_grad, value_weight_grad, input_grad = pl.pallas_call(
         functools.partial(assemble_kernel, weight_list, query_list, "rows", low),
         out_shape=(shape_of((reads, latents // row_devices, columns)),)
-        + (shape_of((features, columns)),) * 2,
-        in_specs=[VMEM] * len(assembled),
-        out_specs=(VMEM,) * 3,
+        + (shape_of((features, columns)),) * 2
+        + (shape_of((row_count, features // head_devices)),),
+        in_specs=[VMEM] * (2 + len(assembled)),
+        out_specs=(VMEM,) * 4,
         compiler_params=params(8),
         name="assemble",
-    )(*assembled)
-    return (query_grad, key_weight_grad, value_weight_grad, total[0])
+    )(*input_terms, *assembled)
+    return (query_grad, key_weight_grad, value_weight_grad, input_grad)
 
 
 def solution(mesh):

time: 76.5 us -> 75.3 us (0.984)
  starting transfers between devices: 33.7 us -> 34.7 us
  waiting for transfers between devices: 23.2 us -> 22.4 us
    ppermute x24, starting transfers between devices: 33.7 us -> 34.7 us  [swap(): return lax.ppermute(array, axis, pairs)]
    ppermute x24, waiting for transfers between devices: 23.2 us -> 22.4 us  [swap(): return lax.ppermute(array, axis, pairs)]
  transfers between devices with their start and end apart: 24 -> 24, of which waited for: 10 -> 11; matrix products, arithmetic and copies ran while one was open for 1% -> 1% of each run, Pallas kernels for 16% -> 15%
where the time goes in v7:
time: 75.3 us; the launch traced here: 75.2 us
  starting transfers between devices  34.7 us (46%)
  waiting for transfers between devices  22.4 us (30%)
  Pallas kernels  16.8 us (22%)
  between operations  0.86 us (1%)
    ppermute x24, starting transfers between devices, swap(): return lax.ppermute(array, axis, pairs)  34.7 us
    ppermute x24, waiting for transfers between devices, swap(): return lax.ppermute(array, axis, pairs)  22.4 us
    pallas_call x4, Pallas kernels, kernel_call(): pl.pallas_call(kernel, out_shape=[shape_of(*item) for item in shapes], in...  8.02 us
    pallas_call x2, Pallas kernels, on_device(): pl.pallas_call(functools.partial(first_kernel, tile) if first else functo...  6.55 us
  transfers between devices with their start and end apart: 24, of which 11 were waited for; matrix products, arithmetic and copies ran while one was open for 1% of the time, Pallas kernels for 15%

profile of v7, /device:TPU:0, one launch (start us, length us, event | category | flops | bytes accessed | tf_op | source)
XLA Modules:
  0.0 75.2 jit_solution(9515615734954813343)
XLA Ops:
  0.7 4.4 %project.2 = (bf16[512,128]{1,0:T(8,128)(2,1)}, bf16[512,128]{1,0:T(8,128)(2,1)}, f32[4,1024]{1,0:T(4,128)}) custom-call(bf16[512,512]{1,0:T(8,128)(2,1)} %inputs.3, bf16[512,256]{1,0:T(8,128)(2,1)} %key_weight.1, bf16[512,256]{1,0:T(8,128)(2,1)} %value_weight.1, bf16[2,1024,256]{2,1,0:T(8,128)(2,1)} %queries.3, bf16[2,1024,256]{2,1,0:T(8,128)(2,1)} %out_grad.3), custom_call_target="tpu_custom_call" | custom-call | flops 1073741824 | bytes 4194304 | tf_op jit(solution)/shard_map/project/pallas_call | solution.py:270
  5.1 3.0 %collective-permute-start = (f32[4,1024]{1,0:T(4,128)}, f32[4,1024]{1,0:T(4,128)S(1)}, u32[]{:S(2)}, u32[]{:S(2)}) collective-permute-start(f32[4,1024]{1,0:T(4,128)} %get-tuple-element.24.mine), channel_id=1, source_target_pairs={{0,4},{4,0},{8,12},{12,8},{16,20},{20,16},{24,28},{28,24},{1,5},{5... | collective-permute-start | bytes 49160 | tf_op jit(solution)/shard_map/ppermute | solution.py:41
  8.2 2.1 %project.3 = (bf16[512,128]{1,0:T(8,128)(2,1)S(1)}, bf16[512,128]{1,0:T(8,128)(2,1)S(1)}, f32[4,1024]{1,0:T(4,128)S(1)}) custom-call(bf16[512,512]{1,0:T(8,128)(2,1)S(1)} %copy-done.3, bf16[512,256]{1,0:T(8,128)(2,1)S(1)} %copy-done.4, bf16[512,256]{1,0:T(8,128)(2,1)S(1)} %copy-done.5, bf16[2,1024,256]{2,1,0:T(8,128)(2,1)S(1)} %copy-done.1, ...), custom_call_target="tpu_custom_call" | custom-call | flops 1073741824 | bytes 4194304 | tf_op jit(solution)/shard_map/project/pallas_call | solution.py:270
  10.4 2.1 %collective-permute-start.1 = (f32[4,1024]{1,0:T(4,128)S(1)}, f32[4,1024]{1,0:T(4,128)S(1)}, u32[]{:S(2)}, u32[]{:S(2)}) collective-permute-start(f32[4,1024]{1,0:T(4,128)S(1)} %merge.4.mine), channel_id=1, source_target_pairs={{0,8},{4,12},{8,0},{12,4},{16,24},{20,28},{24,16},{28,20},{1,9},{5... | collective-permute-start | bytes 49160 | tf_op jit(solution)/shard_map/ppermute | solution.py:41
  12.6 1.5 %collective-permute-done.3.theirs = f32[4,1024]{1,0:T(4,128)S(1)} collective-permute-done((f32[4,1024]{1,0:T(4,128)S(1)}, f32[4,1024]{1,0:T(4,128)S(1)}, u32[]{:S(2)}, u32[]{:S(2)}) %collective-permute-start.3) | collective-permute-done | bytes 16416 | tf_op jit(solution)/shard_map/ppermute | solution.py:41
  14.1 1.6 %collective-permute-start.4 = (f32[4,1024]{1,0:T(4,128)S(1)}, f32[4,1024]{1,0:T(4,128)S(1)}, u32[]{:S(2)}, u32[]{:S(2)}) collective-permute-start(f32[4,1024]{1,0:T(4,128)S(1)} %merge.6.mine), channel_id=1, source_target_pairs={{0,8},{4,12},{8,0},{12,4},{16,24},{20,28},{24,16},{28,20},{1,9},{5... | collective-permute-start | bytes 49160 | tf_op jit(solution)/shard_map/ppermute | solution.py:41
  15.8 2.7 %collective-permute-start.2 = (f32[4,1024]{1,0:T(4,128)S(1)}, f32[4,1024]{1,0:T(4,128)S(1)}, u32[]{:S(2)}, u32[]{:S(2)}) collective-permute-start(f32[4,1024]{1,0:T(4,128)S(1)} %merge.5.after.mine), channel_id=1, source_target_pairs={{0,16},{4,20},{8,24},{12,28},{16,0},{20,4},{24,8},{28,12},{1,17},{... | collective-permute-start | bytes 49160 | tf_op jit(solution)/shard_map/ppermute | solution.py:41
  18.5 2.2 %collective-permute-start.5 = (f32[4,1024]{1,0:T(4,128)S(1)}, f32[4,1024]{1,0:T(4,128)S(1)}, u32[]{:S(2)}, u32[]{:S(2)}) collective-permute-start(f32[4,1024]{1,0:T(4,128)S(1)} %merge.7.mine), channel_id=1, source_target_pairs={{0,16},{4,20},{8,24},{12,28},{16,0},{20,4},{24,8},{28,12},{1,17},{... | collective-permute-start | bytes 49160 | tf_op jit(solution)/shard_map/ppermute | solution.py:41
  20.7 2.9 %grads.2 = (bf16[512,256]{1,0:T(8,128)(2,1)S(1)}, bf16[2,512,1024]{2,1,0:T(8,128)(2,1)S(1)}, f32[2,2,64,256]{3,2,1,0:T(8,128)S(1)}, f32[2,2,64,256]{3,2,1,0:T(8,128)S(1)}) custom-call(f32[4,1024]{1,0:T(4,128)S(1)} %merge.5.after.mine, bf16[512,512]{1,0:T(8,128)(2,1)S(1)} %copy-done.3, bf16[512,128]{1,0:T(8,128)(2,1)S(1)} %copy-done.6, ...), custom_call_target="tpu_custom_call" | custom-call | flops 1073741824 | bytes 4194304 | tf_op jit(solution)/shard_map/grads/pallas_call | solution.py:326
  25.2 1.8 %collective-permute-start.18 = (f32[4,2,128,128]{3,2,1,0:T(8,128)S(1)}, f32[4,2,128,128]{3,2,1,0:T(8,128)S(1)}, u32[]{:S(2)}, u32[]{:S(2)}) collective-permute-start(f32[4,2,128,128]{3,2,1,0:T(8,128)S(1)} %get-tuple-element.42), channel_id=1, source_target_pairs={{0,8},{4,12},{8,0},{12,4},{16,24},{20,28},{24,16},{28,20},{1,9},{5... | collective-permute-start | bytes 1572872 | tf_op jit(solution)/shard_map/ppermute | solution.py:41
  27.0 2.9 %grads.3 = (bf16[512,256]{1,0:T(8,128)(2,1)S(1)}, bf16[2,512,1024]{2,1,0:T(8,128)(2,1)S(1)}, f32[2,2,64,256]{3,2,1,0:T(8,128)S(1)}, f32[2,2,64,256]{3,2,1,0:T(8,128)S(1)}) custom-call(bf16[512,256]{1,0:T(8,128)(2,1)S(1)} %get-tuple-element.27.after.refs_0_, bf16[512,512]{1,0:T(8,128)(2,1)S(1)} %copy-done.3, bf16[512,128]{1,0:T(8,128)(2,1)S(1)} %get-tuple-element.28.keys, ...), custom_call_target="tpu_custom_call" | custom-call | flops 1073741824 | bytes 4194304 | tf_op jit(solution)/shard_map/grads/pallas_call | solution.py:326
  33.4 1.6 %collective-permute-start.6 = (f32[2,512,128]{2,1,0:T(8,128)S(1)}, f32[2,512,128]{2,1,0:T(8,128)S(1)}, u32[]{:S(2)}, u32[]{:S(2)}) collective-permute-start(f32[2,512,128]{2,1,0:T(8,128)S(1)} %get-tuple-element.35), channel_id=1, source_target_pairs={{0,2},{1,3},{2,0},{3,1},{4,6},{5,7},{6,4},{7,5},{8,10},{9,11},{10,... | collective-permute-start | bytes 1572872 | tf_op jit(solution)/shard_map/ppermute | solution.py:41
  36.0 3.1 %collective-permute-done.13 = f32[2,2,64,256]{3,2,1,0:T(8,128)S(1)} collective-permute-done((f32[2,2,64,256]{3,2,1,0:T(8,128)S(1)}, f32[2,2,64,256]{3,2,1,0:T(8,128)S(1)}, u32[]{:S(2)}, u32[]{:S(2)}) %collective-permute-start.13) | collective-permute-done | bytes 262176 | tf_op jit(solution)/shard_map/ppermute | solution.py:41
  39.6 1.6 %collective-permute-done.9 = f32[1,2,64,256]{3,2,1,0:T(8,128)S(1)} collective-permute-done((f32[1,2,64,256]{3,2,1,0:T(8,128)S(1)}, f32[1,2,64,256]{3,2,1,0:T(8,128)S(1)}, u32[]{:S(2)}, u32[]{:S(2)}) %collective-permute-start.9) | collective-permute-done | bytes 131104 | tf_op jit(solution)/shard_map/ppermute | solution.py:41
  41.2 3.3 %collective-permute-start.10 = (f32[1,2,64,256]{3,2,1,0:T(8,128)S(1)}, f32[1,2,64,256]{3,2,1,0:T(8,128)S(1)}, u32[]{:S(2)}, u32[]{:S(2)}) collective-permute-start(f32[1,2,64,256]{3,2,1,0:T(8,128)S(1)} %fusion.1), channel_id=1, source_target_pairs={{0,16},{4,20},{8,24},{12,28},{16,0},{20,4},{24,8},{28,12},{1,17},{... | collective-permute-start | bytes 393224 | tf_op jit(solution)/shard_map/ppermute | solution.py:41
  44.9 2.3 %collective-permute-start.15 = (f32[1,2,64,256]{3,2,1,0:T(8,128)S(1)}, f32[1,2,64,256]{3,2,1,0:T(8,128)S(1)}, u32[]{:S(2)}, u32[]{:S(2)}) collective-permute-start(f32[1,2,64,256]{3,2,1,0:T(8,128)S(1)} %fusion), channel_id=1, source_target_pairs={{0,16},{4,20},{8,24},{12,28},{16,0},{20,4},{24,8},{28,12},{1,17},{... | collective-permute-start | bytes 393224 | tf_op jit(solution)/shard_map/ppermute | solution.py:41
  50.5 1.8 %collective-permute-done.15 = f32[1,2,64,256]{3,2,1,0:T(8,128)S(1)} collective-permute-done((f32[1,2,64,256]{3,2,1,0:T(8,128)S(1)}, f32[1,2,64,256]{3,2,1,0:T(8,128)S(1)}, u32[]{:S(2)}, u32[]{:S(2)}) %collective-permute-start.15) | collective-permute-done | bytes 131104 | tf_op jit(solution)/shard_map/ppermute | solution.py:41
  52.6 2.0 %collective-permute-start.22 = (f32[2,2,128,128]{3,2,1,0:T(8,128)S(1)}, f32[2,2,128,128]{3,2,1,0:T(8,128)S(1)}, u32[]{:S(2)}, u32[]{:S(2)}) collective-permute-start(f32[2,2,128,128]{3,2,1,0:T(8,128)S(1)} %get-tuple-element.45), channel_id=1, source_target_pairs={{0,8},{4,12},{8,0},{12,4},{16,24},{20,28},{24,16},{28,20},{1,9},{5... | collective-permute-start | bytes 786440 | tf_op jit(solution)/shard_map/ppermute | solution.py:41
  55.4 1.5 %collective-permute-start.12 = (f32[2,2,64,256]{3,2,1,0:T(8,128)S(1)}, f32[2,2,64,256]{3,2,1,0:T(8,128)S(1)}, u32[]{:S(2)}, u32[]{:S(2)}) collective-permute-start(f32[2,2,64,256]{3,2,1,0:T(8,128)S(1)} %pad_maximum_fusion.refs_2_), channel_id=1, source_target_pairs={{0,4},{4,0},{8,12},{12,8},{16,20},{20,16},{24,28},{28,24},{1,5},{5... | collective-permute-start | bytes 786440 | tf_op jit(solution)/shard_map/ppermute | solution.py:41
  56.9 1.9 %collective-permute-done.16 = f32[1,2,64,256]{3,2,1,0:T(8,128)S(1)} collective-permute-done((f32[1,2,64,256]{3,2,1,0:T(8,128)S(1)}, f32[1,2,64,256]{3,2,1,0:T(8,128)S(1)}, u32[]{:S(2)}, u32[]{:S(2)}) %collective-permute-start.16) | collective-permute-done | bytes 131104 | tf_op jit(solution)/shard_map/ppermute | solution.py:41
  58.8 1.8 %collective-permute-start.17 = (f32[2,2,64,256]{3,2,1,0:T(8,128)S(1)}, f32[2,2,64,256]{3,2,1,0:T(8,128)S(1)}, u32[]{:S(2)}, u32[]{:S(2)}) collective-permute-start(f32[2,2,64,256]{3,2,1,0:T(8,128)S(1)} %pad_maximum_fusion.1.refs_4_), channel_id=1, source_target_pairs={{0,4},{4,0},{8,12},{12,8},{16,20},{20,16},{24,28},{28,24},{1,5},{5... | collective-permute-start | bytes 786440 | tf_op jit(solution)/shard_map/ppermute | solution.py:41
  61.9 3.0 %collective-permute-done.22 = f32[2,2,128,128]{3,2,1,0:T(8,128)S(1)} collective-permute-done((f32[2,2,128,128]{3,2,1,0:T(8,128)S(1)}, f32[2,2,128,128]{3,2,1,0:T(8,128)S(1)}, u32[]{:S(2)}, u32[]{:S(2)}) %collective-permute-start.22) | collective-permute-done | bytes 262176 | tf_op jit(solution)/shard_map/ppermute | solution.py:41
  66.1 5.7 %collective-permute-done.20.refs_7_ = f32[1,2,128,128]{3,2,1,0:T(8,128)S(1)} collective-permute-done((f32[1,2,128,128]{3,2,1,0:T(8,128)S(1)}, f32[1,2,128,128]{3,2,1,0:T(8,128)S(1)}, u32[]{:S(2)}, u32[]{:S(2)}) %collective-permute-start.20) | collective-permute-done | bytes 131104 | tf_op jit(solution)/shard_map/ppermute | solution.py:41
  71.8 2.1 %collective-permute-done.23.refs_9_ = f32[1,2,128,128]{3,2,1,0:T(8,128)S(1)} collective-permute-done((f32[1,2,128,128]{3,2,1,0:T(8,128)S(1)}, f32[1,2,128,128]{3,2,1,0:T(8,128)S(1)}, u32[]{:S(2)}, u32[]{:S(2)}) %collective-permute-start.23) | collective-permute-done | bytes 131104 | tf_op jit(solution)/shard_map/ppermute | solution.py:41
  (65 shorter events, 15.3 us)
Async XLA Ops:
  5.1 5.3 %collective-permute-start = (f32[4,1024]{1,0:T(4,128)}, f32[4,1024]{1,0:T(4,128)S(1)}, u32[]{:S(2)}, u32[]{:S(2)}) collective-permute-start(f32[4,1024]{1,0:T(4,128)} %get-tuple-element.24.mine), channel_id=1, source_target_pairs={{0,4},{4,0},{8,12},{12,8},{16,20},{20,16},{24,28},{28,24},{1,5},{5... | collective-permute-start | bytes 49160 | tf_op jit(solution)/shard_map/ppermute | solution.py:41
  10.3 3.8 %collective-permute-start.3 = (f32[4,1024]{1,0:T(4,128)S(1)}, f32[4,1024]{1,0:T(4,128)S(1)}, u32[]{:S(2)}, u32[]{:S(2)}) collective-permute-start(f32[4,1024]{1,0:T(4,128)S(1)} %get-tuple-element.30.mine), channel_id=1, source_target_pairs={{0,4},{4,0},{8,12},{12,8},{16,20},{20,16},{24,28},{28,24},{1,5},{5... | collective-permute-start | bytes 49160 | tf_op jit(solution)/shard_map/ppermute | solution.py:41
  10.4 5.3 %collective-permute-start.1 = (f32[4,1024]{1,0:T(4,128)S(1)}, f32[4,1024]{1,0:T(4,128)S(1)}, u32[]{:S(2)}, u32[]{:S(2)}) collective-permute-start(f32[4,1024]{1,0:T(4,128)S(1)} %merge.4.mine), channel_id=1, source_target_pairs={{0,8},{4,12},{8,0},{12,4},{16,24},{20,28},{24,16},{28,20},{1,9},{5... | collective-permute-start | bytes 49160 | tf_op jit(solution)/shard_map/ppermute | solution.py:41
  14.1 4.3 %collective-permute-start.4 = (f32[4,1024]{1,0:T(4,128)S(1)}, f32[4,1024]{1,0:T(4,128)S(1)}, u32[]{:S(2)}, u32[]{:S(2)}) collective-permute-start(f32[4,1024]{1,0:T(4,128)S(1)} %merge.6.mine), channel_id=1, source_target_pairs={{0,8},{4,12},{8,0},{12,4},{16,24},{20,28},{24,16},{28,20},{1,9},{5... | collective-permute-start | bytes 49160 | tf_op jit(solution)/shard_map/ppermute | solution.py:41
  15.8 4.9 %collective-permute-start.2 = (f32[4,1024]{1,0:T(4,128)S(1)}, f32[4,1024]{1,0:T(4,128)S(1)}, u32[]{:S(2)}, u32[]{:S(2)}) collective-permute-start(f32[4,1024]{1,0:T(4,128)S(1)} %merge.5.after.mine), channel_id=1, source_target_pairs={{0,16},{4,20},{8,24},{12,28},{16,0},{20,4},{24,8},{28,12},{1,17},{... | collective-permute-start | bytes 49160 | tf_op jit(solution)/shard_map/ppermute | solution.py:41
  18.5 8.5 %collective-permute-start.5 = (f32[4,1024]{1,0:T(4,128)S(1)}, f32[4,1024]{1,0:T(4,128)S(1)}, u32[]{:S(2)}, u32[]{:S(2)}) collective-permute-start(f32[4,1024]{1,0:T(4,128)S(1)} %merge.7.mine), channel_id=1, source_target_pairs={{0,16},{4,20},{8,24},{12,28},{16,0},{20,4},{24,8},{28,12},{1,17},{... | collective-permute-start | bytes 49160 | tf_op jit(solution)/shard_map/ppermute | solution.py:41
  23.6 12.0 %collective-permute-start.8 = (f32[2,2,64,256]{3,2,1,0:T(8,128)S(1)}, f32[2,2,64,256]{3,2,1,0:T(8,128)S(1)}, u32[]{:S(2)}, u32[]{:S(2)}) collective-permute-start(f32[2,2,64,256]{3,2,1,0:T(8,128)S(1)} %get-tuple-element.37), channel_id=1, source_target_pairs={{0,4},{4,0},{8,12},{12,8},{16,20},{20,16},{24,28},{28,24},{1,5},{5... | collective-permute-start | bytes 786440 | tf_op jit(solution)/shard_map/ppermute | solution.py:41
  25.2 22.0 %collective-permute-start.18 = (f32[4,2,128,128]{3,2,1,0:T(8,128)S(1)}, f32[4,2,128,128]{3,2,1,0:T(8,128)S(1)}, u32[]{:S(2)}, u32[]{:S(2)}) collective-permute-start(f32[4,2,128,128]{3,2,1,0:T(8,128)S(1)} %get-tuple-element.42), channel_id=1, source_target_pairs={{0,8},{4,12},{8,0},{12,4},{16,24},{20,28},{24,16},{28,20},{1,9},{5... | collective-permute-start | bytes 1572872 | tf_op jit(solution)/shard_map/ppermute | solution.py:41
  29.9 9.2 %collective-permute-start.13 = (f32[2,2,64,256]{3,2,1,0:T(8,128)S(1)}, f32[2,2,64,256]{3,2,1,0:T(8,128)S(1)}, u32[]{:S(2)}, u32[]{:S(2)}) collective-permute-start(f32[2,2,64,256]{3,2,1,0:T(8,128)S(1)} %get-tuple-element.39), channel_id=1, source_target_pairs={{0,4},{4,0},{8,12},{12,8},{16,20},{20,16},{24,28},{28,24},{1,5},{5... | collective-permute-start | bytes 786440 | tf_op jit(solution)/shard_map/ppermute | solution.py:41
  33.4 15.1 %collective-permute-start.6 = (f32[2,512,128]{2,1,0:T(8,128)S(1)}, f32[2,512,128]{2,1,0:T(8,128)S(1)}, u32[]{:S(2)}, u32[]{:S(2)}) collective-permute-start(f32[2,512,128]{2,1,0:T(8,128)S(1)} %get-tuple-element.35), channel_id=1, source_target_pairs={{0,2},{1,3},{2,0},{3,1},{4,6},{5,7},{6,4},{7,5},{8,10},{9,11},{10,... | collective-permute-start | bytes 1572872 | tf_op jit(solution)/shard_map/ppermute | solution.py:41
  35.0 17.5 %collective-permute-start.21 = (f32[4,2,128,128]{3,2,1,0:T(8,128)S(1)}, f32[4,2,128,128]{3,2,1,0:T(8,128)S(1)}, u32[]{:S(2)}, u32[]{:S(2)}) collective-permute-start(f32[4,2,128,128]{3,2,1,0:T(8,128)S(1)} %get-tuple-element.43), channel_id=1, source_target_pairs={{0,4},{4,0},{8,12},{12,8},{16,20},{20,16},{24,28},{28,24},{1,5},{5... | collective-permute-start | bytes 1572872 | tf_op jit(solution)/shard_map/ppermute | solution.py:41
  35.7 5.5 %collective-permute-start.9 = (f32[1,2,64,256]{3,2,1,0:T(8,128)S(1)}, f32[1,2,64,256]{3,2,1,0:T(8,128)S(1)}, u32[]{:S(2)}, u32[]{:S(2)}) collective-permute-start(f32[1,2,64,256]{3,2,1,0:T(8,128)S(1)} %slice_add_fusion.12), channel_id=1, source_target_pairs={{0,8},{4,12},{8,0},{12,4},{16,24},{20,28},{24,16},{28,20},{1,9},{5... | collective-permute-start | bytes 393224 | tf_op jit(solution)/shard_map/ppermute | solution.py:41
  39.2 5.7 %collective-permute-start.14 = (f32[1,2,64,256]{3,2,1,0:T(8,128)S(1)}, f32[1,2,64,256]{3,2,1,0:T(8,128)S(1)}, u32[]{:S(2)}, u32[]{:S(2)}) collective-permute-start(f32[1,2,64,256]{3,2,1,0:T(8,128)S(1)} %slice_add_fusion.10), channel_id=1, source_target_pairs={{0,8},{4,12},{8,0},{12,4},{16,24},{20,28},{24,16},{28,20},{1,9},{5... | collective-permute-start | bytes 393224 | tf_op jit(solution)/shard_map/ppermute | solution.py:41
  41.2 7.8 %collective-permute-start.10 = (f32[1,2,64,256]{3,2,1,0:T(8,128)S(1)}, f32[1,2,64,256]{3,2,1,0:T(8,128)S(1)}, u32[]{:S(2)}, u32[]{:S(2)}) collective-permute-start(f32[1,2,64,256]{3,2,1,0:T(8,128)S(1)} %fusion.1), channel_id=1, source_target_pairs={{0,16},{4,20},{8,24},{12,28},{16,0},{20,4},{24,8},{28,12},{1,17},{... | collective-permute-start | bytes 393224 | tf_op jit(solution)/shard_map/ppermute | solution.py:41
  44.9 7.4 %collective-permute-start.15 = (f32[1,2,64,256]{3,2,1,0:T(8,128)S(1)}, f32[1,2,64,256]{3,2,1,0:T(8,128)S(1)}, u32[]{:S(2)}, u32[]{:S(2)}) collective-permute-start(f32[1,2,64,256]{3,2,1,0:T(8,128)S(1)} %fusion), channel_id=1, source_target_pairs={{0,16},{4,20},{8,24},{12,28},{16,0},{20,4},{24,8},{28,12},{1,17},{... | collective-permute-start | bytes 393224 | tf_op jit(solution)/shard_map/ppermute | solution.py:41
  47.3 13.4 %collective-permute-start.19 = (f32[2,2,128,128]{3,2,1,0:T(8,128)S(1)}, f32[2,2,128,128]{3,2,1,0:T(8,128)S(1)}, u32[]{:S(2)}, u32[]{:S(2)}) collective-permute-start(f32[2,2,128,128]{3,2,1,0:T(8,128)S(1)} %get-tuple-element.47), channel_id=1, source_target_pairs={{0,4},{4,0},{8,12},{12,8},{16,20},{20,16},{24,28},{28,24},{1,5},{5... | collective-permute-start | bytes 786440 | tf_op jit(solution)/shard_map/ppermute | solution.py:41
  48.5 17.5 %collective-permute-start.7 = (f32[1,512,128]{2,1,0:T(8,128)S(1)}, f32[1,512,128]{2,1,0:T(8,128)S(1)}, u32[]{:S(2)}, u32[]{:S(2)}) collective-permute-start(f32[1,512,128]{2,1,0:T(8,128)S(1)} %get-tuple-element.48), channel_id=1, source_target_pairs={{0,1},{1,0},{2,3},{3,2},{4,5},{5,4},{6,7},{7,6},{8,9},{9,8},{10,11... | collective-permute-start | bytes 786440 | tf_op jit(solution)/shard_map/ppermute | solution.py:41
  49.0 6.4 %collective-permute-start.11 = (f32[1,2,64,256]{3,2,1,0:T(8,128)S(1)}, f32[1,2,64,256]{3,2,1,0:T(8,128)S(1)}, u32[]{:S(2)}, u32[]{:S(2)}) collective-permute-start(f32[1,2,64,256]{3,2,1,0:T(8,128)S(1)} %add.59), channel_id=1, source_target_pairs={{0,8},{4,12},{8,0},{12,4},{16,24},{20,28},{24,16},{28,20},{1,9},{5... | collective-permute-start | bytes 393224 | tf_op jit(solution)/shard_map/ppermute | solution.py:41
  52.3 6.5 %collective-permute-start.16 = (f32[1,2,64,256]{3,2,1,0:T(8,128)S(1)}, f32[1,2,64,256]{3,2,1,0:T(8,128)S(1)}, u32[]{:S(2)}, u32[]{:S(2)}) collective-permute-start(f32[1,2,64,256]{3,2,1,0:T(8,128)S(1)} %add.63), channel_id=1, source_target_pairs={{0,8},{4,12},{8,0},{12,4},{16,24},{20,28},{24,16},{28,20},{1,9},{5... | collective-permute-start | bytes 393224 | tf_op jit(solution)/shard_map/ppermute | solution.py:41
  52.6 12.3 %collective-permute-start.22 = (f32[2,2,128,128]{3,2,1,0:T(8,128)S(1)}, f32[2,2,128,128]{3,2,1,0:T(8,128)S(1)}, u32[]{:S(2)}, u32[]{:S(2)}) collective-permute-start(f32[2,2,128,128]{3,2,1,0:T(8,128)S(1)} %get-tuple-element.45), channel_id=1, source_target_pairs={{0,8},{4,12},{8,0},{12,4},{16,24},{20,28},{24,16},{28,20},{1,9},{5... | collective-permute-start | bytes 786440 | tf_op jit(solution)/shard_map/ppermute | solution.py:41
  55.4 18.4 %collective-permute-start.12 = (f32[2,2,64,256]{3,2,1,0:T(8,128)S(1)}, f32[2,2,64,256]{3,2,1,0:T(8,128)S(1)}, u32[]{:S(2)}, u32[]{:S(2)}) collective-permute-start(f32[2,2,64,256]{3,2,1,0:T(8,128)S(1)} %pad_maximum_fusion.refs_2_), channel_id=1, source_target_pairs={{0,4},{4,0},{8,12},{12,8},{16,20},{20,16},{24,28},{28,24},{1,5},{5... | collective-permute-start | bytes 786440 | tf_op jit(solution)/shard_map/ppermute | solution.py:41
  58.8 15.1 %collective-permute-start.17 = (f32[2,2,64,256]{3,2,1,0:T(8,128)S(1)}, f32[2,2,64,256]{3,2,1,0:T(8,128)S(1)}, u32[]{:S(2)}, u32[]{:S(2)}) collective-permute-start(f32[2,2,64,256]{3,2,1,0:T(8,128)S(1)} %pad_maximum_fusion.1.refs_4_), channel_id=1, source_target_pairs={{0,4},{4,0},{8,12},{12,8},{16,20},{20,16},{24,28},{28,24},{1,5},{5... | collective-permute-start | bytes 786440 | tf_op jit(solution)/shard_map/ppermute | solution.py:41
  60.7 11.1 %collective-permute-start.20 = (f32[1,2,128,128]{3,2,1,0:T(8,128)S(1)}, f32[1,2,128,128]{3,2,1,0:T(8,128)S(1)}, u32[]{:S(2)}, u32[]{:S(2)}) collective-permute-start(f32[1,2,128,128]{3,2,1,0:T(8,128)S(1)} %get-tuple-element.52), channel_id=1, source_target_pairs={{0,16},{4,20},{8,24},{12,28},{16,0},{20,4},{24,8},{28,12},{1,17},{... | collective-permute-start | bytes 393224 | tf_op jit(solution)/shard_map/ppermute | solution.py:41
  64.9 9.0 %collective-permute-start.23 = (f32[1,2,128,128]{3,2,1,0:T(8,128)S(1)}, f32[1,2,128,128]{3,2,1,0:T(8,128)S(1)}, u32[]{:S(2)}, u32[]{:S(2)}) collective-permute-start(f32[1,2,128,128]{3,2,1,0:T(8,128)S(1)} %get-tuple-element.50), channel_id=1, source_target_pairs={{0,16},{4,20},{8,24},{12,28},{16,0},{20,4},{24,8},{28,12},{1,17},{... | collective-permute-start | bytes 393224 | tf_op jit(solution)/shard_map/ppermute | solution.py:41
  (8 other events, 74.0 us)

commit v8 on v7

--- a/solution.py
+++ b/solution.py
@@ -119,7 +119,7 @@
 LAST_BIT = 4
 WEIGHT_PARTS = (((0, 256, (1, 2)),), ((0, 256, (1, 2)),))
 QUERY_PARTS = (((0, 2, (2, 1, 4)),), ((0, 2, (1, 2, 4)),))
-DIRECT = ()
+AFTER = {'w0.3': 'q0.1', 'w1.4': 'q0.2'}
 
 
 def grads_kernel(
@@ -235,14 +235,15 @@
     return jax.ShapeDtypeStruct(shape, dtype)
 
 
-def scatter_steps(keep, send, count, bits):
-    for index, bit in enumerate(bits):
-        theirs = swap(send, "rows", count, bit)
-        if index + 1 == len(bits):
-            return keep, theirs
-        middle = keep.shape[0] // 2
-        send = keep[middle:] + theirs[middle:]
-        keep = keep[:middle] + theirs[:middle]
+def add_kernel(mine, theirs, after, total):
+    del after
+    total[...] = mine[...] + theirs[...]
+
+
+def stack_kernel(mine, theirs, after, both):
+    del after
+    both[: mine.shape[0]] = mine[...]
+    both[mine.shape[0] :] = theirs[...]
 
 
 def on_device(row_devices, head_devices, inputs, key_weight, value_weight, queries, out_grad):
@@ -375,38 +376,66 @@
             )
         )
 
-    assembled, weight_list, marks = [], [], []
+    def added(kernel, shape, mine, theirs, after):
+        return pl.pallas_call(
+            kernel,
+            out_shape=shape_of(shape),
+            in_specs=[VMEM, VMEM, ANY],
+            out_specs=VMEM,
+            compiler_params=params(4),
+            cost_estimate=pl.CostEstimate(flops=1024, bytes_accessed=1024, transcendentals=0),
+            name="added",
+        )(mine, theirs, after)
+
+    marks = {}
+    query_terms, query_list = [], []
+    for head_index in range(head_count):
+        for part, (begin, end, bits) in enumerate(QUERY_PARTS[head_index]):
+            keep, send = query_out[head_index][2 * part : 2 * part + 2]
+            for place, bit in enumerate(bits):
+                theirs = row_swap(send, bit=bit * low)
+                if place + 1 < len(bits):
+                    middle = keep.shape[0] // 2
+                    send = keep[middle:] + theirs[middle:]
+                    keep = keep[:middle] + theirs[:middle]
+                    marks[f"q{head_index}.{place + 1}"] = send
+            terms = [keep, theirs]
+            if low > 1:
+                terms = [scatter_low((keep + theirs)[0], 1)[None]]
+            query_terms += terms
+            query_list.append((head_index, begin, end, len(terms)))
+
+    weight_terms, weight_list = [], []
     for head_index in range(head_count):
         for part, (begin, end, bits) in enumerate(WEIGHT_PARTS[head_index]):
             keep, send = grads_out[head_index][2 + 2 * part : 4 + 2 * part]
             first, second = (bit * low for bit in bits)
-            mine, theirs = scatter_steps(keep, send, row_devices, (first, second))
-            marks.append(mine)
-            mine = mine + theirs
-            mine = sum_low(mine + row_swap(mine, bit=LAST_BIT * low))
-            near = jnp.concatenate([mine, row_swap(mine, bit=second)], axis=0)
-            assembled += [near, row_swap(near, bit=first)]
+            theirs = row_swap(send, bit=first)
+            send = keep[1:] + theirs[1:]
+            mine = keep[:1] + theirs[:1]
+            marks[f"w{head_index}.1"] = send
+            theirs = row_swap(send, bit=second)
+            for place, bit in ((2, LAST_BIT * low), (3, second)):
+                after = AFTER.get(f"w{head_index}.{place}")
+                if after:
+                    mine = added(add_kernel, mine.shape, mine, theirs, marks[after])
+                else:
+                    mine = mine + theirs
+                if place == 3:
+                    mine = sum_low(mine)
+                theirs = row_swap(mine, bit=bit)
+            after = AFTER.get(f"w{head_index}.4")
+            shape = (2, *mine.shape[1:])
+            if after:
+                near = added(stack_kernel, shape, mine, theirs, marks[after])
+            else:
+                near = jnp.concatenate([mine, theirs], axis=0)
+            weight_terms += [near, row_swap(near, bit=first)]
             weight_list.append((head_index, begin, end, bits))
-    query_list = []
-    for head_index in range(head_count):
-        for part, (begin, end, bits) in enumerate(QUERY_PARTS[head_index]):
-            keep, send = query_out[head_index][2 * part : 2 * part + 2]
-            if (head_index, part) in DIRECT:
-                theirs = row_swap(send, bit=bits[0] * low)
-                terms = [keep[:1] + theirs[:1]]
-                for index in range(1, keep.shape[0]):
-                    bit = (index // 2) * bits[1] + (index % 2) * bits[2]
-                    block = keep[index : index + 1] + theirs[index : index + 1]
-                    terms.append(row_swap(block, bit=bit * low))
-            else:
-                terms = scatter_steps(keep, send, row_devices, [bit * low for bit in bits])
-            if low > 1:
-                terms = [scatter_low(sum(terms)[0], 1)[None]]
-            assembled += terms
-            query_list.append((head_index, begin, end, len(terms)))
+    assembled = weight_terms + query_terms
 
     share = ((head_devices // 2, row_count, features // head_devices),)
-    after = query_out[-1][0]
+    after = marks[AFTER["i.0"]] if "i.0" in AFTER else query_out[-1][0]
     input_keep, input_send = pl.pallas_call(
         functools.partial(input_kernel, "heads"),
         out_shape=[shape_of(*share)] * 2,
@@ -420,8 +449,14 @@
     head_bits = bits_of(head_devices)[::-1]
     keep, theirs = input_keep, swap(input_send, "heads", head_devices, head_bits[0])
     for bit in head_bits[1:]:
-        send = keep[bit:] + theirs[bit:]
-        keep, theirs = keep[:bit] + theirs[:bit], swap(send, "heads", head_devices, bit)
+        after = AFTER.get("i.1")
+        if after:
+            total = added(add_kernel, keep.shape, keep, theirs, marks[after])
+            send, keep = total[bit:], total[:bit]
+        else:
+            send = keep[bit:] + theirs[bit:]
+            keep = keep[:bit] + theirs[:bit]
+        theirs = swap(send, "heads", head_devices, bit)
     input_terms = (keep, theirs)
 
     query_grad, key_weight_grad, value_weight_grad, input_grad = pl.pallas_call(

time: 75.3 us -> 77.4 us (1.028)
  waiting for transfers between devices: 22.4 us -> 26.6 us
  starting transfers between devices: 34.7 us -> 32.6 us
    ppermute x24, waiting for transfers between devices: 22.4 us -> 26.6 us  [swap(): return lax.ppermute(array, axis, pairs)]
    ppermute x24, starting transfers between devices: 34.7 us -> 32.6 us  [swap(): return lax.ppermute(array, axis, pairs)]
  transfers between devices with their start and end apart: 24 -> 24, of which waited for: 11 -> 9; matrix products, arithmetic and copies ran while one was open for 1% -> 0% of each run, Pallas kernels for 15% -> 14%
where the time goes in v8:
time: 77.4 us; the launch traced here: 77.3 us
  starting transfers between devices  32.6 us (42%)
  waiting for transfers between devices  26.6 us (34%)
  Pallas kernels  16.8 us (22%)
  between operations  0.89 us (1%)
    ppermute x24, starting transfers between devices, swap(): return lax.ppermute(array, axis, pairs)  32.6 us
    ppermute x24, waiting for transfers between devices, swap(): return lax.ppermute(array, axis, pairs)  26.6 us
    pallas_call x4, Pallas kernels, kernel_call(): pl.pallas_call(kernel, out_shape=[shape_of(*item) for item in shapes], in...  8.02 us
    pallas_call x2, Pallas kernels, on_device(): pl.pallas_call(functools.partial(first_kernel, tile) if first else functo...  6.55 us
  transfers between devices with their start and end apart: 24, of which 9 were waited for; matrix products, arithmetic and copies ran while one was open for 0% of the time, Pallas kernels for 14%

profile of v8, /device:TPU:0, one launch (start us, length us, event | category | flops | bytes accessed | tf_op | source)
XLA Modules:
  0.0 77.3 jit_solution(3450187822149605022)
XLA Ops:
  0.7 4.4 %project.2 = (bf16[512,128]{1,0:T(8,128)(2,1)}, bf16[512,128]{1,0:T(8,128)(2,1)}, f32[4,1024]{1,0:T(4,128)}) custom-call(bf16[512,512]{1,0:T(8,128)(2,1)} %inputs.3, bf16[512,256]{1,0:T(8,128)(2,1)} %key_weight.1, bf16[512,256]{1,0:T(8,128)(2,1)} %value_weight.1, bf16[2,1024,256]{2,1,0:T(8,128)(2,1)} %queries.3, bf16[2,1024,256]{2,1,0:T(8,128)(2,1)} %out_grad.3), custom_call_target="tpu_custom_call" | custom-call | flops 1073741824 | bytes 4194304 | tf_op jit(solution)/shard_map/project/pallas_call | solution.py:271
  5.1 3.0 %collective-permute-start = (f32[4,1024]{1,0:T(4,128)}, f32[4,1024]{1,0:T(4,128)S(1)}, u32[]{:S(2)}, u32[]{:S(2)}) collective-permute-start(f32[4,1024]{1,0:T(4,128)} %get-tuple-element.24.mine), channel_id=1, source_target_pairs={{0,4},{4,0},{8,12},{12,8},{16,20},{20,16},{24,28},{28,24},{1,5},{5... | collective-permute-start | bytes 49160 | tf_op jit(solution)/shard_map/ppermute | solution.py:41
  8.2 2.1 %project.3 = (bf16[512,128]{1,0:T(8,128)(2,1)S(1)}, bf16[512,128]{1,0:T(8,128)(2,1)S(1)}, f32[4,1024]{1,0:T(4,128)S(1)}) custom-call(bf16[512,512]{1,0:T(8,128)(2,1)S(1)} %copy-done.3, bf16[512,256]{1,0:T(8,128)(2,1)S(1)} %copy-done.4, bf16[512,256]{1,0:T(8,128)(2,1)S(1)} %copy-done.5, bf16[2,1024,256]{2,1,0:T(8,128)(2,1)S(1)} %copy-done.1, ...), custom_call_target="tpu_custom_call" | custom-call | flops 1073741824 | bytes 4194304 | tf_op jit(solution)/shard_map/project/pallas_call | solution.py:271
  10.4 2.1 %collective-permute-start.1 = (f32[4,1024]{1,0:T(4,128)S(1)}, f32[4,1024]{1,0:T(4,128)S(1)}, u32[]{:S(2)}, u32[]{:S(2)}) collective-permute-start(f32[4,1024]{1,0:T(4,128)S(1)} %merge.4.mine), channel_id=1, source_target_pairs={{0,8},{4,12},{8,0},{12,4},{16,24},{20,28},{24,16},{28,20},{1,9},{5... | collective-permute-start | bytes 49160 | tf_op jit(solution)/shard_map/ppermute | solution.py:41
  12.6 1.5 %collective-permute-done.3.theirs = f32[4,1024]{1,0:T(4,128)S(1)} collective-permute-done((f32[4,1024]{1,0:T(4,128)S(1)}, f32[4,1024]{1,0:T(4,128)S(1)}, u32[]{:S(2)}, u32[]{:S(2)}) %collective-permute-start.3) | collective-permute-done | bytes 16416 | tf_op jit(solution)/shard_map/ppermute | solution.py:41
  14.1 1.6 %collective-permute-start.4 = (f32[4,1024]{1,0:T(4,128)S(1)}, f32[4,1024]{1,0:T(4,128)S(1)}, u32[]{:S(2)}, u32[]{:S(2)}) collective-permute-start(f32[4,1024]{1,0:T(4,128)S(1)} %merge.6.mine), channel_id=1, source_target_pairs={{0,8},{4,12},{8,0},{12,4},{16,24},{20,28},{24,16},{28,20},{1,9},{5... | collective-permute-start | bytes 49160 | tf_op jit(solution)/shard_map/ppermute | solution.py:41
  15.8 2.7 %collective-permute-start.2 = (f32[4,1024]{1,0:T(4,128)S(1)}, f32[4,1024]{1,0:T(4,128)S(1)}, u32[]{:S(2)}, u32[]{:S(2)}) collective-permute-start(f32[4,1024]{1,0:T(4,128)S(1)} %merge.5.after.mine), channel_id=1, source_target_pairs={{0,16},{4,20},{8,24},{12,28},{16,0},{20,4},{24,8},{28,12},{1,17},{... | collective-permute-start | bytes 49160 | tf_op jit(solution)/shard_map/ppermute | solution.py:41
  18.5 2.2 %collective-permute-start.5 = (f32[4,1024]{1,0:T(4,128)S(1)}, f32[4,1024]{1,0:T(4,128)S(1)}, u32[]{:S(2)}, u32[]{:S(2)}) collective-permute-start(f32[4,1024]{1,0:T(4,128)S(1)} %merge.7.mine), channel_id=1, source_target_pairs={{0,16},{4,20},{8,24},{12,28},{16,0},{20,4},{24,8},{28,12},{1,17},{... | collective-permute-start | bytes 49160 | tf_op jit(solution)/shard_map/ppermute | solution.py:41
  20.7 2.9 %grads.2 = (bf16[512,256]{1,0:T(8,128)(2,1)S(1)}, bf16[2,512,1024]{2,1,0:T(8,128)(2,1)S(1)}, f32[2,2,64,256]{3,2,1,0:T(8,128)S(1)}, f32[2,2,64,256]{3,2,1,0:T(8,128)S(1)}) custom-call(f32[4,1024]{1,0:T(4,128)S(1)} %merge.5.after.mine, bf16[512,512]{1,0:T(8,128)(2,1)S(1)} %copy-done.3, bf16[512,128]{1,0:T(8,128)(2,1)S(1)} %copy-done.6, ...), custom_call_target="tpu_custom_call" | custom-call | flops 1073741824 | bytes 4194304 | tf_op jit(solution)/shard_map/grads/pallas_call | solution.py:327
  25.2 1.8 %collective-permute-start.11 = (f32[4,2,128,128]{3,2,1,0:T(8,128)S(1)}, f32[4,2,128,128]{3,2,1,0:T(8,128)S(1)}, u32[]{:S(2)}, u32[]{:S(2)}) collective-permute-start(f32[4,2,128,128]{3,2,1,0:T(8,128)S(1)} %get-tuple-element.40), channel_id=1, source_target_pairs={{0,8},{4,12},{8,0},{12,4},{16,24},{20,28},{24,16},{28,20},{1,9},{5... | collective-permute-start | bytes 1572872 | tf_op jit(solution)/shard_map/ppermute | solution.py:41
  27.0 2.9 %grads.3 = (bf16[512,256]{1,0:T(8,128)(2,1)S(1)}, bf16[2,512,1024]{2,1,0:T(8,128)(2,1)S(1)}, f32[2,2,64,256]{3,2,1,0:T(8,128)S(1)}, f32[2,2,64,256]{3,2,1,0:T(8,128)S(1)}) custom-call(bf16[512,256]{1,0:T(8,128)(2,1)S(1)} %get-tuple-element.27.after.refs_0_, bf16[512,512]{1,0:T(8,128)(2,1)S(1)} %copy-done.3, bf16[512,128]{1,0:T(8,128)(2,1)S(1)} %get-tuple-element.28.keys, ...), custom_call_target="tpu_custom_call" | custom-call | flops 1073741824 | bytes 4194304 | tf_op jit(solution)/shard_map/grads/pallas_call | solution.py:327
  29.9 1.5 %collective-permute-start.14 = (f32[2,2,64,256]{3,2,1,0:T(8,128)S(1)}, f32[2,2,64,256]{3,2,1,0:T(8,128)S(1)}, u32[]{:S(2)}, u32[]{:S(2)}) collective-permute-start(f32[2,2,64,256]{3,2,1,0:T(8,128)S(1)} %get-tuple-element.42), channel_id=1, source_target_pairs={{0,4},{4,0},{8,12},{12,8},{16,20},{20,16},{24,28},{28,24},{1,5},{5... | collective-permute-start | bytes 786440 | tf_op jit(solution)/shard_map/ppermute | solution.py:41
  33.4 1.6 %collective-permute-start.6 = (f32[2,512,128]{2,1,0:T(8,128)S(1)}, f32[2,512,128]{2,1,0:T(8,128)S(1)}, u32[]{:S(2)}, u32[]{:S(2)}) collective-permute-start(f32[2,512,128]{2,1,0:T(8,128)S(1)} %get-tuple-element.35), channel_id=1, source_target_pairs={{0,2},{1,3},{2,0},{3,1},{4,6},{5,7},{6,4},{7,5},{8,10},{9,11},{10,... | collective-permute-start | bytes 1572872 | tf_op jit(solution)/shard_map/ppermute | solution.py:41
  36.0 3.1 %collective-permute-done.14 = f32[2,2,64,256]{3,2,1,0:T(8,128)S(1)} collective-permute-done((f32[2,2,64,256]{3,2,1,0:T(8,128)S(1)}, f32[2,2,64,256]{3,2,1,0:T(8,128)S(1)}, u32[]{:S(2)}, u32[]{:S(2)}) %collective-permute-start.14) | collective-permute-done | bytes 262176 | tf_op jit(solution)/shard_map/ppermute | solution.py:41
  39.6 1.6 %collective-permute-done.9 = f32[1,2,64,256]{3,2,1,0:T(8,128)S(1)} collective-permute-done((f32[1,2,64,256]{3,2,1,0:T(8,128)S(1)}, f32[1,2,64,256]{3,2,1,0:T(8,128)S(1)}, u32[]{:S(2)}, u32[]{:S(2)}) %collective-permute-start.9) | collective-permute-done | bytes 131104 | tf_op jit(solution)/shard_map/ppermute | solution.py:41
  41.2 3.3 %collective-permute-start.10 = (f32[1,2,64,256]{3,2,1,0:T(8,128)S(1)}, f32[1,2,64,256]{3,2,1,0:T(8,128)S(1)}, u32[]{:S(2)}, u32[]{:S(2)}) collective-permute-start(f32[1,2,64,256]{3,2,1,0:T(8,128)S(1)} %fusion.1.mine), channel_id=1, source_target_pairs={{0,16},{4,20},{8,24},{12,28},{16,0},{20,4},{24,8},{28,12},{1,17},{... | collective-permute-start | bytes 393224 | tf_op jit(solution)/shard_map/ppermute | solution.py:41
  44.9 2.3 %collective-permute-start.16 = (f32[1,2,64,256]{3,2,1,0:T(8,128)S(1)}, f32[1,2,64,256]{3,2,1,0:T(8,128)S(1)}, u32[]{:S(2)}, u32[]{:S(2)}) collective-permute-start(f32[1,2,64,256]{3,2,1,0:T(8,128)S(1)} %fusion), channel_id=1, source_target_pairs={{0,16},{4,20},{8,24},{12,28},{16,0},{20,4},{24,8},{28,12},{1,17},{... | collective-permute-start | bytes 393224 | tf_op jit(solution)/shard_map/ppermute | solution.py:41
  49.0 1.5 %collective-permute-start.12 = (f32[1,2,64,256]{3,2,1,0:T(8,128)S(1)}, f32[1,2,64,256]{3,2,1,0:T(8,128)S(1)}, u32[]{:S(2)}, u32[]{:S(2)}) collective-permute-start(f32[1,2,64,256]{3,2,1,0:T(8,128)S(1)} %added.2), channel_id=1, source_target_pairs={{0,8},{4,12},{8,0},{12,4},{16,24},{20,28},{24,16},{28,20},{1,9},{5... | collective-permute-start | bytes 393224 | tf_op jit(solution)/shard_map/ppermute | solution.py:41
  52.7 2.7 %collective-permute-done.12 = f32[1,2,64,256]{3,2,1,0:T(8,128)S(1)} collective-permute-done((f32[1,2,64,256]{3,2,1,0:T(8,128)S(1)}, f32[1,2,64,256]{3,2,1,0:T(8,128)S(1)}, u32[]{:S(2)}, u32[]{:S(2)}) %collective-permute-start.12) | collective-permute-done | bytes 131104 | tf_op jit(solution)/shard_map/ppermute | solution.py:41
  55.4 1.5 %collective-permute-start.13 = (f32[2,2,64,256]{3,2,1,0:T(8,128)S(1)}, f32[2,2,64,256]{3,2,1,0:T(8,128)S(1)}, u32[]{:S(2)}, u32[]{:S(2)}) collective-permute-start(f32[2,2,64,256]{3,2,1,0:T(8,128)S(1)} %pad_maximum_fusion.refs_2_), channel_id=1, source_target_pairs={{0,4},{4,0},{8,12},{12,8},{16,20},{20,16},{24,28},{28,24},{1,5},{5... | collective-permute-start | bytes 786440 | tf_op jit(solution)/shard_map/ppermute | solution.py:41
  58.2 8.0 %collective-permute-done.17.theirs = f32[1,2,64,256]{3,2,1,0:T(8,128)S(1)} collective-permute-done((f32[1,2,64,256]{3,2,1,0:T(8,128)S(1)}, f32[1,2,64,256]{3,2,1,0:T(8,128)S(1)}, u32[]{:S(2)}, u32[]{:S(2)}) %collective-permute-start.17) | collective-permute-done | bytes 131104 | tf_op jit(solution)/shard_map/ppermute | solution.py:41
  66.3 1.8 %collective-permute-start.19 = (f32[2,2,64,256]{3,2,1,0:T(8,128)S(1)}, f32[2,2,64,256]{3,2,1,0:T(8,128)S(1)}, u32[]{:S(2)}, u32[]{:S(2)}) collective-permute-start(f32[2,2,64,256]{3,2,1,0:T(8,128)S(1)} %added.3.refs_4_), channel_id=1, source_target_pairs={{0,4},{4,0},{8,12},{12,8},{16,20},{20,16},{24,28},{28,24},{1,5},{5... | collective-permute-start | bytes 786440 | tf_op jit(solution)/shard_map/ppermute | solution.py:41
  68.2 7.8 %collective-permute-done.23.refs_9_ = f32[1,2,128,128]{3,2,1,0:T(8,128)S(1)} collective-permute-done((f32[1,2,128,128]{3,2,1,0:T(8,128)S(1)}, f32[1,2,128,128]{3,2,1,0:T(8,128)S(1)}, u32[]{:S(2)}, u32[]{:S(2)}) %collective-permute-start.23) | collective-permute-done | bytes 131104 | tf_op jit(solution)/shard_map/ppermute | solution.py:41
  76.0 1.3 %assemble.1 = (f32[2,128,256]{2,1,0:T(8,128)}, f32[512,256]{1,0:T(8,128)}, f32[512,256]{1,0:T(8,128)}, f32[512,128]{1,0:T(8,128)}) custom-call(f32[1,512,128]{2,1,0:T(8,128)S(1)} %get-tuple-element.49.refs_0_, f32[1,512,128]{2,1,0:T(8,128)S(1)} %collective-permute-done.7.refs_1_, f32[2,2,64,256]{3,2,1,0:T(8,128)S(1)} %pad_maximum_fusion.refs_2_, ...), custom_call_target="tpu_custom_call" | custom-call | tf_op jit(solution)/shard_map/assemble/pallas_call | solution.py:462
  (65 shorter events, 11.2 us)
Async XLA Ops:
  5.1 5.3 %collective-permute-start = (f32[4,1024]{1,0:T(4,128)}, f32[4,1024]{1,0:T(4,128)S(1)}, u32[]{:S(2)}, u32[]{:S(2)}) collective-permute-start(f32[4,1024]{1,0:T(4,128)} %get-tuple-element.24.mine), channel_id=1, source_target_pairs={{0,4},{4,0},{8,12},{12,8},{16,20},{20,16},{24,28},{28,24},{1,5},{5... | collective-permute-start | bytes 49160 | tf_op jit(solution)/shard_map/ppermute | solution.py:41
  10.3 3.8 %collective-permute-start.3 = (f32[4,1024]{1,0:T(4,128)S(1)}, f32[4,1024]{1,0:T(4,128)S(1)}, u32[]{:S(2)}, u32[]{:S(2)}) collective-permute-start(f32[4,1024]{1,0:T(4,128)S(1)} %get-tuple-element.30.mine), channel_id=1, source_target_pairs={{0,4},{4,0},{8,12},{12,8},{16,20},{20,16},{24,28},{28,24},{1,5},{5... | collective-permute-start | bytes 49160 | tf_op jit(solution)/shard_map/ppermute | solution.py:41
  10.4 5.3 %collective-permute-start.1 = (f32[4,1024]{1,0:T(4,128)S(1)}, f32[4,1024]{1,0:T(4,128)S(1)}, u32[]{:S(2)}, u32[]{:S(2)}) collective-permute-start(f32[4,1024]{1,0:T(4,128)S(1)} %merge.4.mine), channel_id=1, source_target_pairs={{0,8},{4,12},{8,0},{12,4},{16,24},{20,28},{24,16},{28,20},{1,9},{5... | collective-permute-start | bytes 49160 | tf_op jit(solution)/shard_map/ppermute | solution.py:41
  14.1 4.3 %collective-permute-start.4 = (f32[4,1024]{1,0:T(4,128)S(1)}, f32[4,1024]{1,0:T(4,128)S(1)}, u32[]{:S(2)}, u32[]{:S(2)}) collective-permute-start(f32[4,1024]{1,0:T(4,128)S(1)} %merge.6.mine), channel_id=1, source_target_pairs={{0,8},{4,12},{8,0},{12,4},{16,24},{20,28},{24,16},{28,20},{1,9},{5... | collective-permute-start | bytes 49160 | tf_op jit(solution)/shard_map/ppermute | solution.py:41
  15.8 4.9 %collective-permute-start.2 = (f32[4,1024]{1,0:T(4,128)S(1)}, f32[4,1024]{1,0:T(4,128)S(1)}, u32[]{:S(2)}, u32[]{:S(2)}) collective-permute-start(f32[4,1024]{1,0:T(4,128)S(1)} %merge.5.after.mine), channel_id=1, source_target_pairs={{0,16},{4,20},{8,24},{12,28},{16,0},{20,4},{24,8},{28,12},{1,17},{... | collective-permute-start | bytes 49160 | tf_op jit(solution)/shard_map/ppermute | solution.py:41
  18.5 8.5 %collective-permute-start.5 = (f32[4,1024]{1,0:T(4,128)S(1)}, f32[4,1024]{1,0:T(4,128)S(1)}, u32[]{:S(2)}, u32[]{:S(2)}) collective-permute-start(f32[4,1024]{1,0:T(4,128)S(1)} %merge.7.mine), channel_id=1, source_target_pairs={{0,16},{4,20},{8,24},{12,28},{16,0},{20,4},{24,8},{28,12},{1,17},{... | collective-permute-start | bytes 49160 | tf_op jit(solution)/shard_map/ppermute | solution.py:41
  23.6 12.0 %collective-permute-start.8 = (f32[2,2,64,256]{3,2,1,0:T(8,128)S(1)}, f32[2,2,64,256]{3,2,1,0:T(8,128)S(1)}, u32[]{:S(2)}, u32[]{:S(2)}) collective-permute-start(f32[2,2,64,256]{3,2,1,0:T(8,128)S(1)} %get-tuple-element.37), channel_id=1, source_target_pairs={{0,4},{4,0},{8,12},{12,8},{16,20},{20,16},{24,28},{28,24},{1,5},{5... | collective-permute-start | bytes 786440 | tf_op jit(solution)/shard_map/ppermute | solution.py:41
  25.2 22.0 %collective-permute-start.11 = (f32[4,2,128,128]{3,2,1,0:T(8,128)S(1)}, f32[4,2,128,128]{3,2,1,0:T(8,128)S(1)}, u32[]{:S(2)}, u32[]{:S(2)}) collective-permute-start(f32[4,2,128,128]{3,2,1,0:T(8,128)S(1)} %get-tuple-element.40), channel_id=1, source_target_pairs={{0,8},{4,12},{8,0},{12,4},{16,24},{20,28},{24,16},{28,20},{1,9},{5... | collective-permute-start | bytes 1572872 | tf_op jit(solution)/shard_map/ppermute | solution.py:41
  29.9 9.2 %collective-permute-start.14 = (f32[2,2,64,256]{3,2,1,0:T(8,128)S(1)}, f32[2,2,64,256]{3,2,1,0:T(8,128)S(1)}, u32[]{:S(2)}, u32[]{:S(2)}) collective-permute-start(f32[2,2,64,256]{3,2,1,0:T(8,128)S(1)} %get-tuple-element.42), channel_id=1, source_target_pairs={{0,4},{4,0},{8,12},{12,8},{16,20},{20,16},{24,28},{28,24},{1,5},{5... | collective-permute-start | bytes 786440 | tf_op jit(solution)/shard_map/ppermute | solution.py:41
  33.4 15.1 %collective-permute-start.6 = (f32[2,512,128]{2,1,0:T(8,128)S(1)}, f32[2,512,128]{2,1,0:T(8,128)S(1)}, u32[]{:S(2)}, u32[]{:S(2)}) collective-permute-start(f32[2,512,128]{2,1,0:T(8,128)S(1)} %get-tuple-element.35), channel_id=1, source_target_pairs={{0,2},{1,3},{2,0},{3,1},{4,6},{5,7},{6,4},{7,5},{8,10},{9,11},{10,... | collective-permute-start | bytes 1572872 | tf_op jit(solution)/shard_map/ppermute | solution.py:41
  35.0 15.5 %collective-permute-start.21 = (f32[4,2,128,128]{3,2,1,0:T(8,128)S(1)}, f32[4,2,128,128]{3,2,1,0:T(8,128)S(1)}, u32[]{:S(2)}, u32[]{:S(2)}) collective-permute-start(f32[4,2,128,128]{3,2,1,0:T(8,128)S(1)} %get-tuple-element.43), channel_id=1, source_target_pairs={{0,4},{4,0},{8,12},{12,8},{16,20},{20,16},{24,28},{28,24},{1,5},{5... | collective-permute-start | bytes 1572872 | tf_op jit(solution)/shard_map/ppermute | solution.py:41
  35.7 5.5 %collective-permute-start.9 = (f32[1,2,64,256]{3,2,1,0:T(8,128)S(1)}, f32[1,2,64,256]{3,2,1,0:T(8,128)S(1)}, u32[]{:S(2)}, u32[]{:S(2)}) collective-permute-start(f32[1,2,64,256]{3,2,1,0:T(8,128)S(1)} %slice_add_fusion.12), channel_id=1, source_target_pairs={{0,8},{4,12},{8,0},{12,4},{16,24},{20,28},{24,16},{28,20},{1,9},{5... | collective-permute-start | bytes 393224 | tf_op jit(solution)/shard_map/ppermute | solution.py:41
  39.2 5.7 %collective-permute-start.15 = (f32[1,2,64,256]{3,2,1,0:T(8,128)S(1)}, f32[1,2,64,256]{3,2,1,0:T(8,128)S(1)}, u32[]{:S(2)}, u32[]{:S(2)}) collective-permute-start(f32[1,2,64,256]{3,2,1,0:T(8,128)S(1)} %slice_add_fusion.10), channel_id=1, source_target_pairs={{0,8},{4,12},{8,0},{12,4},{16,24},{20,28},{24,16},{28,20},{1,9},{5... | collective-permute-start | bytes 393224 | tf_op jit(solution)/shard_map/ppermute | solution.py:41
  41.2 7.8 %collective-permute-start.10 = (f32[1,2,64,256]{3,2,1,0:T(8,128)S(1)}, f32[1,2,64,256]{3,2,1,0:T(8,128)S(1)}, u32[]{:S(2)}, u32[]{:S(2)}) collective-permute-start(f32[1,2,64,256]{3,2,1,0:T(8,128)S(1)} %fusion.1.mine), channel_id=1, source_target_pairs={{0,16},{4,20},{8,24},{12,28},{16,0},{20,4},{24,8},{28,12},{1,17},{... | collective-permute-start | bytes 393224 | tf_op jit(solution)/shard_map/ppermute | solution.py:41
  44.9 7.4 %collective-permute-start.16 = (f32[1,2,64,256]{3,2,1,0:T(8,128)S(1)}, f32[1,2,64,256]{3,2,1,0:T(8,128)S(1)}, u32[]{:S(2)}, u32[]{:S(2)}) collective-permute-start(f32[1,2,64,256]{3,2,1,0:T(8,128)S(1)} %fusion), channel_id=1, source_target_pairs={{0,16},{4,20},{8,24},{12,28},{16,0},{20,4},{24,8},{28,12},{1,17},{... | collective-permute-start | bytes 393224 | tf_op jit(solution)/shard_map/ppermute | solution.py:41
  47.3 9.6 %collective-permute-start.18 = (f32[2,2,128,128]{3,2,1,0:T(8,128)S(1)}, f32[2,2,128,128]{3,2,1,0:T(8,128)S(1)}, u32[]{:S(2)}, u32[]{:S(2)}) collective-permute-start(f32[2,2,128,128]{3,2,1,0:T(8,128)S(1)} %get-tuple-element.47.after), channel_id=1, source_target_pairs={{0,4},{4,0},{8,12},{12,8},{16,20},{20,16},{24,28},{28,24},{1,5},{5... | collective-permute-start | bytes 786440 | tf_op jit(solution)/shard_map/ppermute | solution.py:41
  48.5 19.6 %collective-permute-start.7 = (f32[1,512,128]{2,1,0:T(8,128)S(1)}, f32[1,512,128]{2,1,0:T(8,128)S(1)}, u32[]{:S(2)}, u32[]{:S(2)}) collective-permute-start(f32[1,512,128]{2,1,0:T(8,128)S(1)} %get-tuple-element.48), channel_id=1, source_target_pairs={{0,1},{1,0},{2,3},{3,2},{4,5},{5,4},{6,7},{7,6},{8,9},{9,8},{10,11... | collective-permute-start | bytes 786440 | tf_op jit(solution)/shard_map/ppermute | solution.py:41
  49.0 6.4 %collective-permute-start.12 = (f32[1,2,64,256]{3,2,1,0:T(8,128)S(1)}, f32[1,2,64,256]{3,2,1,0:T(8,128)S(1)}, u32[]{:S(2)}, u32[]{:S(2)}) collective-permute-start(f32[1,2,64,256]{3,2,1,0:T(8,128)S(1)} %added.2), channel_id=1, source_target_pairs={{0,8},{4,12},{8,0},{12,4},{16,24},{20,28},{24,16},{28,20},{1,9},{5... | collective-permute-start | bytes 393224 | tf_op jit(solution)/shard_map/ppermute | solution.py:41
  50.5 17.5 %collective-permute-start.22 = (f32[2,2,128,128]{3,2,1,0:T(8,128)S(1)}, f32[2,2,128,128]{3,2,1,0:T(8,128)S(1)}, u32[]{:S(2)}, u32[]{:S(2)}) collective-permute-start(f32[2,2,128,128]{3,2,1,0:T(8,128)S(1)} %get-tuple-element.45), channel_id=1, source_target_pairs={{0,8},{4,12},{8,0},{12,4},{16,24},{20,28},{24,16},{28,20},{1,9},{5... | collective-permute-start | bytes 786440 | tf_op jit(solution)/shard_map/ppermute | solution.py:41
  52.3 14.0 %collective-permute-start.17 = (f32[1,2,64,256]{3,2,1,0:T(8,128)S(1)}, f32[1,2,64,256]{3,2,1,0:T(8,128)S(1)}, u32[]{:S(2)}, u32[]{:S(2)}) collective-permute-start(f32[1,2,64,256]{3,2,1,0:T(8,128)S(1)} %add.60.mine), channel_id=1, source_target_pairs={{0,8},{4,12},{8,0},{12,4},{16,24},{20,28},{24,16},{28,20},{1,9},{5... | collective-permute-start | bytes 393224 | tf_op jit(solution)/shard_map/ppermute | solution.py:41
  55.4 20.5 %collective-permute-start.13 = (f32[2,2,64,256]{3,2,1,0:T(8,128)S(1)}, f32[2,2,64,256]{3,2,1,0:T(8,128)S(1)}, u32[]{:S(2)}, u32[]{:S(2)}) collective-permute-start(f32[2,2,64,256]{3,2,1,0:T(8,128)S(1)} %pad_maximum_fusion.refs_2_), channel_id=1, source_target_pairs={{0,4},{4,0},{8,12},{12,8},{16,20},{20,16},{24,28},{28,24},{1,5},{5... | collective-permute-start | bytes 786440 | tf_op jit(solution)/shard_map/ppermute | solution.py:41
  57.0 11.2 %collective-permute-start.20 = (f32[1,2,128,128]{3,2,1,0:T(8,128)S(1)}, f32[1,2,128,128]{3,2,1,0:T(8,128)S(1)}, u32[]{:S(2)}, u32[]{:S(2)}) collective-permute-start(f32[1,2,128,128]{3,2,1,0:T(8,128)S(1)} %get-tuple-element.53.after), channel_id=1, source_target_pairs={{0,16},{4,20},{8,24},{12,28},{16,0},{20,4},{24,8},{28,12},{1,17},{... | collective-permute-start | bytes 393224 | tf_op jit(solution)/shard_map/ppermute | solution.py:41
  66.3 9.7 %collective-permute-start.19 = (f32[2,2,64,256]{3,2,1,0:T(8,128)S(1)}, f32[2,2,64,256]{3,2,1,0:T(8,128)S(1)}, u32[]{:S(2)}, u32[]{:S(2)}) collective-permute-start(f32[2,2,64,256]{3,2,1,0:T(8,128)S(1)} %added.3.refs_4_), channel_id=1, source_target_pairs={{0,4},{4,0},{8,12},{12,8},{16,20},{20,16},{24,28},{28,24},{1,5},{5... | collective-permute-start | bytes 786440 | tf_op jit(solution)/shard_map/ppermute | solution.py:41
  68.1 7.9 %collective-permute-start.23 = (f32[1,2,128,128]{3,2,1,0:T(8,128)S(1)}, f32[1,2,128,128]{3,2,1,0:T(8,128)S(1)}, u32[]{:S(2)}, u32[]{:S(2)}) collective-permute-start(f32[1,2,128,128]{3,2,1,0:T(8,128)S(1)} %get-tuple-element.50), channel_id=1, source_target_pairs={{0,16},{4,20},{8,24},{12,28},{16,0},{20,4},{24,8},{28,12},{1,17},{... | collective-permute-start | bytes 393224 | tf_op jit(solution)/shard_map/ppermute | solution.py:41
  (8 other events, 74.0 us)

commit v9 on v7

--- a/solution.py
+++ b/solution.py
@@ -39,6 +39,21 @@
 def swap(array, axis, count, bit):
     pairs = [(device, device ^ bit) for device in range(count)]
     return lax.ppermute(array, axis, pairs)
+
+
+def counted(group):
+    return group ^ ((group // 4) % 2 * 2)
+
+
+def row_swap_of(array, count, bit):
+    low = count // GROUPS
+    if bit < low:
+        return swap(array, "rows", count, bit)
+    pairs = []
+    for device in range(count):
+        partner = counted(counted(device // low) ^ (bit // low))
+        pairs.append((device, partner * low + device % low))
+    return lax.ppermute(array, "rows", pairs)
 
 
 def bits_of(count):
@@ -108,18 +123,14 @@
     result[:reads], result[reads:] = merged(mine, theirs)
 
 
-def group_at(bits, relative, me):
-    low = me % GROUPS
-    group = 0
-    for bit, flip in zip(bits, relative):
-        group = group + ((low // bit) % 2 ^ flip) * bit
-    return group
+def group_at(bits, relative, high, me):
+    flips = sum(bit * flip for bit, flip in zip(bits, relative))
+    return counted((counted(me) % LAST_BIT ^ flips) + LAST_BIT * high)
 
 
 LAST_BIT = 4
 WEIGHT_PARTS = (((0, 256, (1, 2)),), ((0, 256, (1, 2)),))
 QUERY_PARTS = (((0, 2, (2, 1, 4)),), ((0, 2, (1, 2, 4)),))
-DIRECT = ()
 
 
 def grads_kernel(
@@ -161,9 +172,9 @@
         for first in range(2):
             ref = weight_parts[2 * part + first]
             for second in range(2):
-                base = group_at(bits, (first, second), me)
                 for high in range(2):
-                    start = pl.multiple_of((base + LAST_BIT * high) * piece, piece)
+                    group = group_at(bits, (first, second), high, me)
+                    start = pl.multiple_of(group * piece, piece)
                     ref[second, high] = weights_ref[pl.ds(start, piece), begin:end]
 
 
@@ -191,7 +202,7 @@
     side = lax.rem(me, 2)
     for part, (begin, end, bits) in enumerate(parts):
         for upper in range(GROUPS // 2):
-            pair = (me // 2) ^ upper
+            pair = counted(counted(me) ^ (2 * upper)) // 2
             at = pl.ds(pl.multiple_of(pair * 2 * piece, 2 * piece), 2 * piece)
             for read_index in range(begin, end):
                 slot = upper * reads + read_index
@@ -204,10 +215,11 @@
                     ref[index, read_index - begin] = tile_ref[slot, half, :]
 
 
-def assemble_kernel(weight_parts, query_parts, row_axis, low, *refs):
-    query_out, key_out, value_out, input_out = refs[-4:]
+def weights_kernel(weight_parts, row_axis, low, *refs):
+    key_out, value_out, input_out, done = refs[-4:]
     refs = list(refs[:-4])
     input_out[...] = refs.pop(0)[0] + refs.pop(0)[0]
+    done[...] = jnp.zeros_like(done)
     piece = key_out.shape[0] // GROUPS
     me = lax.axis_index(row_axis) // low
     for head_index, begin, end, bits in weight_parts:
@@ -215,14 +227,20 @@
         for first in range(2):
             source = refs.pop(0)
             for second in range(2):
-                base = group_at(bits, (first, second), me)
                 for high in range(2):
-                    start = pl.multiple_of((base + LAST_BIT * high) * piece, piece)
+                    group = group_at(bits, (first, second), high, me)
+                    start = pl.multiple_of(group * piece, piece)
                     at = pl.ds(start, piece)
                     if begin == 0:
                         key_out[at, cols] = source[second, high, :, :HD]
                     if end == 2 * HD:
                         value_out[at, cols] = source[second, high, :, end - begin - HD :]
+
+
+def queries_kernel(query_parts, after, *refs):
+    del after
+    query_out = refs[-1]
+    refs = list(refs[:-1])
     for head_index, begin, end, terms in query_parts:
         cols = slice(head_index * HD, (head_index + 1) * HD)
         total = refs.pop(0)[0]
@@ -237,7 +255,7 @@
 
 def scatter_steps(keep, send, count, bits):
     for index, bit in enumerate(bits):
-        theirs = swap(send, "rows", count, bit)
+        theirs = row_swap_of(send, count, bit)
         if index + 1 == len(bits):
             return keep, theirs
         middle = keep.shape[0] // 2
@@ -289,7 +307,7 @@
     for head_index in range(head_count):
         stats = projected[head_index][2]
         for bit in bits_of(row_devices)[:-1]:
-            theirs = swap(stats, "rows", row_devices, bit)
+            theirs = row_swap_of(stats, row_devices, bit)
             stats = pl.pallas_call(
                 merge_kernel,
                 out_shape=shape_of(stats.shape),
@@ -298,7 +316,7 @@
                 compiler_params=params(2),
                 name="merge",
             )(stats, theirs)
-        stats_parts.append((stats, swap(stats, "rows", row_devices, bits_of(row_devices)[-1])))
+        stats_parts.append((stats, row_swap_of(stats, row_devices, bits_of(row_devices)[-1])))
 
     order_low = (lax.axis_index("rows") % low) ^ jnp.arange(low, dtype=jnp.int32)
     low_bits = [bit for bit in bits_of(row_devices) if bit < low]
@@ -320,7 +338,7 @@
             block = block + row_swap(block, bit=bit)
         return block
 
-    row_swap = functools.partial(swap, axis="rows", count=row_devices)
+    row_swap = functools.partial(row_swap_of, count=row_devices)
 
     def kernel_call(kernel, shapes, operands, scratch, limit, name):
         return pl.pallas_call(
@@ -375,34 +393,25 @@
             )
         )
 
-    assembled, weight_list, marks = [], [], []
+    weight_terms, weight_list = [], []
     for head_index in range(head_count):
         for part, (begin, end, bits) in enumerate(WEIGHT_PARTS[head_index]):
             keep, send = grads_out[head_index][2 + 2 * part : 4 + 2 * part]
             first, second = (bit * low for bit in bits)
             mine, theirs = scatter_steps(keep, send, row_devices, (first, second))
-            marks.append(mine)
             mine = mine + theirs
             mine = sum_low(mine + row_swap(mine, bit=LAST_BIT * low))
             near = jnp.concatenate([mine, row_swap(mine, bit=second)], axis=0)
-            assembled += [near, row_swap(near, bit=first)]
+            weight_terms += [near, row_swap(near, bit=first)]
             weight_list.append((head_index, begin, end, bits))
-    query_list = []
+    query_terms, query_list = [], []
     for head_index in range(head_count):
         for part, (begin, end, bits) in enumerate(QUERY_PARTS[head_index]):
             keep, send = query_out[head_index][2 * part : 2 * part + 2]
-            if (head_index, part) in DIRECT:
-                theirs = row_swap(send, bit=bits[0] * low)
-                terms = [keep[:1] + theirs[:1]]
-                for index in range(1, keep.shape[0]):
-                    bit = (index // 2) * bits[1] + (index % 2) * bits[2]
-                    block = keep[index : index + 1] + theirs[index : index + 1]
-                    terms.append(row_swap(block, bit=bit * low))
-            else:
-                terms = scatter_steps(keep, send, row_devices, [bit * low for bit in bits])
+            terms = scatter_steps(keep, send, row_devices, [bit * low for bit in bits])
             if low > 1:
                 terms = [scatter_low(sum(terms)[0], 1)[None]]
-            assembled += terms
+            query_terms += terms
             query_list.append((head_index, begin, end, len(terms)))
 
     share = ((head_devices // 2, row_count, features // head_devices),)
@@ -424,16 +433,23 @@
         keep, theirs = keep[:bit] + theirs[:bit], swap(send, "heads", head_devices, bit)
     input_terms = (keep, theirs)
 
-    query_grad, key_weight_grad, value_weight_grad, input_grad = pl.pallas_call(
-        functools.partial(assemble_kernel, weight_list, query_list, "rows", low),
-        out_shape=(shape_of((reads, latents // row_devices, columns)),)
-        + (shape_of((features, columns)),) * 2
-        + (shape_of((row_count, features // head_devices)),),
-        in_specs=[VMEM] * (2 + len(assembled)),
+    key_weight_grad, value_weight_grad, input_grad, done = pl.pallas_call(
+        functools.partial(weights_kernel, weight_list, "rows", low),
+        out_shape=(shape_of((features, columns)),) * 2
+        + (shape_of((row_count, features // head_devices)), shape_of((8, 128))),
+        in_specs=[VMEM] * (2 + len(weight_terms)),
         out_specs=(VMEM,) * 4,
         compiler_params=params(8),
-        name="assemble",
-    )(*input_terms, *assembled)
+        name="weights",
+    )(*input_terms, *weight_terms)
+    query_grad = pl.pallas_call(
+        functools.partial(queries_kernel, query_list),
+        out_shape=shape_of((reads, latents // row_devices, columns)),
+        in_specs=[ANY] + [VMEM] * len(query_terms),
+        out_specs=VMEM,
+        compiler_params=params(4),
+        name="queries",
+    )(done, *query_terms)
     return (query_grad, key_weight_grad, value_weight_grad, input_grad)
 
 

time: 75.3 us -> 72.9 us (0.968)
  waiting for transfers between devices: 22.4 us -> 17.6 us
  starting transfers between devices: 34.7 us -> 36.4 us
    ppermute x0 -> x22, starting transfers between devices: none -> 34.7 us  [row_swap_of(): return lax.ppermute(array, 'rows', pairs)]
    ppermute x24 -> x2, starting transfers between devices: 34.7 us -> 1.69 us  [swap(): return lax.ppermute(array, axis, pairs)]
    ppermute x24 -> x2, waiting for transfers between devices: 22.4 us -> 0.01 us  [swap(): return lax.ppermute(array, axis, pairs)]
    ppermute x0 -> x22, waiting for transfers between devices: none -> 17.6 us  [row_swap_of(): return lax.ppermute(array, 'rows', pairs)]
    pallas_call x1 -> x2, Pallas kernels: 1.29 us -> 1.93 us  [the longest x1 1.2 us: on_device(): pl.pallas_call(functools.partial(weights_kernel, weight_list, 'rows', low...]
  transfers between devices with their start and end apart: 24 -> 24, of which waited for: 11 -> 11; matrix products, arithmetic and copies ran while one was open for 1% -> 1% of each run, Pallas kernels for 15% -> 17%
where the time goes in v9:
time: 72.9 us; the launch traced here: 72.7 us
  starting transfers between devices  36.4 us (50%)
  waiting for transfers between devices  17.6 us (24%)
  Pallas kernels  17.4 us (24%)
  between operations  0.9 us (1%)
    ppermute x22, starting transfers between devices, row_swap_of(): return lax.ppermute(array, 'rows', pairs)  34.7 us
    ppermute x22, waiting for transfers between devices, row_swap_of(): return lax.ppermute(array, 'rows', pairs)  17.6 us
    pallas_call x4, Pallas kernels, kernel_call(): pl.pallas_call(kernel, out_shape=[shape_of(*item) for item in shapes], in...  8.05 us
    pallas_call x2, Pallas kernels, on_device(): pl.pallas_call(functools.partial(first_kernel, tile) if first else functo...  6.55 us
    ppermute x2, starting transfers between devices, swap(): return lax.ppermute(array, axis, pairs)  1.69 us
  transfers between devices with their start and end apart: 24, of which 11 were waited for; matrix products, arithmetic and copies ran while one was open for 1% of the time, Pallas kernels for 17%

profile of v9, /device:TPU:0, one launch (start us, length us, event | category | flops | bytes accessed | tf_op | source)
XLA Modules:
  0.0 72.7 jit_solution(4782165041169689204)
XLA Ops:
  0.7 4.4 %project.2 = (bf16[512,128]{1,0:T(8,128)(2,1)}, bf16[512,128]{1,0:T(8,128)(2,1)}, f32[4,1024]{1,0:T(4,128)}) custom-call(bf16[512,512]{1,0:T(8,128)(2,1)} %inputs.3, bf16[512,256]{1,0:T(8,128)(2,1)} %key_weight.1, bf16[512,256]{1,0:T(8,128)(2,1)} %value_weight.1, bf16[2,1024,256]{2,1,0:T(8,128)(2,1)} %queries.4, bf16[2,1024,256]{2,1,0:T(8,128)(2,1)} %out_grad.3), custom_call_target="tpu_custom_call" | custom-call | flops 1073741824 | bytes 4194304 | tf_op jit(solution)/shard_map/project/pallas_call | solution.py:288
  5.1 3.0 %collective-permute-start = (f32[4,1024]{1,0:T(4,128)}, f32[4,1024]{1,0:T(4,128)S(1)}, u32[]{:S(2)}, u32[]{:S(2)}) collective-permute-start(f32[4,1024]{1,0:T(4,128)} %get-tuple-element.28.mine), channel_id=1, source_target_pairs={{0,4},{4,0},{8,12},{12,8},{16,20},{20,16},{24,28},{28,24},{1,5},{5... | collective-permute-start | bytes 49160 | tf_op jit(solution)/shard_map/ppermute | solution.py:56
  8.2 2.1 %project.3 = (bf16[512,128]{1,0:T(8,128)(2,1)S(1)}, bf16[512,128]{1,0:T(8,128)(2,1)S(1)}, f32[4,1024]{1,0:T(4,128)S(1)}) custom-call(bf16[512,512]{1,0:T(8,128)(2,1)S(1)} %copy-done.3, bf16[512,256]{1,0:T(8,128)(2,1)S(1)} %copy-done.4, bf16[512,256]{1,0:T(8,128)(2,1)S(1)} %copy-done.5, bf16[2,1024,256]{2,1,0:T(8,128)(2,1)S(1)} %copy-done.1, ...), custom_call_target="tpu_custom_call" | custom-call | flops 1073741824 | bytes 4194304 | tf_op jit(solution)/shard_map/project/pallas_call | solution.py:288
  10.4 2.1 %collective-permute-start.1 = (f32[4,1024]{1,0:T(4,128)S(1)}, f32[4,1024]{1,0:T(4,128)S(1)}, u32[]{:S(2)}, u32[]{:S(2)}) collective-permute-start(f32[4,1024]{1,0:T(4,128)S(1)} %merge.4.mine), channel_id=1, source_target_pairs={{0,8},{4,12},{8,0},{12,4},{16,24},{20,28},{24,16},{28,20},{1,9},{5... | collective-permute-start | bytes 49160 | tf_op jit(solution)/shard_map/ppermute | solution.py:56
  12.6 1.5 %collective-permute-done.3.theirs = f32[4,1024]{1,0:T(4,128)S(1)} collective-permute-done((f32[4,1024]{1,0:T(4,128)S(1)}, f32[4,1024]{1,0:T(4,128)S(1)}, u32[]{:S(2)}, u32[]{:S(2)}) %collective-permute-start.3) | collective-permute-done | bytes 16416 | tf_op jit(solution)/shard_map/ppermute | solution.py:56
  14.1 1.6 %collective-permute-start.4 = (f32[4,1024]{1,0:T(4,128)S(1)}, f32[4,1024]{1,0:T(4,128)S(1)}, u32[]{:S(2)}, u32[]{:S(2)}) collective-permute-start(f32[4,1024]{1,0:T(4,128)S(1)} %merge.6.mine), channel_id=1, source_target_pairs={{0,8},{4,12},{8,0},{12,4},{16,24},{20,28},{24,16},{28,20},{1,9},{5... | collective-permute-start | bytes 49160 | tf_op jit(solution)/shard_map/ppermute | solution.py:56
  15.8 2.6 %collective-permute-start.2 = (f32[4,1024]{1,0:T(4,128)S(1)}, f32[4,1024]{1,0:T(4,128)S(1)}, u32[]{:S(2)}, u32[]{:S(2)}) collective-permute-start(f32[4,1024]{1,0:T(4,128)S(1)} %merge.5.after.mine), channel_id=1, source_target_pairs={{0,24},{4,28},{8,16},{12,20},{16,8},{20,12},{24,0},{28,4},{1,25},{... | collective-permute-start | bytes 49160 | tf_op jit(solution)/shard_map/ppermute | solution.py:56
  18.5 3.2 %collective-permute-start.5 = (f32[4,1024]{1,0:T(4,128)S(1)}, f32[4,1024]{1,0:T(4,128)S(1)}, u32[]{:S(2)}, u32[]{:S(2)}) collective-permute-start(f32[4,1024]{1,0:T(4,128)S(1)} %merge.7.mine), channel_id=1, source_target_pairs={{0,24},{4,28},{8,16},{12,20},{16,8},{20,12},{24,0},{28,4},{1,25},{... | collective-permute-start | bytes 49160 | tf_op jit(solution)/shard_map/ppermute | solution.py:56
  21.6 2.9 %grads.2 = (bf16[512,256]{1,0:T(8,128)(2,1)S(1)}, bf16[2,512,1024]{2,1,0:T(8,128)(2,1)S(1)}, f32[2,2,64,256]{3,2,1,0:T(8,128)S(1)}, f32[2,2,64,256]{3,2,1,0:T(8,128)S(1)}) custom-call(f32[4,1024]{1,0:T(4,128)S(1)} %merge.5.after.mine, bf16[512,512]{1,0:T(8,128)(2,1)S(1)} %copy-done.3, bf16[512,128]{1,0:T(8,128)(2,1)S(1)} %copy-done.6, ...), custom_call_target="tpu_custom_call" | custom-call | flops 1073741824 | bytes 4194304 | tf_op jit(solution)/shard_map/grads/pallas_call | solution.py:344
  26.4 2.9 %grads.3 = (bf16[512,256]{1,0:T(8,128)(2,1)S(1)}, bf16[2,512,1024]{2,1,0:T(8,128)(2,1)S(1)}, f32[2,2,64,256]{3,2,1,0:T(8,128)S(1)}, f32[2,2,64,256]{3,2,1,0:T(8,128)S(1)}) custom-call(bf16[512,256]{1,0:T(8,128)(2,1)S(1)} %get-tuple-element.31.after.refs_0_, bf16[512,512]{1,0:T(8,128)(2,1)S(1)} %copy-done.3, bf16[512,128]{1,0:T(8,128)(2,1)S(1)} %get-tuple-element.32.keys, ...), custom_call_target="tpu_custom_call" | custom-call | flops 1073741824 | bytes 4194304 | tf_op jit(solution)/shard_map/grads/pallas_call | solution.py:344
  29.3 1.6 %collective-permute-start.13 = (f32[2,2,64,256]{3,2,1,0:T(8,128)S(1)}, f32[2,2,64,256]{3,2,1,0:T(8,128)S(1)}, u32[]{:S(2)}, u32[]{:S(2)}) collective-permute-start(f32[2,2,64,256]{3,2,1,0:T(8,128)S(1)} %get-tuple-element.43), channel_id=1, source_target_pairs={{0,4},{4,0},{8,12},{12,8},{16,20},{20,16},{24,28},{28,24},{1,5},{5... | collective-permute-start | bytes 786440 | tf_op jit(solution)/shard_map/ppermute | solution.py:56
  32.8 1.6 %collective-permute-start.6 = (f32[2,512,128]{2,1,0:T(8,128)S(1)}, f32[2,512,128]{2,1,0:T(8,128)S(1)}, u32[]{:S(2)}, u32[]{:S(2)}) collective-permute-start(f32[2,512,128]{2,1,0:T(8,128)S(1)} %get-tuple-element.39), channel_id=1, source_target_pairs={{0,2},{1,3},{2,0},{3,1},{4,6},{5,7},{6,4},{7,5},{8,10},{9,11},{10,... | collective-permute-start | bytes 1572872 | tf_op jit(solution)/shard_map/ppermute | solution.py:41
  35.0 2.1 %collective-permute-start.9 = (f32[1,2,64,256]{3,2,1,0:T(8,128)S(1)}, f32[1,2,64,256]{3,2,1,0:T(8,128)S(1)}, u32[]{:S(2)}, u32[]{:S(2)}) collective-permute-start(f32[1,2,64,256]{3,2,1,0:T(8,128)S(1)} %slice_add_fusion.12), channel_id=1, source_target_pairs={{0,8},{4,12},{8,0},{12,4},{16,24},{20,28},{24,16},{28,20},{1,9},{5... | collective-permute-start | bytes 393224 | tf_op jit(solution)/shard_map/ppermute | solution.py:56
  37.1 1.9 %collective-permute-done.13 = f32[2,2,64,256]{3,2,1,0:T(8,128)S(1)} collective-permute-done((f32[2,2,64,256]{3,2,1,0:T(8,128)S(1)}, f32[2,2,64,256]{3,2,1,0:T(8,128)S(1)}, u32[]{:S(2)}, u32[]{:S(2)}) %collective-permute-start.13) | collective-permute-done | bytes 262176 | tf_op jit(solution)/shard_map/ppermute | solution.py:56
  39.0 1.6 %collective-permute-start.14 = (f32[1,2,64,256]{3,2,1,0:T(8,128)S(1)}, f32[1,2,64,256]{3,2,1,0:T(8,128)S(1)}, u32[]{:S(2)}, u32[]{:S(2)}) collective-permute-start(f32[1,2,64,256]{3,2,1,0:T(8,128)S(1)} %slice_add_fusion.10), channel_id=1, source_target_pairs={{0,8},{4,12},{8,0},{12,4},{16,24},{20,28},{24,16},{28,20},{1,9},{5... | collective-permute-start | bytes 393224 | tf_op jit(solution)/shard_map/ppermute | solution.py:56
  41.2 3.6 %collective-permute-start.10 = (f32[1,2,64,256]{3,2,1,0:T(8,128)S(1)}, f32[1,2,64,256]{3,2,1,0:T(8,128)S(1)}, u32[]{:S(2)}, u32[]{:S(2)}) collective-permute-start(f32[1,2,64,256]{3,2,1,0:T(8,128)S(1)} %fusion.1), channel_id=1, source_target_pairs={{0,24},{4,28},{8,16},{12,20},{16,8},{20,12},{24,0},{28,4},{1,25},{... | collective-permute-start | bytes 393224 | tf_op jit(solution)/shard_map/ppermute | solution.py:56
  45.8 1.9 %collective-permute-start.15 = (f32[1,2,64,256]{3,2,1,0:T(8,128)S(1)}, f32[1,2,64,256]{3,2,1,0:T(8,128)S(1)}, u32[]{:S(2)}, u32[]{:S(2)}) collective-permute-start(f32[1,2,64,256]{3,2,1,0:T(8,128)S(1)} %fusion), channel_id=1, source_target_pairs={{0,24},{4,28},{8,16},{12,20},{16,8},{20,12},{24,0},{28,4},{1,25},{... | collective-permute-start | bytes 393224 | tf_op jit(solution)/shard_map/ppermute | solution.py:56
  48.8 1.6 %collective-permute-start.11 = (f32[1,2,64,256]{3,2,1,0:T(8,128)S(1)}, f32[1,2,64,256]{3,2,1,0:T(8,128)S(1)}, u32[]{:S(2)}, u32[]{:S(2)}) collective-permute-start(f32[1,2,64,256]{3,2,1,0:T(8,128)S(1)} %add.59), channel_id=1, source_target_pairs={{0,8},{4,12},{8,0},{12,4},{16,24},{20,28},{24,16},{28,20},{1,9},{5... | collective-permute-start | bytes 393224 | tf_op jit(solution)/shard_map/ppermute | solution.py:56
  50.4 2.3 %collective-permute-done.15 = f32[1,2,64,256]{3,2,1,0:T(8,128)S(1)} collective-permute-done((f32[1,2,64,256]{3,2,1,0:T(8,128)S(1)}, f32[1,2,64,256]{3,2,1,0:T(8,128)S(1)}, u32[]{:S(2)}, u32[]{:S(2)}) %collective-permute-start.15) | collective-permute-done | bytes 131104 | tf_op jit(solution)/shard_map/ppermute | solution.py:56
  52.8 2.1 %collective-permute-start.22 = (f32[2,2,128,128]{3,2,1,0:T(8,128)S(1)}, f32[2,2,128,128]{3,2,1,0:T(8,128)S(1)}, u32[]{:S(2)}, u32[]{:S(2)}) collective-permute-start(f32[2,2,128,128]{3,2,1,0:T(8,128)S(1)} %get-tuple-element.53), channel_id=1, source_target_pairs={{0,8},{4,12},{8,0},{12,4},{16,24},{20,28},{24,16},{28,20},{1,9},{5... | collective-permute-start | bytes 786440 | tf_op jit(solution)/shard_map/ppermute | solution.py:56
  56.7 2.5 %collective-permute-done.16 = f32[1,2,64,256]{3,2,1,0:T(8,128)S(1)} collective-permute-done((f32[1,2,64,256]{3,2,1,0:T(8,128)S(1)}, f32[1,2,64,256]{3,2,1,0:T(8,128)S(1)}, u32[]{:S(2)}, u32[]{:S(2)}) %collective-permute-start.16) | collective-permute-done | bytes 131104 | tf_op jit(solution)/shard_map/ppermute | solution.py:56
  61.9 3.2 %collective-permute-done.22 = f32[2,2,128,128]{3,2,1,0:T(8,128)S(1)} collective-permute-done((f32[2,2,128,128]{3,2,1,0:T(8,128)S(1)}, f32[2,2,128,128]{3,2,1,0:T(8,128)S(1)}, u32[]{:S(2)}, u32[]{:S(2)}) %collective-permute-start.22) | collective-permute-done | bytes 262176 | tf_op jit(solution)/shard_map/ppermute | solution.py:56
  65.1 1.8 %collective-permute-start.23 = (f32[1,2,128,128]{3,2,1,0:T(8,128)S(1)}, f32[1,2,128,128]{3,2,1,0:T(8,128)S(1)}, u32[]{:S(2)}, u32[]{:S(2)}) collective-permute-start(f32[1,2,128,128]{3,2,1,0:T(8,128)S(1)} %get-tuple-element.58), channel_id=1, source_target_pairs={{0,24},{4,28},{8,16},{12,20},{16,8},{20,12},{24,0},{28,4},{1,25},{... | collective-permute-start | bytes 393224 | tf_op jit(solution)/shard_map/ppermute | solution.py:56
  66.9 2.4 %collective-permute-done.17.refs_5_ = f32[2,2,64,256]{3,2,1,0:T(8,128)S(1)} collective-permute-done((f32[2,2,64,256]{3,2,1,0:T(8,128)S(1)}, f32[2,2,64,256]{3,2,1,0:T(8,128)S(1)}, u32[]{:S(2)}, u32[]{:S(2)}) %collective-permute-start.17) | collective-permute-done | bytes 262176 | tf_op jit(solution)/shard_map/ppermute | solution.py:56
  (66 shorter events, 15.3 us)
Async XLA Ops:
  5.1 5.3 %collective-permute-start = (f32[4,1024]{1,0:T(4,128)}, f32[4,1024]{1,0:T(4,128)S(1)}, u32[]{:S(2)}, u32[]{:S(2)}) collective-permute-start(f32[4,1024]{1,0:T(4,128)} %get-tuple-element.28.mine), channel_id=1, source_target_pairs={{0,4},{4,0},{8,12},{12,8},{16,20},{20,16},{24,28},{28,24},{1,5},{5... | collective-permute-start | bytes 49160 | tf_op jit(solution)/shard_map/ppermute | solution.py:56
  10.3 3.8 %collective-permute-start.3 = (f32[4,1024]{1,0:T(4,128)S(1)}, f32[4,1024]{1,0:T(4,128)S(1)}, u32[]{:S(2)}, u32[]{:S(2)}) collective-permute-start(f32[4,1024]{1,0:T(4,128)S(1)} %get-tuple-element.34.mine), channel_id=1, source_target_pairs={{0,4},{4,0},{8,12},{12,8},{16,20},{20,16},{24,28},{28,24},{1,5},{5... | collective-permute-start | bytes 49160 | tf_op jit(solution)/shard_map/ppermute | solution.py:56
  10.4 5.3 %collective-permute-start.1 = (f32[4,1024]{1,0:T(4,128)S(1)}, f32[4,1024]{1,0:T(4,128)S(1)}, u32[]{:S(2)}, u32[]{:S(2)}) collective-permute-start(f32[4,1024]{1,0:T(4,128)S(1)} %merge.4.mine), channel_id=1, source_target_pairs={{0,8},{4,12},{8,0},{12,4},{16,24},{20,28},{24,16},{28,20},{1,9},{5... | collective-permute-start | bytes 49160 | tf_op jit(solution)/shard_map/ppermute | solution.py:56
  14.1 4.3 %collective-permute-start.4 = (f32[4,1024]{1,0:T(4,128)S(1)}, f32[4,1024]{1,0:T(4,128)S(1)}, u32[]{:S(2)}, u32[]{:S(2)}) collective-permute-start(f32[4,1024]{1,0:T(4,128)S(1)} %merge.6.mine), channel_id=1, source_target_pairs={{0,8},{4,12},{8,0},{12,4},{16,24},{20,28},{24,16},{28,20},{1,9},{5... | collective-permute-start | bytes 49160 | tf_op jit(solution)/shard_map/ppermute | solution.py:56
  15.8 5.8 %collective-permute-start.2 = (f32[4,1024]{1,0:T(4,128)S(1)}, f32[4,1024]{1,0:T(4,128)S(1)}, u32[]{:S(2)}, u32[]{:S(2)}) collective-permute-start(f32[4,1024]{1,0:T(4,128)S(1)} %merge.5.after.mine), channel_id=1, source_target_pairs={{0,24},{4,28},{8,16},{12,20},{16,8},{20,12},{24,0},{28,4},{1,25},{... | collective-permute-start | bytes 49160 | tf_op jit(solution)/shard_map/ppermute | solution.py:56
  18.5 7.9 %collective-permute-start.5 = (f32[4,1024]{1,0:T(4,128)S(1)}, f32[4,1024]{1,0:T(4,128)S(1)}, u32[]{:S(2)}, u32[]{:S(2)}) collective-permute-start(f32[4,1024]{1,0:T(4,128)S(1)} %merge.7.mine), channel_id=1, source_target_pairs={{0,24},{4,28},{8,16},{12,20},{16,8},{20,12},{24,0},{28,4},{1,25},{... | collective-permute-start | bytes 49160 | tf_op jit(solution)/shard_map/ppermute | solution.py:56
  24.6 10.4 %collective-permute-start.8 = (f32[2,2,64,256]{3,2,1,0:T(8,128)S(1)}, f32[2,2,64,256]{3,2,1,0:T(8,128)S(1)}, u32[]{:S(2)}, u32[]{:S(2)}) collective-permute-start(f32[2,2,64,256]{3,2,1,0:T(8,128)S(1)} %get-tuple-element.41), channel_id=1, source_target_pairs={{0,4},{4,0},{8,12},{12,8},{16,20},{20,16},{24,28},{28,24},{1,5},{5... | collective-permute-start | bytes 786440 | tf_op jit(solution)/shard_map/ppermute | solution.py:56
  26.3 21.3 %collective-permute-start.18 = (f32[4,2,128,128]{3,2,1,0:T(8,128)S(1)}, f32[4,2,128,128]{3,2,1,0:T(8,128)S(1)}, u32[]{:S(2)}, u32[]{:S(2)}) collective-permute-start(f32[4,2,128,128]{3,2,1,0:T(8,128)S(1)} %get-tuple-element.47), channel_id=1, source_target_pairs={{0,8},{4,12},{8,0},{12,4},{16,24},{20,28},{24,16},{28,20},{1,9},{5... | collective-permute-start | bytes 1572872 | tf_op jit(solution)/shard_map/ppermute | solution.py:56
  29.3 9.7 %collective-permute-start.13 = (f32[2,2,64,256]{3,2,1,0:T(8,128)S(1)}, f32[2,2,64,256]{3,2,1,0:T(8,128)S(1)}, u32[]{:S(2)}, u32[]{:S(2)}) collective-permute-start(f32[2,2,64,256]{3,2,1,0:T(8,128)S(1)} %get-tuple-element.43), channel_id=1, source_target_pairs={{0,4},{4,0},{8,12},{12,8},{16,20},{20,16},{24,28},{28,24},{1,5},{5... | collective-permute-start | bytes 786440 | tf_op jit(solution)/shard_map/ppermute | solution.py:56
  32.8 15.6 %collective-permute-start.6 = (f32[2,512,128]{2,1,0:T(8,128)S(1)}, f32[2,512,128]{2,1,0:T(8,128)S(1)}, u32[]{:S(2)}, u32[]{:S(2)}) collective-permute-start(f32[2,512,128]{2,1,0:T(8,128)S(1)} %get-tuple-element.39), channel_id=1, source_target_pairs={{0,2},{1,3},{2,0},{3,1},{4,6},{5,7},{6,4},{7,5},{8,10},{9,11},{10,... | collective-permute-start | bytes 1572872 | tf_op jit(solution)/shard_map/ppermute | solution.py:41
  34.5 18.3 %collective-permute-start.21 = (f32[4,2,128,128]{3,2,1,0:T(8,128)S(1)}, f32[4,2,128,128]{3,2,1,0:T(8,128)S(1)}, u32[]{:S(2)}, u32[]{:S(2)}) collective-permute-start(f32[4,2,128,128]{3,2,1,0:T(8,128)S(1)} %get-tuple-element.48), channel_id=1, source_target_pairs={{0,4},{4,0},{8,12},{12,8},{16,20},{20,16},{24,28},{28,24},{1,5},{5... | collective-permute-start | bytes 1572872 | tf_op jit(solution)/shard_map/ppermute | solution.py:56
  35.0 6.1 %collective-permute-start.9 = (f32[1,2,64,256]{3,2,1,0:T(8,128)S(1)}, f32[1,2,64,256]{3,2,1,0:T(8,128)S(1)}, u32[]{:S(2)}, u32[]{:S(2)}) collective-permute-start(f32[1,2,64,256]{3,2,1,0:T(8,128)S(1)} %slice_add_fusion.12), channel_id=1, source_target_pairs={{0,8},{4,12},{8,0},{12,4},{16,24},{20,28},{24,16},{28,20},{1,9},{5... | collective-permute-start | bytes 393224 | tf_op jit(solution)/shard_map/ppermute | solution.py:56
  39.0 6.7 %collective-permute-start.14 = (f32[1,2,64,256]{3,2,1,0:T(8,128)S(1)}, f32[1,2,64,256]{3,2,1,0:T(8,128)S(1)}, u32[]{:S(2)}, u32[]{:S(2)}) collective-permute-start(f32[1,2,64,256]{3,2,1,0:T(8,128)S(1)} %slice_add_fusion.10), channel_id=1, source_target_pairs={{0,8},{4,12},{8,0},{12,4},{16,24},{20,28},{24,16},{28,20},{1,9},{5... | collective-permute-start | bytes 393224 | tf_op jit(solution)/shard_map/ppermute | solution.py:56
  41.2 7.7 %collective-permute-start.10 = (f32[1,2,64,256]{3,2,1,0:T(8,128)S(1)}, f32[1,2,64,256]{3,2,1,0:T(8,128)S(1)}, u32[]{:S(2)}, u32[]{:S(2)}) collective-permute-start(f32[1,2,64,256]{3,2,1,0:T(8,128)S(1)} %fusion.1), channel_id=1, source_target_pairs={{0,24},{4,28},{8,16},{12,20},{16,8},{20,12},{24,0},{28,4},{1,25},{... | collective-permute-start | bytes 393224 | tf_op jit(solution)/shard_map/ppermute | solution.py:56
  45.8 6.9 %collective-permute-start.15 = (f32[1,2,64,256]{3,2,1,0:T(8,128)S(1)}, f32[1,2,64,256]{3,2,1,0:T(8,128)S(1)}, u32[]{:S(2)}, u32[]{:S(2)}) collective-permute-start(f32[1,2,64,256]{3,2,1,0:T(8,128)S(1)} %fusion), channel_id=1, source_target_pairs={{0,24},{4,28},{8,16},{12,20},{16,8},{20,12},{24,0},{28,4},{1,25},{... | collective-permute-start | bytes 393224 | tf_op jit(solution)/shard_map/ppermute | solution.py:56
  47.7 12.9 %collective-permute-start.19 = (f32[2,2,128,128]{3,2,1,0:T(8,128)S(1)}, f32[2,2,128,128]{3,2,1,0:T(8,128)S(1)}, u32[]{:S(2)}, u32[]{:S(2)}) collective-permute-start(f32[2,2,128,128]{3,2,1,0:T(8,128)S(1)} %get-tuple-element.55), channel_id=1, source_target_pairs={{0,4},{4,0},{8,12},{12,8},{16,20},{20,16},{24,28},{28,24},{1,5},{5... | collective-permute-start | bytes 786440 | tf_op jit(solution)/shard_map/ppermute | solution.py:56
  48.5 18.4 %collective-permute-start.7 = (f32[1,512,128]{2,1,0:T(8,128)S(1)}, f32[1,512,128]{2,1,0:T(8,128)S(1)}, u32[]{:S(2)}, u32[]{:S(2)}) collective-permute-start(f32[1,512,128]{2,1,0:T(8,128)S(1)} %get-tuple-element.56), channel_id=1, source_target_pairs={{0,1},{1,0},{2,3},{3,2},{4,5},{5,4},{6,7},{7,6},{8,9},{9,8},{10,11... | collective-permute-start | bytes 786440 | tf_op jit(solution)/shard_map/ppermute | solution.py:41
  48.8 6.6 %collective-permute-start.11 = (f32[1,2,64,256]{3,2,1,0:T(8,128)S(1)}, f32[1,2,64,256]{3,2,1,0:T(8,128)S(1)}, u32[]{:S(2)}, u32[]{:S(2)}) collective-permute-start(f32[1,2,64,256]{3,2,1,0:T(8,128)S(1)} %add.59), channel_id=1, source_target_pairs={{0,8},{4,12},{8,0},{12,4},{16,24},{20,28},{24,16},{28,20},{1,9},{5... | collective-permute-start | bytes 393224 | tf_op jit(solution)/shard_map/ppermute | solution.py:56
  52.7 6.5 %collective-permute-start.16 = (f32[1,2,64,256]{3,2,1,0:T(8,128)S(1)}, f32[1,2,64,256]{3,2,1,0:T(8,128)S(1)}, u32[]{:S(2)}, u32[]{:S(2)}) collective-permute-start(f32[1,2,64,256]{3,2,1,0:T(8,128)S(1)} %add.63), channel_id=1, source_target_pairs={{0,8},{4,12},{8,0},{12,4},{16,24},{20,28},{24,16},{28,20},{1,9},{5... | collective-permute-start | bytes 393224 | tf_op jit(solution)/shard_map/ppermute | solution.py:56
  52.8 12.2 %collective-permute-start.22 = (f32[2,2,128,128]{3,2,1,0:T(8,128)S(1)}, f32[2,2,128,128]{3,2,1,0:T(8,128)S(1)}, u32[]{:S(2)}, u32[]{:S(2)}) collective-permute-start(f32[2,2,128,128]{3,2,1,0:T(8,128)S(1)} %get-tuple-element.53), channel_id=1, source_target_pairs={{0,8},{4,12},{8,0},{12,4},{16,24},{20,28},{24,16},{28,20},{1,9},{5... | collective-permute-start | bytes 786440 | tf_op jit(solution)/shard_map/ppermute | solution.py:56
  55.5 11.4 %collective-permute-start.12 = (f32[2,2,64,256]{3,2,1,0:T(8,128)S(1)}, f32[2,2,64,256]{3,2,1,0:T(8,128)S(1)}, u32[]{:S(2)}, u32[]{:S(2)}) collective-permute-start(f32[2,2,64,256]{3,2,1,0:T(8,128)S(1)} %pad_maximum_fusion.refs_2_), channel_id=1, source_target_pairs={{0,4},{4,0},{8,12},{12,8},{16,20},{20,16},{24,28},{28,24},{1,5},{5... | collective-permute-start | bytes 786440 | tf_op jit(solution)/shard_map/ppermute | solution.py:56
  59.2 10.1 %collective-permute-start.17 = (f32[2,2,64,256]{3,2,1,0:T(8,128)S(1)}, f32[2,2,64,256]{3,2,1,0:T(8,128)S(1)}, u32[]{:S(2)}, u32[]{:S(2)}) collective-permute-start(f32[2,2,64,256]{3,2,1,0:T(8,128)S(1)} %pad_maximum_fusion.1.refs_4_), channel_id=1, source_target_pairs={{0,4},{4,0},{8,12},{12,8},{16,20},{20,16},{24,28},{28,24},{1,5},{5... | collective-permute-start | bytes 786440 | tf_op jit(solution)/shard_map/ppermute | solution.py:56
  60.6 9.9 %collective-permute-start.20 = (f32[1,2,128,128]{3,2,1,0:T(8,128)S(1)}, f32[1,2,128,128]{3,2,1,0:T(8,128)S(1)}, u32[]{:S(2)}, u32[]{:S(2)}) collective-permute-start(f32[1,2,128,128]{3,2,1,0:T(8,128)S(1)} %get-tuple-element.60), channel_id=1, source_target_pairs={{0,24},{4,28},{8,16},{12,20},{16,8},{20,12},{24,0},{28,4},{1,25},{... | collective-permute-start | bytes 393224 | tf_op jit(solution)/shard_map/ppermute | solution.py:56
  65.1 6.9 %collective-permute-start.23 = (f32[1,2,128,128]{3,2,1,0:T(8,128)S(1)}, f32[1,2,128,128]{3,2,1,0:T(8,128)S(1)}, u32[]{:S(2)}, u32[]{:S(2)}) collective-permute-start(f32[1,2,128,128]{3,2,1,0:T(8,128)S(1)} %get-tuple-element.58), channel_id=1, source_target_pairs={{0,24},{4,28},{8,16},{12,20},{16,8},{20,12},{24,0},{28,4},{1,25},{... | collective-permute-start | bytes 393224 | tf_op jit(solution)/shard_map/ppermute | solution.py:56
  (8 other events, 75.8 us)

commit v10 on v9

--- a/solution.py
+++ b/solution.py
@@ -131,6 +131,7 @@
 LAST_BIT = 4
 WEIGHT_PARTS = (((0, 256, (1, 2)),), ((0, 256, (1, 2)),))
 QUERY_PARTS = (((0, 2, (2, 1, 4)),), ((0, 2, (1, 2, 4)),))
+AFTER = {'i.0': 'w0.2'}
 
 
 def grads_kernel(
@@ -194,7 +195,8 @@
         ref[relative % (shares // 2)] = total[:, pl.ds(start, width)]
 
 
-def query_kernel(parts, row_axis, low, score_grads, keys, *refs):
+def query_kernel(parts, row_axis, low, after, score_grads, keys, *refs):
+    del after
     tile_ref = refs[-1]
     reads, _, latents = score_grads.shape
     piece = latents // GROUPS
@@ -253,14 +255,9 @@
     return jax.ShapeDtypeStruct(shape, dtype)
 
 
-def scatter_steps(keep, send, count, bits):
-    for index, bit in enumerate(bits):
-        theirs = row_swap_of(send, count, bit)
-        if index + 1 == len(bits):
-            return keep, theirs
-        middle = keep.shape[0] // 2
-        send = keep[middle:] + theirs[middle:]
-        keep = keep[:middle] + theirs[:middle]
+def add_kernel(mine, theirs, after, total):
+    del after
+    total[...] = mine[...] + theirs[...]
 
 
 def on_device(row_devices, head_devices, inputs, key_weight, value_weight, queries, out_grad):
@@ -344,7 +341,7 @@
         return pl.pallas_call(
             kernel,
             out_shape=[shape_of(*item) for item in shapes],
-            in_specs=[ANY if name == "grads" and not place else VMEM for place in range(len(operands))],
+            in_specs=[ANY] + [VMEM] * (len(operands) - 1),
             out_specs=[VMEM] * len(shapes),
             scratch_shapes=scratch,
             compiler_params=params(limit),
@@ -352,7 +349,7 @@
             name=name,
         )(*operands)
 
-    grads_out, query_out = [], []
+    grads_out, weight_steps, marks = [], [], {}
     for head_index in range(head_count):
         keys, values, _ = projected[head_index]
         results = kernel_call(
@@ -378,44 +375,81 @@
             "grads",
         )
         grads_out.append(results)
-        query_out.append(
-            kernel_call(
-                functools.partial(query_kernel, QUERY_PARTS[head_index], "rows", low),
-                [
-                    ((GROUPS // 2, end - begin, latents // GROUPS, HD),)
-                    for begin, end, _ in QUERY_PARTS[head_index]
-                    for _ in range(2)
-                ],
-                [results[1], keys],
-                [pltpu.VMEM((GROUPS // 2 * reads, tile, HD), jnp.float32)],
-                16,
-                "query",
-            )
+        marks[f"A{head_index}"] = results[0]
+        for part, (begin, end, bits) in enumerate(WEIGHT_PARTS[head_index]):
+            keep, send = results[2 + 2 * part : 4 + 2 * part]
+            theirs = row_swap(send, bit=bits[0] * low)
+            send = keep[1:] + theirs[1:]
+            mine = keep[:1] + theirs[:1]
+            marks[f"w{head_index}.1"] = send
+            weight_steps.append((mine, row_swap(send, bit=bits[1] * low)))
+
+    query_terms, query_list = [], []
+    for head_index in range(head_count):
+        results = kernel_call(
+            functools.partial(query_kernel, QUERY_PARTS[head_index], "rows", low),
+            [
+                ((GROUPS // 2, end - begin, latents // GROUPS, HD),)
+                for begin, end, _ in QUERY_PARTS[head_index]
+                for _ in range(2)
+            ],
+            [
+                marks[AFTER.get(f"B{head_index}", f"A{head_index}")],
+                grads_out[head_index][1],
+                projected[head_index][0],
+            ],
+            [pltpu.VMEM((GROUPS // 2 * reads, tile, HD), jnp.float32)],
+            16,
+            "query",
         )
+        marks[f"B{head_index}"] = results[0]
+        for part, (begin, end, bits) in enumerate(QUERY_PARTS[head_index]):
+            keep, send = results[2 * part : 2 * part + 2]
+            for place, bit in enumerate(bits):
+                theirs = row_swap(send, bit=bit * low)
+                if place + 1 < len(bits):
+                    middle = keep.shape[0] // 2
+                    send = keep[middle:] + theirs[middle:]
+                    keep = keep[:middle] + theirs[:middle]
+                    marks[f"q{head_index}.{place + 1}"] = send
+            terms = [keep, theirs]
+            if low > 1:
+                terms = [scatter_low((keep + theirs)[0], 1)[None]]
+            query_terms += terms
+            query_list.append((head_index, begin, end, len(terms)))
+
+    def added(kernel, shape, mine, theirs, after):
+        return pl.pallas_call(
+            kernel,
+            out_shape=shape_of(shape),
+            in_specs=[VMEM, VMEM, ANY],
+            out_specs=VMEM,
+            compiler_params=params(4),
+            cost_estimate=pl.CostEstimate(flops=1024, bytes_accessed=1024, transcendentals=0),
+            name="added",
+        )(mine, theirs, after)
 
     weight_terms, weight_list = [], []
     for head_index in range(head_count):
-        for part, (begin, end, bits) in enumerate(WEIGHT_PARTS[head_index]):
-            keep, send = grads_out[head_index][2 + 2 * part : 4 + 2 * part]
+        for begin, end, bits in WEIGHT_PARTS[head_index]:
+            mine, theirs = weight_steps.pop(0)
             first, second = (bit * low for bit in bits)
-            mine, theirs = scatter_steps(keep, send, row_devices, (first, second))
-            mine = mine + theirs
-            mine = sum_low(mine + row_swap(mine, bit=LAST_BIT * low))
-            near = jnp.concatenate([mine, row_swap(mine, bit=second)], axis=0)
+            for place, bit in ((2, LAST_BIT * low), (3, second)):
+                after = AFTER.get(f"w{head_index}.{place}")
+                if after:
+                    mine = added(add_kernel, mine.shape, mine, theirs, marks[after])
+                else:
+                    mine = mine + theirs
+                if place == 3:
+                    mine = sum_low(mine)
+                theirs = row_swap(mine, bit=bit)
+                marks[f"w{head_index}.{place}"] = mine
+            near = jnp.concatenate([mine, theirs], axis=0)
             weight_terms += [near, row_swap(near, bit=first)]
             weight_list.append((head_index, begin, end, bits))
-    query_terms, query_list = [], []
-    for head_index in range(head_count):
-        for part, (begin, end, bits) in enumerate(QUERY_PARTS[head_index]):
-            keep, send = query_out[head_index][2 * part : 2 * part + 2]
-            terms = scatter_steps(keep, send, row_devices, [bit * low for bit in bits])
-            if low > 1:
-                terms = [scatter_low(sum(terms)[0], 1)[None]]
-            query_terms += terms
-            query_list.append((head_index, begin, end, len(terms)))
 
     share = ((head_devices // 2, row_count, features // head_devices),)
-    after = query_out[-1][0]
+    after = marks[AFTER.get("i.0", "B1")]
     input_keep, input_send = pl.pallas_call(
         functools.partial(input_kernel, "heads"),
         out_shape=[shape_of(*share)] * 2,

time: 72.9 us -> 72.7 us (level)
  starting transfers between devices: 36.4 us -> 35.5 us
    ppermute x22, starting transfers between devices: 34.7 us -> 33.3 us  [row_swap_of(): return lax.ppermute(array, 'rows', pairs)]
  transfers between devices with their start and end apart: 24 -> 24, of which waited for: 11 -> 9; matrix products, arithmetic and copies ran while one was open for 1% -> 1% of each run, Pallas kernels for 17% -> 17%
where the time goes in v10:
time: 72.7 us; the launch traced here: 72.6 us
  starting transfers between devices  35.5 us (49%)
  waiting for transfers between devices  18.2 us (25%)
  Pallas kernels  17.4 us (24%)
  between operations  0.93 us (1%)
    ppermute x22, starting transfers between devices, row_swap_of(): return lax.ppermute(array, 'rows', pairs)  33.3 us
    ppermute x22, waiting for transfers between devices, row_swap_of(): return lax.ppermute(array, 'rows', pairs)  18.2 us
    pallas_call x4, Pallas kernels, kernel_call(): pl.pallas_call(kernel, out_shape=[shape_of(*item) for item in shapes], in...  8.05 us
    pallas_call x2, Pallas kernels, on_device(): pl.pallas_call(functools.partial(first_kernel, tile) if first else functo...  6.55 us
    ppermute x2, starting transfers between devices, swap(): return lax.ppermute(array, axis, pairs)  2.21 us
  transfers between devices with their start and end apart: 24, of which 9 were waited for; matrix products, arithmetic and copies ran while one was open for 1% of the time, Pallas kernels for 17%

profile of v10, /device:TPU:0, one launch (start us, length us, event | category | flops | bytes accessed | tf_op | source)
XLA Modules:
  0.0 72.6 jit_solution(8050218443127623243)
XLA Ops:
  0.7 4.4 %project.2 = (bf16[512,128]{1,0:T(8,128)(2,1)}, bf16[512,128]{1,0:T(8,128)(2,1)}, f32[4,1024]{1,0:T(4,128)}) custom-call(bf16[512,512]{1,0:T(8,128)(2,1)} %inputs.3, bf16[512,256]{1,0:T(8,128)(2,1)} %key_weight.1, bf16[512,256]{1,0:T(8,128)(2,1)} %value_weight.1, bf16[2,1024,256]{2,1,0:T(8,128)(2,1)} %queries.4, bf16[2,1024,256]{2,1,0:T(8,128)(2,1)} %out_grad.3), custom_call_target="tpu_custom_call" | custom-call | flops 1073741824 | bytes 4194304 | tf_op jit(solution)/shard_map/project/pallas_call | solution.py:285
  5.1 3.0 %collective-permute-start = (f32[4,1024]{1,0:T(4,128)}, f32[4,1024]{1,0:T(4,128)S(1)}, u32[]{:S(2)}, u32[]{:S(2)}) collective-permute-start(f32[4,1024]{1,0:T(4,128)} %get-tuple-element.28.mine), channel_id=1, source_target_pairs={{0,4},{4,0},{8,12},{12,8},{16,20},{20,16},{24,28},{28,24},{1,5},{5... | collective-permute-start | bytes 49160 | tf_op jit(solution)/shard_map/ppermute | solution.py:56
  8.2 2.1 %project.3 = (bf16[512,128]{1,0:T(8,128)(2,1)S(1)}, bf16[512,128]{1,0:T(8,128)(2,1)S(1)}, f32[4,1024]{1,0:T(4,128)S(1)}) custom-call(bf16[512,512]{1,0:T(8,128)(2,1)S(1)} %copy-done.3, bf16[512,256]{1,0:T(8,128)(2,1)S(1)} %copy-done.4, bf16[512,256]{1,0:T(8,128)(2,1)S(1)} %copy-done.5, bf16[2,1024,256]{2,1,0:T(8,128)(2,1)S(1)} %copy-done.1, ...), custom_call_target="tpu_custom_call" | custom-call | flops 1073741824 | bytes 4194304 | tf_op jit(solution)/shard_map/project/pallas_call | solution.py:285
  10.4 2.1 %collective-permute-start.1 = (f32[4,1024]{1,0:T(4,128)S(1)}, f32[4,1024]{1,0:T(4,128)S(1)}, u32[]{:S(2)}, u32[]{:S(2)}) collective-permute-start(f32[4,1024]{1,0:T(4,128)S(1)} %merge.4.mine), channel_id=1, source_target_pairs={{0,8},{4,12},{8,0},{12,4},{16,24},{20,28},{24,16},{28,20},{1,9},{5... | collective-permute-start | bytes 49160 | tf_op jit(solution)/shard_map/ppermute | solution.py:56
  12.6 1.5 %collective-permute-done.3.theirs = f32[4,1024]{1,0:T(4,128)S(1)} collective-permute-done((f32[4,1024]{1,0:T(4,128)S(1)}, f32[4,1024]{1,0:T(4,128)S(1)}, u32[]{:S(2)}, u32[]{:S(2)}) %collective-permute-start.3) | collective-permute-done | bytes 16416 | tf_op jit(solution)/shard_map/ppermute | solution.py:56
  14.1 1.6 %collective-permute-start.4 = (f32[4,1024]{1,0:T(4,128)S(1)}, f32[4,1024]{1,0:T(4,128)S(1)}, u32[]{:S(2)}, u32[]{:S(2)}) collective-permute-start(f32[4,1024]{1,0:T(4,128)S(1)} %merge.6.mine), channel_id=1, source_target_pairs={{0,8},{4,12},{8,0},{12,4},{16,24},{20,28},{24,16},{28,20},{1,9},{5... | collective-permute-start | bytes 49160 | tf_op jit(solution)/shard_map/ppermute | solution.py:56
  15.8 2.6 %collective-permute-start.2 = (f32[4,1024]{1,0:T(4,128)S(1)}, f32[4,1024]{1,0:T(4,128)S(1)}, u32[]{:S(2)}, u32[]{:S(2)}) collective-permute-start(f32[4,1024]{1,0:T(4,128)S(1)} %merge.5.after.mine), channel_id=1, source_target_pairs={{0,24},{4,28},{8,16},{12,20},{16,8},{20,12},{24,0},{28,4},{1,25},{... | collective-permute-start | bytes 49160 | tf_op jit(solution)/shard_map/ppermute | solution.py:56
  18.5 3.2 %collective-permute-start.5 = (f32[4,1024]{1,0:T(4,128)S(1)}, f32[4,1024]{1,0:T(4,128)S(1)}, u32[]{:S(2)}, u32[]{:S(2)}) collective-permute-start(f32[4,1024]{1,0:T(4,128)S(1)} %merge.7.mine), channel_id=1, source_target_pairs={{0,24},{4,28},{8,16},{12,20},{16,8},{20,12},{24,0},{28,4},{1,25},{... | collective-permute-start | bytes 49160 | tf_op jit(solution)/shard_map/ppermute | solution.py:56
  21.6 2.9 %grads.2 = (bf16[512,256]{1,0:T(8,128)(2,1)S(1)}, bf16[2,512,1024]{2,1,0:T(8,128)(2,1)S(1)}, f32[2,2,64,256]{3,2,1,0:T(8,128)S(1)}, f32[2,2,64,256]{3,2,1,0:T(8,128)S(1)}) custom-call(f32[4,1024]{1,0:T(4,128)S(1)} %merge.5.after.mine, bf16[512,512]{1,0:T(8,128)(2,1)S(1)} %copy-done.3, bf16[512,128]{1,0:T(8,128)(2,1)S(1)} %copy-done.6, ...), custom_call_target="tpu_custom_call" | custom-call | flops 1073741824 | bytes 4194304 | tf_op jit(solution)/shard_map/grads/pallas_call | solution.py:341
  26.4 2.9 %grads.3 = (bf16[512,256]{1,0:T(8,128)(2,1)S(1)}, bf16[2,512,1024]{2,1,0:T(8,128)(2,1)S(1)}, f32[2,2,64,256]{3,2,1,0:T(8,128)S(1)}, f32[2,2,64,256]{3,2,1,0:T(8,128)S(1)}) custom-call(bf16[512,256]{1,0:T(8,128)(2,1)S(1)} %get-tuple-element.31.after.refs_0_, bf16[512,512]{1,0:T(8,128)(2,1)S(1)} %copy-done.3, bf16[512,128]{1,0:T(8,128)(2,1)S(1)} %get-tuple-element.32.keys, ...), custom_call_target="tpu_custom_call" | custom-call | flops 1073741824 | bytes 4194304 | tf_op jit(solution)/shard_map/grads/pallas_call | solution.py:341
  29.3 1.6 %collective-permute-start.13 = (f32[2,2,64,256]{3,2,1,0:T(8,128)S(1)}, f32[2,2,64,256]{3,2,1,0:T(8,128)S(1)}, u32[]{:S(2)}, u32[]{:S(2)}) collective-permute-start(f32[2,2,64,256]{3,2,1,0:T(8,128)S(1)} %get-tuple-element.41), channel_id=1, source_target_pairs={{0,4},{4,0},{8,12},{12,8},{16,20},{20,16},{24,28},{28,24},{1,5},{5... | collective-permute-start | bytes 786440 | tf_op jit(solution)/shard_map/ppermute | solution.py:56
  34.7 4.3 %collective-permute-done.13 = f32[2,2,64,256]{3,2,1,0:T(8,128)S(1)} collective-permute-done((f32[2,2,64,256]{3,2,1,0:T(8,128)S(1)}, f32[2,2,64,256]{3,2,1,0:T(8,128)S(1)}, u32[]{:S(2)}, u32[]{:S(2)}) %collective-permute-start.13) | collective-permute-done | bytes 262176 | tf_op jit(solution)/shard_map/ppermute | solution.py:56
  39.0 1.7 %collective-permute-start.14 = (f32[1,2,64,256]{3,2,1,0:T(8,128)S(1)}, f32[1,2,64,256]{3,2,1,0:T(8,128)S(1)}, u32[]{:S(2)}, u32[]{:S(2)}) collective-permute-start(f32[1,2,64,256]{3,2,1,0:T(8,128)S(1)} %slice_add_fusion.10), channel_id=1, source_target_pairs={{0,8},{4,12},{8,0},{12,4},{16,24},{20,28},{24,16},{28,20},{1,9},{5... | collective-permute-start | bytes 393224 | tf_op jit(solution)/shard_map/ppermute | solution.py:56
  41.7 4.4 %collective-permute-start.10 = (f32[1,2,64,256]{3,2,1,0:T(8,128)S(1)}, f32[1,2,64,256]{3,2,1,0:T(8,128)S(1)}, u32[]{:S(2)}, u32[]{:S(2)}) collective-permute-start(f32[1,2,64,256]{3,2,1,0:T(8,128)S(1)} %fusion.1.refs_2_), channel_id=1, source_target_pairs={{0,24},{4,28},{8,16},{12,20},{16,8},{20,12},{24,0},{28,4},{1,25},{... | collective-permute-start | bytes 393224 | tf_op jit(solution)/shard_map/ppermute | solution.py:56
  46.2 2.5 %collective-permute-start.15 = (f32[1,2,64,256]{3,2,1,0:T(8,128)S(1)}, f32[1,2,64,256]{3,2,1,0:T(8,128)S(1)}, u32[]{:S(2)}, u32[]{:S(2)}) collective-permute-start(f32[1,2,64,256]{3,2,1,0:T(8,128)S(1)} %fusion), channel_id=1, source_target_pairs={{0,24},{4,28},{8,16},{12,20},{16,8},{20,12},{24,0},{28,4},{1,25},{... | collective-permute-start | bytes 393224 | tf_op jit(solution)/shard_map/ppermute | solution.py:56
  49.5 2.1 %collective-permute-start.8 = (f32[2,512,128]{2,1,0:T(8,128)S(1)}, f32[2,512,128]{2,1,0:T(8,128)S(1)}, u32[]{:S(2)}, u32[]{:S(2)}) collective-permute-start(f32[2,512,128]{2,1,0:T(8,128)S(1)} %get-tuple-element.39), channel_id=1, source_target_pairs={{0,2},{1,3},{2,0},{3,1},{4,6},{5,7},{6,4},{7,5},{8,10},{9,11},{10,... | collective-permute-start | bytes 1572872 | tf_op jit(solution)/shard_map/ppermute | solution.py:41
  52.2 2.2 %collective-permute-done.15 = f32[1,2,64,256]{3,2,1,0:T(8,128)S(1)} collective-permute-done((f32[1,2,64,256]{3,2,1,0:T(8,128)S(1)}, f32[1,2,64,256]{3,2,1,0:T(8,128)S(1)}, u32[]{:S(2)}, u32[]{:S(2)}) %collective-permute-start.15) | collective-permute-done | bytes 131104 | tf_op jit(solution)/shard_map/ppermute | solution.py:56
  54.7 2.1 %collective-permute-start.22 = (f32[2,2,128,128]{3,2,1,0:T(8,128)S(1)}, f32[2,2,128,128]{3,2,1,0:T(8,128)S(1)}, u32[]{:S(2)}, u32[]{:S(2)}) collective-permute-start(f32[2,2,128,128]{3,2,1,0:T(8,128)S(1)} %get-tuple-element.53), channel_id=1, source_target_pairs={{0,8},{4,12},{8,0},{12,4},{16,24},{20,28},{24,16},{28,20},{1,9},{5... | collective-permute-start | bytes 786440 | tf_op jit(solution)/shard_map/ppermute | solution.py:56
  56.7 2.5 %collective-permute-done.11 = f32[1,2,64,256]{3,2,1,0:T(8,128)S(1)} collective-permute-done((f32[1,2,64,256]{3,2,1,0:T(8,128)S(1)}, f32[1,2,64,256]{3,2,1,0:T(8,128)S(1)}, u32[]{:S(2)}, u32[]{:S(2)}) %collective-permute-start.11) | collective-permute-done | bytes 131104 | tf_op jit(solution)/shard_map/ppermute | solution.py:56
  59.4 1.3 %collective-permute-done.16 = f32[1,2,64,256]{3,2,1,0:T(8,128)S(1)} collective-permute-done((f32[1,2,64,256]{3,2,1,0:T(8,128)S(1)}, f32[1,2,64,256]{3,2,1,0:T(8,128)S(1)}, u32[]{:S(2)}, u32[]{:S(2)}) %collective-permute-start.16) | collective-permute-done | bytes 131104 | tf_op jit(solution)/shard_map/ppermute | solution.py:56
  61.8 2.0 %collective-permute-start.20 = (f32[1,2,128,128]{3,2,1,0:T(8,128)S(1)}, f32[1,2,128,128]{3,2,1,0:T(8,128)S(1)}, u32[]{:S(2)}, u32[]{:S(2)}) collective-permute-start(f32[1,2,128,128]{3,2,1,0:T(8,128)S(1)} %get-tuple-element.60), channel_id=1, source_target_pairs={{0,24},{4,28},{8,16},{12,20},{16,8},{20,12},{24,0},{28,4},{1,25},{... | collective-permute-start | bytes 393224 | tf_op jit(solution)/shard_map/ppermute | solution.py:56
  64.0 2.2 %collective-permute-start.23 = (f32[1,2,128,128]{3,2,1,0:T(8,128)S(1)}, f32[1,2,128,128]{3,2,1,0:T(8,128)S(1)}, u32[]{:S(2)}, u32[]{:S(2)}) collective-permute-start(f32[1,2,128,128]{3,2,1,0:T(8,128)S(1)} %get-tuple-element.58), channel_id=1, source_target_pairs={{0,24},{4,28},{8,16},{12,20},{16,8},{20,12},{24,0},{28,4},{1,25},{... | collective-permute-start | bytes 393224 | tf_op jit(solution)/shard_map/ppermute | solution.py:56
  66.2 2.3 %collective-permute-done.17.refs_5_ = f32[2,2,64,256]{3,2,1,0:T(8,128)S(1)} collective-permute-done((f32[2,2,64,256]{3,2,1,0:T(8,128)S(1)}, f32[2,2,64,256]{3,2,1,0:T(8,128)S(1)}, u32[]{:S(2)}, u32[]{:S(2)}) %collective-permute-start.17) | collective-permute-done | bytes 262176 | tf_op jit(solution)/shard_map/ppermute | solution.py:56
  69.7 2.1 %collective-permute-done.23.refs_3_ = f32[1,2,128,128]{3,2,1,0:T(8,128)S(1)} collective-permute-done((f32[1,2,128,128]{3,2,1,0:T(8,128)S(1)}, f32[1,2,128,128]{3,2,1,0:T(8,128)S(1)}, u32[]{:S(2)}, u32[]{:S(2)}) %collective-permute-start.23) | collective-permute-done | bytes 131104 | tf_op jit(solution)/shard_map/ppermute | solution.py:56
  (66 shorter events, 11.8 us)
Async XLA Ops:
  5.1 5.3 %collective-permute-start = (f32[4,1024]{1,0:T(4,128)}, f32[4,1024]{1,0:T(4,128)S(1)}, u32[]{:S(2)}, u32[]{:S(2)}) collective-permute-start(f32[4,1024]{1,0:T(4,128)} %get-tuple-element.28.mine), channel_id=1, source_target_pairs={{0,4},{4,0},{8,12},{12,8},{16,20},{20,16},{24,28},{28,24},{1,5},{5... | collective-permute-start | bytes 49160 | tf_op jit(solution)/shard_map/ppermute | solution.py:56
  10.3 3.8 %collective-permute-start.3 = (f32[4,1024]{1,0:T(4,128)S(1)}, f32[4,1024]{1,0:T(4,128)S(1)}, u32[]{:S(2)}, u32[]{:S(2)}) collective-permute-start(f32[4,1024]{1,0:T(4,128)S(1)} %get-tuple-element.34.mine), channel_id=1, source_target_pairs={{0,4},{4,0},{8,12},{12,8},{16,20},{20,16},{24,28},{28,24},{1,5},{5... | collective-permute-start | bytes 49160 | tf_op jit(solution)/shard_map/ppermute | solution.py:56
  10.4 5.3 %collective-permute-start.1 = (f32[4,1024]{1,0:T(4,128)S(1)}, f32[4,1024]{1,0:T(4,128)S(1)}, u32[]{:S(2)}, u32[]{:S(2)}) collective-permute-start(f32[4,1024]{1,0:T(4,128)S(1)} %merge.4.mine), channel_id=1, source_target_pairs={{0,8},{4,12},{8,0},{12,4},{16,24},{20,28},{24,16},{28,20},{1,9},{5... | collective-permute-start | bytes 49160 | tf_op jit(solution)/shard_map/ppermute | solution.py:56
  14.1 4.3 %collective-permute-start.4 = (f32[4,1024]{1,0:T(4,128)S(1)}, f32[4,1024]{1,0:T(4,128)S(1)}, u32[]{:S(2)}, u32[]{:S(2)}) collective-permute-start(f32[4,1024]{1,0:T(4,128)S(1)} %merge.6.mine), channel_id=1, source_target_pairs={{0,8},{4,12},{8,0},{12,4},{16,24},{20,28},{24,16},{28,20},{1,9},{5... | collective-permute-start | bytes 49160 | tf_op jit(solution)/shard_map/ppermute | solution.py:56
  15.8 5.8 %collective-permute-start.2 = (f32[4,1024]{1,0:T(4,128)S(1)}, f32[4,1024]{1,0:T(4,128)S(1)}, u32[]{:S(2)}, u32[]{:S(2)}) collective-permute-start(f32[4,1024]{1,0:T(4,128)S(1)} %merge.5.after.mine), channel_id=1, source_target_pairs={{0,24},{4,28},{8,16},{12,20},{16,8},{20,12},{24,0},{28,4},{1,25},{... | collective-permute-start | bytes 49160 | tf_op jit(solution)/shard_map/ppermute | solution.py:56
  18.5 7.9 %collective-permute-start.5 = (f32[4,1024]{1,0:T(4,128)S(1)}, f32[4,1024]{1,0:T(4,128)S(1)}, u32[]{:S(2)}, u32[]{:S(2)}) collective-permute-start(f32[4,1024]{1,0:T(4,128)S(1)} %merge.7.mine), channel_id=1, source_target_pairs={{0,24},{4,28},{8,16},{12,20},{16,8},{20,12},{24,0},{28,4},{1,25},{... | collective-permute-start | bytes 49160 | tf_op jit(solution)/shard_map/ppermute | solution.py:56
  24.6 8.8 %collective-permute-start.6 = (f32[2,2,64,256]{3,2,1,0:T(8,128)S(1)}, f32[2,2,64,256]{3,2,1,0:T(8,128)S(1)}, u32[]{:S(2)}, u32[]{:S(2)}) collective-permute-start(f32[2,2,64,256]{3,2,1,0:T(8,128)S(1)} %get-tuple-element.37), channel_id=1, source_target_pairs={{0,4},{4,0},{8,12},{12,8},{16,20},{20,16},{24,28},{28,24},{1,5},{5... | collective-permute-start | bytes 786440 | tf_op jit(solution)/shard_map/ppermute | solution.py:56
  26.3 25.4 %collective-permute-start.18 = (f32[4,2,128,128]{3,2,1,0:T(8,128)S(1)}, f32[4,2,128,128]{3,2,1,0:T(8,128)S(1)}, u32[]{:S(2)}, u32[]{:S(2)}) collective-permute-start(f32[4,2,128,128]{3,2,1,0:T(8,128)S(1)} %get-tuple-element.45), channel_id=1, source_target_pairs={{0,8},{4,12},{8,0},{12,4},{16,24},{20,28},{24,16},{28,20},{1,9},{5... | collective-permute-start | bytes 1572872 | tf_op jit(solution)/shard_map/ppermute | solution.py:56
  29.3 9.7 %collective-permute-start.13 = (f32[2,2,64,256]{3,2,1,0:T(8,128)S(1)}, f32[2,2,64,256]{3,2,1,0:T(8,128)S(1)}, u32[]{:S(2)}, u32[]{:S(2)}) collective-permute-start(f32[2,2,64,256]{3,2,1,0:T(8,128)S(1)} %get-tuple-element.41), channel_id=1, source_target_pairs={{0,4},{4,0},{8,12},{12,8},{16,20},{20,16},{24,28},{28,24},{1,5},{5... | collective-permute-start | bytes 786440 | tf_op jit(solution)/shard_map/ppermute | solution.py:56
  32.0 22.6 %collective-permute-start.21 = (f32[4,2,128,128]{3,2,1,0:T(8,128)S(1)}, f32[4,2,128,128]{3,2,1,0:T(8,128)S(1)}, u32[]{:S(2)}, u32[]{:S(2)}) collective-permute-start(f32[4,2,128,128]{3,2,1,0:T(8,128)S(1)} %get-tuple-element.48), channel_id=1, source_target_pairs={{0,4},{4,0},{8,12},{12,8},{16,20},{20,16},{24,28},{28,24},{1,5},{5... | collective-permute-start | bytes 1572872 | tf_op jit(solution)/shard_map/ppermute | solution.py:56
  33.4 8.3 %collective-permute-start.7 = (f32[1,2,64,256]{3,2,1,0:T(8,128)S(1)}, f32[1,2,64,256]{3,2,1,0:T(8,128)S(1)}, u32[]{:S(2)}, u32[]{:S(2)}) collective-permute-start(f32[1,2,64,256]{3,2,1,0:T(8,128)S(1)} %slice_add_fusion.12), channel_id=1, source_target_pairs={{0,8},{4,12},{8,0},{12,4},{16,24},{20,28},{24,16},{28,20},{1,9},{5... | collective-permute-start | bytes 393224 | tf_op jit(solution)/shard_map/ppermute | solution.py:56
  39.0 7.1 %collective-permute-start.14 = (f32[1,2,64,256]{3,2,1,0:T(8,128)S(1)}, f32[1,2,64,256]{3,2,1,0:T(8,128)S(1)}, u32[]{:S(2)}, u32[]{:S(2)}) collective-permute-start(f32[1,2,64,256]{3,2,1,0:T(8,128)S(1)} %slice_add_fusion.10), channel_id=1, source_target_pairs={{0,8},{4,12},{8,0},{12,4},{16,24},{20,28},{24,16},{28,20},{1,9},{5... | collective-permute-start | bytes 393224 | tf_op jit(solution)/shard_map/ppermute | solution.py:56
  41.7 10.1 %collective-permute-start.10 = (f32[1,2,64,256]{3,2,1,0:T(8,128)S(1)}, f32[1,2,64,256]{3,2,1,0:T(8,128)S(1)}, u32[]{:S(2)}, u32[]{:S(2)}) collective-permute-start(f32[1,2,64,256]{3,2,1,0:T(8,128)S(1)} %fusion.1.refs_2_), channel_id=1, source_target_pairs={{0,24},{4,28},{8,16},{12,20},{16,8},{20,12},{24,0},{28,4},{1,25},{... | collective-permute-start | bytes 393224 | tf_op jit(solution)/shard_map/ppermute | solution.py:56
  46.2 8.3 %collective-permute-start.15 = (f32[1,2,64,256]{3,2,1,0:T(8,128)S(1)}, f32[1,2,64,256]{3,2,1,0:T(8,128)S(1)}, u32[]{:S(2)}, u32[]{:S(2)}) collective-permute-start(f32[1,2,64,256]{3,2,1,0:T(8,128)S(1)} %fusion), channel_id=1, source_target_pairs={{0,24},{4,28},{8,16},{12,20},{16,8},{20,12},{24,0},{28,4},{1,25},{... | collective-permute-start | bytes 393224 | tf_op jit(solution)/shard_map/ppermute | solution.py:56
  49.5 14.3 %collective-permute-start.8 = (f32[2,512,128]{2,1,0:T(8,128)S(1)}, f32[2,512,128]{2,1,0:T(8,128)S(1)}, u32[]{:S(2)}, u32[]{:S(2)}) collective-permute-start(f32[2,512,128]{2,1,0:T(8,128)S(1)} %get-tuple-element.39), channel_id=1, source_target_pairs={{0,2},{1,3},{2,0},{3,1},{4,6},{5,7},{6,4},{7,5},{8,10},{9,11},{10,... | collective-permute-start | bytes 1572872 | tf_op jit(solution)/shard_map/ppermute | solution.py:41
  51.7 10.1 %collective-permute-start.19 = (f32[2,2,128,128]{3,2,1,0:T(8,128)S(1)}, f32[2,2,128,128]{3,2,1,0:T(8,128)S(1)}, u32[]{:S(2)}, u32[]{:S(2)}) collective-permute-start(f32[2,2,128,128]{3,2,1,0:T(8,128)S(1)} %get-tuple-element.55), channel_id=1, source_target_pairs={{0,4},{4,0},{8,12},{12,8},{16,20},{20,16},{24,28},{28,24},{1,5},{5... | collective-permute-start | bytes 786440 | tf_op jit(solution)/shard_map/ppermute | solution.py:56
  51.8 7.5 %collective-permute-start.11 = (f32[1,2,64,256]{3,2,1,0:T(8,128)S(1)}, f32[1,2,64,256]{3,2,1,0:T(8,128)S(1)}, u32[]{:S(2)}, u32[]{:S(2)}) collective-permute-start(f32[1,2,64,256]{3,2,1,0:T(8,128)S(1)} %add.59), channel_id=1, source_target_pairs={{0,8},{4,12},{8,0},{12,4},{16,24},{20,28},{24,16},{28,20},{1,9},{5... | collective-permute-start | bytes 393224 | tf_op jit(solution)/shard_map/ppermute | solution.py:56
  54.5 6.2 %collective-permute-start.16 = (f32[1,2,64,256]{3,2,1,0:T(8,128)S(1)}, f32[1,2,64,256]{3,2,1,0:T(8,128)S(1)}, u32[]{:S(2)}, u32[]{:S(2)}) collective-permute-start(f32[1,2,64,256]{3,2,1,0:T(8,128)S(1)} %add.63), channel_id=1, source_target_pairs={{0,8},{4,12},{8,0},{12,4},{16,24},{20,28},{24,16},{28,20},{1,9},{5... | collective-permute-start | bytes 393224 | tf_op jit(solution)/shard_map/ppermute | solution.py:56
  54.7 9.3 %collective-permute-start.22 = (f32[2,2,128,128]{3,2,1,0:T(8,128)S(1)}, f32[2,2,128,128]{3,2,1,0:T(8,128)S(1)}, u32[]{:S(2)}, u32[]{:S(2)}) collective-permute-start(f32[2,2,128,128]{3,2,1,0:T(8,128)S(1)} %get-tuple-element.53), channel_id=1, source_target_pairs={{0,8},{4,12},{8,0},{12,4},{16,24},{20,28},{24,16},{28,20},{1,9},{5... | collective-permute-start | bytes 786440 | tf_op jit(solution)/shard_map/ppermute | solution.py:56
  59.3 6.9 %collective-permute-start.12 = (f32[2,2,64,256]{3,2,1,0:T(8,128)S(1)}, f32[2,2,64,256]{3,2,1,0:T(8,128)S(1)}, u32[]{:S(2)}, u32[]{:S(2)}) collective-permute-start(f32[2,2,64,256]{3,2,1,0:T(8,128)S(1)} %pad_maximum_fusion.refs_2_), channel_id=1, source_target_pairs={{0,4},{4,0},{8,12},{12,8},{16,20},{20,16},{24,28},{28,24},{1,5},{5... | collective-permute-start | bytes 786440 | tf_op jit(solution)/shard_map/ppermute | solution.py:56
  60.7 7.8 %collective-permute-start.17 = (f32[2,2,64,256]{3,2,1,0:T(8,128)S(1)}, f32[2,2,64,256]{3,2,1,0:T(8,128)S(1)}, u32[]{:S(2)}, u32[]{:S(2)}) collective-permute-start(f32[2,2,64,256]{3,2,1,0:T(8,128)S(1)} %pad_maximum_fusion.1.refs_4_), channel_id=1, source_target_pairs={{0,4},{4,0},{8,12},{12,8},{16,20},{20,16},{24,28},{28,24},{1,5},{5... | collective-permute-start | bytes 786440 | tf_op jit(solution)/shard_map/ppermute | solution.py:56
  61.8 8.0 %collective-permute-start.20 = (f32[1,2,128,128]{3,2,1,0:T(8,128)S(1)}, f32[1,2,128,128]{3,2,1,0:T(8,128)S(1)}, u32[]{:S(2)}, u32[]{:S(2)}) collective-permute-start(f32[1,2,128,128]{3,2,1,0:T(8,128)S(1)} %get-tuple-element.60), channel_id=1, source_target_pairs={{0,24},{4,28},{8,16},{12,20},{16,8},{20,12},{24,0},{28,4},{1,25},{... | collective-permute-start | bytes 393224 | tf_op jit(solution)/shard_map/ppermute | solution.py:56
  63.9 4.6 %collective-permute-start.9 = (f32[1,512,128]{2,1,0:T(8,128)S(1)}, f32[1,512,128]{2,1,0:T(8,128)S(1)}, u32[]{:S(2)}, u32[]{:S(2)}) collective-permute-start(f32[1,512,128]{2,1,0:T(8,128)S(1)} %get-tuple-element.56), channel_id=1, source_target_pairs={{0,1},{1,0},{2,3},{3,2},{4,5},{5,4},{6,7},{7,6},{8,9},{9,8},{10,11... | collective-permute-start | bytes 786440 | tf_op jit(solution)/shard_map/ppermute | solution.py:41
  64.0 7.8 %collective-permute-start.23 = (f32[1,2,128,128]{3,2,1,0:T(8,128)S(1)}, f32[1,2,128,128]{3,2,1,0:T(8,128)S(1)}, u32[]{:S(2)}, u32[]{:S(2)}) collective-permute-start(f32[1,2,128,128]{3,2,1,0:T(8,128)S(1)} %get-tuple-element.58), channel_id=1, source_target_pairs={{0,24},{4,28},{8,16},{12,20},{16,8},{20,12},{24,0},{28,4},{1,25},{... | collective-permute-start | bytes 393224 | tf_op jit(solution)/shard_map/ppermute | solution.py:56
  (8 other events, 75.8 us)

commit v11 on v10

--- a/solution.py
+++ b/solution.py
@@ -131,7 +131,7 @@
 LAST_BIT = 4
 WEIGHT_PARTS = (((0, 256, (1, 2)),), ((0, 256, (1, 2)),))
 QUERY_PARTS = (((0, 2, (2, 1, 4)),), ((0, 2, (1, 2, 4)),))
-AFTER = {'i.0': 'w0.2'}
+AFTER = {'w1.2': 'q0.1', 'i.0': 'w0.3'}
 
 
 def grads_kernel(

time: 72.7 us -> 72.3 us (level)
  waiting for transfers between devices: 18.2 us -> 16.8 us
  starting transfers between devices: 35.5 us -> 36.6 us
    ppermute x22, waiting for transfers between devices: 18.2 us -> 16.8 us  [row_swap_of(): return lax.ppermute(array, 'rows', pairs)]
where the time goes in v11:
time: 72.3 us; the launch traced here: 72.1 us
  starting transfers between devices  36.6 us (51%)
  Pallas kernels  17.5 us (24%)
  waiting for transfers between devices  16.8 us (23%)
  between operations  0.9 us (1%)
    ppermute x22, starting transfers between devices, row_swap_of(): return lax.ppermute(array, 'rows', pairs)  34 us
    ppermute x22, waiting for transfers between devices, row_swap_of(): return lax.ppermute(array, 'rows', pairs)  16.8 us
    pallas_call x4, Pallas kernels, kernel_call(): pl.pallas_call(kernel, out_shape=[shape_of(*item) for item in shapes], in...  8.05 us
    pallas_call x2, Pallas kernels, on_device(): pl.pallas_call(functools.partial(first_kernel, tile) if first else functo...  6.55 us
    ppermute x2, starting transfers between devices, swap(): return lax.ppermute(array, axis, pairs)  2.61 us
  transfers between devices with their start and end apart: 24, of which 9 were waited for; matrix products, arithmetic and copies ran while one was open for 1% of the time, Pallas kernels for 17%

profile of v11, /device:TPU:0, one launch (start us, length us, event | category | flops | bytes accessed | tf_op | source)
XLA Modules:
  0.0 72.1 jit_solution(9055937914448582806)
XLA Ops:
  0.7 4.4 %project.2 = (bf16[512,128]{1,0:T(8,128)(2,1)}, bf16[512,128]{1,0:T(8,128)(2,1)}, f32[4,1024]{1,0:T(4,128)}) custom-call(bf16[512,512]{1,0:T(8,128)(2,1)} %inputs.3, bf16[512,256]{1,0:T(8,128)(2,1)} %key_weight.1, bf16[512,256]{1,0:T(8,128)(2,1)} %value_weight.1, bf16[2,1024,256]{2,1,0:T(8,128)(2,1)} %queries.4, bf16[2,1024,256]{2,1,0:T(8,128)(2,1)} %out_grad.3), custom_call_target="tpu_custom_call" | custom-call | flops 1073741824 | bytes 4194304 | tf_op jit(solution)/shard_map/project/pallas_call | solution.py:285
  5.1 3.0 %collective-permute-start = (f32[4,1024]{1,0:T(4,128)}, f32[4,1024]{1,0:T(4,128)S(1)}, u32[]{:S(2)}, u32[]{:S(2)}) collective-permute-start(f32[4,1024]{1,0:T(4,128)} %get-tuple-element.28.mine), channel_id=1, source_target_pairs={{0,4},{4,0},{8,12},{12,8},{16,20},{20,16},{24,28},{28,24},{1,5},{5... | collective-permute-start | bytes 49160 | tf_op jit(solution)/shard_map/ppermute | solution.py:56
  8.2 2.1 %project.3 = (bf16[512,128]{1,0:T(8,128)(2,1)S(1)}, bf16[512,128]{1,0:T(8,128)(2,1)S(1)}, f32[4,1024]{1,0:T(4,128)S(1)}) custom-call(bf16[512,512]{1,0:T(8,128)(2,1)S(1)} %copy-done.3, bf16[512,256]{1,0:T(8,128)(2,1)S(1)} %copy-done.4, bf16[512,256]{1,0:T(8,128)(2,1)S(1)} %copy-done.5, bf16[2,1024,256]{2,1,0:T(8,128)(2,1)S(1)} %copy-done.1, ...), custom_call_target="tpu_custom_call" | custom-call | flops 1073741824 | bytes 4194304 | tf_op jit(solution)/shard_map/project/pallas_call | solution.py:285
  10.4 2.1 %collective-permute-start.1 = (f32[4,1024]{1,0:T(4,128)S(1)}, f32[4,1024]{1,0:T(4,128)S(1)}, u32[]{:S(2)}, u32[]{:S(2)}) collective-permute-start(f32[4,1024]{1,0:T(4,128)S(1)} %merge.4.mine), channel_id=1, source_target_pairs={{0,8},{4,12},{8,0},{12,4},{16,24},{20,28},{24,16},{28,20},{1,9},{5... | collective-permute-start | bytes 49160 | tf_op jit(solution)/shard_map/ppermute | solution.py:56
  12.6 1.5 %collective-permute-done.3.theirs = f32[4,1024]{1,0:T(4,128)S(1)} collective-permute-done((f32[4,1024]{1,0:T(4,128)S(1)}, f32[4,1024]{1,0:T(4,128)S(1)}, u32[]{:S(2)}, u32[]{:S(2)}) %collective-permute-start.3) | collective-permute-done | bytes 16416 | tf_op jit(solution)/shard_map/ppermute | solution.py:56
  14.1 1.6 %collective-permute-start.4 = (f32[4,1024]{1,0:T(4,128)S(1)}, f32[4,1024]{1,0:T(4,128)S(1)}, u32[]{:S(2)}, u32[]{:S(2)}) collective-permute-start(f32[4,1024]{1,0:T(4,128)S(1)} %merge.6.mine), channel_id=1, source_target_pairs={{0,8},{4,12},{8,0},{12,4},{16,24},{20,28},{24,16},{28,20},{1,9},{5... | collective-permute-start | bytes 49160 | tf_op jit(solution)/shard_map/ppermute | solution.py:56
  15.8 2.6 %collective-permute-start.2 = (f32[4,1024]{1,0:T(4,128)S(1)}, f32[4,1024]{1,0:T(4,128)S(1)}, u32[]{:S(2)}, u32[]{:S(2)}) collective-permute-start(f32[4,1024]{1,0:T(4,128)S(1)} %merge.5.after.mine), channel_id=1, source_target_pairs={{0,24},{4,28},{8,16},{12,20},{16,8},{20,12},{24,0},{28,4},{1,25},{... | collective-permute-start | bytes 49160 | tf_op jit(solution)/shard_map/ppermute | solution.py:56
  18.5 3.2 %collective-permute-start.5 = (f32[4,1024]{1,0:T(4,128)S(1)}, f32[4,1024]{1,0:T(4,128)S(1)}, u32[]{:S(2)}, u32[]{:S(2)}) collective-permute-start(f32[4,1024]{1,0:T(4,128)S(1)} %merge.7.mine), channel_id=1, source_target_pairs={{0,24},{4,28},{8,16},{12,20},{16,8},{20,12},{24,0},{28,4},{1,25},{... | collective-permute-start | bytes 49160 | tf_op jit(solution)/shard_map/ppermute | solution.py:56
  21.6 2.9 %grads.2 = (bf16[512,256]{1,0:T(8,128)(2,1)S(1)}, bf16[2,512,1024]{2,1,0:T(8,128)(2,1)S(1)}, f32[2,2,64,256]{3,2,1,0:T(8,128)S(1)}, f32[2,2,64,256]{3,2,1,0:T(8,128)S(1)}) custom-call(f32[4,1024]{1,0:T(4,128)S(1)} %merge.5.after.mine, bf16[512,512]{1,0:T(8,128)(2,1)S(1)} %copy-done.3, bf16[512,128]{1,0:T(8,128)(2,1)S(1)} %copy-done.6, ...), custom_call_target="tpu_custom_call" | custom-call | flops 1073741824 | bytes 4194304 | tf_op jit(solution)/shard_map/grads/pallas_call | solution.py:341
  26.4 2.9 %grads.3 = (bf16[512,256]{1,0:T(8,128)(2,1)S(1)}, bf16[2,512,1024]{2,1,0:T(8,128)(2,1)S(1)}, f32[2,2,64,256]{3,2,1,0:T(8,128)S(1)}, f32[2,2,64,256]{3,2,1,0:T(8,128)S(1)}) custom-call(bf16[512,256]{1,0:T(8,128)(2,1)S(1)} %get-tuple-element.31.after.refs_0_, bf16[512,512]{1,0:T(8,128)(2,1)S(1)} %copy-done.3, bf16[512,128]{1,0:T(8,128)(2,1)S(1)} %get-tuple-element.32.keys, ...), custom_call_target="tpu_custom_call" | custom-call | flops 1073741824 | bytes 4194304 | tf_op jit(solution)/shard_map/grads/pallas_call | solution.py:341
  29.3 1.6 %collective-permute-start.13 = (f32[2,2,64,256]{3,2,1,0:T(8,128)S(1)}, f32[2,2,64,256]{3,2,1,0:T(8,128)S(1)}, u32[]{:S(2)}, u32[]{:S(2)}) collective-permute-start(f32[2,2,64,256]{3,2,1,0:T(8,128)S(1)} %get-tuple-element.41), channel_id=1, source_target_pairs={{0,4},{4,0},{8,12},{12,8},{16,20},{20,16},{24,28},{28,24},{1,5},{5... | collective-permute-start | bytes 786440 | tf_op jit(solution)/shard_map/ppermute | solution.py:56
  33.4 1.3 %collective-permute-start.7 = (f32[1,2,64,256]{3,2,1,0:T(8,128)S(1)}, f32[1,2,64,256]{3,2,1,0:T(8,128)S(1)}, u32[]{:S(2)}, u32[]{:S(2)}) collective-permute-start(f32[1,2,64,256]{3,2,1,0:T(8,128)S(1)} %slice_add_fusion.12), channel_id=1, source_target_pairs={{0,8},{4,12},{8,0},{12,4},{16,24},{20,28},{24,16},{28,20},{1,9},{5... | collective-permute-start | bytes 393224 | tf_op jit(solution)/shard_map/ppermute | solution.py:56
  34.7 4.3 %collective-permute-done.13 = f32[2,2,64,256]{3,2,1,0:T(8,128)S(1)} collective-permute-done((f32[2,2,64,256]{3,2,1,0:T(8,128)S(1)}, f32[2,2,64,256]{3,2,1,0:T(8,128)S(1)}, u32[]{:S(2)}, u32[]{:S(2)}) %collective-permute-start.13) | collective-permute-done | bytes 262176 | tf_op jit(solution)/shard_map/ppermute | solution.py:56
  39.0 1.7 %collective-permute-start.14 = (f32[1,2,64,256]{3,2,1,0:T(8,128)S(1)}, f32[1,2,64,256]{3,2,1,0:T(8,128)S(1)}, u32[]{:S(2)}, u32[]{:S(2)}) collective-permute-start(f32[1,2,64,256]{3,2,1,0:T(8,128)S(1)} %get-tuple-element.62), channel_id=1, source_target_pairs={{0,8},{4,12},{8,0},{12,4},{16,24},{20,28},{24,16},{28,20},{1,9},{5... | collective-permute-start | bytes 393224 | tf_op jit(solution)/shard_map/ppermute | solution.py:56
  41.7 4.4 %collective-permute-start.8 = (f32[1,2,64,256]{3,2,1,0:T(8,128)S(1)}, f32[1,2,64,256]{3,2,1,0:T(8,128)S(1)}, u32[]{:S(2)}, u32[]{:S(2)}) collective-permute-start(f32[1,2,64,256]{3,2,1,0:T(8,128)S(1)} %fusion), channel_id=1, source_target_pairs={{0,24},{4,28},{8,16},{12,20},{16,8},{20,12},{24,0},{28,4},{1,25},{... | collective-permute-start | bytes 393224 | tf_op jit(solution)/shard_map/ppermute | solution.py:56
  46.6 2.5 %collective-permute-start.16 = (f32[1,2,64,256]{3,2,1,0:T(8,128)S(1)}, f32[1,2,64,256]{3,2,1,0:T(8,128)S(1)}, u32[]{:S(2)}, u32[]{:S(2)}) collective-permute-start(f32[1,2,64,256]{3,2,1,0:T(8,128)S(1)} %added.1), channel_id=1, source_target_pairs={{0,24},{4,28},{8,16},{12,20},{16,8},{20,12},{24,0},{28,4},{1,25},{... | collective-permute-start | bytes 393224 | tf_op jit(solution)/shard_map/ppermute | solution.py:56
  51.2 2.5 %collective-permute-start.9 = (f32[2,512,128]{2,1,0:T(8,128)S(1)}, f32[2,512,128]{2,1,0:T(8,128)S(1)}, u32[]{:S(2)}, u32[]{:S(2)}) collective-permute-start(f32[2,512,128]{2,1,0:T(8,128)S(1)} %get-tuple-element.39), channel_id=1, source_target_pairs={{0,2},{1,3},{2,0},{3,1},{4,6},{5,7},{6,4},{7,5},{8,10},{9,11},{10,... | collective-permute-start | bytes 1572872 | tf_op jit(solution)/shard_map/ppermute | solution.py:41
  53.8 2.1 %collective-permute-start.22 = (f32[2,2,128,128]{3,2,1,0:T(8,128)S(1)}, f32[2,2,128,128]{3,2,1,0:T(8,128)S(1)}, u32[]{:S(2)}, u32[]{:S(2)}) collective-permute-start(f32[2,2,128,128]{3,2,1,0:T(8,128)S(1)} %get-tuple-element.53), channel_id=1, source_target_pairs={{0,8},{4,12},{8,0},{12,4},{16,24},{20,28},{24,16},{28,20},{1,9},{5... | collective-permute-start | bytes 786440 | tf_op jit(solution)/shard_map/ppermute | solution.py:56
  56.0 1.8 %collective-permute-done.11 = f32[1,2,64,256]{3,2,1,0:T(8,128)S(1)} collective-permute-done((f32[1,2,64,256]{3,2,1,0:T(8,128)S(1)}, f32[1,2,64,256]{3,2,1,0:T(8,128)S(1)}, u32[]{:S(2)}, u32[]{:S(2)}) %collective-permute-start.11) | collective-permute-done | bytes 131104 | tf_op jit(solution)/shard_map/ppermute | solution.py:56
  58.6 1.4 %collective-permute-start.20 = (f32[1,2,128,128]{3,2,1,0:T(8,128)S(1)}, f32[1,2,128,128]{3,2,1,0:T(8,128)S(1)}, u32[]{:S(2)}, u32[]{:S(2)}) collective-permute-start(f32[1,2,128,128]{3,2,1,0:T(8,128)S(1)} %get-tuple-element.60), channel_id=1, source_target_pairs={{0,24},{4,28},{8,16},{12,20},{16,8},{20,12},{24,0},{28,4},{1,25},{... | collective-permute-start | bytes 393224 | tf_op jit(solution)/shard_map/ppermute | solution.py:56
  60.1 2.3 %collective-permute-done.17 = f32[1,2,64,256]{3,2,1,0:T(8,128)S(1)} collective-permute-done((f32[1,2,64,256]{3,2,1,0:T(8,128)S(1)}, f32[1,2,64,256]{3,2,1,0:T(8,128)S(1)}, u32[]{:S(2)}, u32[]{:S(2)}) %collective-permute-start.17) | collective-permute-done | bytes 131104 | tf_op jit(solution)/shard_map/ppermute | solution.py:56
  63.6 2.7 %collective-permute-start.23 = (f32[1,2,128,128]{3,2,1,0:T(8,128)S(1)}, f32[1,2,128,128]{3,2,1,0:T(8,128)S(1)}, u32[]{:S(2)}, u32[]{:S(2)}) collective-permute-start(f32[1,2,128,128]{3,2,1,0:T(8,128)S(1)} %get-tuple-element.58), channel_id=1, source_target_pairs={{0,24},{4,28},{8,16},{12,20},{16,8},{20,12},{24,0},{28,4},{1,25},{... | collective-permute-start | bytes 393224 | tf_op jit(solution)/shard_map/ppermute | solution.py:56
  66.2 2.6 %collective-permute-done.18.refs_5_ = f32[2,2,64,256]{3,2,1,0:T(8,128)S(1)} collective-permute-done((f32[2,2,64,256]{3,2,1,0:T(8,128)S(1)}, f32[2,2,64,256]{3,2,1,0:T(8,128)S(1)}, u32[]{:S(2)}, u32[]{:S(2)}) %collective-permute-start.18) | collective-permute-done | bytes 262176 | tf_op jit(solution)/shard_map/ppermute | solution.py:56
  70.0 1.4 %collective-permute-done.23.refs_3_ = f32[1,2,128,128]{3,2,1,0:T(8,128)S(1)} collective-permute-done((f32[1,2,128,128]{3,2,1,0:T(8,128)S(1)}, f32[1,2,128,128]{3,2,1,0:T(8,128)S(1)}, u32[]{:S(2)}, u32[]{:S(2)}) %collective-permute-start.23) | collective-permute-done | bytes 131104 | tf_op jit(solution)/shard_map/ppermute | solution.py:56
  (66 shorter events, 12.3 us)
Async XLA Ops:
  5.1 5.3 %collective-permute-start = (f32[4,1024]{1,0:T(4,128)}, f32[4,1024]{1,0:T(4,128)S(1)}, u32[]{:S(2)}, u32[]{:S(2)}) collective-permute-start(f32[4,1024]{1,0:T(4,128)} %get-tuple-element.28.mine), channel_id=1, source_target_pairs={{0,4},{4,0},{8,12},{12,8},{16,20},{20,16},{24,28},{28,24},{1,5},{5... | collective-permute-start | bytes 49160 | tf_op jit(solution)/shard_map/ppermute | solution.py:56
  10.3 3.8 %collective-permute-start.3 = (f32[4,1024]{1,0:T(4,128)S(1)}, f32[4,1024]{1,0:T(4,128)S(1)}, u32[]{:S(2)}, u32[]{:S(2)}) collective-permute-start(f32[4,1024]{1,0:T(4,128)S(1)} %get-tuple-element.34.mine), channel_id=1, source_target_pairs={{0,4},{4,0},{8,12},{12,8},{16,20},{20,16},{24,28},{28,24},{1,5},{5... | collective-permute-start | bytes 49160 | tf_op jit(solution)/shard_map/ppermute | solution.py:56
  10.4 5.3 %collective-permute-start.1 = (f32[4,1024]{1,0:T(4,128)S(1)}, f32[4,1024]{1,0:T(4,128)S(1)}, u32[]{:S(2)}, u32[]{:S(2)}) collective-permute-start(f32[4,1024]{1,0:T(4,128)S(1)} %merge.4.mine), channel_id=1, source_target_pairs={{0,8},{4,12},{8,0},{12,4},{16,24},{20,28},{24,16},{28,20},{1,9},{5... | collective-permute-start | bytes 49160 | tf_op jit(solution)/shard_map/ppermute | solution.py:56
  14.1 4.3 %collective-permute-start.4 = (f32[4,1024]{1,0:T(4,128)S(1)}, f32[4,1024]{1,0:T(4,128)S(1)}, u32[]{:S(2)}, u32[]{:S(2)}) collective-permute-start(f32[4,1024]{1,0:T(4,128)S(1)} %merge.6.mine), channel_id=1, source_target_pairs={{0,8},{4,12},{8,0},{12,4},{16,24},{20,28},{24,16},{28,20},{1,9},{5... | collective-permute-start | bytes 49160 | tf_op jit(solution)/shard_map/ppermute | solution.py:56
  15.8 5.8 %collective-permute-start.2 = (f32[4,1024]{1,0:T(4,128)S(1)}, f32[4,1024]{1,0:T(4,128)S(1)}, u32[]{:S(2)}, u32[]{:S(2)}) collective-permute-start(f32[4,1024]{1,0:T(4,128)S(1)} %merge.5.after.mine), channel_id=1, source_target_pairs={{0,24},{4,28},{8,16},{12,20},{16,8},{20,12},{24,0},{28,4},{1,25},{... | collective-permute-start | bytes 49160 | tf_op jit(solution)/shard_map/ppermute | solution.py:56
  18.5 7.9 %collective-permute-start.5 = (f32[4,1024]{1,0:T(4,128)S(1)}, f32[4,1024]{1,0:T(4,128)S(1)}, u32[]{:S(2)}, u32[]{:S(2)}) collective-permute-start(f32[4,1024]{1,0:T(4,128)S(1)} %merge.7.mine), channel_id=1, source_target_pairs={{0,24},{4,28},{8,16},{12,20},{16,8},{20,12},{24,0},{28,4},{1,25},{... | collective-permute-start | bytes 49160 | tf_op jit(solution)/shard_map/ppermute | solution.py:56
  24.6 8.8 %collective-permute-start.6 = (f32[2,2,64,256]{3,2,1,0:T(8,128)S(1)}, f32[2,2,64,256]{3,2,1,0:T(8,128)S(1)}, u32[]{:S(2)}, u32[]{:S(2)}) collective-permute-start(f32[2,2,64,256]{3,2,1,0:T(8,128)S(1)} %get-tuple-element.37), channel_id=1, source_target_pairs={{0,4},{4,0},{8,12},{12,8},{16,20},{20,16},{24,28},{28,24},{1,5},{5... | collective-permute-start | bytes 786440 | tf_op jit(solution)/shard_map/ppermute | solution.py:56
  26.3 19.9 %collective-permute-start.15 = (f32[4,2,128,128]{3,2,1,0:T(8,128)S(1)}, f32[4,2,128,128]{3,2,1,0:T(8,128)S(1)}, u32[]{:S(2)}, u32[]{:S(2)}) collective-permute-start(f32[4,2,128,128]{3,2,1,0:T(8,128)S(1)} %get-tuple-element.44), channel_id=1, source_target_pairs={{0,8},{4,12},{8,0},{12,4},{16,24},{20,28},{24,16},{28,20},{1,9},{5... | collective-permute-start | bytes 1572872 | tf_op jit(solution)/shard_map/ppermute | solution.py:56
  29.3 9.7 %collective-permute-start.13 = (f32[2,2,64,256]{3,2,1,0:T(8,128)S(1)}, f32[2,2,64,256]{3,2,1,0:T(8,128)S(1)}, u32[]{:S(2)}, u32[]{:S(2)}) collective-permute-start(f32[2,2,64,256]{3,2,1,0:T(8,128)S(1)} %get-tuple-element.41), channel_id=1, source_target_pairs={{0,4},{4,0},{8,12},{12,8},{16,20},{20,16},{24,28},{28,24},{1,5},{5... | collective-permute-start | bytes 786440 | tf_op jit(solution)/shard_map/ppermute | solution.py:56
  32.0 21.7 %collective-permute-start.21 = (f32[4,2,128,128]{3,2,1,0:T(8,128)S(1)}, f32[4,2,128,128]{3,2,1,0:T(8,128)S(1)}, u32[]{:S(2)}, u32[]{:S(2)}) collective-permute-start(f32[4,2,128,128]{3,2,1,0:T(8,128)S(1)} %get-tuple-element.48), channel_id=1, source_target_pairs={{0,4},{4,0},{8,12},{12,8},{16,20},{20,16},{24,28},{28,24},{1,5},{5... | collective-permute-start | bytes 1572872 | tf_op jit(solution)/shard_map/ppermute | solution.py:56
  33.4 8.3 %collective-permute-start.7 = (f32[1,2,64,256]{3,2,1,0:T(8,128)S(1)}, f32[1,2,64,256]{3,2,1,0:T(8,128)S(1)}, u32[]{:S(2)}, u32[]{:S(2)}) collective-permute-start(f32[1,2,64,256]{3,2,1,0:T(8,128)S(1)} %slice_add_fusion.12), channel_id=1, source_target_pairs={{0,8},{4,12},{8,0},{12,4},{16,24},{20,28},{24,16},{28,20},{1,9},{5... | collective-permute-start | bytes 393224 | tf_op jit(solution)/shard_map/ppermute | solution.py:56
  39.0 7.6 %collective-permute-start.14 = (f32[1,2,64,256]{3,2,1,0:T(8,128)S(1)}, f32[1,2,64,256]{3,2,1,0:T(8,128)S(1)}, u32[]{:S(2)}, u32[]{:S(2)}) collective-permute-start(f32[1,2,64,256]{3,2,1,0:T(8,128)S(1)} %get-tuple-element.62), channel_id=1, source_target_pairs={{0,8},{4,12},{8,0},{12,4},{16,24},{20,28},{24,16},{28,20},{1,9},{5... | collective-permute-start | bytes 393224 | tf_op jit(solution)/shard_map/ppermute | solution.py:56
  41.7 8.5 %collective-permute-start.8 = (f32[1,2,64,256]{3,2,1,0:T(8,128)S(1)}, f32[1,2,64,256]{3,2,1,0:T(8,128)S(1)}, u32[]{:S(2)}, u32[]{:S(2)}) collective-permute-start(f32[1,2,64,256]{3,2,1,0:T(8,128)S(1)} %fusion), channel_id=1, source_target_pairs={{0,24},{4,28},{8,16},{12,20},{16,8},{20,12},{24,0},{28,4},{1,25},{... | collective-permute-start | bytes 393224 | tf_op jit(solution)/shard_map/ppermute | solution.py:56
  46.2 12.4 %collective-permute-start.19 = (f32[2,2,128,128]{3,2,1,0:T(8,128)S(1)}, f32[2,2,128,128]{3,2,1,0:T(8,128)S(1)}, u32[]{:S(2)}, u32[]{:S(2)}) collective-permute-start(f32[2,2,128,128]{3,2,1,0:T(8,128)S(1)} %get-tuple-element.55.after), channel_id=1, source_target_pairs={{0,4},{4,0},{8,12},{12,8},{16,20},{20,16},{24,28},{28,24},{1,5},{5... | collective-permute-start | bytes 786440 | tf_op jit(solution)/shard_map/ppermute | solution.py:56
  46.6 9.2 %collective-permute-start.16 = (f32[1,2,64,256]{3,2,1,0:T(8,128)S(1)}, f32[1,2,64,256]{3,2,1,0:T(8,128)S(1)}, u32[]{:S(2)}, u32[]{:S(2)}) collective-permute-start(f32[1,2,64,256]{3,2,1,0:T(8,128)S(1)} %added.1), channel_id=1, source_target_pairs={{0,24},{4,28},{8,16},{12,20},{16,8},{20,12},{24,0},{28,4},{1,25},{... | collective-permute-start | bytes 393224 | tf_op jit(solution)/shard_map/ppermute | solution.py:56
  50.2 7.5 %collective-permute-start.11 = (f32[1,2,64,256]{3,2,1,0:T(8,128)S(1)}, f32[1,2,64,256]{3,2,1,0:T(8,128)S(1)}, u32[]{:S(2)}, u32[]{:S(2)}) collective-permute-start(f32[1,2,64,256]{3,2,1,0:T(8,128)S(1)} %add.54.refs_2_), channel_id=1, source_target_pairs={{0,8},{4,12},{8,0},{12,4},{16,24},{20,28},{24,16},{28,20},{1,9},{5... | collective-permute-start | bytes 393224 | tf_op jit(solution)/shard_map/ppermute | solution.py:56
  51.2 12.2 %collective-permute-start.9 = (f32[2,512,128]{2,1,0:T(8,128)S(1)}, f32[2,512,128]{2,1,0:T(8,128)S(1)}, u32[]{:S(2)}, u32[]{:S(2)}) collective-permute-start(f32[2,512,128]{2,1,0:T(8,128)S(1)} %get-tuple-element.39), channel_id=1, source_target_pairs={{0,2},{1,3},{2,0},{3,1},{4,6},{5,7},{6,4},{7,5},{8,10},{9,11},{10,... | collective-permute-start | bytes 1572872 | tf_op jit(solution)/shard_map/ppermute | solution.py:41
  53.8 9.7 %collective-permute-start.22 = (f32[2,2,128,128]{3,2,1,0:T(8,128)S(1)}, f32[2,2,128,128]{3,2,1,0:T(8,128)S(1)}, u32[]{:S(2)}, u32[]{:S(2)}) collective-permute-start(f32[2,2,128,128]{3,2,1,0:T(8,128)S(1)} %get-tuple-element.53), channel_id=1, source_target_pairs={{0,8},{4,12},{8,0},{12,4},{16,24},{20,28},{24,16},{28,20},{1,9},{5... | collective-permute-start | bytes 786440 | tf_op jit(solution)/shard_map/ppermute | solution.py:56
  55.9 6.5 %collective-permute-start.17 = (f32[1,2,64,256]{3,2,1,0:T(8,128)S(1)}, f32[1,2,64,256]{3,2,1,0:T(8,128)S(1)}, u32[]{:S(2)}, u32[]{:S(2)}) collective-permute-start(f32[1,2,64,256]{3,2,1,0:T(8,128)S(1)} %add.60), channel_id=1, source_target_pairs={{0,8},{4,12},{8,0},{12,4},{16,24},{20,28},{24,16},{28,20},{1,9},{5... | collective-permute-start | bytes 393224 | tf_op jit(solution)/shard_map/ppermute | solution.py:56
  57.8 8.5 %collective-permute-start.12 = (f32[2,2,64,256]{3,2,1,0:T(8,128)S(1)}, f32[2,2,64,256]{3,2,1,0:T(8,128)S(1)}, u32[]{:S(2)}, u32[]{:S(2)}) collective-permute-start(f32[2,2,64,256]{3,2,1,0:T(8,128)S(1)} %pad_maximum_fusion.refs_2_), channel_id=1, source_target_pairs={{0,4},{4,0},{8,12},{12,8},{16,20},{20,16},{24,28},{28,24},{1,5},{5... | collective-permute-start | bytes 786440 | tf_op jit(solution)/shard_map/ppermute | solution.py:56
  58.6 11.3 %collective-permute-start.20 = (f32[1,2,128,128]{3,2,1,0:T(8,128)S(1)}, f32[1,2,128,128]{3,2,1,0:T(8,128)S(1)}, u32[]{:S(2)}, u32[]{:S(2)}) collective-permute-start(f32[1,2,128,128]{3,2,1,0:T(8,128)S(1)} %get-tuple-element.60), channel_id=1, source_target_pairs={{0,24},{4,28},{8,16},{12,20},{16,8},{20,12},{24,0},{28,4},{1,25},{... | collective-permute-start | bytes 393224 | tf_op jit(solution)/shard_map/ppermute | solution.py:56
  62.4 6.4 %collective-permute-start.18 = (f32[2,2,64,256]{3,2,1,0:T(8,128)S(1)}, f32[2,2,64,256]{3,2,1,0:T(8,128)S(1)}, u32[]{:S(2)}, u32[]{:S(2)}) collective-permute-start(f32[2,2,64,256]{3,2,1,0:T(8,128)S(1)} %pad_maximum_fusion.1.refs_4_), channel_id=1, source_target_pairs={{0,4},{4,0},{8,12},{12,8},{16,20},{20,16},{24,28},{28,24},{1,5},{5... | collective-permute-start | bytes 786440 | tf_op jit(solution)/shard_map/ppermute | solution.py:56
  63.4 5.4 %collective-permute-start.10 = (f32[1,512,128]{2,1,0:T(8,128)S(1)}, f32[1,512,128]{2,1,0:T(8,128)S(1)}, u32[]{:S(2)}, u32[]{:S(2)}) collective-permute-start(f32[1,512,128]{2,1,0:T(8,128)S(1)} %get-tuple-element.56), channel_id=1, source_target_pairs={{0,1},{1,0},{2,3},{3,2},{4,5},{5,4},{6,7},{7,6},{8,9},{9,8},{10,11... | collective-permute-start | bytes 786440 | tf_op jit(solution)/shard_map/ppermute | solution.py:41
  63.6 7.9 %collective-permute-start.23 = (f32[1,2,128,128]{3,2,1,0:T(8,128)S(1)}, f32[1,2,128,128]{3,2,1,0:T(8,128)S(1)}, u32[]{:S(2)}, u32[]{:S(2)}) collective-permute-start(f32[1,2,128,128]{3,2,1,0:T(8,128)S(1)} %get-tuple-element.58), channel_id=1, source_target_pairs={{0,24},{4,28},{8,16},{12,20},{16,8},{20,12},{24,0},{28,4},{1,25},{... | collective-permute-start | bytes 393224 | tf_op jit(solution)/shard_map/ppermute | solution.py:56
  (8 other events, 75.8 us)

commit v12 on v11

--- a/solution.py
+++ b/solution.py
@@ -304,7 +304,7 @@
     for head_index in range(head_count):
         stats = projected[head_index][2]
         for bit in bits_of(row_devices)[:-1]:
-            theirs = row_swap_of(stats, row_devices, bit)
+            theirs = swap(stats, "rows", row_devices, bit)
             stats = pl.pallas_call(
                 merge_kernel,
                 out_shape=shape_of(stats.shape),
@@ -313,7 +313,7 @@
                 compiler_params=params(2),
                 name="merge",
             )(stats, theirs)
-        stats_parts.append((stats, row_swap_of(stats, row_devices, bits_of(row_devices)[-1])))
+        stats_parts.append((stats, swap(stats, "rows", row_devices, bits_of(row_devices)[-1])))
 
     order_low = (lax.axis_index("rows") % low) ^ jnp.arange(low, dtype=jnp.int32)
     low_bits = [bit for bit in bits_of(row_devices) if bit < low]

time: 72.3 us -> 71.6 us (level)
  waiting for transfers between devices: 16.8 us -> 15.5 us
    ppermute x2 -> x8, starting transfers between devices: 2.61 us -> 14.1 us  [swap(): return lax.ppermute(array, axis, pairs)]
    ppermute x22 -> x16, starting transfers between devices: 34 us -> 23 us  [row_swap_of(): return lax.ppermute(array, 'rows', pairs)]
    ppermute x22 -> x16, waiting for transfers between devices: 16.8 us -> 14 us  [row_swap_of(): return lax.ppermute(array, 'rows', pairs)]
    ppermute x2 -> x8, waiting for transfers between devices: 0.01 us -> 1.54 us  [swap(): return lax.ppermute(array, axis, pairs)]
where the time goes in v12:
time: 71.6 us; the launch traced here: 71.5 us
  starting transfers between devices  37.2 us (52%)
  Pallas kernels  17.4 us (24%)
  waiting for transfers between devices  15.5 us (22%)
  between operations  0.89 us (1%)
    ppermute x16, starting transfers between devices, row_swap_of(): return lax.ppermute(array, 'rows', pairs)  23 us
    ppermute x8, starting transfers between devices, swap(): return lax.ppermute(array, axis, pairs)  14.1 us
    ppermute x16, waiting for transfers between devices, row_swap_of(): return lax.ppermute(array, 'rows', pairs)  14 us
    pallas_call x4, Pallas kernels, kernel_call(): pl.pallas_call(kernel, out_shape=[shape_of(*item) for item in shapes], in...  8.03 us
    pallas_call x2, Pallas kernels, on_device(): pl.pallas_call(functools.partial(first_kernel, tile) if first else functo...  6.55 us
    ppermute x8, waiting for transfers between devices, swap(): return lax.ppermute(array, axis, pairs)  1.54 us
  transfers between devices with their start and end apart: 24, of which 9 were waited for; matrix products, arithmetic and copies ran while one was open for 1% of the time, Pallas kernels for 17%

profile of v12, /device:TPU:0, one launch (start us, length us, event | category | flops | bytes accessed | tf_op | source)
XLA Modules:
  0.0 71.5 jit_solution(17441351672940793781)
XLA Ops:
  0.7 4.4 %project.2 = (bf16[512,128]{1,0:T(8,128)(2,1)}, bf16[512,128]{1,0:T(8,128)(2,1)}, f32[4,1024]{1,0:T(4,128)}) custom-call(bf16[512,512]{1,0:T(8,128)(2,1)} %inputs.3, bf16[512,256]{1,0:T(8,128)(2,1)} %key_weight.1, bf16[512,256]{1,0:T(8,128)(2,1)} %value_weight.1, bf16[2,1024,256]{2,1,0:T(8,128)(2,1)} %queries.4, bf16[2,1024,256]{2,1,0:T(8,128)(2,1)} %out_grad.3), custom_call_target="tpu_custom_call" | custom-call | flops 1073741824 | bytes 4194304 | tf_op jit(solution)/shard_map/project/pallas_call | solution.py:285
  5.1 3.0 %collective-permute-start = (f32[4,1024]{1,0:T(4,128)}, f32[4,1024]{1,0:T(4,128)S(1)}, u32[]{:S(2)}, u32[]{:S(2)}) collective-permute-start(f32[4,1024]{1,0:T(4,128)} %get-tuple-element.28.mine), channel_id=1, source_target_pairs={{0,4},{4,0},{8,12},{12,8},{16,20},{20,16},{24,28},{28,24},{1,5},{5... | collective-permute-start | bytes 49160 | tf_op jit(solution)/shard_map/ppermute | solution.py:41
  8.2 2.1 %project.3 = (bf16[512,128]{1,0:T(8,128)(2,1)S(1)}, bf16[512,128]{1,0:T(8,128)(2,1)S(1)}, f32[4,1024]{1,0:T(4,128)S(1)}) custom-call(bf16[512,512]{1,0:T(8,128)(2,1)S(1)} %copy-done.3, bf16[512,256]{1,0:T(8,128)(2,1)S(1)} %copy-done.4, bf16[512,256]{1,0:T(8,128)(2,1)S(1)} %copy-done.5, bf16[2,1024,256]{2,1,0:T(8,128)(2,1)S(1)} %copy-done.1, ...), custom_call_target="tpu_custom_call" | custom-call | flops 1073741824 | bytes 4194304 | tf_op jit(solution)/shard_map/project/pallas_call | solution.py:285
  10.4 2.1 %collective-permute-start.1 = (f32[4,1024]{1,0:T(4,128)S(1)}, f32[4,1024]{1,0:T(4,128)S(1)}, u32[]{:S(2)}, u32[]{:S(2)}) collective-permute-start(f32[4,1024]{1,0:T(4,128)S(1)} %merge.4.mine), channel_id=1, source_target_pairs={{0,8},{4,12},{8,0},{12,4},{16,24},{20,28},{24,16},{28,20},{1,9},{5... | collective-permute-start | bytes 49160 | tf_op jit(solution)/shard_map/ppermute | solution.py:41
  12.6 1.5 %collective-permute-done.3.theirs = f32[4,1024]{1,0:T(4,128)S(1)} collective-permute-done((f32[4,1024]{1,0:T(4,128)S(1)}, f32[4,1024]{1,0:T(4,128)S(1)}, u32[]{:S(2)}, u32[]{:S(2)}) %collective-permute-start.3) | collective-permute-done | bytes 16416 | tf_op jit(solution)/shard_map/ppermute | solution.py:41
  14.1 1.6 %collective-permute-start.4 = (f32[4,1024]{1,0:T(4,128)S(1)}, f32[4,1024]{1,0:T(4,128)S(1)}, u32[]{:S(2)}, u32[]{:S(2)}) collective-permute-start(f32[4,1024]{1,0:T(4,128)S(1)} %merge.6.mine), channel_id=1, source_target_pairs={{0,8},{4,12},{8,0},{12,4},{16,24},{20,28},{24,16},{28,20},{1,9},{5... | collective-permute-start | bytes 49160 | tf_op jit(solution)/shard_map/ppermute | solution.py:41
  15.8 2.7 %collective-permute-start.2 = (f32[4,1024]{1,0:T(4,128)S(1)}, f32[4,1024]{1,0:T(4,128)S(1)}, u32[]{:S(2)}, u32[]{:S(2)}) collective-permute-start(f32[4,1024]{1,0:T(4,128)S(1)} %merge.5.after.mine), channel_id=1, source_target_pairs={{0,16},{4,20},{8,24},{12,28},{16,0},{20,4},{24,8},{28,12},{1,17},{... | collective-permute-start | bytes 49160 | tf_op jit(solution)/shard_map/ppermute | solution.py:41
  18.5 2.2 %collective-permute-start.5 = (f32[4,1024]{1,0:T(4,128)S(1)}, f32[4,1024]{1,0:T(4,128)S(1)}, u32[]{:S(2)}, u32[]{:S(2)}) collective-permute-start(f32[4,1024]{1,0:T(4,128)S(1)} %merge.7.mine), channel_id=1, source_target_pairs={{0,16},{4,20},{8,24},{12,28},{16,0},{20,4},{24,8},{28,12},{1,17},{... | collective-permute-start | bytes 49160 | tf_op jit(solution)/shard_map/ppermute | solution.py:41
  20.7 2.9 %grads.2 = (bf16[512,256]{1,0:T(8,128)(2,1)S(1)}, bf16[2,512,1024]{2,1,0:T(8,128)(2,1)S(1)}, f32[2,2,64,256]{3,2,1,0:T(8,128)S(1)}, f32[2,2,64,256]{3,2,1,0:T(8,128)S(1)}) custom-call(f32[4,1024]{1,0:T(4,128)S(1)} %merge.5.after.mine, bf16[512,512]{1,0:T(8,128)(2,1)S(1)} %copy-done.3, bf16[512,128]{1,0:T(8,128)(2,1)S(1)} %copy-done.6, ...), custom_call_target="tpu_custom_call" | custom-call | flops 1073741824 | bytes 4194304 | tf_op jit(solution)/shard_map/grads/pallas_call | solution.py:341
  25.3 1.8 %collective-permute-start.15 = (f32[4,2,128,128]{3,2,1,0:T(8,128)S(1)}, f32[4,2,128,128]{3,2,1,0:T(8,128)S(1)}, u32[]{:S(2)}, u32[]{:S(2)}) collective-permute-start(f32[4,2,128,128]{3,2,1,0:T(8,128)S(1)} %get-tuple-element.44), channel_id=1, source_target_pairs={{0,8},{4,12},{8,0},{12,4},{16,24},{20,28},{24,16},{28,20},{1,9},{5... | collective-permute-start | bytes 1572872 | tf_op jit(solution)/shard_map/ppermute | solution.py:56
  27.1 2.9 %grads.3 = (bf16[512,256]{1,0:T(8,128)(2,1)S(1)}, bf16[2,512,1024]{2,1,0:T(8,128)(2,1)S(1)}, f32[2,2,64,256]{3,2,1,0:T(8,128)S(1)}, f32[2,2,64,256]{3,2,1,0:T(8,128)S(1)}) custom-call(bf16[512,256]{1,0:T(8,128)(2,1)S(1)} %get-tuple-element.31.after.refs_0_, bf16[512,512]{1,0:T(8,128)(2,1)S(1)} %copy-done.3, bf16[512,128]{1,0:T(8,128)(2,1)S(1)} %get-tuple-element.32.keys, ...), custom_call_target="tpu_custom_call" | custom-call | flops 1073741824 | bytes 4194304 | tf_op jit(solution)/shard_map/grads/pallas_call | solution.py:341
  30.0 1.5 %collective-permute-start.13 = (f32[2,2,64,256]{3,2,1,0:T(8,128)S(1)}, f32[2,2,64,256]{3,2,1,0:T(8,128)S(1)}, u32[]{:S(2)}, u32[]{:S(2)}) collective-permute-start(f32[2,2,64,256]{3,2,1,0:T(8,128)S(1)} %get-tuple-element.41), channel_id=1, source_target_pairs={{0,4},{4,0},{8,12},{12,8},{16,20},{20,16},{24,28},{28,24},{1,5},{5... | collective-permute-start | bytes 786440 | tf_op jit(solution)/shard_map/ppermute | solution.py:56
  31.4 1.1 %query.3 = (f32[4,2,128,128]{3,2,1,0:T(8,128)S(1)}, f32[4,2,128,128]{3,2,1,0:T(8,128)S(1)}) custom-call(bf16[512,256]{1,0:T(8,128)(2,1)S(1)} %get-tuple-element.35.refs_1_.after, bf16[2,512,1024]{2,1,0:T(8,128)(2,1)S(1)} %get-tuple-element.46.score_grads, bf16[512,128]{1,0:T(8,128)(2,1)S(1)} %get-tuple-element.32.keys), custom_call_target="tpu_custom_call" | custom-call | flops 1073741824 | bytes 4194304 | tf_op jit(solution)/shard_map/query/pallas_call | solution.py:341
  33.9 5.4 %collective-permute-done.13 = f32[2,2,64,256]{3,2,1,0:T(8,128)S(1)} collective-permute-done((f32[2,2,64,256]{3,2,1,0:T(8,128)S(1)}, f32[2,2,64,256]{3,2,1,0:T(8,128)S(1)}, u32[]{:S(2)}, u32[]{:S(2)}) %collective-permute-start.13) | collective-permute-done | bytes 262176 | tf_op jit(solution)/shard_map/ppermute | solution.py:56
  40.1 5.3 %collective-permute-start.8 = (f32[1,2,64,256]{3,2,1,0:T(8,128)S(1)}, f32[1,2,64,256]{3,2,1,0:T(8,128)S(1)}, u32[]{:S(2)}, u32[]{:S(2)}) collective-permute-start(f32[1,2,64,256]{3,2,1,0:T(8,128)S(1)} %fusion), channel_id=1, source_target_pairs={{0,24},{4,28},{8,16},{12,20},{16,8},{20,12},{24,0},{28,4},{1,25},{... | collective-permute-start | bytes 393224 | tf_op jit(solution)/shard_map/ppermute | solution.py:56
  46.0 2.5 %collective-permute-start.16 = (f32[1,2,64,256]{3,2,1,0:T(8,128)S(1)}, f32[1,2,64,256]{3,2,1,0:T(8,128)S(1)}, u32[]{:S(2)}, u32[]{:S(2)}) collective-permute-start(f32[1,2,64,256]{3,2,1,0:T(8,128)S(1)} %added.1), channel_id=1, source_target_pairs={{0,24},{4,28},{8,16},{12,20},{16,8},{20,12},{24,0},{28,4},{1,25},{... | collective-permute-start | bytes 393224 | tf_op jit(solution)/shard_map/ppermute | solution.py:56
  50.5 2.3 %collective-permute-start.9 = (f32[2,512,128]{2,1,0:T(8,128)S(1)}, f32[2,512,128]{2,1,0:T(8,128)S(1)}, u32[]{:S(2)}, u32[]{:S(2)}) collective-permute-start(f32[2,512,128]{2,1,0:T(8,128)S(1)} %get-tuple-element.39), channel_id=1, source_target_pairs={{0,2},{1,3},{2,0},{3,1},{4,6},{5,7},{6,4},{7,5},{8,10},{9,11},{10,... | collective-permute-start | bytes 1572872 | tf_op jit(solution)/shard_map/ppermute | solution.py:41
  52.9 2.1 %collective-permute-start.22 = (f32[2,2,128,128]{3,2,1,0:T(8,128)S(1)}, f32[2,2,128,128]{3,2,1,0:T(8,128)S(1)}, u32[]{:S(2)}, u32[]{:S(2)}) collective-permute-start(f32[2,2,128,128]{3,2,1,0:T(8,128)S(1)} %get-tuple-element.53), channel_id=1, source_target_pairs={{0,8},{4,12},{8,0},{12,4},{16,24},{20,28},{24,16},{28,20},{1,9},{5... | collective-permute-start | bytes 786440 | tf_op jit(solution)/shard_map/ppermute | solution.py:56
  55.1 1.4 %collective-permute-done.11 = f32[1,2,64,256]{3,2,1,0:T(8,128)S(1)} collective-permute-done((f32[1,2,64,256]{3,2,1,0:T(8,128)S(1)}, f32[1,2,64,256]{3,2,1,0:T(8,128)S(1)}, u32[]{:S(2)}, u32[]{:S(2)}) %collective-permute-start.11) | collective-permute-done | bytes 131104 | tf_op jit(solution)/shard_map/ppermute | solution.py:56
  57.1 3.6 %collective-permute-start.20 = (f32[1,2,128,128]{3,2,1,0:T(8,128)S(1)}, f32[1,2,128,128]{3,2,1,0:T(8,128)S(1)}, u32[]{:S(2)}, u32[]{:S(2)}) collective-permute-start(f32[1,2,128,128]{3,2,1,0:T(8,128)S(1)} %get-tuple-element.60), channel_id=1, source_target_pairs={{0,24},{4,28},{8,16},{12,20},{16,8},{20,12},{24,0},{28,4},{1,25},{... | collective-permute-start | bytes 393224 | tf_op jit(solution)/shard_map/ppermute | solution.py:56
  62.9 2.4 %collective-permute-start.23 = (f32[1,2,128,128]{3,2,1,0:T(8,128)S(1)}, f32[1,2,128,128]{3,2,1,0:T(8,128)S(1)}, u32[]{:S(2)}, u32[]{:S(2)}) collective-permute-start(f32[1,2,128,128]{3,2,1,0:T(8,128)S(1)} %get-tuple-element.58), channel_id=1, source_target_pairs={{0,24},{4,28},{8,16},{12,20},{16,8},{20,12},{24,0},{28,4},{1,25},{... | collective-permute-start | bytes 393224 | tf_op jit(solution)/shard_map/ppermute | solution.py:56
  65.3 3.0 %collective-permute-done.18.refs_5_ = f32[2,2,64,256]{3,2,1,0:T(8,128)S(1)} collective-permute-done((f32[2,2,64,256]{3,2,1,0:T(8,128)S(1)}, f32[2,2,64,256]{3,2,1,0:T(8,128)S(1)}, u32[]{:S(2)}, u32[]{:S(2)}) %collective-permute-start.18) | collective-permute-done | bytes 262176 | tf_op jit(solution)/shard_map/ppermute | solution.py:56
  68.3 1.2 %weights.1 = (f32[512,256]{1,0:T(8,128)}, f32[512,256]{1,0:T(8,128)}, f32[512,128]{1,0:T(8,128)}, f32[8,128]{1,0:T(8,128)S(1)}) custom-call(f32[1,512,128]{2,1,0:T(8,128)S(1)} %get-tuple-element.57.refs_0_, f32[1,512,128]{2,1,0:T(8,128)S(1)} %collective-permute-done.10.refs_1_, f32[2,2,64,256]{3,2,1,0:T(8,128)S(1)} %pad_maximum_fusion.refs_2_, ...), custom_call_target="tpu_custom_call" | custom-call | tf_op jit(solution)/shard_map/weights/pallas_call | solution.py:470
  69.5 1.3 %collective-permute-done.23.refs_3_ = f32[1,2,128,128]{3,2,1,0:T(8,128)S(1)} collective-permute-done((f32[1,2,128,128]{3,2,1,0:T(8,128)S(1)}, f32[1,2,128,128]{3,2,1,0:T(8,128)S(1)}, u32[]{:S(2)}, u32[]{:S(2)}) %collective-permute-start.23) | collective-permute-done | bytes 131104 | tf_op jit(solution)/shard_map/ppermute | solution.py:56
  (66 shorter events, 10.3 us)
Async XLA Ops:
  5.1 5.3 %collective-permute-start = (f32[4,1024]{1,0:T(4,128)}, f32[4,1024]{1,0:T(4,128)S(1)}, u32[]{:S(2)}, u32[]{:S(2)}) collective-permute-start(f32[4,1024]{1,0:T(4,128)} %get-tuple-element.28.mine), channel_id=1, source_target_pairs={{0,4},{4,0},{8,12},{12,8},{16,20},{20,16},{24,28},{28,24},{1,5},{5... | collective-permute-start | bytes 49160 | tf_op jit(solution)/shard_map/ppermute | solution.py:41
  10.3 3.8 %collective-permute-start.3 = (f32[4,1024]{1,0:T(4,128)S(1)}, f32[4,1024]{1,0:T(4,128)S(1)}, u32[]{:S(2)}, u32[]{:S(2)}) collective-permute-start(f32[4,1024]{1,0:T(4,128)S(1)} %get-tuple-element.34.mine), channel_id=1, source_target_pairs={{0,4},{4,0},{8,12},{12,8},{16,20},{20,16},{24,28},{28,24},{1,5},{5... | collective-permute-start | bytes 49160 | tf_op jit(solution)/shard_map/ppermute | solution.py:41
  10.4 5.3 %collective-permute-start.1 = (f32[4,1024]{1,0:T(4,128)S(1)}, f32[4,1024]{1,0:T(4,128)S(1)}, u32[]{:S(2)}, u32[]{:S(2)}) collective-permute-start(f32[4,1024]{1,0:T(4,128)S(1)} %merge.4.mine), channel_id=1, source_target_pairs={{0,8},{4,12},{8,0},{12,4},{16,24},{20,28},{24,16},{28,20},{1,9},{5... | collective-permute-start | bytes 49160 | tf_op jit(solution)/shard_map/ppermute | solution.py:41
  14.1 4.3 %collective-permute-start.4 = (f32[4,1024]{1,0:T(4,128)S(1)}, f32[4,1024]{1,0:T(4,128)S(1)}, u32[]{:S(2)}, u32[]{:S(2)}) collective-permute-start(f32[4,1024]{1,0:T(4,128)S(1)} %merge.6.mine), channel_id=1, source_target_pairs={{0,8},{4,12},{8,0},{12,4},{16,24},{20,28},{24,16},{28,20},{1,9},{5... | collective-permute-start | bytes 49160 | tf_op jit(solution)/shard_map/ppermute | solution.py:41
  15.8 4.9 %collective-permute-start.2 = (f32[4,1024]{1,0:T(4,128)S(1)}, f32[4,1024]{1,0:T(4,128)S(1)}, u32[]{:S(2)}, u32[]{:S(2)}) collective-permute-start(f32[4,1024]{1,0:T(4,128)S(1)} %merge.5.after.mine), channel_id=1, source_target_pairs={{0,16},{4,20},{8,24},{12,28},{16,0},{20,4},{24,8},{28,12},{1,17},{... | collective-permute-start | bytes 49160 | tf_op jit(solution)/shard_map/ppermute | solution.py:41
  18.5 8.6 %collective-permute-start.5 = (f32[4,1024]{1,0:T(4,128)S(1)}, f32[4,1024]{1,0:T(4,128)S(1)}, u32[]{:S(2)}, u32[]{:S(2)}) collective-permute-start(f32[4,1024]{1,0:T(4,128)S(1)} %merge.7.mine), channel_id=1, source_target_pairs={{0,16},{4,20},{8,24},{12,28},{16,0},{20,4},{24,8},{28,12},{1,17},{... | collective-permute-start | bytes 49160 | tf_op jit(solution)/shard_map/ppermute | solution.py:41
  23.6 9.6 %collective-permute-start.6 = (f32[2,2,64,256]{3,2,1,0:T(8,128)S(1)}, f32[2,2,64,256]{3,2,1,0:T(8,128)S(1)}, u32[]{:S(2)}, u32[]{:S(2)}) collective-permute-start(f32[2,2,64,256]{3,2,1,0:T(8,128)S(1)} %get-tuple-element.37), channel_id=1, source_target_pairs={{0,4},{4,0},{8,12},{12,8},{16,20},{20,16},{24,28},{28,24},{1,5},{5... | collective-permute-start | bytes 786440 | tf_op jit(solution)/shard_map/ppermute | solution.py:56
  25.3 20.2 %collective-permute-start.15 = (f32[4,2,128,128]{3,2,1,0:T(8,128)S(1)}, f32[4,2,128,128]{3,2,1,0:T(8,128)S(1)}, u32[]{:S(2)}, u32[]{:S(2)}) collective-permute-start(f32[4,2,128,128]{3,2,1,0:T(8,128)S(1)} %get-tuple-element.44), channel_id=1, source_target_pairs={{0,8},{4,12},{8,0},{12,4},{16,24},{20,28},{24,16},{28,20},{1,9},{5... | collective-permute-start | bytes 1572872 | tf_op jit(solution)/shard_map/ppermute | solution.py:56
  30.0 9.3 %collective-permute-start.13 = (f32[2,2,64,256]{3,2,1,0:T(8,128)S(1)}, f32[2,2,64,256]{3,2,1,0:T(8,128)S(1)}, u32[]{:S(2)}, u32[]{:S(2)}) collective-permute-start(f32[2,2,64,256]{3,2,1,0:T(8,128)S(1)} %get-tuple-element.41), channel_id=1, source_target_pairs={{0,4},{4,0},{8,12},{12,8},{16,20},{20,16},{24,28},{28,24},{1,5},{5... | collective-permute-start | bytes 786440 | tf_op jit(solution)/shard_map/ppermute | solution.py:56
  32.5 20.3 %collective-permute-start.21 = (f32[4,2,128,128]{3,2,1,0:T(8,128)S(1)}, f32[4,2,128,128]{3,2,1,0:T(8,128)S(1)}, u32[]{:S(2)}, u32[]{:S(2)}) collective-permute-start(f32[4,2,128,128]{3,2,1,0:T(8,128)S(1)} %get-tuple-element.48), channel_id=1, source_target_pairs={{0,4},{4,0},{8,12},{12,8},{16,20},{20,16},{24,28},{28,24},{1,5},{5... | collective-permute-start | bytes 1572872 | tf_op jit(solution)/shard_map/ppermute | solution.py:56
  33.3 6.8 %collective-permute-start.7 = (f32[1,2,64,256]{3,2,1,0:T(8,128)S(1)}, f32[1,2,64,256]{3,2,1,0:T(8,128)S(1)}, u32[]{:S(2)}, u32[]{:S(2)}) collective-permute-start(f32[1,2,64,256]{3,2,1,0:T(8,128)S(1)} %slice_add_fusion.12), channel_id=1, source_target_pairs={{0,8},{4,12},{8,0},{12,4},{16,24},{20,28},{24,16},{28,20},{1,9},{5... | collective-permute-start | bytes 393224 | tf_op jit(solution)/shard_map/ppermute | solution.py:56
  39.3 6.7 %collective-permute-start.14 = (f32[1,2,64,256]{3,2,1,0:T(8,128)S(1)}, f32[1,2,64,256]{3,2,1,0:T(8,128)S(1)}, u32[]{:S(2)}, u32[]{:S(2)}) collective-permute-start(f32[1,2,64,256]{3,2,1,0:T(8,128)S(1)} %get-tuple-element.62), channel_id=1, source_target_pairs={{0,8},{4,12},{8,0},{12,4},{16,24},{20,28},{24,16},{28,20},{1,9},{5... | collective-permute-start | bytes 393224 | tf_op jit(solution)/shard_map/ppermute | solution.py:56
  40.1 9.4 %collective-permute-start.8 = (f32[1,2,64,256]{3,2,1,0:T(8,128)S(1)}, f32[1,2,64,256]{3,2,1,0:T(8,128)S(1)}, u32[]{:S(2)}, u32[]{:S(2)}) collective-permute-start(f32[1,2,64,256]{3,2,1,0:T(8,128)S(1)} %fusion), channel_id=1, source_target_pairs={{0,24},{4,28},{8,16},{12,20},{16,8},{20,12},{24,0},{28,4},{1,25},{... | collective-permute-start | bytes 393224 | tf_op jit(solution)/shard_map/ppermute | solution.py:56
  45.5 11.6 %collective-permute-start.19 = (f32[2,2,128,128]{3,2,1,0:T(8,128)S(1)}, f32[2,2,128,128]{3,2,1,0:T(8,128)S(1)}, u32[]{:S(2)}, u32[]{:S(2)}) collective-permute-start(f32[2,2,128,128]{3,2,1,0:T(8,128)S(1)} %get-tuple-element.55.after), channel_id=1, source_target_pairs={{0,4},{4,0},{8,12},{12,8},{16,20},{20,16},{24,28},{28,24},{1,5},{5... | collective-permute-start | bytes 786440 | tf_op jit(solution)/shard_map/ppermute | solution.py:56
  46.0 9.0 %collective-permute-start.16 = (f32[1,2,64,256]{3,2,1,0:T(8,128)S(1)}, f32[1,2,64,256]{3,2,1,0:T(8,128)S(1)}, u32[]{:S(2)}, u32[]{:S(2)}) collective-permute-start(f32[1,2,64,256]{3,2,1,0:T(8,128)S(1)} %added.1), channel_id=1, source_target_pairs={{0,24},{4,28},{8,16},{12,20},{16,8},{20,12},{24,0},{28,4},{1,25},{... | collective-permute-start | bytes 393224 | tf_op jit(solution)/shard_map/ppermute | solution.py:56
  49.6 6.9 %collective-permute-start.11 = (f32[1,2,64,256]{3,2,1,0:T(8,128)S(1)}, f32[1,2,64,256]{3,2,1,0:T(8,128)S(1)}, u32[]{:S(2)}, u32[]{:S(2)}) collective-permute-start(f32[1,2,64,256]{3,2,1,0:T(8,128)S(1)} %add.54.refs_2_), channel_id=1, source_target_pairs={{0,8},{4,12},{8,0},{12,4},{16,24},{20,28},{24,16},{28,20},{1,9},{5... | collective-permute-start | bytes 393224 | tf_op jit(solution)/shard_map/ppermute | solution.py:56
  50.5 12.2 %collective-permute-start.9 = (f32[2,512,128]{2,1,0:T(8,128)S(1)}, f32[2,512,128]{2,1,0:T(8,128)S(1)}, u32[]{:S(2)}, u32[]{:S(2)}) collective-permute-start(f32[2,512,128]{2,1,0:T(8,128)S(1)} %get-tuple-element.39), channel_id=1, source_target_pairs={{0,2},{1,3},{2,0},{3,1},{4,6},{5,7},{6,4},{7,5},{8,10},{9,11},{10,... | collective-permute-start | bytes 1572872 | tf_op jit(solution)/shard_map/ppermute | solution.py:41
  52.9 10.0 %collective-permute-start.22 = (f32[2,2,128,128]{3,2,1,0:T(8,128)S(1)}, f32[2,2,128,128]{3,2,1,0:T(8,128)S(1)}, u32[]{:S(2)}, u32[]{:S(2)}) collective-permute-start(f32[2,2,128,128]{3,2,1,0:T(8,128)S(1)} %get-tuple-element.53), channel_id=1, source_target_pairs={{0,8},{4,12},{8,0},{12,4},{16,24},{20,28},{24,16},{28,20},{1,9},{5... | collective-permute-start | bytes 786440 | tf_op jit(solution)/shard_map/ppermute | solution.py:56
  55.0 6.8 %collective-permute-start.17 = (f32[1,2,64,256]{3,2,1,0:T(8,128)S(1)}, f32[1,2,64,256]{3,2,1,0:T(8,128)S(1)}, u32[]{:S(2)}, u32[]{:S(2)}) collective-permute-start(f32[1,2,64,256]{3,2,1,0:T(8,128)S(1)} %add.60), channel_id=1, source_target_pairs={{0,8},{4,12},{8,0},{12,4},{16,24},{20,28},{24,16},{28,20},{1,9},{5... | collective-permute-start | bytes 393224 | tf_op jit(solution)/shard_map/ppermute | solution.py:56
  56.5 8.8 %collective-permute-start.12 = (f32[2,2,64,256]{3,2,1,0:T(8,128)S(1)}, f32[2,2,64,256]{3,2,1,0:T(8,128)S(1)}, u32[]{:S(2)}, u32[]{:S(2)}) collective-permute-start(f32[2,2,64,256]{3,2,1,0:T(8,128)S(1)} %pad_maximum_fusion.refs_2_), channel_id=1, source_target_pairs={{0,4},{4,0},{8,12},{12,8},{16,20},{20,16},{24,28},{28,24},{1,5},{5... | collective-permute-start | bytes 786440 | tf_op jit(solution)/shard_map/ppermute | solution.py:56
  57.1 12.3 %collective-permute-start.20 = (f32[1,2,128,128]{3,2,1,0:T(8,128)S(1)}, f32[1,2,128,128]{3,2,1,0:T(8,128)S(1)}, u32[]{:S(2)}, u32[]{:S(2)}) collective-permute-start(f32[1,2,128,128]{3,2,1,0:T(8,128)S(1)} %get-tuple-element.60), channel_id=1, source_target_pairs={{0,24},{4,28},{8,16},{12,20},{16,8},{20,12},{24,0},{28,4},{1,25},{... | collective-permute-start | bytes 393224 | tf_op jit(solution)/shard_map/ppermute | solution.py:56
  61.8 6.4 %collective-permute-start.18 = (f32[2,2,64,256]{3,2,1,0:T(8,128)S(1)}, f32[2,2,64,256]{3,2,1,0:T(8,128)S(1)}, u32[]{:S(2)}, u32[]{:S(2)}) collective-permute-start(f32[2,2,64,256]{3,2,1,0:T(8,128)S(1)} %pad_maximum_fusion.1.refs_4_), channel_id=1, source_target_pairs={{0,4},{4,0},{8,12},{12,8},{16,20},{20,16},{24,28},{28,24},{1,5},{5... | collective-permute-start | bytes 786440 | tf_op jit(solution)/shard_map/ppermute | solution.py:56
  62.8 5.5 %collective-permute-start.10 = (f32[1,512,128]{2,1,0:T(8,128)S(1)}, f32[1,512,128]{2,1,0:T(8,128)S(1)}, u32[]{:S(2)}, u32[]{:S(2)}) collective-permute-start(f32[1,512,128]{2,1,0:T(8,128)S(1)} %get-tuple-element.56), channel_id=1, source_target_pairs={{0,1},{1,0},{2,3},{3,2},{4,5},{5,4},{6,7},{7,6},{8,9},{9,8},{10,11... | collective-permute-start | bytes 786440 | tf_op jit(solution)/shard_map/ppermute | solution.py:41
  62.9 7.9 %collective-permute-start.23 = (f32[1,2,128,128]{3,2,1,0:T(8,128)S(1)}, f32[1,2,128,128]{3,2,1,0:T(8,128)S(1)}, u32[]{:S(2)}, u32[]{:S(2)}) collective-permute-start(f32[1,2,128,128]{3,2,1,0:T(8,128)S(1)} %get-tuple-element.58), channel_id=1, source_target_pairs={{0,24},{4,28},{8,16},{12,20},{16,8},{20,12},{24,0},{28,4},{1,25},{... | collective-permute-start | bytes 393224 | tf_op jit(solution)/shard_map/ppermute | solution.py:56
  (8 other events, 74.0 us)

commit v13 on v12

--- a/solution.py
+++ b/solution.py
@@ -204,7 +204,7 @@
     side = lax.rem(me, 2)
     for part, (begin, end, bits) in enumerate(parts):
         for upper in range(GROUPS // 2):
-            pair = counted(counted(me) ^ (2 * upper)) // 2
+            pair = (me // 2) ^ upper
             at = pl.ds(pl.multiple_of(pair * 2 * piece, 2 * piece), 2 * piece)
             for read_index in range(begin, end):
                 slot = upper * reads + read_index
@@ -406,7 +406,7 @@
         for part, (begin, end, bits) in enumerate(QUERY_PARTS[head_index]):
             keep, send = results[2 * part : 2 * part + 2]
             for place, bit in enumerate(bits):
-                theirs = row_swap(send, bit=bit * low)
+                theirs = swap(send, "rows", row_devices, bit * low)
                 if place + 1 < len(bits):
                     middle = keep.shape[0] // 2
                     send = keep[middle:] + theirs[middle:]

time: 71.6 us -> 73.4 us (1.025)
  waiting for transfers between devices: 15.5 us -> 19.9 us
  starting transfers between devices: 37.2 us -> 34.6 us
    ppermute x16 -> x10, starting transfers between devices: 23 us -> 12.7 us  [row_swap_of(): return lax.ppermute(array, 'rows', pairs)]
    ppermute x8 -> x14, starting transfers between devices: 14.1 us -> 21.9 us  [swap(): return lax.ppermute(array, axis, pairs)]
    ppermute x8 -> x14, waiting for transfers between devices: 1.54 us -> 4.47 us  [swap(): return lax.ppermute(array, axis, pairs)]
    ppermute x16 -> x10, waiting for transfers between devices: 14 us -> 15.4 us  [row_swap_of(): return lax.ppermute(array, 'rows', pairs)]
  transfers between devices with their start and end apart: 24 -> 24, of which waited for: 9 -> 10; matrix products, arithmetic and copies ran while one was open for 1% -> 1% of each run, Pallas kernels for 17% -> 17%
where the time goes in v13:
time: 73.4 us; the launch traced here: 73.2 us
  starting transfers between devices  34.6 us (47%)
  waiting for transfers between devices  19.9 us (27%)
  Pallas kernels  17.4 us (24%)
  between operations  0.89 us (1%)
    ppermute x14, starting transfers between devices, swap(): return lax.ppermute(array, axis, pairs)  21.9 us
    ppermute x10, waiting for transfers between devices, row_swap_of(): return lax.ppermute(array, 'rows', pairs)  15.4 us
    ppermute x10, starting transfers between devices, row_swap_of(): return lax.ppermute(array, 'rows', pairs)  12.7 us
    pallas_call x4, Pallas kernels, kernel_call(): pl.pallas_call(kernel, out_shape=[shape_of(*item) for item in shapes], in...  8.02 us
    pallas_call x2, Pallas kernels, on_device(): pl.pallas_call(functools.partial(first_kernel, tile) if first else functo...  6.55 us
    ppermute x14, waiting for transfers between devices, swap(): return lax.ppermute(array, axis, pairs)  4.47 us
  transfers between devices with their start and end apart: 24, of which 10 were waited for; matrix products, arithmetic and copies ran while one was open for 1% of the time, Pallas kernels for 17%

profile of v13, /device:TPU:0, one launch (start us, length us, event | category | flops | bytes accessed | tf_op | source)
XLA Modules:
  0.0 73.2 jit_solution(17728571781330410690)
XLA Ops:
  0.7 4.4 %project.2 = (bf16[512,128]{1,0:T(8,128)(2,1)}, bf16[512,128]{1,0:T(8,128)(2,1)}, f32[4,1024]{1,0:T(4,128)}) custom-call(bf16[512,512]{1,0:T(8,128)(2,1)} %inputs.3, bf16[512,256]{1,0:T(8,128)(2,1)} %key_weight.1, bf16[512,256]{1,0:T(8,128)(2,1)} %value_weight.1, bf16[2,1024,256]{2,1,0:T(8,128)(2,1)} %queries.4, bf16[2,1024,256]{2,1,0:T(8,128)(2,1)} %out_grad.3), custom_call_target="tpu_custom_call" | custom-call | flops 1073741824 | bytes 4194304 | tf_op jit(solution)/shard_map/project/pallas_call | solution.py:285
  5.1 3.0 %collective-permute-start = (f32[4,1024]{1,0:T(4,128)}, f32[4,1024]{1,0:T(4,128)S(1)}, u32[]{:S(2)}, u32[]{:S(2)}) collective-permute-start(f32[4,1024]{1,0:T(4,128)} %get-tuple-element.28.mine), channel_id=1, source_target_pairs={{0,4},{4,0},{8,12},{12,8},{16,20},{20,16},{24,28},{28,24},{1,5},{5... | collective-permute-start | bytes 49160 | tf_op jit(solution)/shard_map/ppermute | solution.py:41
  8.2 2.1 %project.3 = (bf16[512,128]{1,0:T(8,128)(2,1)S(1)}, bf16[512,128]{1,0:T(8,128)(2,1)S(1)}, f32[4,1024]{1,0:T(4,128)S(1)}) custom-call(bf16[512,512]{1,0:T(8,128)(2,1)S(1)} %copy-done.3, bf16[512,256]{1,0:T(8,128)(2,1)S(1)} %copy-done.4, bf16[512,256]{1,0:T(8,128)(2,1)S(1)} %copy-done.5, bf16[2,1024,256]{2,1,0:T(8,128)(2,1)S(1)} %copy-done.1, ...), custom_call_target="tpu_custom_call" | custom-call | flops 1073741824 | bytes 4194304 | tf_op jit(solution)/shard_map/project/pallas_call | solution.py:285
  10.4 2.1 %collective-permute-start.1 = (f32[4,1024]{1,0:T(4,128)S(1)}, f32[4,1024]{1,0:T(4,128)S(1)}, u32[]{:S(2)}, u32[]{:S(2)}) collective-permute-start(f32[4,1024]{1,0:T(4,128)S(1)} %merge.4.mine), channel_id=1, source_target_pairs={{0,8},{4,12},{8,0},{12,4},{16,24},{20,28},{24,16},{28,20},{1,9},{5... | collective-permute-start | bytes 49160 | tf_op jit(solution)/shard_map/ppermute | solution.py:41
  12.6 1.5 %collective-permute-done.3.theirs = f32[4,1024]{1,0:T(4,128)S(1)} collective-permute-done((f32[4,1024]{1,0:T(4,128)S(1)}, f32[4,1024]{1,0:T(4,128)S(1)}, u32[]{:S(2)}, u32[]{:S(2)}) %collective-permute-start.3) | collective-permute-done | bytes 16416 | tf_op jit(solution)/shard_map/ppermute | solution.py:41
  14.1 1.6 %collective-permute-start.4 = (f32[4,1024]{1,0:T(4,128)S(1)}, f32[4,1024]{1,0:T(4,128)S(1)}, u32[]{:S(2)}, u32[]{:S(2)}) collective-permute-start(f32[4,1024]{1,0:T(4,128)S(1)} %merge.6.mine), channel_id=1, source_target_pairs={{0,8},{4,12},{8,0},{12,4},{16,24},{20,28},{24,16},{28,20},{1,9},{5... | collective-permute-start | bytes 49160 | tf_op jit(solution)/shard_map/ppermute | solution.py:41
  15.8 2.7 %collective-permute-start.2 = (f32[4,1024]{1,0:T(4,128)S(1)}, f32[4,1024]{1,0:T(4,128)S(1)}, u32[]{:S(2)}, u32[]{:S(2)}) collective-permute-start(f32[4,1024]{1,0:T(4,128)S(1)} %merge.5.after.mine), channel_id=1, source_target_pairs={{0,16},{4,20},{8,24},{12,28},{16,0},{20,4},{24,8},{28,12},{1,17},{... | collective-permute-start | bytes 49160 | tf_op jit(solution)/shard_map/ppermute | solution.py:41
  18.5 2.2 %collective-permute-start.5 = (f32[4,1024]{1,0:T(4,128)S(1)}, f32[4,1024]{1,0:T(4,128)S(1)}, u32[]{:S(2)}, u32[]{:S(2)}) collective-permute-start(f32[4,1024]{1,0:T(4,128)S(1)} %merge.7.mine), channel_id=1, source_target_pairs={{0,16},{4,20},{8,24},{12,28},{16,0},{20,4},{24,8},{28,12},{1,17},{... | collective-permute-start | bytes 49160 | tf_op jit(solution)/shard_map/ppermute | solution.py:41
  20.7 2.9 %grads.2 = (bf16[512,256]{1,0:T(8,128)(2,1)S(1)}, bf16[2,512,1024]{2,1,0:T(8,128)(2,1)S(1)}, f32[2,2,64,256]{3,2,1,0:T(8,128)S(1)}, f32[2,2,64,256]{3,2,1,0:T(8,128)S(1)}) custom-call(f32[4,1024]{1,0:T(4,128)S(1)} %merge.5.after.mine, bf16[512,512]{1,0:T(8,128)(2,1)S(1)} %copy-done.3, bf16[512,128]{1,0:T(8,128)(2,1)S(1)} %copy-done.6, ...), custom_call_target="tpu_custom_call" | custom-call | flops 1073741824 | bytes 4194304 | tf_op jit(solution)/shard_map/grads/pallas_call | solution.py:341
  25.2 1.8 %collective-permute-start.15 = (f32[4,2,128,128]{3,2,1,0:T(8,128)S(1)}, f32[4,2,128,128]{3,2,1,0:T(8,128)S(1)}, u32[]{:S(2)}, u32[]{:S(2)}) collective-permute-start(f32[4,2,128,128]{3,2,1,0:T(8,128)S(1)} %get-tuple-element.44), channel_id=1, source_target_pairs={{0,8},{4,12},{8,0},{12,4},{16,24},{20,28},{24,16},{28,20},{1,9},{5... | collective-permute-start | bytes 1572872 | tf_op jit(solution)/shard_map/ppermute | solution.py:41
  27.0 2.9 %grads.3 = (bf16[512,256]{1,0:T(8,128)(2,1)S(1)}, bf16[2,512,1024]{2,1,0:T(8,128)(2,1)S(1)}, f32[2,2,64,256]{3,2,1,0:T(8,128)S(1)}, f32[2,2,64,256]{3,2,1,0:T(8,128)S(1)}) custom-call(bf16[512,256]{1,0:T(8,128)(2,1)S(1)} %get-tuple-element.31.after.refs_0_, bf16[512,512]{1,0:T(8,128)(2,1)S(1)} %copy-done.3, bf16[512,128]{1,0:T(8,128)(2,1)S(1)} %get-tuple-element.32.keys, ...), custom_call_target="tpu_custom_call" | custom-call | flops 1073741824 | bytes 4194304 | tf_op jit(solution)/shard_map/grads/pallas_call | solution.py:341
  29.9 1.5 %collective-permute-start.13 = (f32[2,2,64,256]{3,2,1,0:T(8,128)S(1)}, f32[2,2,64,256]{3,2,1,0:T(8,128)S(1)}, u32[]{:S(2)}, u32[]{:S(2)}) collective-permute-start(f32[2,2,64,256]{3,2,1,0:T(8,128)S(1)} %get-tuple-element.41), channel_id=1, source_target_pairs={{0,4},{4,0},{8,12},{12,8},{16,20},{20,16},{24,28},{28,24},{1,5},{5... | collective-permute-start | bytes 786440 | tf_op jit(solution)/shard_map/ppermute | solution.py:56
  31.4 1.1 %query.3 = (f32[4,2,128,128]{3,2,1,0:T(8,128)S(1)}, f32[4,2,128,128]{3,2,1,0:T(8,128)S(1)}) custom-call(bf16[512,256]{1,0:T(8,128)(2,1)S(1)} %get-tuple-element.35.refs_1_.after, bf16[2,512,1024]{2,1,0:T(8,128)(2,1)S(1)} %get-tuple-element.46.score_grads, bf16[512,128]{1,0:T(8,128)(2,1)S(1)} %get-tuple-element.32.keys), custom_call_target="tpu_custom_call" | custom-call | flops 1073741824 | bytes 4194304 | tf_op jit(solution)/shard_map/query/pallas_call | solution.py:341
  33.9 5.3 %collective-permute-done.13 = f32[2,2,64,256]{3,2,1,0:T(8,128)S(1)} collective-permute-done((f32[2,2,64,256]{3,2,1,0:T(8,128)S(1)}, f32[2,2,64,256]{3,2,1,0:T(8,128)S(1)}, u32[]{:S(2)}, u32[]{:S(2)}) %collective-permute-start.13) | collective-permute-done | bytes 262176 | tf_op jit(solution)/shard_map/ppermute | solution.py:56
  40.1 5.3 %collective-permute-start.8 = (f32[1,2,64,256]{3,2,1,0:T(8,128)S(1)}, f32[1,2,64,256]{3,2,1,0:T(8,128)S(1)}, u32[]{:S(2)}, u32[]{:S(2)}) collective-permute-start(f32[1,2,64,256]{3,2,1,0:T(8,128)S(1)} %fusion), channel_id=1, source_target_pairs={{0,24},{4,28},{8,16},{12,20},{16,8},{20,12},{24,0},{28,4},{1,25},{... | collective-permute-start | bytes 393224 | tf_op jit(solution)/shard_map/ppermute | solution.py:56
  46.0 2.5 %collective-permute-start.16 = (f32[1,2,64,256]{3,2,1,0:T(8,128)S(1)}, f32[1,2,64,256]{3,2,1,0:T(8,128)S(1)}, u32[]{:S(2)}, u32[]{:S(2)}) collective-permute-start(f32[1,2,64,256]{3,2,1,0:T(8,128)S(1)} %added.1), channel_id=1, source_target_pairs={{0,24},{4,28},{8,16},{12,20},{16,8},{20,12},{24,0},{28,4},{1,25},{... | collective-permute-start | bytes 393224 | tf_op jit(solution)/shard_map/ppermute | solution.py:56
  50.4 2.3 %collective-permute-start.9 = (f32[2,512,128]{2,1,0:T(8,128)S(1)}, f32[2,512,128]{2,1,0:T(8,128)S(1)}, u32[]{:S(2)}, u32[]{:S(2)}) collective-permute-start(f32[2,512,128]{2,1,0:T(8,128)S(1)} %get-tuple-element.39), channel_id=1, source_target_pairs={{0,2},{1,3},{2,0},{3,1},{4,6},{5,7},{6,4},{7,5},{8,10},{9,11},{10,... | collective-permute-start | bytes 1572872 | tf_op jit(solution)/shard_map/ppermute | solution.py:41
  52.8 2.1 %collective-permute-start.22 = (f32[2,2,128,128]{3,2,1,0:T(8,128)S(1)}, f32[2,2,128,128]{3,2,1,0:T(8,128)S(1)}, u32[]{:S(2)}, u32[]{:S(2)}) collective-permute-start(f32[2,2,128,128]{3,2,1,0:T(8,128)S(1)} %get-tuple-element.53), channel_id=1, source_target_pairs={{0,8},{4,12},{8,0},{12,4},{16,24},{20,28},{24,16},{28,20},{1,9},{5... | collective-permute-start | bytes 786440 | tf_op jit(solution)/shard_map/ppermute | solution.py:41
  55.0 2.6 %collective-permute-done.11 = f32[1,2,64,256]{3,2,1,0:T(8,128)S(1)} collective-permute-done((f32[1,2,64,256]{3,2,1,0:T(8,128)S(1)}, f32[1,2,64,256]{3,2,1,0:T(8,128)S(1)}, u32[]{:S(2)}, u32[]{:S(2)}) %collective-permute-start.11) | collective-permute-done | bytes 131104 | tf_op jit(solution)/shard_map/ppermute | solution.py:56
  59.5 2.3 %collective-permute-done.17 = f32[1,2,64,256]{3,2,1,0:T(8,128)S(1)} collective-permute-done((f32[1,2,64,256]{3,2,1,0:T(8,128)S(1)}, f32[1,2,64,256]{3,2,1,0:T(8,128)S(1)}, u32[]{:S(2)}, u32[]{:S(2)}) %collective-permute-start.17) | collective-permute-done | bytes 131104 | tf_op jit(solution)/shard_map/ppermute | solution.py:56
  62.9 2.1 %collective-permute-start.23 = (f32[1,2,128,128]{3,2,1,0:T(8,128)S(1)}, f32[1,2,128,128]{3,2,1,0:T(8,128)S(1)}, u32[]{:S(2)}, u32[]{:S(2)}) collective-permute-start(f32[1,2,128,128]{3,2,1,0:T(8,128)S(1)} %get-tuple-element.58), channel_id=1, source_target_pairs={{0,16},{4,20},{8,24},{12,28},{16,0},{20,4},{24,8},{28,12},{1,17},{... | collective-permute-start | bytes 393224 | tf_op jit(solution)/shard_map/ppermute | solution.py:41
  65.6 2.8 %collective-permute-done.18.refs_5_ = f32[2,2,64,256]{3,2,1,0:T(8,128)S(1)} collective-permute-done((f32[2,2,64,256]{3,2,1,0:T(8,128)S(1)}, f32[2,2,64,256]{3,2,1,0:T(8,128)S(1)}, u32[]{:S(2)}, u32[]{:S(2)}) %collective-permute-start.18) | collective-permute-done | bytes 262176 | tf_op jit(solution)/shard_map/ppermute | solution.py:56
  68.4 1.2 %weights.1 = (f32[512,256]{1,0:T(8,128)}, f32[512,256]{1,0:T(8,128)}, f32[512,128]{1,0:T(8,128)}, f32[8,128]{1,0:T(8,128)S(1)}) custom-call(f32[1,512,128]{2,1,0:T(8,128)S(1)} %get-tuple-element.57.refs_0_, f32[1,512,128]{2,1,0:T(8,128)S(1)} %collective-permute-done.10.refs_1_, f32[2,2,64,256]{3,2,1,0:T(8,128)S(1)} %pad_maximum_fusion.refs_2_, ...), custom_call_target="tpu_custom_call" | custom-call | tf_op jit(solution)/shard_map/weights/pallas_call | solution.py:470
  69.6 2.9 %collective-permute-done.23.refs_3_ = f32[1,2,128,128]{3,2,1,0:T(8,128)S(1)} collective-permute-done((f32[1,2,128,128]{3,2,1,0:T(8,128)S(1)}, f32[1,2,128,128]{3,2,1,0:T(8,128)S(1)}, u32[]{:S(2)}, u32[]{:S(2)}) %collective-permute-start.23) | collective-permute-done | bytes 131104 | tf_op jit(solution)/shard_map/ppermute | solution.py:41
  (66 shorter events, 11.1 us)
Async XLA Ops:
  5.1 5.3 %collective-permute-start = (f32[4,1024]{1,0:T(4,128)}, f32[4,1024]{1,0:T(4,128)S(1)}, u32[]{:S(2)}, u32[]{:S(2)}) collective-permute-start(f32[4,1024]{1,0:T(4,128)} %get-tuple-element.28.mine), channel_id=1, source_target_pairs={{0,4},{4,0},{8,12},{12,8},{16,20},{20,16},{24,28},{28,24},{1,5},{5... | collective-permute-start | bytes 49160 | tf_op jit(solution)/shard_map/ppermute | solution.py:41
  10.3 3.8 %collective-permute-start.3 = (f32[4,1024]{1,0:T(4,128)S(1)}, f32[4,1024]{1,0:T(4,128)S(1)}, u32[]{:S(2)}, u32[]{:S(2)}) collective-permute-start(f32[4,1024]{1,0:T(4,128)S(1)} %get-tuple-element.34.mine), channel_id=1, source_target_pairs={{0,4},{4,0},{8,12},{12,8},{16,20},{20,16},{24,28},{28,24},{1,5},{5... | collective-permute-start | bytes 49160 | tf_op jit(solution)/shard_map/ppermute | solution.py:41
  10.4 5.3 %collective-permute-start.1 = (f32[4,1024]{1,0:T(4,128)S(1)}, f32[4,1024]{1,0:T(4,128)S(1)}, u32[]{:S(2)}, u32[]{:S(2)}) collective-permute-start(f32[4,1024]{1,0:T(4,128)S(1)} %merge.4.mine), channel_id=1, source_target_pairs={{0,8},{4,12},{8,0},{12,4},{16,24},{20,28},{24,16},{28,20},{1,9},{5... | collective-permute-start | bytes 49160 | tf_op jit(solution)/shard_map/ppermute | solution.py:41
  14.1 4.3 %collective-permute-start.4 = (f32[4,1024]{1,0:T(4,128)S(1)}, f32[4,1024]{1,0:T(4,128)S(1)}, u32[]{:S(2)}, u32[]{:S(2)}) collective-permute-start(f32[4,1024]{1,0:T(4,128)S(1)} %merge.6.mine), channel_id=1, source_target_pairs={{0,8},{4,12},{8,0},{12,4},{16,24},{20,28},{24,16},{28,20},{1,9},{5... | collective-permute-start | bytes 49160 | tf_op jit(solution)/shard_map/ppermute | solution.py:41
  15.8 4.9 %collective-permute-start.2 = (f32[4,1024]{1,0:T(4,128)S(1)}, f32[4,1024]{1,0:T(4,128)S(1)}, u32[]{:S(2)}, u32[]{:S(2)}) collective-permute-start(f32[4,1024]{1,0:T(4,128)S(1)} %merge.5.after.mine), channel_id=1, source_target_pairs={{0,16},{4,20},{8,24},{12,28},{16,0},{20,4},{24,8},{28,12},{1,17},{... | collective-permute-start | bytes 49160 | tf_op jit(solution)/shard_map/ppermute | solution.py:41
  18.5 8.5 %collective-permute-start.5 = (f32[4,1024]{1,0:T(4,128)S(1)}, f32[4,1024]{1,0:T(4,128)S(1)}, u32[]{:S(2)}, u32[]{:S(2)}) collective-permute-start(f32[4,1024]{1,0:T(4,128)S(1)} %merge.7.mine), channel_id=1, source_target_pairs={{0,16},{4,20},{8,24},{12,28},{16,0},{20,4},{24,8},{28,12},{1,17},{... | collective-permute-start | bytes 49160 | tf_op jit(solution)/shard_map/ppermute | solution.py:41
  23.6 9.6 %collective-permute-start.6 = (f32[2,2,64,256]{3,2,1,0:T(8,128)S(1)}, f32[2,2,64,256]{3,2,1,0:T(8,128)S(1)}, u32[]{:S(2)}, u32[]{:S(2)}) collective-permute-start(f32[2,2,64,256]{3,2,1,0:T(8,128)S(1)} %get-tuple-element.37), channel_id=1, source_target_pairs={{0,4},{4,0},{8,12},{12,8},{16,20},{20,16},{24,28},{28,24},{1,5},{5... | collective-permute-start | bytes 786440 | tf_op jit(solution)/shard_map/ppermute | solution.py:56
  25.2 20.2 %collective-permute-start.15 = (f32[4,2,128,128]{3,2,1,0:T(8,128)S(1)}, f32[4,2,128,128]{3,2,1,0:T(8,128)S(1)}, u32[]{:S(2)}, u32[]{:S(2)}) collective-permute-start(f32[4,2,128,128]{3,2,1,0:T(8,128)S(1)} %get-tuple-element.44), channel_id=1, source_target_pairs={{0,8},{4,12},{8,0},{12,4},{16,24},{20,28},{24,16},{28,20},{1,9},{5... | collective-permute-start | bytes 1572872 | tf_op jit(solution)/shard_map/ppermute | solution.py:41
  29.9 9.3 %collective-permute-start.13 = (f32[2,2,64,256]{3,2,1,0:T(8,128)S(1)}, f32[2,2,64,256]{3,2,1,0:T(8,128)S(1)}, u32[]{:S(2)}, u32[]{:S(2)}) collective-permute-start(f32[2,2,64,256]{3,2,1,0:T(8,128)S(1)} %get-tuple-element.41), channel_id=1, source_target_pairs={{0,4},{4,0},{8,12},{12,8},{16,20},{20,16},{24,28},{28,24},{1,5},{5... | collective-permute-start | bytes 786440 | tf_op jit(solution)/shard_map/ppermute | solution.py:56
  32.5 20.2 %collective-permute-start.21 = (f32[4,2,128,128]{3,2,1,0:T(8,128)S(1)}, f32[4,2,128,128]{3,2,1,0:T(8,128)S(1)}, u32[]{:S(2)}, u32[]{:S(2)}) collective-permute-start(f32[4,2,128,128]{3,2,1,0:T(8,128)S(1)} %get-tuple-element.48), channel_id=1, source_target_pairs={{0,4},{4,0},{8,12},{12,8},{16,20},{20,16},{24,28},{28,24},{1,5},{5... | collective-permute-start | bytes 1572872 | tf_op jit(solution)/shard_map/ppermute | solution.py:41
  33.3 6.8 %collective-permute-start.7 = (f32[1,2,64,256]{3,2,1,0:T(8,128)S(1)}, f32[1,2,64,256]{3,2,1,0:T(8,128)S(1)}, u32[]{:S(2)}, u32[]{:S(2)}) collective-permute-start(f32[1,2,64,256]{3,2,1,0:T(8,128)S(1)} %slice_add_fusion.12), channel_id=1, source_target_pairs={{0,8},{4,12},{8,0},{12,4},{16,24},{20,28},{24,16},{28,20},{1,9},{5... | collective-permute-start | bytes 393224 | tf_op jit(solution)/shard_map/ppermute | solution.py:56
  39.3 6.7 %collective-permute-start.14 = (f32[1,2,64,256]{3,2,1,0:T(8,128)S(1)}, f32[1,2,64,256]{3,2,1,0:T(8,128)S(1)}, u32[]{:S(2)}, u32[]{:S(2)}) collective-permute-start(f32[1,2,64,256]{3,2,1,0:T(8,128)S(1)} %get-tuple-element.62), channel_id=1, source_target_pairs={{0,8},{4,12},{8,0},{12,4},{16,24},{20,28},{24,16},{28,20},{1,9},{5... | collective-permute-start | bytes 393224 | tf_op jit(solution)/shard_map/ppermute | solution.py:56
  40.1 9.4 %collective-permute-start.8 = (f32[1,2,64,256]{3,2,1,0:T(8,128)S(1)}, f32[1,2,64,256]{3,2,1,0:T(8,128)S(1)}, u32[]{:S(2)}, u32[]{:S(2)}) collective-permute-start(f32[1,2,64,256]{3,2,1,0:T(8,128)S(1)} %fusion), channel_id=1, source_target_pairs={{0,24},{4,28},{8,16},{12,20},{16,8},{20,12},{24,0},{28,4},{1,25},{... | collective-permute-start | bytes 393224 | tf_op jit(solution)/shard_map/ppermute | solution.py:56
  45.5 13.0 %collective-permute-start.19 = (f32[2,2,128,128]{3,2,1,0:T(8,128)S(1)}, f32[2,2,128,128]{3,2,1,0:T(8,128)S(1)}, u32[]{:S(2)}, u32[]{:S(2)}) collective-permute-start(f32[2,2,128,128]{3,2,1,0:T(8,128)S(1)} %get-tuple-element.55.after), channel_id=1, source_target_pairs={{0,4},{4,0},{8,12},{12,8},{16,20},{20,16},{24,28},{28,24},{1,5},{5... | collective-permute-start | bytes 786440 | tf_op jit(solution)/shard_map/ppermute | solution.py:41
  46.0 8.9 %collective-permute-start.16 = (f32[1,2,64,256]{3,2,1,0:T(8,128)S(1)}, f32[1,2,64,256]{3,2,1,0:T(8,128)S(1)}, u32[]{:S(2)}, u32[]{:S(2)}) collective-permute-start(f32[1,2,64,256]{3,2,1,0:T(8,128)S(1)} %added.1), channel_id=1, source_target_pairs={{0,24},{4,28},{8,16},{12,20},{16,8},{20,12},{24,0},{28,4},{1,25},{... | collective-permute-start | bytes 393224 | tf_op jit(solution)/shard_map/ppermute | solution.py:56
  49.5 8.0 %collective-permute-start.11 = (f32[1,2,64,256]{3,2,1,0:T(8,128)S(1)}, f32[1,2,64,256]{3,2,1,0:T(8,128)S(1)}, u32[]{:S(2)}, u32[]{:S(2)}) collective-permute-start(f32[1,2,64,256]{3,2,1,0:T(8,128)S(1)} %add.54.refs_2_), channel_id=1, source_target_pairs={{0,8},{4,12},{8,0},{12,4},{16,24},{20,28},{24,16},{28,20},{1,9},{5... | collective-permute-start | bytes 393224 | tf_op jit(solution)/shard_map/ppermute | solution.py:56
  50.4 12.2 %collective-permute-start.9 = (f32[2,512,128]{2,1,0:T(8,128)S(1)}, f32[2,512,128]{2,1,0:T(8,128)S(1)}, u32[]{:S(2)}, u32[]{:S(2)}) collective-permute-start(f32[2,512,128]{2,1,0:T(8,128)S(1)} %get-tuple-element.39), channel_id=1, source_target_pairs={{0,2},{1,3},{2,0},{3,1},{4,6},{5,7},{6,4},{7,5},{8,10},{9,11},{10,... | collective-permute-start | bytes 1572872 | tf_op jit(solution)/shard_map/ppermute | solution.py:41
  52.8 10.0 %collective-permute-start.22 = (f32[2,2,128,128]{3,2,1,0:T(8,128)S(1)}, f32[2,2,128,128]{3,2,1,0:T(8,128)S(1)}, u32[]{:S(2)}, u32[]{:S(2)}) collective-permute-start(f32[2,2,128,128]{3,2,1,0:T(8,128)S(1)} %get-tuple-element.53), channel_id=1, source_target_pairs={{0,8},{4,12},{8,0},{12,4},{16,24},{20,28},{24,16},{28,20},{1,9},{5... | collective-permute-start | bytes 786440 | tf_op jit(solution)/shard_map/ppermute | solution.py:41
  54.9 6.9 %collective-permute-start.17 = (f32[1,2,64,256]{3,2,1,0:T(8,128)S(1)}, f32[1,2,64,256]{3,2,1,0:T(8,128)S(1)}, u32[]{:S(2)}, u32[]{:S(2)}) collective-permute-start(f32[1,2,64,256]{3,2,1,0:T(8,128)S(1)} %add.60), channel_id=1, source_target_pairs={{0,8},{4,12},{8,0},{12,4},{16,24},{20,28},{24,16},{28,20},{1,9},{5... | collective-permute-start | bytes 393224 | tf_op jit(solution)/shard_map/ppermute | solution.py:56
  57.5 8.0 %collective-permute-start.12 = (f32[2,2,64,256]{3,2,1,0:T(8,128)S(1)}, f32[2,2,64,256]{3,2,1,0:T(8,128)S(1)}, u32[]{:S(2)}, u32[]{:S(2)}) collective-permute-start(f32[2,2,64,256]{3,2,1,0:T(8,128)S(1)} %pad_maximum_fusion.refs_2_), channel_id=1, source_target_pairs={{0,4},{4,0},{8,12},{12,8},{16,20},{20,16},{24,28},{28,24},{1,5},{5... | collective-permute-start | bytes 786440 | tf_op jit(solution)/shard_map/ppermute | solution.py:56
  58.5 11.1 %collective-permute-start.20 = (f32[1,2,128,128]{3,2,1,0:T(8,128)S(1)}, f32[1,2,128,128]{3,2,1,0:T(8,128)S(1)}, u32[]{:S(2)}, u32[]{:S(2)}) collective-permute-start(f32[1,2,128,128]{3,2,1,0:T(8,128)S(1)} %get-tuple-element.60), channel_id=1, source_target_pairs={{0,16},{4,20},{8,24},{12,28},{16,0},{20,4},{24,8},{28,12},{1,17},{... | collective-permute-start | bytes 393224 | tf_op jit(solution)/shard_map/ppermute | solution.py:41
  61.8 6.6 %collective-permute-start.18 = (f32[2,2,64,256]{3,2,1,0:T(8,128)S(1)}, f32[2,2,64,256]{3,2,1,0:T(8,128)S(1)}, u32[]{:S(2)}, u32[]{:S(2)}) collective-permute-start(f32[2,2,64,256]{3,2,1,0:T(8,128)S(1)} %pad_maximum_fusion.1.refs_4_), channel_id=1, source_target_pairs={{0,4},{4,0},{8,12},{12,8},{16,20},{20,16},{24,28},{28,24},{1,5},{5... | collective-permute-start | bytes 786440 | tf_op jit(solution)/shard_map/ppermute | solution.py:56
  62.7 5.7 %collective-permute-start.10 = (f32[1,512,128]{2,1,0:T(8,128)S(1)}, f32[1,512,128]{2,1,0:T(8,128)S(1)}, u32[]{:S(2)}, u32[]{:S(2)}) collective-permute-start(f32[1,512,128]{2,1,0:T(8,128)S(1)} %get-tuple-element.56), channel_id=1, source_target_pairs={{0,1},{1,0},{2,3},{3,2},{4,5},{5,4},{6,7},{7,6},{8,9},{9,8},{10,11... | collective-permute-start | bytes 786440 | tf_op jit(solution)/shard_map/ppermute | solution.py:41
  62.9 9.7 %collective-permute-start.23 = (f32[1,2,128,128]{3,2,1,0:T(8,128)S(1)}, f32[1,2,128,128]{3,2,1,0:T(8,128)S(1)}, u32[]{:S(2)}, u32[]{:S(2)}) collective-permute-start(f32[1,2,128,128]{3,2,1,0:T(8,128)S(1)} %get-tuple-element.58), channel_id=1, source_target_pairs={{0,16},{4,20},{8,24},{12,28},{16,0},{20,4},{24,8},{28,12},{1,17},{... | collective-permute-start | bytes 393224 | tf_op jit(solution)/shard_map/ppermute | solution.py:41
  (8 other events, 74.0 us)

commit v14 on v12

--- a/solution.py
+++ b/solution.py
@@ -118,7 +118,8 @@
     return top + jnp.log2(total), delta
 
 
-def merge_kernel(mine, theirs, result):
+def merge_kernel(mine, theirs, after, result):
+    del after
     reads = mine.shape[0] // 2
     result[:reads], result[reads:] = merged(mine, theirs)
 
@@ -131,7 +132,8 @@
 LAST_BIT = 4
 WEIGHT_PARTS = (((0, 256, (1, 2)),), ((0, 256, (1, 2)),))
 QUERY_PARTS = (((0, 2, (2, 1, 4)),), ((0, 2, (1, 2, 4)),))
-AFTER = {'w1.2': 'q0.1', 'i.0': 'w0.3'}
+AFTER = {'w1.3': 'q1.1'}
+CHAIN = ()
 
 
 def grads_kernel(
@@ -253,6 +255,12 @@
 
 def shape_of(shape, dtype=jnp.float32):
     return jax.ShapeDtypeStruct(shape, dtype)
+
+
+def split_kernel(keep, theirs, after, stays, goes):
+    del after
+    stays[...] = keep[:1] + theirs[:1]
+    goes[...] = keep[1:] + theirs[1:]
 
 
 def add_kernel(mine, theirs, after, total):
@@ -300,20 +308,25 @@
             )(*operands)
         )
 
-    stats_parts = []
-    for head_index in range(head_count):
-        stats = projected[head_index][2]
-        for bit in bits_of(row_devices)[:-1]:
-            theirs = swap(stats, "rows", row_devices, bit)
-            stats = pl.pallas_call(
-                merge_kernel,
-                out_shape=shape_of(stats.shape),
-                in_specs=[VMEM] * 2,
-                out_specs=VMEM,
-                compiler_params=params(2),
-                name="merge",
-            )(stats, theirs)
-        stats_parts.append((stats, swap(stats, "rows", row_devices, bits_of(row_devices)[-1])))
+    stats = [item[2] for item in projected]
+    stats_got = [None] * head_count
+    after = stats[-1]
+    for place, bit in enumerate(bits_of(row_devices)):
+        for head_index in range(head_count):
+            if place:
+                own = stats[head_index]
+                use = (place, head_index) in CHAIN
+                after = pl.pallas_call(
+                    merge_kernel,
+                    out_shape=shape_of(stats[head_index].shape),
+                    in_specs=[VMEM, VMEM, ANY],
+                    out_specs=VMEM,
+                    compiler_params=params(2),
+                    name="merge",
+                )(stats[head_index], stats_got[head_index], after if use else own)
+                stats[head_index] = after
+            stats_got[head_index] = swap(stats[head_index], "rows", row_devices, bit)
+    stats_parts = list(zip(stats, stats_got))
 
     order_low = (lax.axis_index("rows") % low) ^ jnp.arange(low, dtype=jnp.int32)
     low_bits = [bit for bit in bits_of(row_devices) if bit < low]
@@ -348,6 +361,19 @@
             cost_estimate=block_work,
             name=name,
         )(*operands)
+
+    def input_products(after):
+        share = shape_of((head_devices // 2, row_count, features // head_devices))
+        return pl.pallas_call(
+            functools.partial(input_kernel, "heads"),
+            out_shape=(share, share),
+            in_specs=[VMEM] * (2 + head_count) + [ANY],
+            out_specs=(VMEM,) * 2,
+            scratch_shapes=[pltpu.VMEM((row_count, features), jnp.float32)],
+            compiler_params=params(16),
+            cost_estimate=block_work,
+            name="input",
+        )(key_weight, value_weight, *(item[0] for item in grads_out), after)
 
     grads_out, weight_steps, marks = [], [], {}
     for head_index in range(head_count):
@@ -361,7 +387,7 @@
                 for _ in range(2)
             ],
             [
-                grads_out[-1][0] if grads_out else stats_parts[0][0],
+                grads_out[-1][0] if grads_out else stats_parts[1][0],
                 *(inputs, keys, values, queries, out_grad),
                 *stats_parts[head_index],
             ],
@@ -379,8 +405,19 @@
         for part, (begin, end, bits) in enumerate(WEIGHT_PARTS[head_index]):
             keep, send = results[2 + 2 * part : 4 + 2 * part]
             theirs = row_swap(send, bit=bits[0] * low)
-            send = keep[1:] + theirs[1:]
-            mine = keep[:1] + theirs[:1]
+            if head_index + 1 == head_count:
+                input_keep, input_send = input_products(marks["w0.1"])
+                mine, send = pl.pallas_call(
+                    split_kernel,
+                    out_shape=(shape_of((1, *keep.shape[1:])),) * 2,
+                    in_specs=[VMEM, VMEM, ANY],
+                    out_specs=(VMEM,) * 2,
+                    compiler_params=params(4),
+                    name="split",
+                )(keep, theirs, input_keep)
+            else:
+                send = keep[1:] + theirs[1:]
+                mine = keep[:1] + theirs[:1]
             marks[f"w{head_index}.1"] = send
             weight_steps.append((mine, row_swap(send, bit=bits[1] * low)))
 
@@ -448,18 +485,6 @@
             weight_terms += [near, row_swap(near, bit=first)]
             weight_list.append((head_index, begin, end, bits))
 
-    share = ((head_devices // 2, row_count, features // head_devices),)
-    after = marks[AFTER.get("i.0", "B1")]
-    input_keep, input_send = pl.pallas_call(
-        functools.partial(input_kernel, "heads"),
-        out_shape=[shape_of(*share)] * 2,
-        in_specs=[VMEM] * (2 + head_count) + [ANY],
-        out_specs=[VMEM] * 2,
-        scratch_shapes=[pltpu.VMEM((row_count, features), jnp.float32)],
-        compiler_params=params(16),
-        cost_estimate=block_work,
-        name="input",
-    )(key_weight, value_weight, *(item[0] for item in grads_out), after)
     head_bits = bits_of(head_devices)[::-1]
     keep, theirs = input_keep, swap(input_send, "heads", head_devices, head_bits[0])
     for bit in head_bits[1:]:

time: 71.6 us -> 74.2 us (1.036)
  waiting for transfers between devices: 15.5 us -> 21.5 us
  starting transfers between devices: 37.2 us -> 33.8 us
    ppermute x16, waiting for transfers between devices: 14 us -> 17.8 us  [row_swap_of(): return lax.ppermute(array, 'rows', pairs)]
    ppermute x16, starting transfers between devices: 23 us -> 20 us  [row_swap_of(): return lax.ppermute(array, 'rows', pairs)]
    ppermute x8, waiting for transfers between devices: 1.54 us -> 3.71 us  [swap(): return lax.ppermute(array, axis, pairs)]
  transfers between devices with their start and end apart: 24 -> 24, of which waited for: 9 -> 10; matrix products, arithmetic and copies ran while one was open for 1% -> 1% of each run, Pallas kernels for 17% -> 13%
where the time goes in v14:
time: 74.2 us; the launch traced here: 74.1 us
  starting transfers between devices  33.8 us (46%)
  waiting for transfers between devices  21.5 us (29%)
  Pallas kernels  17.5 us (24%)
  between operations  0.88 us (1%)
    ppermute x16, starting transfers between devices, row_swap_of(): return lax.ppermute(array, 'rows', pairs)  20 us
    ppermute x16, waiting for transfers between devices, row_swap_of(): return lax.ppermute(array, 'rows', pairs)  17.8 us
    ppermute x8, starting transfers between devices, swap(): return lax.ppermute(array, axis, pairs)  13.7 us
    pallas_call x4, Pallas kernels, kernel_call(): pl.pallas_call(kernel, out_shape=[shape_of(*item) for item in shapes], in...  8.03 us
    pallas_call x2, Pallas kernels, on_device(): pl.pallas_call(functools.partial(first_kernel, tile) if first else functo...  6.55 us
    ppermute x8, waiting for transfers between devices, swap(): return lax.ppermute(array, axis, pairs)  3.71 us
  transfers between devices with their start and end apart: 24, of which 10 were waited for; matrix products, arithmetic and copies ran while one was open for 1% of the time, Pallas kernels for 13%

profile of v14, /device:TPU:0, one launch (start us, length us, event | category | flops | bytes accessed | tf_op | source)
XLA Modules:
  0.0 74.1 jit_solution(4548181625222337070)
XLA Ops:
  0.7 4.4 %project.3 = (bf16[512,128]{1,0:T(8,128)(2,1)}, bf16[512,128]{1,0:T(8,128)(2,1)}, f32[4,1024]{1,0:T(4,128)}) custom-call(bf16[512,512]{1,0:T(8,128)(2,1)} %inputs.3, bf16[512,256]{1,0:T(8,128)(2,1)} %key_weight.1, bf16[512,256]{1,0:T(8,128)(2,1)} %value_weight.1, bf16[2,1024,256]{2,1,0:T(8,128)(2,1)} %queries.4, bf16[2,1024,256]{2,1,0:T(8,128)(2,1)} %out_grad.3), custom_call_target="tpu_custom_call" | custom-call | flops 1073741824 | bytes 4194304 | tf_op jit(solution)/shard_map/project/pallas_call | solution.py:293
  5.1 3.0 %collective-permute-start.2 = (f32[4,1024]{1,0:T(4,128)}, f32[4,1024]{1,0:T(4,128)S(1)}, u32[]{:S(2)}, u32[]{:S(2)}) collective-permute-start(f32[4,1024]{1,0:T(4,128)} %get-tuple-element.33.mine.after), channel_id=1, source_target_pairs={{0,4},{4,0},{8,12},{12,8},{16,20},{20,16},{24,28},{28,24},{1,5},{5... | collective-permute-start | bytes 49160 | tf_op jit(solution)/shard_map/ppermute | solution.py:41
  8.2 2.1 %project.2 = (bf16[512,128]{1,0:T(8,128)(2,1)S(1)}, bf16[512,128]{1,0:T(8,128)(2,1)S(1)}, f32[4,1024]{1,0:T(4,128)S(1)}) custom-call(bf16[512,512]{1,0:T(8,128)(2,1)S(1)} %copy-done.3, bf16[512,256]{1,0:T(8,128)(2,1)S(1)} %copy-done.4, bf16[512,256]{1,0:T(8,128)(2,1)S(1)} %copy-done.5, bf16[2,1024,256]{2,1,0:T(8,128)(2,1)S(1)} %copy-done.1, ...), custom_call_target="tpu_custom_call" | custom-call | flops 1073741824 | bytes 4194304 | tf_op jit(solution)/shard_map/project/pallas_call | solution.py:293
  10.4 2.1 %collective-permute-start.3 = (f32[4,1024]{1,0:T(4,128)S(1)}, f32[4,1024]{1,0:T(4,128)S(1)}, u32[]{:S(2)}, u32[]{:S(2)}) collective-permute-start(f32[4,1024]{1,0:T(4,128)S(1)} %merge.6.mine.after), channel_id=1, source_target_pairs={{0,8},{4,12},{8,0},{12,4},{16,24},{20,28},{24,16},{28,20},{1,9},{5... | collective-permute-start | bytes 49160 | tf_op jit(solution)/shard_map/ppermute | solution.py:41
  12.6 1.5 %collective-permute-done.theirs = f32[4,1024]{1,0:T(4,128)S(1)} collective-permute-done((f32[4,1024]{1,0:T(4,128)S(1)}, f32[4,1024]{1,0:T(4,128)S(1)}, u32[]{:S(2)}, u32[]{:S(2)}) %collective-permute-start) | collective-permute-done | bytes 16416 | tf_op jit(solution)/shard_map/ppermute | solution.py:41
  14.1 1.6 %collective-permute-start.1 = (f32[4,1024]{1,0:T(4,128)S(1)}, f32[4,1024]{1,0:T(4,128)S(1)}, u32[]{:S(2)}, u32[]{:S(2)}) collective-permute-start(f32[4,1024]{1,0:T(4,128)S(1)} %merge.4.mine.after), channel_id=1, source_target_pairs={{0,8},{4,12},{8,0},{12,4},{16,24},{20,28},{24,16},{28,20},{1,9},{5... | collective-permute-start | bytes 49160 | tf_op jit(solution)/shard_map/ppermute | solution.py:41
  15.8 2.7 %collective-permute-start.4 = (f32[4,1024]{1,0:T(4,128)S(1)}, f32[4,1024]{1,0:T(4,128)S(1)}, u32[]{:S(2)}, u32[]{:S(2)}) collective-permute-start(f32[4,1024]{1,0:T(4,128)S(1)} %merge.7.mine), channel_id=1, source_target_pairs={{0,16},{4,20},{8,24},{12,28},{16,0},{20,4},{24,8},{28,12},{1,17},{... | collective-permute-start | bytes 49160 | tf_op jit(solution)/shard_map/ppermute | solution.py:41
  18.5 2.2 %collective-permute-done.4.theirs = f32[4,1024]{1,0:T(4,128)S(1)} collective-permute-done((f32[4,1024]{1,0:T(4,128)S(1)}, f32[4,1024]{1,0:T(4,128)S(1)}, u32[]{:S(2)}, u32[]{:S(2)}) %collective-permute-start.4) | collective-permute-done | bytes 16416 | tf_op jit(solution)/shard_map/ppermute | solution.py:41
  20.7 2.9 %grads.2 = (bf16[512,256]{1,0:T(8,128)(2,1)S(1)}, bf16[2,512,1024]{2,1,0:T(8,128)(2,1)S(1)}, f32[2,2,64,256]{3,2,1,0:T(8,128)S(1)}, f32[2,2,64,256]{3,2,1,0:T(8,128)S(1)}) custom-call(f32[4,1024]{1,0:T(4,128)S(1)} %merge.5.after.mine, bf16[512,512]{1,0:T(8,128)(2,1)S(1)} %copy-done.3, bf16[512,128]{1,0:T(8,128)(2,1)S(1)} %copy-done.6, ...), custom_call_target="tpu_custom_call" | custom-call | flops 1073741824 | bytes 4194304 | tf_op jit(solution)/shard_map/grads/pallas_call | solution.py:354
  24.0 2.6 %collective-permute-start.5 = (f32[4,1024]{1,0:T(4,128)S(1)}, f32[4,1024]{1,0:T(4,128)S(1)}, u32[]{:S(2)}, u32[]{:S(2)}) collective-permute-start(f32[4,1024]{1,0:T(4,128)S(1)} %merge.5.after.mine), channel_id=1, source_target_pairs={{0,16},{4,20},{8,24},{12,28},{16,0},{20,4},{24,8},{28,12},{1,17},{... | collective-permute-start | bytes 49160 | tf_op jit(solution)/shard_map/ppermute | solution.py:41
  27.7 1.7 %collective-permute-start.19 = (f32[4,2,128,128]{3,2,1,0:T(8,128)S(1)}, f32[4,2,128,128]{3,2,1,0:T(8,128)S(1)}, u32[]{:S(2)}, u32[]{:S(2)}) collective-permute-start(f32[4,2,128,128]{3,2,1,0:T(8,128)S(1)} %get-tuple-element.52), channel_id=1, source_target_pairs={{0,8},{4,12},{8,0},{12,4},{16,24},{20,28},{24,16},{28,20},{1,9},{5... | collective-permute-start | bytes 1572872 | tf_op jit(solution)/shard_map/ppermute | solution.py:56
  29.4 2.9 %grads.3 = (bf16[512,256]{1,0:T(8,128)(2,1)S(1)}, bf16[2,512,1024]{2,1,0:T(8,128)(2,1)S(1)}, f32[2,2,64,256]{3,2,1,0:T(8,128)S(1)}, f32[2,2,64,256]{3,2,1,0:T(8,128)S(1)}) custom-call(bf16[512,256]{1,0:T(8,128)(2,1)S(1)} %get-tuple-element.34.after.refs_0_, bf16[512,512]{1,0:T(8,128)(2,1)S(1)} %copy-done.3, bf16[512,128]{1,0:T(8,128)(2,1)S(1)} %get-tuple-element.35.keys, ...), custom_call_target="tpu_custom_call" | custom-call | flops 1073741824 | bytes 4194304 | tf_op jit(solution)/shard_map/grads/pallas_call | solution.py:354
  37.5 4.1 %collective-permute-done.13.theirs = f32[2,2,64,256]{3,2,1,0:T(8,128)S(1)} collective-permute-done((f32[2,2,64,256]{3,2,1,0:T(8,128)S(1)}, f32[2,2,64,256]{3,2,1,0:T(8,128)S(1)}, u32[]{:S(2)}, u32[]{:S(2)}) %collective-permute-start.13) | collective-permute-done | bytes 262176 | tf_op jit(solution)/shard_map/ppermute | solution.py:56
  42.7 1.5 %collective-permute-start.7 = (f32[2,512,128]{2,1,0:T(8,128)S(1)}, f32[2,512,128]{2,1,0:T(8,128)S(1)}, u32[]{:S(2)}, u32[]{:S(2)}) collective-permute-start(f32[2,512,128]{2,1,0:T(8,128)S(1)} %get-tuple-element.41), channel_id=1, source_target_pairs={{0,2},{1,3},{2,0},{3,1},{4,6},{5,7},{6,4},{7,5},{8,10},{9,11},{10,... | collective-permute-start | bytes 1572872 | tf_op jit(solution)/shard_map/ppermute | solution.py:41
  44.3 2.5 %collective-permute-start.10 = (f32[1,2,64,256]{3,2,1,0:T(8,128)S(1)}, f32[1,2,64,256]{3,2,1,0:T(8,128)S(1)}, u32[]{:S(2)}, u32[]{:S(2)}) collective-permute-start(f32[1,2,64,256]{3,2,1,0:T(8,128)S(1)} %fusion), channel_id=1, source_target_pairs={{0,24},{4,28},{8,16},{12,20},{16,8},{20,12},{24,0},{28,4},{1,25},{... | collective-permute-start | bytes 393224 | tf_op jit(solution)/shard_map/ppermute | solution.py:56
  46.8 2.1 %collective-permute-done.14 = f32[1,2,64,256]{3,2,1,0:T(8,128)S(1)} collective-permute-done((f32[1,2,64,256]{3,2,1,0:T(8,128)S(1)}, f32[1,2,64,256]{3,2,1,0:T(8,128)S(1)}, u32[]{:S(2)}, u32[]{:S(2)}) %collective-permute-start.14) | collective-permute-done | bytes 131104 | tf_op jit(solution)/shard_map/ppermute | solution.py:56
  49.0 2.8 %collective-permute-start.15 = (f32[1,2,64,256]{3,2,1,0:T(8,128)S(1)}, f32[1,2,64,256]{3,2,1,0:T(8,128)S(1)}, u32[]{:S(2)}, u32[]{:S(2)}) collective-permute-start(f32[1,2,64,256]{3,2,1,0:T(8,128)S(1)} %add.51.mine), channel_id=1, source_target_pairs={{0,24},{4,28},{8,16},{12,20},{16,8},{20,12},{24,0},{28,4},{1,25},{... | collective-permute-start | bytes 393224 | tf_op jit(solution)/shard_map/ppermute | solution.py:56
  53.1 3.9 %collective-permute-done.15.theirs = f32[1,2,64,256]{3,2,1,0:T(8,128)S(1)} collective-permute-done((f32[1,2,64,256]{3,2,1,0:T(8,128)S(1)}, f32[1,2,64,256]{3,2,1,0:T(8,128)S(1)}, u32[]{:S(2)}, u32[]{:S(2)}) %collective-permute-start.15) | collective-permute-done | bytes 131104 | tf_op jit(solution)/shard_map/ppermute | solution.py:56
  57.1 2.0 %collective-permute-start.22 = (f32[2,2,128,128]{3,2,1,0:T(8,128)S(1)}, f32[2,2,128,128]{3,2,1,0:T(8,128)S(1)}, u32[]{:S(2)}, u32[]{:S(2)}) collective-permute-start(f32[2,2,128,128]{3,2,1,0:T(8,128)S(1)} %get-tuple-element.57.after), channel_id=1, source_target_pairs={{0,8},{4,12},{8,0},{12,4},{16,24},{20,28},{24,16},{28,20},{1,9},{5... | collective-permute-start | bytes 786440 | tf_op jit(solution)/shard_map/ppermute | solution.py:56
  59.7 2.3 %collective-permute-done.17 = f32[1,2,64,256]{3,2,1,0:T(8,128)S(1)} collective-permute-done((f32[1,2,64,256]{3,2,1,0:T(8,128)S(1)}, f32[1,2,64,256]{3,2,1,0:T(8,128)S(1)}, u32[]{:S(2)}, u32[]{:S(2)}) %collective-permute-start.17) | collective-permute-done | bytes 131104 | tf_op jit(solution)/shard_map/ppermute | solution.py:56
  62.5 2.8 %collective-permute-start.21 = (f32[1,2,128,128]{3,2,1,0:T(8,128)S(1)}, f32[1,2,128,128]{3,2,1,0:T(8,128)S(1)}, u32[]{:S(2)}, u32[]{:S(2)}) collective-permute-start(f32[1,2,128,128]{3,2,1,0:T(8,128)S(1)} %get-tuple-element.64), channel_id=1, source_target_pairs={{0,24},{4,28},{8,16},{12,20},{16,8},{20,12},{24,0},{28,4},{1,25},{... | collective-permute-start | bytes 393224 | tf_op jit(solution)/shard_map/ppermute | solution.py:56
  65.5 1.6 %collective-permute-start.23 = (f32[1,2,128,128]{3,2,1,0:T(8,128)S(1)}, f32[1,2,128,128]{3,2,1,0:T(8,128)S(1)}, u32[]{:S(2)}, u32[]{:S(2)}) collective-permute-start(f32[1,2,128,128]{3,2,1,0:T(8,128)S(1)} %get-tuple-element.62), channel_id=1, source_target_pairs={{0,24},{4,28},{8,16},{12,20},{16,8},{20,12},{24,0},{28,4},{1,25},{... | collective-permute-start | bytes 393224 | tf_op jit(solution)/shard_map/ppermute | solution.py:56
  67.1 1.5 %collective-permute-done.18.refs_5_ = f32[2,2,64,256]{3,2,1,0:T(8,128)S(1)} collective-permute-done((f32[2,2,64,256]{3,2,1,0:T(8,128)S(1)}, f32[2,2,64,256]{3,2,1,0:T(8,128)S(1)}, u32[]{:S(2)}, u32[]{:S(2)}) %collective-permute-start.18) | collective-permute-done | bytes 262176 | tf_op jit(solution)/shard_map/ppermute | solution.py:56
  69.8 3.5 %collective-permute-done.23.refs_3_ = f32[1,2,128,128]{3,2,1,0:T(8,128)S(1)} collective-permute-done((f32[1,2,128,128]{3,2,1,0:T(8,128)S(1)}, f32[1,2,128,128]{3,2,1,0:T(8,128)S(1)}, u32[]{:S(2)}, u32[]{:S(2)}) %collective-permute-start.23) | collective-permute-done | bytes 131104 | tf_op jit(solution)/shard_map/ppermute | solution.py:56
  (66 shorter events, 12.7 us)
Async XLA Ops:
  5.1 5.3 %collective-permute-start.2 = (f32[4,1024]{1,0:T(4,128)}, f32[4,1024]{1,0:T(4,128)S(1)}, u32[]{:S(2)}, u32[]{:S(2)}) collective-permute-start(f32[4,1024]{1,0:T(4,128)} %get-tuple-element.33.mine.after), channel_id=1, source_target_pairs={{0,4},{4,0},{8,12},{12,8},{16,20},{20,16},{24,28},{28,24},{1,5},{5... | collective-permute-start | bytes 49160 | tf_op jit(solution)/shard_map/ppermute | solution.py:41
  10.3 3.8 %collective-permute-start = (f32[4,1024]{1,0:T(4,128)S(1)}, f32[4,1024]{1,0:T(4,128)S(1)}, u32[]{:S(2)}, u32[]{:S(2)}) collective-permute-start(f32[4,1024]{1,0:T(4,128)S(1)} %get-tuple-element.30.mine.after), channel_id=1, source_target_pairs={{0,4},{4,0},{8,12},{12,8},{16,20},{20,16},{24,28},{28,24},{1,5},{5... | collective-permute-start | bytes 49160 | tf_op jit(solution)/shard_map/ppermute | solution.py:41
  10.4 5.3 %collective-permute-start.3 = (f32[4,1024]{1,0:T(4,128)S(1)}, f32[4,1024]{1,0:T(4,128)S(1)}, u32[]{:S(2)}, u32[]{:S(2)}) collective-permute-start(f32[4,1024]{1,0:T(4,128)S(1)} %merge.6.mine.after), channel_id=1, source_target_pairs={{0,8},{4,12},{8,0},{12,4},{16,24},{20,28},{24,16},{28,20},{1,9},{5... | collective-permute-start | bytes 49160 | tf_op jit(solution)/shard_map/ppermute | solution.py:41
  14.1 4.3 %collective-permute-start.1 = (f32[4,1024]{1,0:T(4,128)S(1)}, f32[4,1024]{1,0:T(4,128)S(1)}, u32[]{:S(2)}, u32[]{:S(2)}) collective-permute-start(f32[4,1024]{1,0:T(4,128)S(1)} %merge.4.mine.after), channel_id=1, source_target_pairs={{0,8},{4,12},{8,0},{12,4},{16,24},{20,28},{24,16},{28,20},{1,9},{5... | collective-permute-start | bytes 49160 | tf_op jit(solution)/shard_map/ppermute | solution.py:41
  15.8 4.9 %collective-permute-start.4 = (f32[4,1024]{1,0:T(4,128)S(1)}, f32[4,1024]{1,0:T(4,128)S(1)}, u32[]{:S(2)}, u32[]{:S(2)}) collective-permute-start(f32[4,1024]{1,0:T(4,128)S(1)} %merge.7.mine), channel_id=1, source_target_pairs={{0,16},{4,20},{8,24},{12,28},{16,0},{20,4},{24,8},{28,12},{1,17},{... | collective-permute-start | bytes 49160 | tf_op jit(solution)/shard_map/ppermute | solution.py:41
  23.6 9.9 %collective-permute-start.6 = (f32[2,2,64,256]{3,2,1,0:T(8,128)S(1)}, f32[2,2,64,256]{3,2,1,0:T(8,128)S(1)}, u32[]{:S(2)}, u32[]{:S(2)}) collective-permute-start(f32[2,2,64,256]{3,2,1,0:T(8,128)S(1)} %get-tuple-element.39), channel_id=1, source_target_pairs={{0,4},{4,0},{8,12},{12,8},{16,20},{20,16},{24,28},{28,24},{1,5},{5... | collective-permute-start | bytes 786440 | tf_op jit(solution)/shard_map/ppermute | solution.py:56
  24.0 5.4 %collective-permute-start.5 = (f32[4,1024]{1,0:T(4,128)S(1)}, f32[4,1024]{1,0:T(4,128)S(1)}, u32[]{:S(2)}, u32[]{:S(2)}) collective-permute-start(f32[4,1024]{1,0:T(4,128)S(1)} %merge.5.after.mine), channel_id=1, source_target_pairs={{0,16},{4,20},{8,24},{12,28},{16,0},{20,4},{24,8},{28,12},{1,17},{... | collective-permute-start | bytes 49160 | tf_op jit(solution)/shard_map/ppermute | solution.py:41
  27.7 24.0 %collective-permute-start.19 = (f32[4,2,128,128]{3,2,1,0:T(8,128)S(1)}, f32[4,2,128,128]{3,2,1,0:T(8,128)S(1)}, u32[]{:S(2)}, u32[]{:S(2)}) collective-permute-start(f32[4,2,128,128]{3,2,1,0:T(8,128)S(1)} %get-tuple-element.52), channel_id=1, source_target_pairs={{0,8},{4,12},{8,0},{12,4},{16,24},{20,28},{24,16},{28,20},{1,9},{5... | collective-permute-start | bytes 1572872 | tf_op jit(solution)/shard_map/ppermute | solution.py:56
  32.3 9.3 %collective-permute-start.13 = (f32[2,2,64,256]{3,2,1,0:T(8,128)S(1)}, f32[2,2,64,256]{3,2,1,0:T(8,128)S(1)}, u32[]{:S(2)}, u32[]{:S(2)}) collective-permute-start(f32[2,2,64,256]{3,2,1,0:T(8,128)S(1)} %get-tuple-element.43), channel_id=1, source_target_pairs={{0,4},{4,0},{8,12},{12,8},{16,20},{20,16},{24,28},{28,24},{1,5},{5... | collective-permute-start | bytes 786440 | tf_op jit(solution)/shard_map/ppermute | solution.py:56
  33.5 10.7 %collective-permute-start.9 = (f32[1,2,64,256]{3,2,1,0:T(8,128)S(1)}, f32[1,2,64,256]{3,2,1,0:T(8,128)S(1)}, u32[]{:S(2)}, u32[]{:S(2)}) collective-permute-start(f32[1,2,64,256]{3,2,1,0:T(8,128)S(1)} %slice_add_fusion.11.refs_2_), channel_id=1, source_target_pairs={{0,8},{4,12},{8,0},{12,4},{16,24},{20,28},{24,16},{28,20},{1,9},{5... | collective-permute-start | bytes 393224 | tf_op jit(solution)/shard_map/ppermute | solution.py:56
  35.5 17.5 %collective-permute-start.16 = (f32[4,2,128,128]{3,2,1,0:T(8,128)S(1)}, f32[4,2,128,128]{3,2,1,0:T(8,128)S(1)}, u32[]{:S(2)}, u32[]{:S(2)}) collective-permute-start(f32[4,2,128,128]{3,2,1,0:T(8,128)S(1)} %get-tuple-element.48), channel_id=1, source_target_pairs={{0,4},{4,0},{8,12},{12,8},{16,20},{20,16},{24,28},{28,24},{1,5},{5... | collective-permute-start | bytes 1572872 | tf_op jit(solution)/shard_map/ppermute | solution.py:56
  41.7 7.3 %collective-permute-start.14 = (f32[1,2,64,256]{3,2,1,0:T(8,128)S(1)}, f32[1,2,64,256]{3,2,1,0:T(8,128)S(1)}, u32[]{:S(2)}, u32[]{:S(2)}) collective-permute-start(f32[1,2,64,256]{3,2,1,0:T(8,128)S(1)} %get-tuple-element.45), channel_id=1, source_target_pairs={{0,8},{4,12},{8,0},{12,4},{16,24},{20,28},{24,16},{28,20},{1,9},{5... | collective-permute-start | bytes 393224 | tf_op jit(solution)/shard_map/ppermute | solution.py:56
  42.7 22.6 %collective-permute-start.7 = (f32[2,512,128]{2,1,0:T(8,128)S(1)}, f32[2,512,128]{2,1,0:T(8,128)S(1)}, u32[]{:S(2)}, u32[]{:S(2)}) collective-permute-start(f32[2,512,128]{2,1,0:T(8,128)S(1)} %get-tuple-element.41), channel_id=1, source_target_pairs={{0,2},{1,3},{2,0},{3,1},{4,6},{5,7},{6,4},{7,5},{8,10},{9,11},{10,... | collective-permute-start | bytes 1572872 | tf_op jit(solution)/shard_map/ppermute | solution.py:41
  44.3 8.0 %collective-permute-start.10 = (f32[1,2,64,256]{3,2,1,0:T(8,128)S(1)}, f32[1,2,64,256]{3,2,1,0:T(8,128)S(1)}, u32[]{:S(2)}, u32[]{:S(2)}) collective-permute-start(f32[1,2,64,256]{3,2,1,0:T(8,128)S(1)} %fusion), channel_id=1, source_target_pairs={{0,24},{4,28},{8,16},{12,20},{16,8},{20,12},{24,0},{28,4},{1,25},{... | collective-permute-start | bytes 393224 | tf_op jit(solution)/shard_map/ppermute | solution.py:56
  49.0 8.0 %collective-permute-start.15 = (f32[1,2,64,256]{3,2,1,0:T(8,128)S(1)}, f32[1,2,64,256]{3,2,1,0:T(8,128)S(1)}, u32[]{:S(2)}, u32[]{:S(2)}) collective-permute-start(f32[1,2,64,256]{3,2,1,0:T(8,128)S(1)} %add.51.mine), channel_id=1, source_target_pairs={{0,24},{4,28},{8,16},{12,20},{16,8},{20,12},{24,0},{28,4},{1,25},{... | collective-permute-start | bytes 393224 | tf_op jit(solution)/shard_map/ppermute | solution.py:56
  51.8 10.6 %collective-permute-start.20 = (f32[2,2,128,128]{3,2,1,0:T(8,128)S(1)}, f32[2,2,128,128]{3,2,1,0:T(8,128)S(1)}, u32[]{:S(2)}, u32[]{:S(2)}) collective-permute-start(f32[2,2,128,128]{3,2,1,0:T(8,128)S(1)} %get-tuple-element.59), channel_id=1, source_target_pairs={{0,4},{4,0},{8,12},{12,8},{16,20},{20,16},{24,28},{28,24},{1,5},{5... | collective-permute-start | bytes 786440 | tf_op jit(solution)/shard_map/ppermute | solution.py:56
  52.3 7.0 %collective-permute-start.11 = (f32[1,2,64,256]{3,2,1,0:T(8,128)S(1)}, f32[1,2,64,256]{3,2,1,0:T(8,128)S(1)}, u32[]{:S(2)}, u32[]{:S(2)}) collective-permute-start(f32[1,2,64,256]{3,2,1,0:T(8,128)S(1)} %add.50), channel_id=1, source_target_pairs={{0,8},{4,12},{8,0},{12,4},{16,24},{20,28},{24,16},{28,20},{1,9},{5... | collective-permute-start | bytes 393224 | tf_op jit(solution)/shard_map/ppermute | solution.py:56
  57.0 5.0 %collective-permute-start.17 = (f32[1,2,64,256]{3,2,1,0:T(8,128)S(1)}, f32[1,2,64,256]{3,2,1,0:T(8,128)S(1)}, u32[]{:S(2)}, u32[]{:S(2)}) collective-permute-start(f32[1,2,64,256]{3,2,1,0:T(8,128)S(1)} %added.1), channel_id=1, source_target_pairs={{0,8},{4,12},{8,0},{12,4},{16,24},{20,28},{24,16},{28,20},{1,9},{5... | collective-permute-start | bytes 393224 | tf_op jit(solution)/shard_map/ppermute | solution.py:56
  57.1 8.4 %collective-permute-start.22 = (f32[2,2,128,128]{3,2,1,0:T(8,128)S(1)}, f32[2,2,128,128]{3,2,1,0:T(8,128)S(1)}, u32[]{:S(2)}, u32[]{:S(2)}) collective-permute-start(f32[2,2,128,128]{3,2,1,0:T(8,128)S(1)} %get-tuple-element.57.after), channel_id=1, source_target_pairs={{0,8},{4,12},{8,0},{12,4},{16,24},{20,28},{24,16},{28,20},{1,9},{5... | collective-permute-start | bytes 786440 | tf_op jit(solution)/shard_map/ppermute | solution.py:56
  59.4 7.7 %collective-permute-start.12 = (f32[2,2,64,256]{3,2,1,0:T(8,128)S(1)}, f32[2,2,64,256]{3,2,1,0:T(8,128)S(1)}, u32[]{:S(2)}, u32[]{:S(2)}) collective-permute-start(f32[2,2,64,256]{3,2,1,0:T(8,128)S(1)} %pad_maximum_fusion.refs_2_), channel_id=1, source_target_pairs={{0,4},{4,0},{8,12},{12,8},{16,20},{20,16},{24,28},{28,24},{1,5},{5... | collective-permute-start | bytes 786440 | tf_op jit(solution)/shard_map/ppermute | solution.py:56
  62.1 6.6 %collective-permute-start.18 = (f32[2,2,64,256]{3,2,1,0:T(8,128)S(1)}, f32[2,2,64,256]{3,2,1,0:T(8,128)S(1)}, u32[]{:S(2)}, u32[]{:S(2)}) collective-permute-start(f32[2,2,64,256]{3,2,1,0:T(8,128)S(1)} %pad_maximum_fusion.1.refs_4_), channel_id=1, source_target_pairs={{0,4},{4,0},{8,12},{12,8},{16,20},{20,16},{24,28},{28,24},{1,5},{5... | collective-permute-start | bytes 786440 | tf_op jit(solution)/shard_map/ppermute | solution.py:56
  62.5 7.4 %collective-permute-start.21 = (f32[1,2,128,128]{3,2,1,0:T(8,128)S(1)}, f32[1,2,128,128]{3,2,1,0:T(8,128)S(1)}, u32[]{:S(2)}, u32[]{:S(2)}) collective-permute-start(f32[1,2,128,128]{3,2,1,0:T(8,128)S(1)} %get-tuple-element.64), channel_id=1, source_target_pairs={{0,24},{4,28},{8,16},{12,20},{16,8},{20,12},{24,0},{28,4},{1,25},{... | collective-permute-start | bytes 393224 | tf_op jit(solution)/shard_map/ppermute | solution.py:56
  65.4 3.3 %collective-permute-start.8 = (f32[1,512,128]{2,1,0:T(8,128)S(1)}, f32[1,512,128]{2,1,0:T(8,128)S(1)}, u32[]{:S(2)}, u32[]{:S(2)}) collective-permute-start(f32[1,512,128]{2,1,0:T(8,128)S(1)} %get-tuple-element.60), channel_id=1, source_target_pairs={{0,1},{1,0},{2,3},{3,2},{4,5},{5,4},{6,7},{7,6},{8,9},{9,8},{10,11... | collective-permute-start | bytes 786440 | tf_op jit(solution)/shard_map/ppermute | solution.py:41
  65.5 7.9 %collective-permute-start.23 = (f32[1,2,128,128]{3,2,1,0:T(8,128)S(1)}, f32[1,2,128,128]{3,2,1,0:T(8,128)S(1)}, u32[]{:S(2)}, u32[]{:S(2)}) collective-permute-start(f32[1,2,128,128]{3,2,1,0:T(8,128)S(1)} %get-tuple-element.62), channel_id=1, source_target_pairs={{0,24},{4,28},{8,16},{12,20},{16,8},{20,12},{24,0},{28,4},{1,25},{... | collective-permute-start | bytes 393224 | tf_op jit(solution)/shard_map/ppermute | solution.py:56
  (8 other events, 73.9 us)

commit v15 on v12

--- a/solution.py
+++ b/solution.py
@@ -64,16 +64,15 @@
     tile, cols, wait, inputs, key_weight, value_weight, queries, out_grad, keys, values, stats
 ):
     reads, latents, _ = queries.shape
-    wait(0, 1)
+    wait("inputs")
+    wait("key_weight")
     keys[...] = plain_dot(inputs[...], key_weight[:, cols]).astype(jnp.bfloat16)
-    wait(2)
+    wait("value_weight")
     values[...] = plain_dot(inputs[...], value_weight[:, cols]).astype(jnp.bfloat16)
-    wait(3, 4)
-
-    @pl.loop(0, latents // tile, unroll=True)
-    def _(step):
-        at = pl.ds(pl.multiple_of(step * tile, tile), tile)
+    for step in range(latents // tile):
+        at = slice(step * tile, (step + 1) * tile)
         for read_index in range(reads):
+            wait((read_index, step))
             scores = last_contract(keys[...], queries[read_index, at, cols])
             scores = scores * (FACTOR * LOG2_E)
             weighted = last_contract(values[...], out_grad[read_index, at, cols])
@@ -87,17 +86,30 @@
 
 def first_kernel(tile, *refs):
     sources, results, targets, sems = refs[:5], refs[5:8], refs[8:13], refs[13]
-    loads = []
-    for index, (source, target) in enumerate(zip(sources, targets)):
-        if index:
-            source = source.at[..., :HD]
-        loads.append(pltpu.make_async_copy(source, target, sems.at[index]))
-    for load in loads:
-        load.start()
-
-    def wait(*places):
-        for place in places:
-            loads[place].wait()
+    reads, latents, _ = targets[3].shape
+    loads = {}
+
+    def load(name, source, target):
+        sem = sems.at[sum(len(copies) for copies in loads.values())]
+        loads.setdefault(name, []).append(pltpu.make_async_copy(source, target, sem))
+        loads[name][-1].start()
+
+    load("inputs", sources[0], targets[0])
+    load("key_weight", sources[1].at[:, :HD], targets[1])
+    load("value_weight", sources[2].at[:, :HD], targets[2])
+    for step in range(latents // tile):
+        at = pl.ds(step * tile, tile)
+        for read_index in range(reads):
+            for source, target in zip(sources[3:], targets[3:]):
+                load(
+                    (read_index, step),
+                    source.at[read_index, at, :HD],
+                    target.at[read_index, at, :],
+                )
+
+    def wait(name):
+        for copy in loads[name]:
+            copy.wait()
 
     head_statistics(tile, slice(0, HD), wait, *targets, *results)
 
@@ -293,7 +305,9 @@
                 ),
                 in_specs=[HBM if first else VMEM] * 5,
                 out_specs=(VMEM,) * 3,
-                scratch_shapes=loaded + [pltpu.SemaphoreType.DMA((5,))] if first else [],
+                scratch_shapes=loaded + [pltpu.SemaphoreType.DMA((3 + 2 * reads * (latents // tile),))]
+                if first
+                else [],
                 compiler_params=params(57 if first else 16),
                 cost_estimate=block_work,
                 name="project",

time: 71.6 us -> 73.6 us (1.028)
  Pallas kernels: 17.4 us -> 19.6 us
    pallas_call x2, Pallas kernels: 6.55 us -> 8.47 us  [on_device(): pl.pallas_call(functools.partial(first_kernel, tile) if first else functo...]
where the time goes in v15:
time: 73.6 us; the launch traced here: 73.4 us
  starting transfers between devices  37 us (50%)
  Pallas kernels  19.6 us (27%)
  waiting for transfers between devices  15.5 us (21%)
  between operations  0.89 us (1%)
    ppermute x16, starting transfers between devices, row_swap_of(): return lax.ppermute(array, 'rows', pairs)  22.9 us
    ppermute x8, starting transfers between devices, swap(): return lax.ppermute(array, axis, pairs)  14.1 us
    ppermute x16, waiting for transfers between devices, row_swap_of(): return lax.ppermute(array, 'rows', pairs)  14 us
    pallas_call x2, Pallas kernels, on_device(): pl.pallas_call(functools.partial(first_kernel, tile) if first else functo...  8.47 us
    pallas_call x4, Pallas kernels, kernel_call(): pl.pallas_call(kernel, out_shape=[shape_of(*item) for item in shapes], in...  8.23 us
    ppermute x8, waiting for transfers between devices, swap(): return lax.ppermute(array, axis, pairs)  1.54 us
  transfers between devices with their start and end apart: 24, of which 9 were waited for; matrix products, arithmetic and copies ran while one was open for 1% of the time, Pallas kernels for 17%

profile of v15, /device:TPU:0, one launch (start us, length us, event | category | flops | bytes accessed | tf_op | source)
XLA Modules:
  0.0 73.4 jit_solution(16580991699055489539)
XLA Ops:
  0.7 6.3 %project.2 = (bf16[512,128]{1,0:T(8,128)(2,1)}, bf16[512,128]{1,0:T(8,128)(2,1)}, f32[4,1024]{1,0:T(4,128)}) custom-call(bf16[512,512]{1,0:T(8,128)(2,1)} %inputs.3, bf16[512,256]{1,0:T(8,128)(2,1)} %key_weight.1, bf16[512,256]{1,0:T(8,128)(2,1)} %value_weight.1, bf16[2,1024,256]{2,1,0:T(8,128)(2,1)} %queries.4, bf16[2,1024,256]{2,1,0:T(8,128)(2,1)} %out_grad.3), custom_call_target="tpu_custom_call" | custom-call | flops 1073741824 | bytes 4194304 | tf_op jit(solution)/shard_map/project/pallas_call | solution.py:297
  7.1 3.0 %collective-permute-start = (f32[4,1024]{1,0:T(4,128)}, f32[4,1024]{1,0:T(4,128)S(1)}, u32[]{:S(2)}, u32[]{:S(2)}) collective-permute-start(f32[4,1024]{1,0:T(4,128)} %get-tuple-element.28.mine), channel_id=1, source_target_pairs={{0,4},{4,0},{8,12},{12,8},{16,20},{20,16},{24,28},{28,24},{1,5},{5... | collective-permute-start | bytes 49160 | tf_op jit(solution)/shard_map/ppermute | solution.py:41
  10.1 2.1 %project.3 = (bf16[512,128]{1,0:T(8,128)(2,1)S(1)}, bf16[512,128]{1,0:T(8,128)(2,1)S(1)}, f32[4,1024]{1,0:T(4,128)S(1)}) custom-call(bf16[512,512]{1,0:T(8,128)(2,1)S(1)} %copy-done.3, bf16[512,256]{1,0:T(8,128)(2,1)S(1)} %copy-done.4, bf16[512,256]{1,0:T(8,128)(2,1)S(1)} %copy-done.5, bf16[2,1024,256]{2,1,0:T(8,128)(2,1)S(1)} %copy-done.1, ...), custom_call_target="tpu_custom_call" | custom-call | flops 1073741824 | bytes 4194304 | tf_op jit(solution)/shard_map/project/pallas_call | solution.py:297
  12.4 2.1 %collective-permute-start.1 = (f32[4,1024]{1,0:T(4,128)S(1)}, f32[4,1024]{1,0:T(4,128)S(1)}, u32[]{:S(2)}, u32[]{:S(2)}) collective-permute-start(f32[4,1024]{1,0:T(4,128)S(1)} %merge.4.mine), channel_id=1, source_target_pairs={{0,8},{4,12},{8,0},{12,4},{16,24},{20,28},{24,16},{28,20},{1,9},{5... | collective-permute-start | bytes 49160 | tf_op jit(solution)/shard_map/ppermute | solution.py:41
  14.5 1.5 %collective-permute-done.3.theirs = f32[4,1024]{1,0:T(4,128)S(1)} collective-permute-done((f32[4,1024]{1,0:T(4,128)S(1)}, f32[4,1024]{1,0:T(4,128)S(1)}, u32[]{:S(2)}, u32[]{:S(2)}) %collective-permute-start.3) | collective-permute-done | bytes 16416 | tf_op jit(solution)/shard_map/ppermute | solution.py:41
  16.1 1.6 %collective-permute-start.4 = (f32[4,1024]{1,0:T(4,128)S(1)}, f32[4,1024]{1,0:T(4,128)S(1)}, u32[]{:S(2)}, u32[]{:S(2)}) collective-permute-start(f32[4,1024]{1,0:T(4,128)S(1)} %merge.6.mine), channel_id=1, source_target_pairs={{0,8},{4,12},{8,0},{12,4},{16,24},{20,28},{24,16},{28,20},{1,9},{5... | collective-permute-start | bytes 49160 | tf_op jit(solution)/shard_map/ppermute | solution.py:41
  17.7 2.7 %collective-permute-start.2 = (f32[4,1024]{1,0:T(4,128)S(1)}, f32[4,1024]{1,0:T(4,128)S(1)}, u32[]{:S(2)}, u32[]{:S(2)}) collective-permute-start(f32[4,1024]{1,0:T(4,128)S(1)} %merge.5.after.mine), channel_id=1, source_target_pairs={{0,16},{4,20},{8,24},{12,28},{16,0},{20,4},{24,8},{28,12},{1,17},{... | collective-permute-start | bytes 49160 | tf_op jit(solution)/shard_map/ppermute | solution.py:41
  20.4 2.2 %collective-permute-start.5 = (f32[4,1024]{1,0:T(4,128)S(1)}, f32[4,1024]{1,0:T(4,128)S(1)}, u32[]{:S(2)}, u32[]{:S(2)}) collective-permute-start(f32[4,1024]{1,0:T(4,128)S(1)} %merge.7.mine), channel_id=1, source_target_pairs={{0,16},{4,20},{8,24},{12,28},{16,0},{20,4},{24,8},{28,12},{1,17},{... | collective-permute-start | bytes 49160 | tf_op jit(solution)/shard_map/ppermute | solution.py:41
  22.7 2.9 %grads.2 = (bf16[512,256]{1,0:T(8,128)(2,1)S(1)}, bf16[2,512,1024]{2,1,0:T(8,128)(2,1)S(1)}, f32[2,2,64,256]{3,2,1,0:T(8,128)S(1)}, f32[2,2,64,256]{3,2,1,0:T(8,128)S(1)}) custom-call(f32[4,1024]{1,0:T(4,128)S(1)} %merge.5.after.mine, bf16[512,512]{1,0:T(8,128)(2,1)S(1)} %copy-done.3, bf16[512,128]{1,0:T(8,128)(2,1)S(1)} %copy-done.6, ...), custom_call_target="tpu_custom_call" | custom-call | flops 1073741824 | bytes 4194304 | tf_op jit(solution)/shard_map/grads/pallas_call | solution.py:355
  27.2 1.8 %collective-permute-start.15 = (f32[4,2,128,128]{3,2,1,0:T(8,128)S(1)}, f32[4,2,128,128]{3,2,1,0:T(8,128)S(1)}, u32[]{:S(2)}, u32[]{:S(2)}) collective-permute-start(f32[4,2,128,128]{3,2,1,0:T(8,128)S(1)} %get-tuple-element.44), channel_id=1, source_target_pairs={{0,8},{4,12},{8,0},{12,4},{16,24},{20,28},{24,16},{28,20},{1,9},{5... | collective-permute-start | bytes 1572872 | tf_op jit(solution)/shard_map/ppermute | solution.py:56
  29.0 2.9 %grads.3 = (bf16[512,256]{1,0:T(8,128)(2,1)S(1)}, bf16[2,512,1024]{2,1,0:T(8,128)(2,1)S(1)}, f32[2,2,64,256]{3,2,1,0:T(8,128)S(1)}, f32[2,2,64,256]{3,2,1,0:T(8,128)S(1)}) custom-call(bf16[512,256]{1,0:T(8,128)(2,1)S(1)} %get-tuple-element.31.after.refs_0_, bf16[512,512]{1,0:T(8,128)(2,1)S(1)} %copy-done.3, bf16[512,128]{1,0:T(8,128)(2,1)S(1)} %get-tuple-element.32.keys, ...), custom_call_target="tpu_custom_call" | custom-call | flops 1073741824 | bytes 4194304 | tf_op jit(solution)/shard_map/grads/pallas_call | solution.py:355
  31.9 1.5 %collective-permute-start.13 = (f32[2,2,64,256]{3,2,1,0:T(8,128)S(1)}, f32[2,2,64,256]{3,2,1,0:T(8,128)S(1)}, u32[]{:S(2)}, u32[]{:S(2)}) collective-permute-start(f32[2,2,64,256]{3,2,1,0:T(8,128)S(1)} %get-tuple-element.41), channel_id=1, source_target_pairs={{0,4},{4,0},{8,12},{12,8},{16,20},{20,16},{24,28},{28,24},{1,5},{5... | collective-permute-start | bytes 786440 | tf_op jit(solution)/shard_map/ppermute | solution.py:56
  33.3 1.3 %query.3 = (f32[4,2,128,128]{3,2,1,0:T(8,128)S(1)}, f32[4,2,128,128]{3,2,1,0:T(8,128)S(1)}) custom-call(bf16[512,256]{1,0:T(8,128)(2,1)S(1)} %get-tuple-element.35.refs_1_.after, bf16[2,512,1024]{2,1,0:T(8,128)(2,1)S(1)} %get-tuple-element.46.score_grads, bf16[512,128]{1,0:T(8,128)(2,1)S(1)} %get-tuple-element.32.keys), custom_call_target="tpu_custom_call" | custom-call | flops 1073741824 | bytes 4194304 | tf_op jit(solution)/shard_map/query/pallas_call | solution.py:355
  35.8 5.4 %collective-permute-done.13 = f32[2,2,64,256]{3,2,1,0:T(8,128)S(1)} collective-permute-done((f32[2,2,64,256]{3,2,1,0:T(8,128)S(1)}, f32[2,2,64,256]{3,2,1,0:T(8,128)S(1)}, u32[]{:S(2)}, u32[]{:S(2)}) %collective-permute-start.13) | collective-permute-done | bytes 262176 | tf_op jit(solution)/shard_map/ppermute | solution.py:56
  42.1 5.3 %collective-permute-start.8 = (f32[1,2,64,256]{3,2,1,0:T(8,128)S(1)}, f32[1,2,64,256]{3,2,1,0:T(8,128)S(1)}, u32[]{:S(2)}, u32[]{:S(2)}) collective-permute-start(f32[1,2,64,256]{3,2,1,0:T(8,128)S(1)} %fusion), channel_id=1, source_target_pairs={{0,24},{4,28},{8,16},{12,20},{16,8},{20,12},{24,0},{28,4},{1,25},{... | collective-permute-start | bytes 393224 | tf_op jit(solution)/shard_map/ppermute | solution.py:56
  47.9 2.5 %collective-permute-start.16 = (f32[1,2,64,256]{3,2,1,0:T(8,128)S(1)}, f32[1,2,64,256]{3,2,1,0:T(8,128)S(1)}, u32[]{:S(2)}, u32[]{:S(2)}) collective-permute-start(f32[1,2,64,256]{3,2,1,0:T(8,128)S(1)} %added.1), channel_id=1, source_target_pairs={{0,24},{4,28},{8,16},{12,20},{16,8},{20,12},{24,0},{28,4},{1,25},{... | collective-permute-start | bytes 393224 | tf_op jit(solution)/shard_map/ppermute | solution.py:56
  52.4 2.3 %collective-permute-start.9 = (f32[2,512,128]{2,1,0:T(8,128)S(1)}, f32[2,512,128]{2,1,0:T(8,128)S(1)}, u32[]{:S(2)}, u32[]{:S(2)}) collective-permute-start(f32[2,512,128]{2,1,0:T(8,128)S(1)} %get-tuple-element.39), channel_id=1, source_target_pairs={{0,2},{1,3},{2,0},{3,1},{4,6},{5,7},{6,4},{7,5},{8,10},{9,11},{10,... | collective-permute-start | bytes 1572872 | tf_op jit(solution)/shard_map/ppermute | solution.py:41
  54.8 2.1 %collective-permute-start.22 = (f32[2,2,128,128]{3,2,1,0:T(8,128)S(1)}, f32[2,2,128,128]{3,2,1,0:T(8,128)S(1)}, u32[]{:S(2)}, u32[]{:S(2)}) collective-permute-start(f32[2,2,128,128]{3,2,1,0:T(8,128)S(1)} %get-tuple-element.53), channel_id=1, source_target_pairs={{0,8},{4,12},{8,0},{12,4},{16,24},{20,28},{24,16},{28,20},{1,9},{5... | collective-permute-start | bytes 786440 | tf_op jit(solution)/shard_map/ppermute | solution.py:56
  57.0 1.4 %collective-permute-done.11 = f32[1,2,64,256]{3,2,1,0:T(8,128)S(1)} collective-permute-done((f32[1,2,64,256]{3,2,1,0:T(8,128)S(1)}, f32[1,2,64,256]{3,2,1,0:T(8,128)S(1)}, u32[]{:S(2)}, u32[]{:S(2)}) %collective-permute-start.11) | collective-permute-done | bytes 131104 | tf_op jit(solution)/shard_map/ppermute | solution.py:56
  59.0 3.6 %collective-permute-start.20 = (f32[1,2,128,128]{3,2,1,0:T(8,128)S(1)}, f32[1,2,128,128]{3,2,1,0:T(8,128)S(1)}, u32[]{:S(2)}, u32[]{:S(2)}) collective-permute-start(f32[1,2,128,128]{3,2,1,0:T(8,128)S(1)} %get-tuple-element.60), channel_id=1, source_target_pairs={{0,24},{4,28},{8,16},{12,20},{16,8},{20,12},{24,0},{28,4},{1,25},{... | collective-permute-start | bytes 393224 | tf_op jit(solution)/shard_map/ppermute | solution.py:56
  64.8 2.4 %collective-permute-start.23 = (f32[1,2,128,128]{3,2,1,0:T(8,128)S(1)}, f32[1,2,128,128]{3,2,1,0:T(8,128)S(1)}, u32[]{:S(2)}, u32[]{:S(2)}) collective-permute-start(f32[1,2,128,128]{3,2,1,0:T(8,128)S(1)} %get-tuple-element.58), channel_id=1, source_target_pairs={{0,24},{4,28},{8,16},{12,20},{16,8},{20,12},{24,0},{28,4},{1,25},{... | collective-permute-start | bytes 393224 | tf_op jit(solution)/shard_map/ppermute | solution.py:56
  67.2 3.0 %collective-permute-done.18.refs_5_ = f32[2,2,64,256]{3,2,1,0:T(8,128)S(1)} collective-permute-done((f32[2,2,64,256]{3,2,1,0:T(8,128)S(1)}, f32[2,2,64,256]{3,2,1,0:T(8,128)S(1)}, u32[]{:S(2)}, u32[]{:S(2)}) %collective-permute-start.18) | collective-permute-done | bytes 262176 | tf_op jit(solution)/shard_map/ppermute | solution.py:56
  70.2 1.2 %weights.1 = (f32[512,256]{1,0:T(8,128)}, f32[512,256]{1,0:T(8,128)}, f32[512,128]{1,0:T(8,128)}, f32[8,128]{1,0:T(8,128)S(1)}) custom-call(f32[1,512,128]{2,1,0:T(8,128)S(1)} %get-tuple-element.57.refs_0_, f32[1,512,128]{2,1,0:T(8,128)S(1)} %collective-permute-done.10.refs_1_, f32[2,2,64,256]{3,2,1,0:T(8,128)S(1)} %pad_maximum_fusion.refs_2_, ...), custom_call_target="tpu_custom_call" | custom-call | tf_op jit(solution)/shard_map/weights/pallas_call | solution.py:484
  71.4 1.3 %collective-permute-done.23.refs_3_ = f32[1,2,128,128]{3,2,1,0:T(8,128)S(1)} collective-permute-done((f32[1,2,128,128]{3,2,1,0:T(8,128)S(1)}, f32[1,2,128,128]{3,2,1,0:T(8,128)S(1)}, u32[]{:S(2)}, u32[]{:S(2)}) %collective-permute-start.23) | collective-permute-done | bytes 131104 | tf_op jit(solution)/shard_map/ppermute | solution.py:56
  (66 shorter events, 10.1 us)
Async XLA Ops:
  7.1 5.3 %collective-permute-start = (f32[4,1024]{1,0:T(4,128)}, f32[4,1024]{1,0:T(4,128)S(1)}, u32[]{:S(2)}, u32[]{:S(2)}) collective-permute-start(f32[4,1024]{1,0:T(4,128)} %get-tuple-element.28.mine), channel_id=1, source_target_pairs={{0,4},{4,0},{8,12},{12,8},{16,20},{20,16},{24,28},{28,24},{1,5},{5... | collective-permute-start | bytes 49160 | tf_op jit(solution)/shard_map/ppermute | solution.py:41
  12.2 3.8 %collective-permute-start.3 = (f32[4,1024]{1,0:T(4,128)S(1)}, f32[4,1024]{1,0:T(4,128)S(1)}, u32[]{:S(2)}, u32[]{:S(2)}) collective-permute-start(f32[4,1024]{1,0:T(4,128)S(1)} %get-tuple-element.34.mine), channel_id=1, source_target_pairs={{0,4},{4,0},{8,12},{12,8},{16,20},{20,16},{24,28},{28,24},{1,5},{5... | collective-permute-start | bytes 49160 | tf_op jit(solution)/shard_map/ppermute | solution.py:41
  12.4 5.3 %collective-permute-start.1 = (f32[4,1024]{1,0:T(4,128)S(1)}, f32[4,1024]{1,0:T(4,128)S(1)}, u32[]{:S(2)}, u32[]{:S(2)}) collective-permute-start(f32[4,1024]{1,0:T(4,128)S(1)} %merge.4.mine), channel_id=1, source_target_pairs={{0,8},{4,12},{8,0},{12,4},{16,24},{20,28},{24,16},{28,20},{1,9},{5... | collective-permute-start | bytes 49160 | tf_op jit(solution)/shard_map/ppermute | solution.py:41
  16.1 4.3 %collective-permute-start.4 = (f32[4,1024]{1,0:T(4,128)S(1)}, f32[4,1024]{1,0:T(4,128)S(1)}, u32[]{:S(2)}, u32[]{:S(2)}) collective-permute-start(f32[4,1024]{1,0:T(4,128)S(1)} %merge.6.mine), channel_id=1, source_target_pairs={{0,8},{4,12},{8,0},{12,4},{16,24},{20,28},{24,16},{28,20},{1,9},{5... | collective-permute-start | bytes 49160 | tf_op jit(solution)/shard_map/ppermute | solution.py:41
  17.7 4.9 %collective-permute-start.2 = (f32[4,1024]{1,0:T(4,128)S(1)}, f32[4,1024]{1,0:T(4,128)S(1)}, u32[]{:S(2)}, u32[]{:S(2)}) collective-permute-start(f32[4,1024]{1,0:T(4,128)S(1)} %merge.5.after.mine), channel_id=1, source_target_pairs={{0,16},{4,20},{8,24},{12,28},{16,0},{20,4},{24,8},{28,12},{1,17},{... | collective-permute-start | bytes 49160 | tf_op jit(solution)/shard_map/ppermute | solution.py:41
  20.4 8.6 %collective-permute-start.5 = (f32[4,1024]{1,0:T(4,128)S(1)}, f32[4,1024]{1,0:T(4,128)S(1)}, u32[]{:S(2)}, u32[]{:S(2)}) collective-permute-start(f32[4,1024]{1,0:T(4,128)S(1)} %merge.7.mine), channel_id=1, source_target_pairs={{0,16},{4,20},{8,24},{12,28},{16,0},{20,4},{24,8},{28,12},{1,17},{... | collective-permute-start | bytes 49160 | tf_op jit(solution)/shard_map/ppermute | solution.py:41
  25.6 9.8 %collective-permute-start.6 = (f32[2,2,64,256]{3,2,1,0:T(8,128)S(1)}, f32[2,2,64,256]{3,2,1,0:T(8,128)S(1)}, u32[]{:S(2)}, u32[]{:S(2)}) collective-permute-start(f32[2,2,64,256]{3,2,1,0:T(8,128)S(1)} %get-tuple-element.37), channel_id=1, source_target_pairs={{0,4},{4,0},{8,12},{12,8},{16,20},{20,16},{24,28},{28,24},{1,5},{5... | collective-permute-start | bytes 786440 | tf_op jit(solution)/shard_map/ppermute | solution.py:56
  27.2 20.2 %collective-permute-start.15 = (f32[4,2,128,128]{3,2,1,0:T(8,128)S(1)}, f32[4,2,128,128]{3,2,1,0:T(8,128)S(1)}, u32[]{:S(2)}, u32[]{:S(2)}) collective-permute-start(f32[4,2,128,128]{3,2,1,0:T(8,128)S(1)} %get-tuple-element.44), channel_id=1, source_target_pairs={{0,8},{4,12},{8,0},{12,4},{16,24},{20,28},{24,16},{28,20},{1,9},{5... | collective-permute-start | bytes 1572872 | tf_op jit(solution)/shard_map/ppermute | solution.py:56
  31.9 9.3 %collective-permute-start.13 = (f32[2,2,64,256]{3,2,1,0:T(8,128)S(1)}, f32[2,2,64,256]{3,2,1,0:T(8,128)S(1)}, u32[]{:S(2)}, u32[]{:S(2)}) collective-permute-start(f32[2,2,64,256]{3,2,1,0:T(8,128)S(1)} %get-tuple-element.41), channel_id=1, source_target_pairs={{0,4},{4,0},{8,12},{12,8},{16,20},{20,16},{24,28},{28,24},{1,5},{5... | collective-permute-start | bytes 786440 | tf_op jit(solution)/shard_map/ppermute | solution.py:56
  34.7 20.0 %collective-permute-start.21 = (f32[4,2,128,128]{3,2,1,0:T(8,128)S(1)}, f32[4,2,128,128]{3,2,1,0:T(8,128)S(1)}, u32[]{:S(2)}, u32[]{:S(2)}) collective-permute-start(f32[4,2,128,128]{3,2,1,0:T(8,128)S(1)} %get-tuple-element.48), channel_id=1, source_target_pairs={{0,4},{4,0},{8,12},{12,8},{16,20},{20,16},{24,28},{28,24},{1,5},{5... | collective-permute-start | bytes 1572872 | tf_op jit(solution)/shard_map/ppermute | solution.py:56
  35.4 6.6 %collective-permute-start.7 = (f32[1,2,64,256]{3,2,1,0:T(8,128)S(1)}, f32[1,2,64,256]{3,2,1,0:T(8,128)S(1)}, u32[]{:S(2)}, u32[]{:S(2)}) collective-permute-start(f32[1,2,64,256]{3,2,1,0:T(8,128)S(1)} %slice_add_fusion.12), channel_id=1, source_target_pairs={{0,8},{4,12},{8,0},{12,4},{16,24},{20,28},{24,16},{28,20},{1,9},{5... | collective-permute-start | bytes 393224 | tf_op jit(solution)/shard_map/ppermute | solution.py:56
  41.2 6.7 %collective-permute-start.14 = (f32[1,2,64,256]{3,2,1,0:T(8,128)S(1)}, f32[1,2,64,256]{3,2,1,0:T(8,128)S(1)}, u32[]{:S(2)}, u32[]{:S(2)}) collective-permute-start(f32[1,2,64,256]{3,2,1,0:T(8,128)S(1)} %get-tuple-element.62), channel_id=1, source_target_pairs={{0,8},{4,12},{8,0},{12,4},{16,24},{20,28},{24,16},{28,20},{1,9},{5... | collective-permute-start | bytes 393224 | tf_op jit(solution)/shard_map/ppermute | solution.py:56
  42.1 9.4 %collective-permute-start.8 = (f32[1,2,64,256]{3,2,1,0:T(8,128)S(1)}, f32[1,2,64,256]{3,2,1,0:T(8,128)S(1)}, u32[]{:S(2)}, u32[]{:S(2)}) collective-permute-start(f32[1,2,64,256]{3,2,1,0:T(8,128)S(1)} %fusion), channel_id=1, source_target_pairs={{0,24},{4,28},{8,16},{12,20},{16,8},{20,12},{24,0},{28,4},{1,25},{... | collective-permute-start | bytes 393224 | tf_op jit(solution)/shard_map/ppermute | solution.py:56
  47.5 11.6 %collective-permute-start.19 = (f32[2,2,128,128]{3,2,1,0:T(8,128)S(1)}, f32[2,2,128,128]{3,2,1,0:T(8,128)S(1)}, u32[]{:S(2)}, u32[]{:S(2)}) collective-permute-start(f32[2,2,128,128]{3,2,1,0:T(8,128)S(1)} %get-tuple-element.55.after), channel_id=1, source_target_pairs={{0,4},{4,0},{8,12},{12,8},{16,20},{20,16},{24,28},{28,24},{1,5},{5... | collective-permute-start | bytes 786440 | tf_op jit(solution)/shard_map/ppermute | solution.py:56
  47.9 8.9 %collective-permute-start.16 = (f32[1,2,64,256]{3,2,1,0:T(8,128)S(1)}, f32[1,2,64,256]{3,2,1,0:T(8,128)S(1)}, u32[]{:S(2)}, u32[]{:S(2)}) collective-permute-start(f32[1,2,64,256]{3,2,1,0:T(8,128)S(1)} %added.1), channel_id=1, source_target_pairs={{0,24},{4,28},{8,16},{12,20},{16,8},{20,12},{24,0},{28,4},{1,25},{... | collective-permute-start | bytes 393224 | tf_op jit(solution)/shard_map/ppermute | solution.py:56
  51.5 6.9 %collective-permute-start.11 = (f32[1,2,64,256]{3,2,1,0:T(8,128)S(1)}, f32[1,2,64,256]{3,2,1,0:T(8,128)S(1)}, u32[]{:S(2)}, u32[]{:S(2)}) collective-permute-start(f32[1,2,64,256]{3,2,1,0:T(8,128)S(1)} %add.54.refs_2_), channel_id=1, source_target_pairs={{0,8},{4,12},{8,0},{12,4},{16,24},{20,28},{24,16},{28,20},{1,9},{5... | collective-permute-start | bytes 393224 | tf_op jit(solution)/shard_map/ppermute | solution.py:56
  52.4 12.2 %collective-permute-start.9 = (f32[2,512,128]{2,1,0:T(8,128)S(1)}, f32[2,512,128]{2,1,0:T(8,128)S(1)}, u32[]{:S(2)}, u32[]{:S(2)}) collective-permute-start(f32[2,512,128]{2,1,0:T(8,128)S(1)} %get-tuple-element.39), channel_id=1, source_target_pairs={{0,2},{1,3},{2,0},{3,1},{4,6},{5,7},{6,4},{7,5},{8,10},{9,11},{10,... | collective-permute-start | bytes 1572872 | tf_op jit(solution)/shard_map/ppermute | solution.py:41
  54.8 10.0 %collective-permute-start.22 = (f32[2,2,128,128]{3,2,1,0:T(8,128)S(1)}, f32[2,2,128,128]{3,2,1,0:T(8,128)S(1)}, u32[]{:S(2)}, u32[]{:S(2)}) collective-permute-start(f32[2,2,128,128]{3,2,1,0:T(8,128)S(1)} %get-tuple-element.53), channel_id=1, source_target_pairs={{0,8},{4,12},{8,0},{12,4},{16,24},{20,28},{24,16},{28,20},{1,9},{5... | collective-permute-start | bytes 786440 | tf_op jit(solution)/shard_map/ppermute | solution.py:56
  56.9 6.8 %collective-permute-start.17 = (f32[1,2,64,256]{3,2,1,0:T(8,128)S(1)}, f32[1,2,64,256]{3,2,1,0:T(8,128)S(1)}, u32[]{:S(2)}, u32[]{:S(2)}) collective-permute-start(f32[1,2,64,256]{3,2,1,0:T(8,128)S(1)} %add.60), channel_id=1, source_target_pairs={{0,8},{4,12},{8,0},{12,4},{16,24},{20,28},{24,16},{28,20},{1,9},{5... | collective-permute-start | bytes 393224 | tf_op jit(solution)/shard_map/ppermute | solution.py:56
  58.4 8.8 %collective-permute-start.12 = (f32[2,2,64,256]{3,2,1,0:T(8,128)S(1)}, f32[2,2,64,256]{3,2,1,0:T(8,128)S(1)}, u32[]{:S(2)}, u32[]{:S(2)}) collective-permute-start(f32[2,2,64,256]{3,2,1,0:T(8,128)S(1)} %pad_maximum_fusion.refs_2_), channel_id=1, source_target_pairs={{0,4},{4,0},{8,12},{12,8},{16,20},{20,16},{24,28},{28,24},{1,5},{5... | collective-permute-start | bytes 786440 | tf_op jit(solution)/shard_map/ppermute | solution.py:56
  59.0 12.3 %collective-permute-start.20 = (f32[1,2,128,128]{3,2,1,0:T(8,128)S(1)}, f32[1,2,128,128]{3,2,1,0:T(8,128)S(1)}, u32[]{:S(2)}, u32[]{:S(2)}) collective-permute-start(f32[1,2,128,128]{3,2,1,0:T(8,128)S(1)} %get-tuple-element.60), channel_id=1, source_target_pairs={{0,24},{4,28},{8,16},{12,20},{16,8},{20,12},{24,0},{28,4},{1,25},{... | collective-permute-start | bytes 393224 | tf_op jit(solution)/shard_map/ppermute | solution.py:56
  63.7 6.4 %collective-permute-start.18 = (f32[2,2,64,256]{3,2,1,0:T(8,128)S(1)}, f32[2,2,64,256]{3,2,1,0:T(8,128)S(1)}, u32[]{:S(2)}, u32[]{:S(2)}) collective-permute-start(f32[2,2,64,256]{3,2,1,0:T(8,128)S(1)} %pad_maximum_fusion.1.refs_4_), channel_id=1, source_target_pairs={{0,4},{4,0},{8,12},{12,8},{16,20},{20,16},{24,28},{28,24},{1,5},{5... | collective-permute-start | bytes 786440 | tf_op jit(solution)/shard_map/ppermute | solution.py:56
  64.7 5.5 %collective-permute-start.10 = (f32[1,512,128]{2,1,0:T(8,128)S(1)}, f32[1,512,128]{2,1,0:T(8,128)S(1)}, u32[]{:S(2)}, u32[]{:S(2)}) collective-permute-start(f32[1,512,128]{2,1,0:T(8,128)S(1)} %get-tuple-element.56), channel_id=1, source_target_pairs={{0,1},{1,0},{2,3},{3,2},{4,5},{5,4},{6,7},{7,6},{8,9},{9,8},{10,11... | collective-permute-start | bytes 786440 | tf_op jit(solution)/shard_map/ppermute | solution.py:41
  64.8 7.9 %collective-permute-start.23 = (f32[1,2,128,128]{3,2,1,0:T(8,128)S(1)}, f32[1,2,128,128]{3,2,1,0:T(8,128)S(1)}, u32[]{:S(2)}, u32[]{:S(2)}) collective-permute-start(f32[1,2,128,128]{3,2,1,0:T(8,128)S(1)} %get-tuple-element.58), channel_id=1, source_target_pairs={{0,24},{4,28},{8,16},{12,20},{16,8},{20,12},{24,0},{28,4},{1,25},{... | collective-permute-start | bytes 393224 | tf_op jit(solution)/shard_map/ppermute | solution.py:56
  (8 other events, 83.6 us)

commit v16 on v12

--- a/solution.py
+++ b/solution.py
@@ -142,7 +142,7 @@
     weight_parts = refs[2:-4]
     key_acc, value_acc, weights_ref, stats = refs[-4:]
     reads, latents, _ = queries.shape
-    tile = latents // (GROUPS // 2)
+    tile = latents // 2
     cols = slice(head_index * HD, (head_index + 1) * HD)
     stats[:reads], stats[reads:] = merged(mine, theirs)
     key_acc[...] = jnp.zeros_like(key_acc)
@@ -283,9 +283,9 @@
         ]
         projected.append(
             pl.pallas_call(
-                functools.partial(first_kernel, tile)
+                functools.partial(first_kernel, latents // 2)
                 if first
-                else functools.partial(later_kernel, tile, head_index),
+                else functools.partial(later_kernel, latents // 2, head_index),
                 out_shape=(
                     shape_of((row_count, HD), jnp.bfloat16),
                     shape_of((row_count, HD), jnp.bfloat16),

time: 71.6 us -> 71.4 us (level)
  no operation moved by 1% of the time
where the time goes in v16:
time: 71.4 us; the launch traced here: 71.3 us
  starting transfers between devices  37.1 us (52%)
  Pallas kernels  17.3 us (24%)
  waiting for transfers between devices  15.6 us (22%)
  between operations  0.89 us (1%)
    ppermute x16, starting transfers between devices, row_swap_of(): return lax.ppermute(array, 'rows', pairs)  23 us
    ppermute x8, starting transfers between devices, swap(): return lax.ppermute(array, axis, pairs)  14.2 us
    ppermute x16, waiting for transfers between devices, row_swap_of(): return lax.ppermute(array, 'rows', pairs)  14 us
    pallas_call x4, Pallas kernels, kernel_call(): pl.pallas_call(kernel, out_shape=[shape_of(*item) for item in shapes], in...  8.04 us
    pallas_call x2, Pallas kernels, on_device(): pl.pallas_call(functools.partial(first_kernel, latents // 2) if first els...  6.38 us
    ppermute x8, waiting for transfers between devices, swap(): return lax.ppermute(array, axis, pairs)  1.51 us
  transfers between devices with their start and end apart: 24, of which 9 were waited for; matrix products, arithmetic and copies ran while one was open for 1% of the time, Pallas kernels for 17%

profile of v16, /device:TPU:0, one launch (start us, length us, event | category | flops | bytes accessed | tf_op | source)
XLA Modules:
  0.0 71.3 jit_solution(4690508561031280699)
XLA Ops:
  0.7 4.6 %project.2 = (bf16[512,128]{1,0:T(8,128)(2,1)}, bf16[512,128]{1,0:T(8,128)(2,1)}, f32[4,1024]{1,0:T(4,128)}) custom-call(bf16[512,512]{1,0:T(8,128)(2,1)} %inputs.3, bf16[512,256]{1,0:T(8,128)(2,1)} %key_weight.1, bf16[512,256]{1,0:T(8,128)(2,1)} %value_weight.1, bf16[2,1024,256]{2,1,0:T(8,128)(2,1)} %queries.4, bf16[2,1024,256]{2,1,0:T(8,128)(2,1)} %out_grad.3), custom_call_target="tpu_custom_call" | custom-call | flops 1073741824 | bytes 4194304 | tf_op jit(solution)/shard_map/project/pallas_call | solution.py:285
  5.3 3.0 %collective-permute-start = (f32[4,1024]{1,0:T(4,128)}, f32[4,1024]{1,0:T(4,128)S(1)}, u32[]{:S(2)}, u32[]{:S(2)}) collective-permute-start(f32[4,1024]{1,0:T(4,128)} %get-tuple-element.28.mine), channel_id=1, source_target_pairs={{0,4},{4,0},{8,12},{12,8},{16,20},{20,16},{24,28},{28,24},{1,5},{5... | collective-permute-start | bytes 49160 | tf_op jit(solution)/shard_map/ppermute | solution.py:41
  8.3 1.8 %project.3 = (bf16[512,128]{1,0:T(8,128)(2,1)S(1)}, bf16[512,128]{1,0:T(8,128)(2,1)S(1)}, f32[4,1024]{1,0:T(4,128)S(1)}) custom-call(bf16[512,512]{1,0:T(8,128)(2,1)S(1)} %copy-done.3, bf16[512,256]{1,0:T(8,128)(2,1)S(1)} %copy-done.4, bf16[512,256]{1,0:T(8,128)(2,1)S(1)} %copy-done.5, bf16[2,1024,256]{2,1,0:T(8,128)(2,1)S(1)} %copy-done.1, ...), custom_call_target="tpu_custom_call" | custom-call | flops 1073741824 | bytes 4194304 | tf_op jit(solution)/shard_map/project/pallas_call | solution.py:285
  10.3 2.2 %collective-permute-start.1 = (f32[4,1024]{1,0:T(4,128)S(1)}, f32[4,1024]{1,0:T(4,128)S(1)}, u32[]{:S(2)}, u32[]{:S(2)}) collective-permute-start(f32[4,1024]{1,0:T(4,128)S(1)} %merge.4.mine), channel_id=1, source_target_pairs={{0,8},{4,12},{8,0},{12,4},{16,24},{20,28},{24,16},{28,20},{1,9},{5... | collective-permute-start | bytes 49160 | tf_op jit(solution)/shard_map/ppermute | solution.py:41
  12.4 1.5 %collective-permute-done.3.theirs = f32[4,1024]{1,0:T(4,128)S(1)} collective-permute-done((f32[4,1024]{1,0:T(4,128)S(1)}, f32[4,1024]{1,0:T(4,128)S(1)}, u32[]{:S(2)}, u32[]{:S(2)}) %collective-permute-start.3) | collective-permute-done | bytes 16416 | tf_op jit(solution)/shard_map/ppermute | solution.py:41
  14.0 1.6 %collective-permute-start.4 = (f32[4,1024]{1,0:T(4,128)S(1)}, f32[4,1024]{1,0:T(4,128)S(1)}, u32[]{:S(2)}, u32[]{:S(2)}) collective-permute-start(f32[4,1024]{1,0:T(4,128)S(1)} %merge.6.mine), channel_id=1, source_target_pairs={{0,8},{4,12},{8,0},{12,4},{16,24},{20,28},{24,16},{28,20},{1,9},{5... | collective-permute-start | bytes 49160 | tf_op jit(solution)/shard_map/ppermute | solution.py:41
  15.6 2.7 %collective-permute-start.2 = (f32[4,1024]{1,0:T(4,128)S(1)}, f32[4,1024]{1,0:T(4,128)S(1)}, u32[]{:S(2)}, u32[]{:S(2)}) collective-permute-start(f32[4,1024]{1,0:T(4,128)S(1)} %merge.5.after.mine), channel_id=1, source_target_pairs={{0,16},{4,20},{8,24},{12,28},{16,0},{20,4},{24,8},{28,12},{1,17},{... | collective-permute-start | bytes 49160 | tf_op jit(solution)/shard_map/ppermute | solution.py:41
  18.3 2.2 %collective-permute-start.5 = (f32[4,1024]{1,0:T(4,128)S(1)}, f32[4,1024]{1,0:T(4,128)S(1)}, u32[]{:S(2)}, u32[]{:S(2)}) collective-permute-start(f32[4,1024]{1,0:T(4,128)S(1)} %merge.7.mine), channel_id=1, source_target_pairs={{0,16},{4,20},{8,24},{12,28},{16,0},{20,4},{24,8},{28,12},{1,17},{... | collective-permute-start | bytes 49160 | tf_op jit(solution)/shard_map/ppermute | solution.py:41
  20.6 2.9 %grads.2 = (bf16[512,256]{1,0:T(8,128)(2,1)S(1)}, bf16[2,512,1024]{2,1,0:T(8,128)(2,1)S(1)}, f32[2,2,64,256]{3,2,1,0:T(8,128)S(1)}, f32[2,2,64,256]{3,2,1,0:T(8,128)S(1)}) custom-call(f32[4,1024]{1,0:T(4,128)S(1)} %merge.5.after.mine, bf16[512,512]{1,0:T(8,128)(2,1)S(1)} %copy-done.3, bf16[512,128]{1,0:T(8,128)(2,1)S(1)} %copy-done.6, ...), custom_call_target="tpu_custom_call" | custom-call | flops 1073741824 | bytes 4194304 | tf_op jit(solution)/shard_map/grads/pallas_call | solution.py:341
  25.1 1.8 %collective-permute-start.15 = (f32[4,2,128,128]{3,2,1,0:T(8,128)S(1)}, f32[4,2,128,128]{3,2,1,0:T(8,128)S(1)}, u32[]{:S(2)}, u32[]{:S(2)}) collective-permute-start(f32[4,2,128,128]{3,2,1,0:T(8,128)S(1)} %get-tuple-element.44), channel_id=1, source_target_pairs={{0,8},{4,12},{8,0},{12,4},{16,24},{20,28},{24,16},{28,20},{1,9},{5... | collective-permute-start | bytes 1572872 | tf_op jit(solution)/shard_map/ppermute | solution.py:56
  26.9 2.9 %grads.3 = (bf16[512,256]{1,0:T(8,128)(2,1)S(1)}, bf16[2,512,1024]{2,1,0:T(8,128)(2,1)S(1)}, f32[2,2,64,256]{3,2,1,0:T(8,128)S(1)}, f32[2,2,64,256]{3,2,1,0:T(8,128)S(1)}) custom-call(bf16[512,256]{1,0:T(8,128)(2,1)S(1)} %get-tuple-element.31.after.refs_0_, bf16[512,512]{1,0:T(8,128)(2,1)S(1)} %copy-done.3, bf16[512,128]{1,0:T(8,128)(2,1)S(1)} %get-tuple-element.32.keys, ...), custom_call_target="tpu_custom_call" | custom-call | flops 1073741824 | bytes 4194304 | tf_op jit(solution)/shard_map/grads/pallas_call | solution.py:341
  29.8 1.4 %collective-permute-start.13 = (f32[2,2,64,256]{3,2,1,0:T(8,128)S(1)}, f32[2,2,64,256]{3,2,1,0:T(8,128)S(1)}, u32[]{:S(2)}, u32[]{:S(2)}) collective-permute-start(f32[2,2,64,256]{3,2,1,0:T(8,128)S(1)} %get-tuple-element.41), channel_id=1, source_target_pairs={{0,4},{4,0},{8,12},{12,8},{16,20},{20,16},{24,28},{28,24},{1,5},{5... | collective-permute-start | bytes 786440 | tf_op jit(solution)/shard_map/ppermute | solution.py:56
  31.2 1.1 %query.3 = (f32[4,2,128,128]{3,2,1,0:T(8,128)S(1)}, f32[4,2,128,128]{3,2,1,0:T(8,128)S(1)}) custom-call(bf16[512,256]{1,0:T(8,128)(2,1)S(1)} %get-tuple-element.35.refs_1_.after, bf16[2,512,1024]{2,1,0:T(8,128)(2,1)S(1)} %get-tuple-element.46.score_grads, bf16[512,128]{1,0:T(8,128)(2,1)S(1)} %get-tuple-element.32.keys), custom_call_target="tpu_custom_call" | custom-call | flops 1073741824 | bytes 4194304 | tf_op jit(solution)/shard_map/query/pallas_call | solution.py:341
  33.7 5.4 %collective-permute-done.13 = f32[2,2,64,256]{3,2,1,0:T(8,128)S(1)} collective-permute-done((f32[2,2,64,256]{3,2,1,0:T(8,128)S(1)}, f32[2,2,64,256]{3,2,1,0:T(8,128)S(1)}, u32[]{:S(2)}, u32[]{:S(2)}) %collective-permute-start.13) | collective-permute-done | bytes 262176 | tf_op jit(solution)/shard_map/ppermute | solution.py:56
  40.0 5.3 %collective-permute-start.8 = (f32[1,2,64,256]{3,2,1,0:T(8,128)S(1)}, f32[1,2,64,256]{3,2,1,0:T(8,128)S(1)}, u32[]{:S(2)}, u32[]{:S(2)}) collective-permute-start(f32[1,2,64,256]{3,2,1,0:T(8,128)S(1)} %fusion), channel_id=1, source_target_pairs={{0,24},{4,28},{8,16},{12,20},{16,8},{20,12},{24,0},{28,4},{1,25},{... | collective-permute-start | bytes 393224 | tf_op jit(solution)/shard_map/ppermute | solution.py:56
  45.8 2.4 %collective-permute-start.16 = (f32[1,2,64,256]{3,2,1,0:T(8,128)S(1)}, f32[1,2,64,256]{3,2,1,0:T(8,128)S(1)}, u32[]{:S(2)}, u32[]{:S(2)}) collective-permute-start(f32[1,2,64,256]{3,2,1,0:T(8,128)S(1)} %added.1), channel_id=1, source_target_pairs={{0,24},{4,28},{8,16},{12,20},{16,8},{20,12},{24,0},{28,4},{1,25},{... | collective-permute-start | bytes 393224 | tf_op jit(solution)/shard_map/ppermute | solution.py:56
  50.3 2.3 %collective-permute-start.9 = (f32[2,512,128]{2,1,0:T(8,128)S(1)}, f32[2,512,128]{2,1,0:T(8,128)S(1)}, u32[]{:S(2)}, u32[]{:S(2)}) collective-permute-start(f32[2,512,128]{2,1,0:T(8,128)S(1)} %get-tuple-element.39), channel_id=1, source_target_pairs={{0,2},{1,3},{2,0},{3,1},{4,6},{5,7},{6,4},{7,5},{8,10},{9,11},{10,... | collective-permute-start | bytes 1572872 | tf_op jit(solution)/shard_map/ppermute | solution.py:41
  52.7 2.1 %collective-permute-start.22 = (f32[2,2,128,128]{3,2,1,0:T(8,128)S(1)}, f32[2,2,128,128]{3,2,1,0:T(8,128)S(1)}, u32[]{:S(2)}, u32[]{:S(2)}) collective-permute-start(f32[2,2,128,128]{3,2,1,0:T(8,128)S(1)} %get-tuple-element.53), channel_id=1, source_target_pairs={{0,8},{4,12},{8,0},{12,4},{16,24},{20,28},{24,16},{28,20},{1,9},{5... | collective-permute-start | bytes 786440 | tf_op jit(solution)/shard_map/ppermute | solution.py:56
  54.9 1.4 %collective-permute-done.11 = f32[1,2,64,256]{3,2,1,0:T(8,128)S(1)} collective-permute-done((f32[1,2,64,256]{3,2,1,0:T(8,128)S(1)}, f32[1,2,64,256]{3,2,1,0:T(8,128)S(1)}, u32[]{:S(2)}, u32[]{:S(2)}) %collective-permute-start.11) | collective-permute-done | bytes 131104 | tf_op jit(solution)/shard_map/ppermute | solution.py:56
  57.0 3.6 %collective-permute-start.20 = (f32[1,2,128,128]{3,2,1,0:T(8,128)S(1)}, f32[1,2,128,128]{3,2,1,0:T(8,128)S(1)}, u32[]{:S(2)}, u32[]{:S(2)}) collective-permute-start(f32[1,2,128,128]{3,2,1,0:T(8,128)S(1)} %get-tuple-element.60), channel_id=1, source_target_pairs={{0,24},{4,28},{8,16},{12,20},{16,8},{20,12},{24,0},{28,4},{1,25},{... | collective-permute-start | bytes 393224 | tf_op jit(solution)/shard_map/ppermute | solution.py:56
  62.7 2.4 %collective-permute-start.23 = (f32[1,2,128,128]{3,2,1,0:T(8,128)S(1)}, f32[1,2,128,128]{3,2,1,0:T(8,128)S(1)}, u32[]{:S(2)}, u32[]{:S(2)}) collective-permute-start(f32[1,2,128,128]{3,2,1,0:T(8,128)S(1)} %get-tuple-element.58), channel_id=1, source_target_pairs={{0,24},{4,28},{8,16},{12,20},{16,8},{20,12},{24,0},{28,4},{1,25},{... | collective-permute-start | bytes 393224 | tf_op jit(solution)/shard_map/ppermute | solution.py:56
  65.1 3.0 %collective-permute-done.18.refs_5_ = f32[2,2,64,256]{3,2,1,0:T(8,128)S(1)} collective-permute-done((f32[2,2,64,256]{3,2,1,0:T(8,128)S(1)}, f32[2,2,64,256]{3,2,1,0:T(8,128)S(1)}, u32[]{:S(2)}, u32[]{:S(2)}) %collective-permute-start.18) | collective-permute-done | bytes 262176 | tf_op jit(solution)/shard_map/ppermute | solution.py:56
  68.1 1.2 %weights.1 = (f32[512,256]{1,0:T(8,128)}, f32[512,256]{1,0:T(8,128)}, f32[512,128]{1,0:T(8,128)}, f32[8,128]{1,0:T(8,128)S(1)}) custom-call(f32[1,512,128]{2,1,0:T(8,128)S(1)} %get-tuple-element.57.refs_0_, f32[1,512,128]{2,1,0:T(8,128)S(1)} %collective-permute-done.10.refs_1_, f32[2,2,64,256]{3,2,1,0:T(8,128)S(1)} %pad_maximum_fusion.refs_2_, ...), custom_call_target="tpu_custom_call" | custom-call | tf_op jit(solution)/shard_map/weights/pallas_call | solution.py:470
  69.3 1.3 %collective-permute-done.23.refs_3_ = f32[1,2,128,128]{3,2,1,0:T(8,128)S(1)} collective-permute-done((f32[1,2,128,128]{3,2,1,0:T(8,128)S(1)}, f32[1,2,128,128]{3,2,1,0:T(8,128)S(1)}, u32[]{:S(2)}, u32[]{:S(2)}) %collective-permute-start.23) | collective-permute-done | bytes 131104 | tf_op jit(solution)/shard_map/ppermute | solution.py:56
  (66 shorter events, 10.3 us)
Async XLA Ops:
  5.3 4.9 %collective-permute-start = (f32[4,1024]{1,0:T(4,128)}, f32[4,1024]{1,0:T(4,128)S(1)}, u32[]{:S(2)}, u32[]{:S(2)}) collective-permute-start(f32[4,1024]{1,0:T(4,128)} %get-tuple-element.28.mine), channel_id=1, source_target_pairs={{0,4},{4,0},{8,12},{12,8},{16,20},{20,16},{24,28},{28,24},{1,5},{5... | collective-permute-start | bytes 49160 | tf_op jit(solution)/shard_map/ppermute | solution.py:41
  10.1 3.8 %collective-permute-start.3 = (f32[4,1024]{1,0:T(4,128)S(1)}, f32[4,1024]{1,0:T(4,128)S(1)}, u32[]{:S(2)}, u32[]{:S(2)}) collective-permute-start(f32[4,1024]{1,0:T(4,128)S(1)} %get-tuple-element.34.mine), channel_id=1, source_target_pairs={{0,4},{4,0},{8,12},{12,8},{16,20},{20,16},{24,28},{28,24},{1,5},{5... | collective-permute-start | bytes 49160 | tf_op jit(solution)/shard_map/ppermute | solution.py:41
  10.3 5.3 %collective-permute-start.1 = (f32[4,1024]{1,0:T(4,128)S(1)}, f32[4,1024]{1,0:T(4,128)S(1)}, u32[]{:S(2)}, u32[]{:S(2)}) collective-permute-start(f32[4,1024]{1,0:T(4,128)S(1)} %merge.4.mine), channel_id=1, source_target_pairs={{0,8},{4,12},{8,0},{12,4},{16,24},{20,28},{24,16},{28,20},{1,9},{5... | collective-permute-start | bytes 49160 | tf_op jit(solution)/shard_map/ppermute | solution.py:41
  14.0 4.3 %collective-permute-start.4 = (f32[4,1024]{1,0:T(4,128)S(1)}, f32[4,1024]{1,0:T(4,128)S(1)}, u32[]{:S(2)}, u32[]{:S(2)}) collective-permute-start(f32[4,1024]{1,0:T(4,128)S(1)} %merge.6.mine), channel_id=1, source_target_pairs={{0,8},{4,12},{8,0},{12,4},{16,24},{20,28},{24,16},{28,20},{1,9},{5... | collective-permute-start | bytes 49160 | tf_op jit(solution)/shard_map/ppermute | solution.py:41
  15.6 4.9 %collective-permute-start.2 = (f32[4,1024]{1,0:T(4,128)S(1)}, f32[4,1024]{1,0:T(4,128)S(1)}, u32[]{:S(2)}, u32[]{:S(2)}) collective-permute-start(f32[4,1024]{1,0:T(4,128)S(1)} %merge.5.after.mine), channel_id=1, source_target_pairs={{0,16},{4,20},{8,24},{12,28},{16,0},{20,4},{24,8},{28,12},{1,17},{... | collective-permute-start | bytes 49160 | tf_op jit(solution)/shard_map/ppermute | solution.py:41
  18.3 8.6 %collective-permute-start.5 = (f32[4,1024]{1,0:T(4,128)S(1)}, f32[4,1024]{1,0:T(4,128)S(1)}, u32[]{:S(2)}, u32[]{:S(2)}) collective-permute-start(f32[4,1024]{1,0:T(4,128)S(1)} %merge.7.mine), channel_id=1, source_target_pairs={{0,16},{4,20},{8,24},{12,28},{16,0},{20,4},{24,8},{28,12},{1,17},{... | collective-permute-start | bytes 49160 | tf_op jit(solution)/shard_map/ppermute | solution.py:41
  23.5 9.6 %collective-permute-start.6 = (f32[2,2,64,256]{3,2,1,0:T(8,128)S(1)}, f32[2,2,64,256]{3,2,1,0:T(8,128)S(1)}, u32[]{:S(2)}, u32[]{:S(2)}) collective-permute-start(f32[2,2,64,256]{3,2,1,0:T(8,128)S(1)} %get-tuple-element.37), channel_id=1, source_target_pairs={{0,4},{4,0},{8,12},{12,8},{16,20},{20,16},{24,28},{28,24},{1,5},{5... | collective-permute-start | bytes 786440 | tf_op jit(solution)/shard_map/ppermute | solution.py:56
  25.1 20.2 %collective-permute-start.15 = (f32[4,2,128,128]{3,2,1,0:T(8,128)S(1)}, f32[4,2,128,128]{3,2,1,0:T(8,128)S(1)}, u32[]{:S(2)}, u32[]{:S(2)}) collective-permute-start(f32[4,2,128,128]{3,2,1,0:T(8,128)S(1)} %get-tuple-element.44), channel_id=1, source_target_pairs={{0,8},{4,12},{8,0},{12,4},{16,24},{20,28},{24,16},{28,20},{1,9},{5... | collective-permute-start | bytes 1572872 | tf_op jit(solution)/shard_map/ppermute | solution.py:56
  29.8 9.3 %collective-permute-start.13 = (f32[2,2,64,256]{3,2,1,0:T(8,128)S(1)}, f32[2,2,64,256]{3,2,1,0:T(8,128)S(1)}, u32[]{:S(2)}, u32[]{:S(2)}) collective-permute-start(f32[2,2,64,256]{3,2,1,0:T(8,128)S(1)} %get-tuple-element.41), channel_id=1, source_target_pairs={{0,4},{4,0},{8,12},{12,8},{16,20},{20,16},{24,28},{28,24},{1,5},{5... | collective-permute-start | bytes 786440 | tf_op jit(solution)/shard_map/ppermute | solution.py:56
  32.4 20.3 %collective-permute-start.21 = (f32[4,2,128,128]{3,2,1,0:T(8,128)S(1)}, f32[4,2,128,128]{3,2,1,0:T(8,128)S(1)}, u32[]{:S(2)}, u32[]{:S(2)}) collective-permute-start(f32[4,2,128,128]{3,2,1,0:T(8,128)S(1)} %get-tuple-element.48), channel_id=1, source_target_pairs={{0,4},{4,0},{8,12},{12,8},{16,20},{20,16},{24,28},{28,24},{1,5},{5... | collective-permute-start | bytes 1572872 | tf_op jit(solution)/shard_map/ppermute | solution.py:56
  33.1 6.8 %collective-permute-start.7 = (f32[1,2,64,256]{3,2,1,0:T(8,128)S(1)}, f32[1,2,64,256]{3,2,1,0:T(8,128)S(1)}, u32[]{:S(2)}, u32[]{:S(2)}) collective-permute-start(f32[1,2,64,256]{3,2,1,0:T(8,128)S(1)} %slice_add_fusion.12), channel_id=1, source_target_pairs={{0,8},{4,12},{8,0},{12,4},{16,24},{20,28},{24,16},{28,20},{1,9},{5... | collective-permute-start | bytes 393224 | tf_op jit(solution)/shard_map/ppermute | solution.py:56
  39.2 6.7 %collective-permute-start.14 = (f32[1,2,64,256]{3,2,1,0:T(8,128)S(1)}, f32[1,2,64,256]{3,2,1,0:T(8,128)S(1)}, u32[]{:S(2)}, u32[]{:S(2)}) collective-permute-start(f32[1,2,64,256]{3,2,1,0:T(8,128)S(1)} %get-tuple-element.62), channel_id=1, source_target_pairs={{0,8},{4,12},{8,0},{12,4},{16,24},{20,28},{24,16},{28,20},{1,9},{5... | collective-permute-start | bytes 393224 | tf_op jit(solution)/shard_map/ppermute | solution.py:56
  40.0 9.4 %collective-permute-start.8 = (f32[1,2,64,256]{3,2,1,0:T(8,128)S(1)}, f32[1,2,64,256]{3,2,1,0:T(8,128)S(1)}, u32[]{:S(2)}, u32[]{:S(2)}) collective-permute-start(f32[1,2,64,256]{3,2,1,0:T(8,128)S(1)} %fusion), channel_id=1, source_target_pairs={{0,24},{4,28},{8,16},{12,20},{16,8},{20,12},{24,0},{28,4},{1,25},{... | collective-permute-start | bytes 393224 | tf_op jit(solution)/shard_map/ppermute | solution.py:56
  45.4 11.6 %collective-permute-start.19 = (f32[2,2,128,128]{3,2,1,0:T(8,128)S(1)}, f32[2,2,128,128]{3,2,1,0:T(8,128)S(1)}, u32[]{:S(2)}, u32[]{:S(2)}) collective-permute-start(f32[2,2,128,128]{3,2,1,0:T(8,128)S(1)} %get-tuple-element.55.after), channel_id=1, source_target_pairs={{0,4},{4,0},{8,12},{12,8},{16,20},{20,16},{24,28},{28,24},{1,5},{5... | collective-permute-start | bytes 786440 | tf_op jit(solution)/shard_map/ppermute | solution.py:56
  45.8 8.9 %collective-permute-start.16 = (f32[1,2,64,256]{3,2,1,0:T(8,128)S(1)}, f32[1,2,64,256]{3,2,1,0:T(8,128)S(1)}, u32[]{:S(2)}, u32[]{:S(2)}) collective-permute-start(f32[1,2,64,256]{3,2,1,0:T(8,128)S(1)} %added.1), channel_id=1, source_target_pairs={{0,24},{4,28},{8,16},{12,20},{16,8},{20,12},{24,0},{28,4},{1,25},{... | collective-permute-start | bytes 393224 | tf_op jit(solution)/shard_map/ppermute | solution.py:56
  49.4 6.9 %collective-permute-start.11 = (f32[1,2,64,256]{3,2,1,0:T(8,128)S(1)}, f32[1,2,64,256]{3,2,1,0:T(8,128)S(1)}, u32[]{:S(2)}, u32[]{:S(2)}) collective-permute-start(f32[1,2,64,256]{3,2,1,0:T(8,128)S(1)} %add.54.refs_2_), channel_id=1, source_target_pairs={{0,8},{4,12},{8,0},{12,4},{16,24},{20,28},{24,16},{28,20},{1,9},{5... | collective-permute-start | bytes 393224 | tf_op jit(solution)/shard_map/ppermute | solution.py:56
  50.3 12.2 %collective-permute-start.9 = (f32[2,512,128]{2,1,0:T(8,128)S(1)}, f32[2,512,128]{2,1,0:T(8,128)S(1)}, u32[]{:S(2)}, u32[]{:S(2)}) collective-permute-start(f32[2,512,128]{2,1,0:T(8,128)S(1)} %get-tuple-element.39), channel_id=1, source_target_pairs={{0,2},{1,3},{2,0},{3,1},{4,6},{5,7},{6,4},{7,5},{8,10},{9,11},{10,... | collective-permute-start | bytes 1572872 | tf_op jit(solution)/shard_map/ppermute | solution.py:41
  52.7 9.9 %collective-permute-start.22 = (f32[2,2,128,128]{3,2,1,0:T(8,128)S(1)}, f32[2,2,128,128]{3,2,1,0:T(8,128)S(1)}, u32[]{:S(2)}, u32[]{:S(2)}) collective-permute-start(f32[2,2,128,128]{3,2,1,0:T(8,128)S(1)} %get-tuple-element.53), channel_id=1, source_target_pairs={{0,8},{4,12},{8,0},{12,4},{16,24},{20,28},{24,16},{28,20},{1,9},{5... | collective-permute-start | bytes 786440 | tf_op jit(solution)/shard_map/ppermute | solution.py:56
  54.8 6.8 %collective-permute-start.17 = (f32[1,2,64,256]{3,2,1,0:T(8,128)S(1)}, f32[1,2,64,256]{3,2,1,0:T(8,128)S(1)}, u32[]{:S(2)}, u32[]{:S(2)}) collective-permute-start(f32[1,2,64,256]{3,2,1,0:T(8,128)S(1)} %add.60), channel_id=1, source_target_pairs={{0,8},{4,12},{8,0},{12,4},{16,24},{20,28},{24,16},{28,20},{1,9},{5... | collective-permute-start | bytes 393224 | tf_op jit(solution)/shard_map/ppermute | solution.py:56
  56.3 8.7 %collective-permute-start.12 = (f32[2,2,64,256]{3,2,1,0:T(8,128)S(1)}, f32[2,2,64,256]{3,2,1,0:T(8,128)S(1)}, u32[]{:S(2)}, u32[]{:S(2)}) collective-permute-start(f32[2,2,64,256]{3,2,1,0:T(8,128)S(1)} %pad_maximum_fusion.refs_2_), channel_id=1, source_target_pairs={{0,4},{4,0},{8,12},{12,8},{16,20},{20,16},{24,28},{28,24},{1,5},{5... | collective-permute-start | bytes 786440 | tf_op jit(solution)/shard_map/ppermute | solution.py:56
  57.0 12.3 %collective-permute-start.20 = (f32[1,2,128,128]{3,2,1,0:T(8,128)S(1)}, f32[1,2,128,128]{3,2,1,0:T(8,128)S(1)}, u32[]{:S(2)}, u32[]{:S(2)}) collective-permute-start(f32[1,2,128,128]{3,2,1,0:T(8,128)S(1)} %get-tuple-element.60), channel_id=1, source_target_pairs={{0,24},{4,28},{8,16},{12,20},{16,8},{20,12},{24,0},{28,4},{1,25},{... | collective-permute-start | bytes 393224 | tf_op jit(solution)/shard_map/ppermute | solution.py:56
  61.7 6.4 %collective-permute-start.18 = (f32[2,2,64,256]{3,2,1,0:T(8,128)S(1)}, f32[2,2,64,256]{3,2,1,0:T(8,128)S(1)}, u32[]{:S(2)}, u32[]{:S(2)}) collective-permute-start(f32[2,2,64,256]{3,2,1,0:T(8,128)S(1)} %pad_maximum_fusion.1.refs_4_), channel_id=1, source_target_pairs={{0,4},{4,0},{8,12},{12,8},{16,20},{20,16},{24,28},{28,24},{1,5},{5... | collective-permute-start | bytes 786440 | tf_op jit(solution)/shard_map/ppermute | solution.py:56
  62.6 5.5 %collective-permute-start.10 = (f32[1,512,128]{2,1,0:T(8,128)S(1)}, f32[1,512,128]{2,1,0:T(8,128)S(1)}, u32[]{:S(2)}, u32[]{:S(2)}) collective-permute-start(f32[1,512,128]{2,1,0:T(8,128)S(1)} %get-tuple-element.56), channel_id=1, source_target_pairs={{0,1},{1,0},{2,3},{3,2},{4,5},{5,4},{6,7},{7,6},{8,9},{9,8},{10,11... | collective-permute-start | bytes 786440 | tf_op jit(solution)/shard_map/ppermute | solution.py:41
  62.7 7.9 %collective-permute-start.23 = (f32[1,2,128,128]{3,2,1,0:T(8,128)S(1)}, f32[1,2,128,128]{3,2,1,0:T(8,128)S(1)}, u32[]{:S(2)}, u32[]{:S(2)}) collective-permute-start(f32[1,2,128,128]{3,2,1,0:T(8,128)S(1)} %get-tuple-element.58), channel_id=1, source_target_pairs={{0,24},{4,28},{8,16},{12,20},{16,8},{20,12},{24,0},{28,4},{1,25},{... | collective-permute-start | bytes 393224 | tf_op jit(solution)/shard_map/ppermute | solution.py:56
  (8 other events, 73.9 us)

commit v17 on v16

--- a/solution.py
+++ b/solution.py
@@ -125,7 +125,7 @@
 
 def group_at(bits, relative, high, me):
     flips = sum(bit * flip for bit, flip in zip(bits, relative))
-    return counted((counted(me) % LAST_BIT ^ flips) + LAST_BIT * high)
+    return (me % LAST_BIT ^ flips) + LAST_BIT * high
 
 
 LAST_BIT = 4
@@ -283,7 +283,7 @@
         ]
         projected.append(
             pl.pallas_call(
-                functools.partial(first_kernel, latents // 2)
+                functools.partial(first_kernel, tile)
                 if first
                 else functools.partial(later_kernel, latents // 2, head_index),
                 out_shape=(
@@ -378,11 +378,11 @@
         marks[f"A{head_index}"] = results[0]
         for part, (begin, end, bits) in enumerate(WEIGHT_PARTS[head_index]):
             keep, send = results[2 + 2 * part : 4 + 2 * part]
-            theirs = row_swap(send, bit=bits[0] * low)
+            theirs = swap(send, "rows", row_devices, bits[0] * low)
             send = keep[1:] + theirs[1:]
             mine = keep[:1] + theirs[:1]
             marks[f"w{head_index}.1"] = send
-            weight_steps.append((mine, row_swap(send, bit=bits[1] * low)))
+            weight_steps.append((mine, swap(send, "rows", row_devices, bits[1] * low)))
 
     query_terms, query_list = [], []
     for head_index in range(head_count):
@@ -442,10 +442,10 @@
                     mine = mine + theirs
                 if place == 3:
                     mine = sum_low(mine)
-                theirs = row_swap(mine, bit=bit)
+                theirs = swap(mine, "rows", row_devices, bit)
                 marks[f"w{head_index}.{place}"] = mine
             near = jnp.concatenate([mine, theirs], axis=0)
-            weight_terms += [near, row_swap(near, bit=first)]
+            weight_terms += [near, swap(near, "rows", row_devices, first)]
             weight_list.append((head_index, begin, end, bits))
 
     share = ((head_devices // 2, row_count, features // head_devices),)

time: 71.4 us -> 71.8 us (level)
  starting transfers between devices: 37.1 us -> 39.1 us
  waiting for transfers between devices: 15.6 us -> 14.1 us
    ppermute x8 -> x18, starting transfers between devices: 14.2 us -> 29.2 us  [swap(): return lax.ppermute(array, axis, pairs)]
    ppermute x16 -> x6, starting transfers between devices: 23 us -> 9.92 us  [row_swap_of(): return lax.ppermute(array, 'rows', pairs)]
    ppermute x16 -> x6, waiting for transfers between devices: 14 us -> 1.56 us  [row_swap_of(): return lax.ppermute(array, 'rows', pairs)]
    ppermute x8 -> x18, waiting for transfers between devices: 1.51 us -> 12.5 us  [swap(): return lax.ppermute(array, axis, pairs)]
  transfers between devices with their start and end apart: 24 -> 24, of which waited for: 9 -> 7; matrix products, arithmetic and copies ran while one was open for 1% -> 1% of each run, Pallas kernels for 17% -> 17%
where the time goes in v17:
time: 71.8 us; the launch traced here: 71.6 us
  starting transfers between devices  39.1 us (54%)
  Pallas kernels  17.1 us (24%)
  waiting for transfers between devices  14.1 us (20%)
  between operations  0.89 us (1%)
    ppermute x18, starting transfers between devices, swap(): return lax.ppermute(array, axis, pairs)  29.2 us
    ppermute x18, waiting for transfers between devices, swap(): return lax.ppermute(array, axis, pairs)  12.5 us
    ppermute x6, starting transfers between devices, row_swap_of(): return lax.ppermute(array, 'rows', pairs)  9.92 us
    pallas_call x4, Pallas kernels, kernel_call(): pl.pallas_call(kernel, out_shape=[shape_of(*item) for item in shapes], in...  8.05 us
    pallas_call x2, Pallas kernels, on_device(): pl.pallas_call(functools.partial(first_kernel, tile) if first else functo...  6.2 us
    ppermute x6, waiting for transfers between devices, row_swap_of(): return lax.ppermute(array, 'rows', pairs)  1.56 us
  transfers between devices with their start and end apart: 24, of which 7 were waited for; matrix products, arithmetic and copies ran while one was open for 1% of the time, Pallas kernels for 17%

profile of v17, /device:TPU:0, one launch (start us, length us, event | category | flops | bytes accessed | tf_op | source)
XLA Modules:
  0.0 71.6 jit_solution(16647104762899299833)
XLA Ops:
  0.7 4.4 %project.2 = (bf16[512,128]{1,0:T(8,128)(2,1)}, bf16[512,128]{1,0:T(8,128)(2,1)}, f32[4,1024]{1,0:T(4,128)}) custom-call(bf16[512,512]{1,0:T(8,128)(2,1)} %inputs.3, bf16[512,256]{1,0:T(8,128)(2,1)} %key_weight.1, bf16[512,256]{1,0:T(8,128)(2,1)} %value_weight.1, bf16[2,1024,256]{2,1,0:T(8,128)(2,1)} %queries.4, bf16[2,1024,256]{2,1,0:T(8,128)(2,1)} %out_grad.3), custom_call_target="tpu_custom_call" | custom-call | flops 1073741824 | bytes 4194304 | tf_op jit(solution)/shard_map/project/pallas_call | solution.py:285
  5.1 3.0 %collective-permute-start = (f32[4,1024]{1,0:T(4,128)}, f32[4,1024]{1,0:T(4,128)S(1)}, u32[]{:S(2)}, u32[]{:S(2)}) collective-permute-start(f32[4,1024]{1,0:T(4,128)} %get-tuple-element.28.mine), channel_id=1, source_target_pairs={{0,4},{4,0},{8,12},{12,8},{16,20},{20,16},{24,28},{28,24},{1,5},{5... | collective-permute-start | bytes 49160 | tf_op jit(solution)/shard_map/ppermute | solution.py:41
  8.2 1.8 %project.3 = (bf16[512,128]{1,0:T(8,128)(2,1)S(1)}, bf16[512,128]{1,0:T(8,128)(2,1)S(1)}, f32[4,1024]{1,0:T(4,128)S(1)}) custom-call(bf16[512,512]{1,0:T(8,128)(2,1)S(1)} %copy-done.3, bf16[512,256]{1,0:T(8,128)(2,1)S(1)} %copy-done.4, bf16[512,256]{1,0:T(8,128)(2,1)S(1)} %copy-done.5, bf16[2,1024,256]{2,1,0:T(8,128)(2,1)S(1)} %copy-done.1, ...), custom_call_target="tpu_custom_call" | custom-call | flops 1073741824 | bytes 4194304 | tf_op jit(solution)/shard_map/project/pallas_call | solution.py:285
  10.1 2.2 %collective-permute-start.1 = (f32[4,1024]{1,0:T(4,128)S(1)}, f32[4,1024]{1,0:T(4,128)S(1)}, u32[]{:S(2)}, u32[]{:S(2)}) collective-permute-start(f32[4,1024]{1,0:T(4,128)S(1)} %merge.4.mine), channel_id=1, source_target_pairs={{0,8},{4,12},{8,0},{12,4},{16,24},{20,28},{24,16},{28,20},{1,9},{5... | collective-permute-start | bytes 49160 | tf_op jit(solution)/shard_map/ppermute | solution.py:41
  12.3 1.5 %collective-permute-done.3.theirs = f32[4,1024]{1,0:T(4,128)S(1)} collective-permute-done((f32[4,1024]{1,0:T(4,128)S(1)}, f32[4,1024]{1,0:T(4,128)S(1)}, u32[]{:S(2)}, u32[]{:S(2)}) %collective-permute-start.3) | collective-permute-done | bytes 16416 | tf_op jit(solution)/shard_map/ppermute | solution.py:41
  13.8 1.6 %collective-permute-start.4 = (f32[4,1024]{1,0:T(4,128)S(1)}, f32[4,1024]{1,0:T(4,128)S(1)}, u32[]{:S(2)}, u32[]{:S(2)}) collective-permute-start(f32[4,1024]{1,0:T(4,128)S(1)} %merge.6.mine), channel_id=1, source_target_pairs={{0,8},{4,12},{8,0},{12,4},{16,24},{20,28},{24,16},{28,20},{1,9},{5... | collective-permute-start | bytes 49160 | tf_op jit(solution)/shard_map/ppermute | solution.py:41
  15.5 2.7 %collective-permute-start.2 = (f32[4,1024]{1,0:T(4,128)S(1)}, f32[4,1024]{1,0:T(4,128)S(1)}, u32[]{:S(2)}, u32[]{:S(2)}) collective-permute-start(f32[4,1024]{1,0:T(4,128)S(1)} %merge.5.after.mine), channel_id=1, source_target_pairs={{0,16},{4,20},{8,24},{12,28},{16,0},{20,4},{24,8},{28,12},{1,17},{... | collective-permute-start | bytes 49160 | tf_op jit(solution)/shard_map/ppermute | solution.py:41
  18.1 2.2 %collective-permute-start.5 = (f32[4,1024]{1,0:T(4,128)S(1)}, f32[4,1024]{1,0:T(4,128)S(1)}, u32[]{:S(2)}, u32[]{:S(2)}) collective-permute-start(f32[4,1024]{1,0:T(4,128)S(1)} %merge.7.mine), channel_id=1, source_target_pairs={{0,16},{4,20},{8,24},{12,28},{16,0},{20,4},{24,8},{28,12},{1,17},{... | collective-permute-start | bytes 49160 | tf_op jit(solution)/shard_map/ppermute | solution.py:41
  20.4 2.9 %grads.2 = (bf16[512,256]{1,0:T(8,128)(2,1)S(1)}, bf16[2,512,1024]{2,1,0:T(8,128)(2,1)S(1)}, f32[2,2,64,256]{3,2,1,0:T(8,128)S(1)}, f32[2,2,64,256]{3,2,1,0:T(8,128)S(1)}) custom-call(f32[4,1024]{1,0:T(4,128)S(1)} %merge.5.after.mine, bf16[512,512]{1,0:T(8,128)(2,1)S(1)} %copy-done.3, bf16[512,128]{1,0:T(8,128)(2,1)S(1)} %copy-done.6, ...), custom_call_target="tpu_custom_call" | custom-call | flops 1073741824 | bytes 4194304 | tf_op jit(solution)/shard_map/grads/pallas_call | solution.py:341
  24.9 1.8 %collective-permute-start.15 = (f32[4,2,128,128]{3,2,1,0:T(8,128)S(1)}, f32[4,2,128,128]{3,2,1,0:T(8,128)S(1)}, u32[]{:S(2)}, u32[]{:S(2)}) collective-permute-start(f32[4,2,128,128]{3,2,1,0:T(8,128)S(1)} %get-tuple-element.44), channel_id=1, source_target_pairs={{0,8},{4,12},{8,0},{12,4},{16,24},{20,28},{24,16},{28,20},{1,9},{5... | collective-permute-start | bytes 1572872 | tf_op jit(solution)/shard_map/ppermute | solution.py:56
  26.7 2.9 %grads.3 = (bf16[512,256]{1,0:T(8,128)(2,1)S(1)}, bf16[2,512,1024]{2,1,0:T(8,128)(2,1)S(1)}, f32[2,2,64,256]{3,2,1,0:T(8,128)S(1)}, f32[2,2,64,256]{3,2,1,0:T(8,128)S(1)}) custom-call(bf16[512,256]{1,0:T(8,128)(2,1)S(1)} %get-tuple-element.31.after.refs_0_, bf16[512,512]{1,0:T(8,128)(2,1)S(1)} %copy-done.3, bf16[512,128]{1,0:T(8,128)(2,1)S(1)} %get-tuple-element.32.keys, ...), custom_call_target="tpu_custom_call" | custom-call | flops 1073741824 | bytes 4194304 | tf_op jit(solution)/shard_map/grads/pallas_call | solution.py:341
  33.5 5.4 %collective-permute-done.13 = f32[2,2,64,256]{3,2,1,0:T(8,128)S(1)} collective-permute-done((f32[2,2,64,256]{3,2,1,0:T(8,128)S(1)}, f32[2,2,64,256]{3,2,1,0:T(8,128)S(1)}, u32[]{:S(2)}, u32[]{:S(2)}) %collective-permute-start.13) | collective-permute-done | bytes 262176 | tf_op jit(solution)/shard_map/ppermute | solution.py:41
  39.3 1.8 %collective-permute-done.7 = f32[1,2,64,256]{3,2,1,0:T(8,128)S(1)} collective-permute-done((f32[1,2,64,256]{3,2,1,0:T(8,128)S(1)}, f32[1,2,64,256]{3,2,1,0:T(8,128)S(1)}, u32[]{:S(2)}, u32[]{:S(2)}) %collective-permute-start.7) | collective-permute-done | bytes 131104 | tf_op jit(solution)/shard_map/ppermute | solution.py:41
  41.2 3.1 %collective-permute-start.8 = (f32[1,2,64,256]{3,2,1,0:T(8,128)S(1)}, f32[1,2,64,256]{3,2,1,0:T(8,128)S(1)}, u32[]{:S(2)}, u32[]{:S(2)}) collective-permute-start(f32[1,2,64,256]{3,2,1,0:T(8,128)S(1)} %fusion), channel_id=1, source_target_pairs={{0,16},{4,20},{8,24},{12,28},{16,0},{20,4},{24,8},{28,12},{1,17},{... | collective-permute-start | bytes 393224 | tf_op jit(solution)/shard_map/ppermute | solution.py:41
  44.4 1.5 %collective-permute-start.19 = (f32[2,2,128,128]{3,2,1,0:T(8,128)S(1)}, f32[2,2,128,128]{3,2,1,0:T(8,128)S(1)}, u32[]{:S(2)}, u32[]{:S(2)}) collective-permute-start(f32[2,2,128,128]{3,2,1,0:T(8,128)S(1)} %get-tuple-element.55.after), channel_id=1, source_target_pairs={{0,4},{4,0},{8,12},{12,8},{16,20},{20,16},{24,28},{28,24},{1,5},{5... | collective-permute-start | bytes 786440 | tf_op jit(solution)/shard_map/ppermute | solution.py:56
  46.0 1.5 %collective-permute-start.16 = (f32[1,2,64,256]{3,2,1,0:T(8,128)S(1)}, f32[1,2,64,256]{3,2,1,0:T(8,128)S(1)}, u32[]{:S(2)}, u32[]{:S(2)}) collective-permute-start(f32[1,2,64,256]{3,2,1,0:T(8,128)S(1)} %added.1), channel_id=1, source_target_pairs={{0,16},{4,20},{8,24},{12,28},{16,0},{20,4},{24,8},{28,12},{1,17},{... | collective-permute-start | bytes 393224 | tf_op jit(solution)/shard_map/ppermute | solution.py:41
  47.8 2.1 %collective-permute-start.11 = (f32[1,2,64,256]{3,2,1,0:T(8,128)S(1)}, f32[1,2,64,256]{3,2,1,0:T(8,128)S(1)}, u32[]{:S(2)}, u32[]{:S(2)}) collective-permute-start(f32[1,2,64,256]{3,2,1,0:T(8,128)S(1)} %add.54.refs_2_), channel_id=1, source_target_pairs={{0,8},{4,12},{8,0},{12,4},{16,24},{20,28},{24,16},{28,20},{1,9},{5... | collective-permute-start | bytes 393224 | tf_op jit(solution)/shard_map/ppermute | solution.py:41
  50.7 2.6 %collective-permute-start.9 = (f32[2,512,128]{2,1,0:T(8,128)S(1)}, f32[2,512,128]{2,1,0:T(8,128)S(1)}, u32[]{:S(2)}, u32[]{:S(2)}) collective-permute-start(f32[2,512,128]{2,1,0:T(8,128)S(1)} %get-tuple-element.39), channel_id=1, source_target_pairs={{0,2},{1,3},{2,0},{3,1},{4,6},{5,7},{6,4},{7,5},{8,10},{9,11},{10,... | collective-permute-start | bytes 1572872 | tf_op jit(solution)/shard_map/ppermute | solution.py:41
  53.5 2.1 %collective-permute-start.17 = (f32[1,2,64,256]{3,2,1,0:T(8,128)S(1)}, f32[1,2,64,256]{3,2,1,0:T(8,128)S(1)}, u32[]{:S(2)}, u32[]{:S(2)}) collective-permute-start(f32[1,2,64,256]{3,2,1,0:T(8,128)S(1)} %add.60), channel_id=1, source_target_pairs={{0,8},{4,12},{8,0},{12,4},{16,24},{20,28},{24,16},{28,20},{1,9},{5... | collective-permute-start | bytes 393224 | tf_op jit(solution)/shard_map/ppermute | solution.py:41
  55.6 2.0 %collective-permute-start.12 = (f32[2,2,64,256]{3,2,1,0:T(8,128)S(1)}, f32[2,2,64,256]{3,2,1,0:T(8,128)S(1)}, u32[]{:S(2)}, u32[]{:S(2)}) collective-permute-start(f32[2,2,64,256]{3,2,1,0:T(8,128)S(1)} %pad_maximum_fusion.refs_2_), channel_id=1, source_target_pairs={{0,4},{4,0},{8,12},{12,8},{16,20},{20,16},{24,28},{28,24},{1,5},{5... | collective-permute-start | bytes 786440 | tf_op jit(solution)/shard_map/ppermute | solution.py:41
  57.6 3.0 %collective-permute-start.20 = (f32[1,2,128,128]{3,2,1,0:T(8,128)S(1)}, f32[1,2,128,128]{3,2,1,0:T(8,128)S(1)}, u32[]{:S(2)}, u32[]{:S(2)}) collective-permute-start(f32[1,2,128,128]{3,2,1,0:T(8,128)S(1)} %get-tuple-element.60), channel_id=1, source_target_pairs={{0,24},{4,28},{8,16},{12,20},{16,8},{20,12},{24,0},{28,4},{1,25},{... | collective-permute-start | bytes 393224 | tf_op jit(solution)/shard_map/ppermute | solution.py:56
  63.0 2.7 %collective-permute-start.23 = (f32[1,2,128,128]{3,2,1,0:T(8,128)S(1)}, f32[1,2,128,128]{3,2,1,0:T(8,128)S(1)}, u32[]{:S(2)}, u32[]{:S(2)}) collective-permute-start(f32[1,2,128,128]{3,2,1,0:T(8,128)S(1)} %get-tuple-element.58), channel_id=1, source_target_pairs={{0,24},{4,28},{8,16},{12,20},{16,8},{20,12},{24,0},{28,4},{1,25},{... | collective-permute-start | bytes 393224 | tf_op jit(solution)/shard_map/ppermute | solution.py:56
  65.8 2.4 %collective-permute-done.18.refs_5_ = f32[2,2,64,256]{3,2,1,0:T(8,128)S(1)} collective-permute-done((f32[2,2,64,256]{3,2,1,0:T(8,128)S(1)}, f32[2,2,64,256]{3,2,1,0:T(8,128)S(1)}, u32[]{:S(2)}, u32[]{:S(2)}) %collective-permute-start.18) | collective-permute-done | bytes 262176 | tf_op jit(solution)/shard_map/ppermute | solution.py:41
  69.3 1.6 %collective-permute-done.23.refs_3_ = f32[1,2,128,128]{3,2,1,0:T(8,128)S(1)} collective-permute-done((f32[1,2,128,128]{3,2,1,0:T(8,128)S(1)}, f32[1,2,128,128]{3,2,1,0:T(8,128)S(1)}, u32[]{:S(2)}, u32[]{:S(2)}) %collective-permute-start.23) | collective-permute-done | bytes 131104 | tf_op jit(solution)/shard_map/ppermute | solution.py:56
  (66 shorter events, 11.8 us)
Async XLA Ops:
  5.1 4.9 %collective-permute-start = (f32[4,1024]{1,0:T(4,128)}, f32[4,1024]{1,0:T(4,128)S(1)}, u32[]{:S(2)}, u32[]{:S(2)}) collective-permute-start(f32[4,1024]{1,0:T(4,128)} %get-tuple-element.28.mine), channel_id=1, source_target_pairs={{0,4},{4,0},{8,12},{12,8},{16,20},{20,16},{24,28},{28,24},{1,5},{5... | collective-permute-start | bytes 49160 | tf_op jit(solution)/shard_map/ppermute | solution.py:41
  10.0 3.8 %collective-permute-start.3 = (f32[4,1024]{1,0:T(4,128)S(1)}, f32[4,1024]{1,0:T(4,128)S(1)}, u32[]{:S(2)}, u32[]{:S(2)}) collective-permute-start(f32[4,1024]{1,0:T(4,128)S(1)} %get-tuple-element.34.mine), channel_id=1, source_target_pairs={{0,4},{4,0},{8,12},{12,8},{16,20},{20,16},{24,28},{28,24},{1,5},{5... | collective-permute-start | bytes 49160 | tf_op jit(solution)/shard_map/ppermute | solution.py:41
  10.1 5.3 %collective-permute-start.1 = (f32[4,1024]{1,0:T(4,128)S(1)}, f32[4,1024]{1,0:T(4,128)S(1)}, u32[]{:S(2)}, u32[]{:S(2)}) collective-permute-start(f32[4,1024]{1,0:T(4,128)S(1)} %merge.4.mine), channel_id=1, source_target_pairs={{0,8},{4,12},{8,0},{12,4},{16,24},{20,28},{24,16},{28,20},{1,9},{5... | collective-permute-start | bytes 49160 | tf_op jit(solution)/shard_map/ppermute | solution.py:41
  13.8 4.3 %collective-permute-start.4 = (f32[4,1024]{1,0:T(4,128)S(1)}, f32[4,1024]{1,0:T(4,128)S(1)}, u32[]{:S(2)}, u32[]{:S(2)}) collective-permute-start(f32[4,1024]{1,0:T(4,128)S(1)} %merge.6.mine), channel_id=1, source_target_pairs={{0,8},{4,12},{8,0},{12,4},{16,24},{20,28},{24,16},{28,20},{1,9},{5... | collective-permute-start | bytes 49160 | tf_op jit(solution)/shard_map/ppermute | solution.py:41
  15.5 4.9 %collective-permute-start.2 = (f32[4,1024]{1,0:T(4,128)S(1)}, f32[4,1024]{1,0:T(4,128)S(1)}, u32[]{:S(2)}, u32[]{:S(2)}) collective-permute-start(f32[4,1024]{1,0:T(4,128)S(1)} %merge.5.after.mine), channel_id=1, source_target_pairs={{0,16},{4,20},{8,24},{12,28},{16,0},{20,4},{24,8},{28,12},{1,17},{... | collective-permute-start | bytes 49160 | tf_op jit(solution)/shard_map/ppermute | solution.py:41
  18.1 8.6 %collective-permute-start.5 = (f32[4,1024]{1,0:T(4,128)S(1)}, f32[4,1024]{1,0:T(4,128)S(1)}, u32[]{:S(2)}, u32[]{:S(2)}) collective-permute-start(f32[4,1024]{1,0:T(4,128)S(1)} %merge.7.mine), channel_id=1, source_target_pairs={{0,16},{4,20},{8,24},{12,28},{16,0},{20,4},{24,8},{28,12},{1,17},{... | collective-permute-start | bytes 49160 | tf_op jit(solution)/shard_map/ppermute | solution.py:41
  23.3 9.7 %collective-permute-start.6 = (f32[2,2,64,256]{3,2,1,0:T(8,128)S(1)}, f32[2,2,64,256]{3,2,1,0:T(8,128)S(1)}, u32[]{:S(2)}, u32[]{:S(2)}) collective-permute-start(f32[2,2,64,256]{3,2,1,0:T(8,128)S(1)} %get-tuple-element.37), channel_id=1, source_target_pairs={{0,4},{4,0},{8,12},{12,8},{16,20},{20,16},{24,28},{28,24},{1,5},{5... | collective-permute-start | bytes 786440 | tf_op jit(solution)/shard_map/ppermute | solution.py:41
  24.9 19.4 %collective-permute-start.15 = (f32[4,2,128,128]{3,2,1,0:T(8,128)S(1)}, f32[4,2,128,128]{3,2,1,0:T(8,128)S(1)}, u32[]{:S(2)}, u32[]{:S(2)}) collective-permute-start(f32[4,2,128,128]{3,2,1,0:T(8,128)S(1)} %get-tuple-element.44), channel_id=1, source_target_pairs={{0,8},{4,12},{8,0},{12,4},{16,24},{20,28},{24,16},{28,20},{1,9},{5... | collective-permute-start | bytes 1572872 | tf_op jit(solution)/shard_map/ppermute | solution.py:56
  29.6 9.3 %collective-permute-start.13 = (f32[2,2,64,256]{3,2,1,0:T(8,128)S(1)}, f32[2,2,64,256]{3,2,1,0:T(8,128)S(1)}, u32[]{:S(2)}, u32[]{:S(2)}) collective-permute-start(f32[2,2,64,256]{3,2,1,0:T(8,128)S(1)} %get-tuple-element.41), channel_id=1, source_target_pairs={{0,4},{4,0},{8,12},{12,8},{16,20},{20,16},{24,28},{28,24},{1,5},{5... | collective-permute-start | bytes 786440 | tf_op jit(solution)/shard_map/ppermute | solution.py:41
  32.2 21.1 %collective-permute-start.21 = (f32[4,2,128,128]{3,2,1,0:T(8,128)S(1)}, f32[4,2,128,128]{3,2,1,0:T(8,128)S(1)}, u32[]{:S(2)}, u32[]{:S(2)}) collective-permute-start(f32[4,2,128,128]{3,2,1,0:T(8,128)S(1)} %get-tuple-element.48), channel_id=1, source_target_pairs={{0,4},{4,0},{8,12},{12,8},{16,20},{20,16},{24,28},{28,24},{1,5},{5... | collective-permute-start | bytes 1572872 | tf_op jit(solution)/shard_map/ppermute | solution.py:56
  33.0 8.2 %collective-permute-start.7 = (f32[1,2,64,256]{3,2,1,0:T(8,128)S(1)}, f32[1,2,64,256]{3,2,1,0:T(8,128)S(1)}, u32[]{:S(2)}, u32[]{:S(2)}) collective-permute-start(f32[1,2,64,256]{3,2,1,0:T(8,128)S(1)} %slice_add_fusion.12), channel_id=1, source_target_pairs={{0,8},{4,12},{8,0},{12,4},{16,24},{20,28},{24,16},{28,20},{1,9},{5... | collective-permute-start | bytes 393224 | tf_op jit(solution)/shard_map/ppermute | solution.py:41
  39.0 7.0 %collective-permute-start.14 = (f32[1,2,64,256]{3,2,1,0:T(8,128)S(1)}, f32[1,2,64,256]{3,2,1,0:T(8,128)S(1)}, u32[]{:S(2)}, u32[]{:S(2)}) collective-permute-start(f32[1,2,64,256]{3,2,1,0:T(8,128)S(1)} %get-tuple-element.62), channel_id=1, source_target_pairs={{0,8},{4,12},{8,0},{12,4},{16,24},{20,28},{24,16},{28,20},{1,9},{5... | collective-permute-start | bytes 393224 | tf_op jit(solution)/shard_map/ppermute | solution.py:41
  41.2 6.6 %collective-permute-start.8 = (f32[1,2,64,256]{3,2,1,0:T(8,128)S(1)}, f32[1,2,64,256]{3,2,1,0:T(8,128)S(1)}, u32[]{:S(2)}, u32[]{:S(2)}) collective-permute-start(f32[1,2,64,256]{3,2,1,0:T(8,128)S(1)} %fusion), channel_id=1, source_target_pairs={{0,16},{4,20},{8,24},{12,28},{16,0},{20,4},{24,8},{28,12},{1,17},{... | collective-permute-start | bytes 393224 | tf_op jit(solution)/shard_map/ppermute | solution.py:41
  44.4 13.2 %collective-permute-start.19 = (f32[2,2,128,128]{3,2,1,0:T(8,128)S(1)}, f32[2,2,128,128]{3,2,1,0:T(8,128)S(1)}, u32[]{:S(2)}, u32[]{:S(2)}) collective-permute-start(f32[2,2,128,128]{3,2,1,0:T(8,128)S(1)} %get-tuple-element.55.after), channel_id=1, source_target_pairs={{0,4},{4,0},{8,12},{12,8},{16,20},{20,16},{24,28},{28,24},{1,5},{5... | collective-permute-start | bytes 786440 | tf_op jit(solution)/shard_map/ppermute | solution.py:56
  46.0 7.5 %collective-permute-start.16 = (f32[1,2,64,256]{3,2,1,0:T(8,128)S(1)}, f32[1,2,64,256]{3,2,1,0:T(8,128)S(1)}, u32[]{:S(2)}, u32[]{:S(2)}) collective-permute-start(f32[1,2,64,256]{3,2,1,0:T(8,128)S(1)} %added.1), channel_id=1, source_target_pairs={{0,16},{4,20},{8,24},{12,28},{16,0},{20,4},{24,8},{28,12},{1,17},{... | collective-permute-start | bytes 393224 | tf_op jit(solution)/shard_map/ppermute | solution.py:41
  47.8 7.8 %collective-permute-start.11 = (f32[1,2,64,256]{3,2,1,0:T(8,128)S(1)}, f32[1,2,64,256]{3,2,1,0:T(8,128)S(1)}, u32[]{:S(2)}, u32[]{:S(2)}) collective-permute-start(f32[1,2,64,256]{3,2,1,0:T(8,128)S(1)} %add.54.refs_2_), channel_id=1, source_target_pairs={{0,8},{4,12},{8,0},{12,4},{16,24},{20,28},{24,16},{28,20},{1,9},{5... | collective-permute-start | bytes 393224 | tf_op jit(solution)/shard_map/ppermute | solution.py:41
  50.7 12.1 %collective-permute-start.9 = (f32[2,512,128]{2,1,0:T(8,128)S(1)}, f32[2,512,128]{2,1,0:T(8,128)S(1)}, u32[]{:S(2)}, u32[]{:S(2)}) collective-permute-start(f32[2,512,128]{2,1,0:T(8,128)S(1)} %get-tuple-element.39), channel_id=1, source_target_pairs={{0,2},{1,3},{2,0},{3,1},{4,6},{5,7},{6,4},{7,5},{8,10},{9,11},{10,... | collective-permute-start | bytes 1572872 | tf_op jit(solution)/shard_map/ppermute | solution.py:41
  53.4 9.6 %collective-permute-start.22 = (f32[2,2,128,128]{3,2,1,0:T(8,128)S(1)}, f32[2,2,128,128]{3,2,1,0:T(8,128)S(1)}, u32[]{:S(2)}, u32[]{:S(2)}) collective-permute-start(f32[2,2,128,128]{3,2,1,0:T(8,128)S(1)} %get-tuple-element.53), channel_id=1, source_target_pairs={{0,8},{4,12},{8,0},{12,4},{16,24},{20,28},{24,16},{28,20},{1,9},{5... | collective-permute-start | bytes 786440 | tf_op jit(solution)/shard_map/ppermute | solution.py:56
  53.5 8.2 %collective-permute-start.17 = (f32[1,2,64,256]{3,2,1,0:T(8,128)S(1)}, f32[1,2,64,256]{3,2,1,0:T(8,128)S(1)}, u32[]{:S(2)}, u32[]{:S(2)}) collective-permute-start(f32[1,2,64,256]{3,2,1,0:T(8,128)S(1)} %add.60), channel_id=1, source_target_pairs={{0,8},{4,12},{8,0},{12,4},{16,24},{20,28},{24,16},{28,20},{1,9},{5... | collective-permute-start | bytes 393224 | tf_op jit(solution)/shard_map/ppermute | solution.py:41
  55.6 10.2 %collective-permute-start.12 = (f32[2,2,64,256]{3,2,1,0:T(8,128)S(1)}, f32[2,2,64,256]{3,2,1,0:T(8,128)S(1)}, u32[]{:S(2)}, u32[]{:S(2)}) collective-permute-start(f32[2,2,64,256]{3,2,1,0:T(8,128)S(1)} %pad_maximum_fusion.refs_2_), channel_id=1, source_target_pairs={{0,4},{4,0},{8,12},{12,8},{16,20},{20,16},{24,28},{28,24},{1,5},{5... | collective-permute-start | bytes 786440 | tf_op jit(solution)/shard_map/ppermute | solution.py:41
  57.6 11.7 %collective-permute-start.20 = (f32[1,2,128,128]{3,2,1,0:T(8,128)S(1)}, f32[1,2,128,128]{3,2,1,0:T(8,128)S(1)}, u32[]{:S(2)}, u32[]{:S(2)}) collective-permute-start(f32[1,2,128,128]{3,2,1,0:T(8,128)S(1)} %get-tuple-element.60), channel_id=1, source_target_pairs={{0,24},{4,28},{8,16},{12,20},{16,8},{20,12},{24,0},{28,4},{1,25},{... | collective-permute-start | bytes 393224 | tf_op jit(solution)/shard_map/ppermute | solution.py:56
  61.7 6.4 %collective-permute-start.18 = (f32[2,2,64,256]{3,2,1,0:T(8,128)S(1)}, f32[2,2,64,256]{3,2,1,0:T(8,128)S(1)}, u32[]{:S(2)}, u32[]{:S(2)}) collective-permute-start(f32[2,2,64,256]{3,2,1,0:T(8,128)S(1)} %pad_maximum_fusion.1.refs_4_), channel_id=1, source_target_pairs={{0,4},{4,0},{8,12},{12,8},{16,20},{20,16},{24,28},{28,24},{1,5},{5... | collective-permute-start | bytes 786440 | tf_op jit(solution)/shard_map/ppermute | solution.py:41
  62.9 5.3 %collective-permute-start.10 = (f32[1,512,128]{2,1,0:T(8,128)S(1)}, f32[1,512,128]{2,1,0:T(8,128)S(1)}, u32[]{:S(2)}, u32[]{:S(2)}) collective-permute-start(f32[1,512,128]{2,1,0:T(8,128)S(1)} %get-tuple-element.56), channel_id=1, source_target_pairs={{0,1},{1,0},{2,3},{3,2},{4,5},{5,4},{6,7},{7,6},{8,9},{9,8},{10,11... | collective-permute-start | bytes 786440 | tf_op jit(solution)/shard_map/ppermute | solution.py:41
  63.0 7.9 %collective-permute-start.23 = (f32[1,2,128,128]{3,2,1,0:T(8,128)S(1)}, f32[1,2,128,128]{3,2,1,0:T(8,128)S(1)}, u32[]{:S(2)}, u32[]{:S(2)}) collective-permute-start(f32[1,2,128,128]{3,2,1,0:T(8,128)S(1)} %get-tuple-element.58), channel_id=1, source_target_pairs={{0,24},{4,28},{8,16},{12,20},{16,8},{20,12},{24,0},{28,4},{1,25},{... | collective-permute-start | bytes 393224 | tf_op jit(solution)/shard_map/ppermute | solution.py:56
  (8 other events, 73.0 us)

commit v18 on v16

--- a/solution.py
+++ b/solution.py
@@ -283,7 +283,7 @@
         ]
         projected.append(
             pl.pallas_call(
-                functools.partial(first_kernel, latents // 2)
+                functools.partial(first_kernel, tile)
                 if first
                 else functools.partial(later_kernel, latents // 2, head_index),
                 out_shape=(

time: 71.4 us -> 71.3 us (level)
  no operation moved by 1% of the time
where the time goes in v18:
time: 71.3 us; the launch traced here: 71.1 us
  starting transfers between devices  37.1 us (52%)
  Pallas kernels  17.1 us (24%)
  waiting for transfers between devices  15.6 us (22%)
  between operations  0.89 us (1%)
    ppermute x16, starting transfers between devices, row_swap_of(): return lax.ppermute(array, 'rows', pairs)  22.9 us
    ppermute x8, starting transfers between devices, swap(): return lax.ppermute(array, axis, pairs)  14.2 us
    ppermute x16, waiting for transfers between devices, row_swap_of(): return lax.ppermute(array, 'rows', pairs)  14.1 us
    pallas_call x4, Pallas kernels, kernel_call(): pl.pallas_call(kernel, out_shape=[shape_of(*item) for item in shapes], in...  8.05 us
    pallas_call x2, Pallas kernels, on_device(): pl.pallas_call(functools.partial(first_kernel, tile) if first else functo...  6.2 us
    ppermute x8, waiting for transfers between devices, swap(): return lax.ppermute(array, axis, pairs)  1.51 us
  transfers between devices with their start and end apart: 24, of which 9 were waited for; matrix products, arithmetic and copies ran while one was open for 1% of the time, Pallas kernels for 17%

profile of v18, /device:TPU:0, one launch (start us, length us, event | category | flops | bytes accessed | tf_op | source)
XLA Modules:
  0.0 71.1 jit_solution(16835600772411102043)
XLA Ops:
  0.7 4.4 %project.2 = (bf16[512,128]{1,0:T(8,128)(2,1)}, bf16[512,128]{1,0:T(8,128)(2,1)}, f32[4,1024]{1,0:T(4,128)}) custom-call(bf16[512,512]{1,0:T(8,128)(2,1)} %inputs.3, bf16[512,256]{1,0:T(8,128)(2,1)} %key_weight.1, bf16[512,256]{1,0:T(8,128)(2,1)} %value_weight.1, bf16[2,1024,256]{2,1,0:T(8,128)(2,1)} %queries.4, bf16[2,1024,256]{2,1,0:T(8,128)(2,1)} %out_grad.3), custom_call_target="tpu_custom_call" | custom-call | flops 1073741824 | bytes 4194304 | tf_op jit(solution)/shard_map/project/pallas_call | solution.py:285
  5.1 3.0 %collective-permute-start = (f32[4,1024]{1,0:T(4,128)}, f32[4,1024]{1,0:T(4,128)S(1)}, u32[]{:S(2)}, u32[]{:S(2)}) collective-permute-start(f32[4,1024]{1,0:T(4,128)} %get-tuple-element.28.mine), channel_id=1, source_target_pairs={{0,4},{4,0},{8,12},{12,8},{16,20},{20,16},{24,28},{28,24},{1,5},{5... | collective-permute-start | bytes 49160 | tf_op jit(solution)/shard_map/ppermute | solution.py:41
  8.2 1.8 %project.3 = (bf16[512,128]{1,0:T(8,128)(2,1)S(1)}, bf16[512,128]{1,0:T(8,128)(2,1)S(1)}, f32[4,1024]{1,0:T(4,128)S(1)}) custom-call(bf16[512,512]{1,0:T(8,128)(2,1)S(1)} %copy-done.3, bf16[512,256]{1,0:T(8,128)(2,1)S(1)} %copy-done.4, bf16[512,256]{1,0:T(8,128)(2,1)S(1)} %copy-done.5, bf16[2,1024,256]{2,1,0:T(8,128)(2,1)S(1)} %copy-done.1, ...), custom_call_target="tpu_custom_call" | custom-call | flops 1073741824 | bytes 4194304 | tf_op jit(solution)/shard_map/project/pallas_call | solution.py:285
  10.1 2.2 %collective-permute-start.1 = (f32[4,1024]{1,0:T(4,128)S(1)}, f32[4,1024]{1,0:T(4,128)S(1)}, u32[]{:S(2)}, u32[]{:S(2)}) collective-permute-start(f32[4,1024]{1,0:T(4,128)S(1)} %merge.4.mine), channel_id=1, source_target_pairs={{0,8},{4,12},{8,0},{12,4},{16,24},{20,28},{24,16},{28,20},{1,9},{5... | collective-permute-start | bytes 49160 | tf_op jit(solution)/shard_map/ppermute | solution.py:41
  12.3 1.5 %collective-permute-done.3.theirs = f32[4,1024]{1,0:T(4,128)S(1)} collective-permute-done((f32[4,1024]{1,0:T(4,128)S(1)}, f32[4,1024]{1,0:T(4,128)S(1)}, u32[]{:S(2)}, u32[]{:S(2)}) %collective-permute-start.3) | collective-permute-done | bytes 16416 | tf_op jit(solution)/shard_map/ppermute | solution.py:41
  13.8 1.6 %collective-permute-start.4 = (f32[4,1024]{1,0:T(4,128)S(1)}, f32[4,1024]{1,0:T(4,128)S(1)}, u32[]{:S(2)}, u32[]{:S(2)}) collective-permute-start(f32[4,1024]{1,0:T(4,128)S(1)} %merge.6.mine), channel_id=1, source_target_pairs={{0,8},{4,12},{8,0},{12,4},{16,24},{20,28},{24,16},{28,20},{1,9},{5... | collective-permute-start | bytes 49160 | tf_op jit(solution)/shard_map/ppermute | solution.py:41
  15.5 2.7 %collective-permute-start.2 = (f32[4,1024]{1,0:T(4,128)S(1)}, f32[4,1024]{1,0:T(4,128)S(1)}, u32[]{:S(2)}, u32[]{:S(2)}) collective-permute-start(f32[4,1024]{1,0:T(4,128)S(1)} %merge.5.after.mine), channel_id=1, source_target_pairs={{0,16},{4,20},{8,24},{12,28},{16,0},{20,4},{24,8},{28,12},{1,17},{... | collective-permute-start | bytes 49160 | tf_op jit(solution)/shard_map/ppermute | solution.py:41
  18.1 2.2 %collective-permute-start.5 = (f32[4,1024]{1,0:T(4,128)S(1)}, f32[4,1024]{1,0:T(4,128)S(1)}, u32[]{:S(2)}, u32[]{:S(2)}) collective-permute-start(f32[4,1024]{1,0:T(4,128)S(1)} %merge.7.mine), channel_id=1, source_target_pairs={{0,16},{4,20},{8,24},{12,28},{16,0},{20,4},{24,8},{28,12},{1,17},{... | collective-permute-start | bytes 49160 | tf_op jit(solution)/shard_map/ppermute | solution.py:41
  20.4 2.9 %grads.2 = (bf16[512,256]{1,0:T(8,128)(2,1)S(1)}, bf16[2,512,1024]{2,1,0:T(8,128)(2,1)S(1)}, f32[2,2,64,256]{3,2,1,0:T(8,128)S(1)}, f32[2,2,64,256]{3,2,1,0:T(8,128)S(1)}) custom-call(f32[4,1024]{1,0:T(4,128)S(1)} %merge.5.after.mine, bf16[512,512]{1,0:T(8,128)(2,1)S(1)} %copy-done.3, bf16[512,128]{1,0:T(8,128)(2,1)S(1)} %copy-done.6, ...), custom_call_target="tpu_custom_call" | custom-call | flops 1073741824 | bytes 4194304 | tf_op jit(solution)/shard_map/grads/pallas_call | solution.py:341
  24.9 1.8 %collective-permute-start.15 = (f32[4,2,128,128]{3,2,1,0:T(8,128)S(1)}, f32[4,2,128,128]{3,2,1,0:T(8,128)S(1)}, u32[]{:S(2)}, u32[]{:S(2)}) collective-permute-start(f32[4,2,128,128]{3,2,1,0:T(8,128)S(1)} %get-tuple-element.44), channel_id=1, source_target_pairs={{0,8},{4,12},{8,0},{12,4},{16,24},{20,28},{24,16},{28,20},{1,9},{5... | collective-permute-start | bytes 1572872 | tf_op jit(solution)/shard_map/ppermute | solution.py:56
  26.7 2.9 %grads.3 = (bf16[512,256]{1,0:T(8,128)(2,1)S(1)}, bf16[2,512,1024]{2,1,0:T(8,128)(2,1)S(1)}, f32[2,2,64,256]{3,2,1,0:T(8,128)S(1)}, f32[2,2,64,256]{3,2,1,0:T(8,128)S(1)}) custom-call(bf16[512,256]{1,0:T(8,128)(2,1)S(1)} %get-tuple-element.31.after.refs_0_, bf16[512,512]{1,0:T(8,128)(2,1)S(1)} %copy-done.3, bf16[512,128]{1,0:T(8,128)(2,1)S(1)} %get-tuple-element.32.keys, ...), custom_call_target="tpu_custom_call" | custom-call | flops 1073741824 | bytes 4194304 | tf_op jit(solution)/shard_map/grads/pallas_call | solution.py:341
  29.6 1.4 %collective-permute-start.13 = (f32[2,2,64,256]{3,2,1,0:T(8,128)S(1)}, f32[2,2,64,256]{3,2,1,0:T(8,128)S(1)}, u32[]{:S(2)}, u32[]{:S(2)}) collective-permute-start(f32[2,2,64,256]{3,2,1,0:T(8,128)S(1)} %get-tuple-element.41), channel_id=1, source_target_pairs={{0,4},{4,0},{8,12},{12,8},{16,20},{20,16},{24,28},{28,24},{1,5},{5... | collective-permute-start | bytes 786440 | tf_op jit(solution)/shard_map/ppermute | solution.py:56
  31.1 1.1 %query.3 = (f32[4,2,128,128]{3,2,1,0:T(8,128)S(1)}, f32[4,2,128,128]{3,2,1,0:T(8,128)S(1)}) custom-call(bf16[512,256]{1,0:T(8,128)(2,1)S(1)} %get-tuple-element.35.refs_1_.after, bf16[2,512,1024]{2,1,0:T(8,128)(2,1)S(1)} %get-tuple-element.46.score_grads, bf16[512,128]{1,0:T(8,128)(2,1)S(1)} %get-tuple-element.32.keys), custom_call_target="tpu_custom_call" | custom-call | flops 1073741824 | bytes 4194304 | tf_op jit(solution)/shard_map/query/pallas_call | solution.py:341
  33.5 5.4 %collective-permute-done.13 = f32[2,2,64,256]{3,2,1,0:T(8,128)S(1)} collective-permute-done((f32[2,2,64,256]{3,2,1,0:T(8,128)S(1)}, f32[2,2,64,256]{3,2,1,0:T(8,128)S(1)}, u32[]{:S(2)}, u32[]{:S(2)}) %collective-permute-start.13) | collective-permute-done | bytes 262176 | tf_op jit(solution)/shard_map/ppermute | solution.py:56
  39.8 5.3 %collective-permute-start.8 = (f32[1,2,64,256]{3,2,1,0:T(8,128)S(1)}, f32[1,2,64,256]{3,2,1,0:T(8,128)S(1)}, u32[]{:S(2)}, u32[]{:S(2)}) collective-permute-start(f32[1,2,64,256]{3,2,1,0:T(8,128)S(1)} %fusion), channel_id=1, source_target_pairs={{0,24},{4,28},{8,16},{12,20},{16,8},{20,12},{24,0},{28,4},{1,25},{... | collective-permute-start | bytes 393224 | tf_op jit(solution)/shard_map/ppermute | solution.py:56
  45.7 2.4 %collective-permute-start.16 = (f32[1,2,64,256]{3,2,1,0:T(8,128)S(1)}, f32[1,2,64,256]{3,2,1,0:T(8,128)S(1)}, u32[]{:S(2)}, u32[]{:S(2)}) collective-permute-start(f32[1,2,64,256]{3,2,1,0:T(8,128)S(1)} %added.1), channel_id=1, source_target_pairs={{0,24},{4,28},{8,16},{12,20},{16,8},{20,12},{24,0},{28,4},{1,25},{... | collective-permute-start | bytes 393224 | tf_op jit(solution)/shard_map/ppermute | solution.py:56
  50.1 2.3 %collective-permute-start.9 = (f32[2,512,128]{2,1,0:T(8,128)S(1)}, f32[2,512,128]{2,1,0:T(8,128)S(1)}, u32[]{:S(2)}, u32[]{:S(2)}) collective-permute-start(f32[2,512,128]{2,1,0:T(8,128)S(1)} %get-tuple-element.39), channel_id=1, source_target_pairs={{0,2},{1,3},{2,0},{3,1},{4,6},{5,7},{6,4},{7,5},{8,10},{9,11},{10,... | collective-permute-start | bytes 1572872 | tf_op jit(solution)/shard_map/ppermute | solution.py:41
  52.5 2.1 %collective-permute-start.22 = (f32[2,2,128,128]{3,2,1,0:T(8,128)S(1)}, f32[2,2,128,128]{3,2,1,0:T(8,128)S(1)}, u32[]{:S(2)}, u32[]{:S(2)}) collective-permute-start(f32[2,2,128,128]{3,2,1,0:T(8,128)S(1)} %get-tuple-element.53), channel_id=1, source_target_pairs={{0,8},{4,12},{8,0},{12,4},{16,24},{20,28},{24,16},{28,20},{1,9},{5... | collective-permute-start | bytes 786440 | tf_op jit(solution)/shard_map/ppermute | solution.py:56
  54.7 1.4 %collective-permute-done.11 = f32[1,2,64,256]{3,2,1,0:T(8,128)S(1)} collective-permute-done((f32[1,2,64,256]{3,2,1,0:T(8,128)S(1)}, f32[1,2,64,256]{3,2,1,0:T(8,128)S(1)}, u32[]{:S(2)}, u32[]{:S(2)}) %collective-permute-start.11) | collective-permute-done | bytes 131104 | tf_op jit(solution)/shard_map/ppermute | solution.py:56
  56.8 3.6 %collective-permute-start.20 = (f32[1,2,128,128]{3,2,1,0:T(8,128)S(1)}, f32[1,2,128,128]{3,2,1,0:T(8,128)S(1)}, u32[]{:S(2)}, u32[]{:S(2)}) collective-permute-start(f32[1,2,128,128]{3,2,1,0:T(8,128)S(1)} %get-tuple-element.60), channel_id=1, source_target_pairs={{0,24},{4,28},{8,16},{12,20},{16,8},{20,12},{24,0},{28,4},{1,25},{... | collective-permute-start | bytes 393224 | tf_op jit(solution)/shard_map/ppermute | solution.py:56
  62.5 2.4 %collective-permute-start.23 = (f32[1,2,128,128]{3,2,1,0:T(8,128)S(1)}, f32[1,2,128,128]{3,2,1,0:T(8,128)S(1)}, u32[]{:S(2)}, u32[]{:S(2)}) collective-permute-start(f32[1,2,128,128]{3,2,1,0:T(8,128)S(1)} %get-tuple-element.58), channel_id=1, source_target_pairs={{0,24},{4,28},{8,16},{12,20},{16,8},{20,12},{24,0},{28,4},{1,25},{... | collective-permute-start | bytes 393224 | tf_op jit(solution)/shard_map/ppermute | solution.py:56
  64.9 3.0 %collective-permute-done.18.refs_5_ = f32[2,2,64,256]{3,2,1,0:T(8,128)S(1)} collective-permute-done((f32[2,2,64,256]{3,2,1,0:T(8,128)S(1)}, f32[2,2,64,256]{3,2,1,0:T(8,128)S(1)}, u32[]{:S(2)}, u32[]{:S(2)}) %collective-permute-start.18) | collective-permute-done | bytes 262176 | tf_op jit(solution)/shard_map/ppermute | solution.py:56
  67.9 1.2 %weights.1 = (f32[512,256]{1,0:T(8,128)}, f32[512,256]{1,0:T(8,128)}, f32[512,128]{1,0:T(8,128)}, f32[8,128]{1,0:T(8,128)S(1)}) custom-call(f32[1,512,128]{2,1,0:T(8,128)S(1)} %get-tuple-element.57.refs_0_, f32[1,512,128]{2,1,0:T(8,128)S(1)} %collective-permute-done.10.refs_1_, f32[2,2,64,256]{3,2,1,0:T(8,128)S(1)} %pad_maximum_fusion.refs_2_, ...), custom_call_target="tpu_custom_call" | custom-call | tf_op jit(solution)/shard_map/weights/pallas_call | solution.py:470
  69.1 1.3 %collective-permute-done.23.refs_3_ = f32[1,2,128,128]{3,2,1,0:T(8,128)S(1)} collective-permute-done((f32[1,2,128,128]{3,2,1,0:T(8,128)S(1)}, f32[1,2,128,128]{3,2,1,0:T(8,128)S(1)}, u32[]{:S(2)}, u32[]{:S(2)}) %collective-permute-start.23) | collective-permute-done | bytes 131104 | tf_op jit(solution)/shard_map/ppermute | solution.py:56
  (66 shorter events, 10.2 us)
Async XLA Ops:
  5.1 4.9 %collective-permute-start = (f32[4,1024]{1,0:T(4,128)}, f32[4,1024]{1,0:T(4,128)S(1)}, u32[]{:S(2)}, u32[]{:S(2)}) collective-permute-start(f32[4,1024]{1,0:T(4,128)} %get-tuple-element.28.mine), channel_id=1, source_target_pairs={{0,4},{4,0},{8,12},{12,8},{16,20},{20,16},{24,28},{28,24},{1,5},{5... | collective-permute-start | bytes 49160 | tf_op jit(solution)/shard_map/ppermute | solution.py:41
  10.0 3.8 %collective-permute-start.3 = (f32[4,1024]{1,0:T(4,128)S(1)}, f32[4,1024]{1,0:T(4,128)S(1)}, u32[]{:S(2)}, u32[]{:S(2)}) collective-permute-start(f32[4,1024]{1,0:T(4,128)S(1)} %get-tuple-element.34.mine), channel_id=1, source_target_pairs={{0,4},{4,0},{8,12},{12,8},{16,20},{20,16},{24,28},{28,24},{1,5},{5... | collective-permute-start | bytes 49160 | tf_op jit(solution)/shard_map/ppermute | solution.py:41
  10.1 5.3 %collective-permute-start.1 = (f32[4,1024]{1,0:T(4,128)S(1)}, f32[4,1024]{1,0:T(4,128)S(1)}, u32[]{:S(2)}, u32[]{:S(2)}) collective-permute-start(f32[4,1024]{1,0:T(4,128)S(1)} %merge.4.mine), channel_id=1, source_target_pairs={{0,8},{4,12},{8,0},{12,4},{16,24},{20,28},{24,16},{28,20},{1,9},{5... | collective-permute-start | bytes 49160 | tf_op jit(solution)/shard_map/ppermute | solution.py:41
  13.8 4.3 %collective-permute-start.4 = (f32[4,1024]{1,0:T(4,128)S(1)}, f32[4,1024]{1,0:T(4,128)S(1)}, u32[]{:S(2)}, u32[]{:S(2)}) collective-permute-start(f32[4,1024]{1,0:T(4,128)S(1)} %merge.6.mine), channel_id=1, source_target_pairs={{0,8},{4,12},{8,0},{12,4},{16,24},{20,28},{24,16},{28,20},{1,9},{5... | collective-permute-start | bytes 49160 | tf_op jit(solution)/shard_map/ppermute | solution.py:41
  15.5 4.9 %collective-permute-start.2 = (f32[4,1024]{1,0:T(4,128)S(1)}, f32[4,1024]{1,0:T(4,128)S(1)}, u32[]{:S(2)}, u32[]{:S(2)}) collective-permute-start(f32[4,1024]{1,0:T(4,128)S(1)} %merge.5.after.mine), channel_id=1, source_target_pairs={{0,16},{4,20},{8,24},{12,28},{16,0},{20,4},{24,8},{28,12},{1,17},{... | collective-permute-start | bytes 49160 | tf_op jit(solution)/shard_map/ppermute | solution.py:41
  18.1 8.6 %collective-permute-start.5 = (f32[4,1024]{1,0:T(4,128)S(1)}, f32[4,1024]{1,0:T(4,128)S(1)}, u32[]{:S(2)}, u32[]{:S(2)}) collective-permute-start(f32[4,1024]{1,0:T(4,128)S(1)} %merge.7.mine), channel_id=1, source_target_pairs={{0,16},{4,20},{8,24},{12,28},{16,0},{20,4},{24,8},{28,12},{1,17},{... | collective-permute-start | bytes 49160 | tf_op jit(solution)/shard_map/ppermute | solution.py:41
  23.3 9.7 %collective-permute-start.6 = (f32[2,2,64,256]{3,2,1,0:T(8,128)S(1)}, f32[2,2,64,256]{3,2,1,0:T(8,128)S(1)}, u32[]{:S(2)}, u32[]{:S(2)}) collective-permute-start(f32[2,2,64,256]{3,2,1,0:T(8,128)S(1)} %get-tuple-element.37), channel_id=1, source_target_pairs={{0,4},{4,0},{8,12},{12,8},{16,20},{20,16},{24,28},{28,24},{1,5},{5... | collective-permute-start | bytes 786440 | tf_op jit(solution)/shard_map/ppermute | solution.py:56
  24.9 20.2 %collective-permute-start.15 = (f32[4,2,128,128]{3,2,1,0:T(8,128)S(1)}, f32[4,2,128,128]{3,2,1,0:T(8,128)S(1)}, u32[]{:S(2)}, u32[]{:S(2)}) collective-permute-start(f32[4,2,128,128]{3,2,1,0:T(8,128)S(1)} %get-tuple-element.44), channel_id=1, source_target_pairs={{0,8},{4,12},{8,0},{12,4},{16,24},{20,28},{24,16},{28,20},{1,9},{5... | collective-permute-start | bytes 1572872 | tf_op jit(solution)/shard_map/ppermute | solution.py:56
  29.6 9.3 %collective-permute-start.13 = (f32[2,2,64,256]{3,2,1,0:T(8,128)S(1)}, f32[2,2,64,256]{3,2,1,0:T(8,128)S(1)}, u32[]{:S(2)}, u32[]{:S(2)}) collective-permute-start(f32[2,2,64,256]{3,2,1,0:T(8,128)S(1)} %get-tuple-element.41), channel_id=1, source_target_pairs={{0,4},{4,0},{8,12},{12,8},{16,20},{20,16},{24,28},{28,24},{1,5},{5... | collective-permute-start | bytes 786440 | tf_op jit(solution)/shard_map/ppermute | solution.py:56
  32.2 20.3 %collective-permute-start.21 = (f32[4,2,128,128]{3,2,1,0:T(8,128)S(1)}, f32[4,2,128,128]{3,2,1,0:T(8,128)S(1)}, u32[]{:S(2)}, u32[]{:S(2)}) collective-permute-start(f32[4,2,128,128]{3,2,1,0:T(8,128)S(1)} %get-tuple-element.48), channel_id=1, source_target_pairs={{0,4},{4,0},{8,12},{12,8},{16,20},{20,16},{24,28},{28,24},{1,5},{5... | collective-permute-start | bytes 1572872 | tf_op jit(solution)/shard_map/ppermute | solution.py:56
  33.0 6.8 %collective-permute-start.7 = (f32[1,2,64,256]{3,2,1,0:T(8,128)S(1)}, f32[1,2,64,256]{3,2,1,0:T(8,128)S(1)}, u32[]{:S(2)}, u32[]{:S(2)}) collective-permute-start(f32[1,2,64,256]{3,2,1,0:T(8,128)S(1)} %slice_add_fusion.12), channel_id=1, source_target_pairs={{0,8},{4,12},{8,0},{12,4},{16,24},{20,28},{24,16},{28,20},{1,9},{5... | collective-permute-start | bytes 393224 | tf_op jit(solution)/shard_map/ppermute | solution.py:56
  39.0 6.7 %collective-permute-start.14 = (f32[1,2,64,256]{3,2,1,0:T(8,128)S(1)}, f32[1,2,64,256]{3,2,1,0:T(8,128)S(1)}, u32[]{:S(2)}, u32[]{:S(2)}) collective-permute-start(f32[1,2,64,256]{3,2,1,0:T(8,128)S(1)} %get-tuple-element.62), channel_id=1, source_target_pairs={{0,8},{4,12},{8,0},{12,4},{16,24},{20,28},{24,16},{28,20},{1,9},{5... | collective-permute-start | bytes 393224 | tf_op jit(solution)/shard_map/ppermute | solution.py:56
  39.8 9.4 %collective-permute-start.8 = (f32[1,2,64,256]{3,2,1,0:T(8,128)S(1)}, f32[1,2,64,256]{3,2,1,0:T(8,128)S(1)}, u32[]{:S(2)}, u32[]{:S(2)}) collective-permute-start(f32[1,2,64,256]{3,2,1,0:T(8,128)S(1)} %fusion), channel_id=1, source_target_pairs={{0,24},{4,28},{8,16},{12,20},{16,8},{20,12},{24,0},{28,4},{1,25},{... | collective-permute-start | bytes 393224 | tf_op jit(solution)/shard_map/ppermute | solution.py:56
  45.2 11.6 %collective-permute-start.19 = (f32[2,2,128,128]{3,2,1,0:T(8,128)S(1)}, f32[2,2,128,128]{3,2,1,0:T(8,128)S(1)}, u32[]{:S(2)}, u32[]{:S(2)}) collective-permute-start(f32[2,2,128,128]{3,2,1,0:T(8,128)S(1)} %get-tuple-element.55.after), channel_id=1, source_target_pairs={{0,4},{4,0},{8,12},{12,8},{16,20},{20,16},{24,28},{28,24},{1,5},{5... | collective-permute-start | bytes 786440 | tf_op jit(solution)/shard_map/ppermute | solution.py:56
  45.7 8.9 %collective-permute-start.16 = (f32[1,2,64,256]{3,2,1,0:T(8,128)S(1)}, f32[1,2,64,256]{3,2,1,0:T(8,128)S(1)}, u32[]{:S(2)}, u32[]{:S(2)}) collective-permute-start(f32[1,2,64,256]{3,2,1,0:T(8,128)S(1)} %added.1), channel_id=1, source_target_pairs={{0,24},{4,28},{8,16},{12,20},{16,8},{20,12},{24,0},{28,4},{1,25},{... | collective-permute-start | bytes 393224 | tf_op jit(solution)/shard_map/ppermute | solution.py:56
  49.2 6.9 %collective-permute-start.11 = (f32[1,2,64,256]{3,2,1,0:T(8,128)S(1)}, f32[1,2,64,256]{3,2,1,0:T(8,128)S(1)}, u32[]{:S(2)}, u32[]{:S(2)}) collective-permute-start(f32[1,2,64,256]{3,2,1,0:T(8,128)S(1)} %add.54.refs_2_), channel_id=1, source_target_pairs={{0,8},{4,12},{8,0},{12,4},{16,24},{20,28},{24,16},{28,20},{1,9},{5... | collective-permute-start | bytes 393224 | tf_op jit(solution)/shard_map/ppermute | solution.py:56
  50.1 12.2 %collective-permute-start.9 = (f32[2,512,128]{2,1,0:T(8,128)S(1)}, f32[2,512,128]{2,1,0:T(8,128)S(1)}, u32[]{:S(2)}, u32[]{:S(2)}) collective-permute-start(f32[2,512,128]{2,1,0:T(8,128)S(1)} %get-tuple-element.39), channel_id=1, source_target_pairs={{0,2},{1,3},{2,0},{3,1},{4,6},{5,7},{6,4},{7,5},{8,10},{9,11},{10,... | collective-permute-start | bytes 1572872 | tf_op jit(solution)/shard_map/ppermute | solution.py:41
  52.5 10.0 %collective-permute-start.22 = (f32[2,2,128,128]{3,2,1,0:T(8,128)S(1)}, f32[2,2,128,128]{3,2,1,0:T(8,128)S(1)}, u32[]{:S(2)}, u32[]{:S(2)}) collective-permute-start(f32[2,2,128,128]{3,2,1,0:T(8,128)S(1)} %get-tuple-element.53), channel_id=1, source_target_pairs={{0,8},{4,12},{8,0},{12,4},{16,24},{20,28},{24,16},{28,20},{1,9},{5... | collective-permute-start | bytes 786440 | tf_op jit(solution)/shard_map/ppermute | solution.py:56
  54.6 6.8 %collective-permute-start.17 = (f32[1,2,64,256]{3,2,1,0:T(8,128)S(1)}, f32[1,2,64,256]{3,2,1,0:T(8,128)S(1)}, u32[]{:S(2)}, u32[]{:S(2)}) collective-permute-start(f32[1,2,64,256]{3,2,1,0:T(8,128)S(1)} %add.60), channel_id=1, source_target_pairs={{0,8},{4,12},{8,0},{12,4},{16,24},{20,28},{24,16},{28,20},{1,9},{5... | collective-permute-start | bytes 393224 | tf_op jit(solution)/shard_map/ppermute | solution.py:56
  56.2 8.8 %collective-permute-start.12 = (f32[2,2,64,256]{3,2,1,0:T(8,128)S(1)}, f32[2,2,64,256]{3,2,1,0:T(8,128)S(1)}, u32[]{:S(2)}, u32[]{:S(2)}) collective-permute-start(f32[2,2,64,256]{3,2,1,0:T(8,128)S(1)} %pad_maximum_fusion.refs_2_), channel_id=1, source_target_pairs={{0,4},{4,0},{8,12},{12,8},{16,20},{20,16},{24,28},{28,24},{1,5},{5... | collective-permute-start | bytes 786440 | tf_op jit(solution)/shard_map/ppermute | solution.py:56
  56.8 12.3 %collective-permute-start.20 = (f32[1,2,128,128]{3,2,1,0:T(8,128)S(1)}, f32[1,2,128,128]{3,2,1,0:T(8,128)S(1)}, u32[]{:S(2)}, u32[]{:S(2)}) collective-permute-start(f32[1,2,128,128]{3,2,1,0:T(8,128)S(1)} %get-tuple-element.60), channel_id=1, source_target_pairs={{0,24},{4,28},{8,16},{12,20},{16,8},{20,12},{24,0},{28,4},{1,25},{... | collective-permute-start | bytes 393224 | tf_op jit(solution)/shard_map/ppermute | solution.py:56
  61.5 6.4 %collective-permute-start.18 = (f32[2,2,64,256]{3,2,1,0:T(8,128)S(1)}, f32[2,2,64,256]{3,2,1,0:T(8,128)S(1)}, u32[]{:S(2)}, u32[]{:S(2)}) collective-permute-start(f32[2,2,64,256]{3,2,1,0:T(8,128)S(1)} %pad_maximum_fusion.1.refs_4_), channel_id=1, source_target_pairs={{0,4},{4,0},{8,12},{12,8},{16,20},{20,16},{24,28},{28,24},{1,5},{5... | collective-permute-start | bytes 786440 | tf_op jit(solution)/shard_map/ppermute | solution.py:56
  62.4 5.5 %collective-permute-start.10 = (f32[1,512,128]{2,1,0:T(8,128)S(1)}, f32[1,512,128]{2,1,0:T(8,128)S(1)}, u32[]{:S(2)}, u32[]{:S(2)}) collective-permute-start(f32[1,512,128]{2,1,0:T(8,128)S(1)} %get-tuple-element.56), channel_id=1, source_target_pairs={{0,1},{1,0},{2,3},{3,2},{4,5},{5,4},{6,7},{7,6},{8,9},{9,8},{10,11... | collective-permute-start | bytes 786440 | tf_op jit(solution)/shard_map/ppermute | solution.py:41
  62.5 7.9 %collective-permute-start.23 = (f32[1,2,128,128]{3,2,1,0:T(8,128)S(1)}, f32[1,2,128,128]{3,2,1,0:T(8,128)S(1)}, u32[]{:S(2)}, u32[]{:S(2)}) collective-permute-start(f32[1,2,128,128]{3,2,1,0:T(8,128)S(1)} %get-tuple-element.58), channel_id=1, source_target_pairs={{0,24},{4,28},{8,16},{12,20},{16,8},{20,12},{24,0},{28,4},{1,25},{... | collective-permute-start | bytes 393224 | tf_op jit(solution)/shard_map/ppermute | solution.py:56
  (8 other events, 73.0 us)

commit v19 on v18

--- a/solution.py
+++ b/solution.py
@@ -285,7 +285,7 @@
             pl.pallas_call(
                 functools.partial(first_kernel, tile)
                 if first
-                else functools.partial(later_kernel, latents // 2, head_index),
+                else functools.partial(later_kernel, latents, head_index),
                 out_shape=(
                     shape_of((row_count, HD), jnp.bfloat16),
                     shape_of((row_count, HD), jnp.bfloat16),

time: 71.3 us -> 71.2 us (level)
  no operation moved by 1% of the time
where the time goes in v19:
time: 71.2 us; the launch traced here: 71.1 us
  starting transfers between devices  37.2 us (52%)
  Pallas kernels  17.1 us (24%)
  waiting for transfers between devices  15.5 us (22%)
  between operations  0.89 us (1%)
    ppermute x16, starting transfers between devices, row_swap_of(): return lax.ppermute(array, 'rows', pairs)  23 us
    ppermute x8, starting transfers between devices, swap(): return lax.ppermute(array, axis, pairs)  14.2 us
    ppermute x16, waiting for transfers between devices, row_swap_of(): return lax.ppermute(array, 'rows', pairs)  14 us
    pallas_call x4, Pallas kernels, kernel_call(): pl.pallas_call(kernel, out_shape=[shape_of(*item) for item in shapes], in...  8.05 us
    pallas_call x2, Pallas kernels, on_device(): pl.pallas_call(functools.partial(first_kernel, tile) if first else functo...  6.2 us
    ppermute x8, waiting for transfers between devices, swap(): return lax.ppermute(array, axis, pairs)  1.52 us
  transfers between devices with their start and end apart: 24, of which 9 were waited for; matrix products, arithmetic and copies ran while one was open for 1% of the time, Pallas kernels for 17%

profile of v19, /device:TPU:0, one launch (start us, length us, event | category | flops | bytes accessed | tf_op | source)
XLA Modules:
  0.0 71.1 jit_solution(14831888478711759364)
XLA Ops:
  0.7 4.4 %project.2 = (bf16[512,128]{1,0:T(8,128)(2,1)}, bf16[512,128]{1,0:T(8,128)(2,1)}, f32[4,1024]{1,0:T(4,128)}) custom-call(bf16[512,512]{1,0:T(8,128)(2,1)} %inputs.3, bf16[512,256]{1,0:T(8,128)(2,1)} %key_weight.1, bf16[512,256]{1,0:T(8,128)(2,1)} %value_weight.1, bf16[2,1024,256]{2,1,0:T(8,128)(2,1)} %queries.4, bf16[2,1024,256]{2,1,0:T(8,128)(2,1)} %out_grad.3), custom_call_target="tpu_custom_call" | custom-call | flops 1073741824 | bytes 4194304 | tf_op jit(solution)/shard_map/project/pallas_call | solution.py:285
  5.1 3.0 %collective-permute-start = (f32[4,1024]{1,0:T(4,128)}, f32[4,1024]{1,0:T(4,128)S(1)}, u32[]{:S(2)}, u32[]{:S(2)}) collective-permute-start(f32[4,1024]{1,0:T(4,128)} %get-tuple-element.28.mine), channel_id=1, source_target_pairs={{0,4},{4,0},{8,12},{12,8},{16,20},{20,16},{24,28},{28,24},{1,5},{5... | collective-permute-start | bytes 49160 | tf_op jit(solution)/shard_map/ppermute | solution.py:41
  8.2 1.8 %project.3 = (bf16[512,128]{1,0:T(8,128)(2,1)S(1)}, bf16[512,128]{1,0:T(8,128)(2,1)S(1)}, f32[4,1024]{1,0:T(4,128)S(1)}) custom-call(bf16[512,512]{1,0:T(8,128)(2,1)S(1)} %copy-done.3, bf16[512,256]{1,0:T(8,128)(2,1)S(1)} %copy-done.4, bf16[512,256]{1,0:T(8,128)(2,1)S(1)} %copy-done.5, bf16[2,1024,256]{2,1,0:T(8,128)(2,1)S(1)} %copy-done.1, ...), custom_call_target="tpu_custom_call" | custom-call | flops 1073741824 | bytes 4194304 | tf_op jit(solution)/shard_map/project/pallas_call | solution.py:285
  10.1 2.2 %collective-permute-start.1 = (f32[4,1024]{1,0:T(4,128)S(1)}, f32[4,1024]{1,0:T(4,128)S(1)}, u32[]{:S(2)}, u32[]{:S(2)}) collective-permute-start(f32[4,1024]{1,0:T(4,128)S(1)} %merge.4.mine), channel_id=1, source_target_pairs={{0,8},{4,12},{8,0},{12,4},{16,24},{20,28},{24,16},{28,20},{1,9},{5... | collective-permute-start | bytes 49160 | tf_op jit(solution)/shard_map/ppermute | solution.py:41
  12.3 1.5 %collective-permute-done.3.theirs = f32[4,1024]{1,0:T(4,128)S(1)} collective-permute-done((f32[4,1024]{1,0:T(4,128)S(1)}, f32[4,1024]{1,0:T(4,128)S(1)}, u32[]{:S(2)}, u32[]{:S(2)}) %collective-permute-start.3) | collective-permute-done | bytes 16416 | tf_op jit(solution)/shard_map/ppermute | solution.py:41
  13.8 1.6 %collective-permute-start.4 = (f32[4,1024]{1,0:T(4,128)S(1)}, f32[4,1024]{1,0:T(4,128)S(1)}, u32[]{:S(2)}, u32[]{:S(2)}) collective-permute-start(f32[4,1024]{1,0:T(4,128)S(1)} %merge.6.mine), channel_id=1, source_target_pairs={{0,8},{4,12},{8,0},{12,4},{16,24},{20,28},{24,16},{28,20},{1,9},{5... | collective-permute-start | bytes 49160 | tf_op jit(solution)/shard_map/ppermute | solution.py:41
  15.5 2.7 %collective-permute-start.2 = (f32[4,1024]{1,0:T(4,128)S(1)}, f32[4,1024]{1,0:T(4,128)S(1)}, u32[]{:S(2)}, u32[]{:S(2)}) collective-permute-start(f32[4,1024]{1,0:T(4,128)S(1)} %merge.5.after.mine), channel_id=1, source_target_pairs={{0,16},{4,20},{8,24},{12,28},{16,0},{20,4},{24,8},{28,12},{1,17},{... | collective-permute-start | bytes 49160 | tf_op jit(solution)/shard_map/ppermute | solution.py:41
  18.2 2.2 %collective-permute-start.5 = (f32[4,1024]{1,0:T(4,128)S(1)}, f32[4,1024]{1,0:T(4,128)S(1)}, u32[]{:S(2)}, u32[]{:S(2)}) collective-permute-start(f32[4,1024]{1,0:T(4,128)S(1)} %merge.7.mine), channel_id=1, source_target_pairs={{0,16},{4,20},{8,24},{12,28},{16,0},{20,4},{24,8},{28,12},{1,17},{... | collective-permute-start | bytes 49160 | tf_op jit(solution)/shard_map/ppermute | solution.py:41
  20.4 2.9 %grads.2 = (bf16[512,256]{1,0:T(8,128)(2,1)S(1)}, bf16[2,512,1024]{2,1,0:T(8,128)(2,1)S(1)}, f32[2,2,64,256]{3,2,1,0:T(8,128)S(1)}, f32[2,2,64,256]{3,2,1,0:T(8,128)S(1)}) custom-call(f32[4,1024]{1,0:T(4,128)S(1)} %merge.5.after.mine, bf16[512,512]{1,0:T(8,128)(2,1)S(1)} %copy-done.3, bf16[512,128]{1,0:T(8,128)(2,1)S(1)} %copy-done.6, ...), custom_call_target="tpu_custom_call" | custom-call | flops 1073741824 | bytes 4194304 | tf_op jit(solution)/shard_map/grads/pallas_call | solution.py:341
  24.9 1.8 %collective-permute-start.15 = (f32[4,2,128,128]{3,2,1,0:T(8,128)S(1)}, f32[4,2,128,128]{3,2,1,0:T(8,128)S(1)}, u32[]{:S(2)}, u32[]{:S(2)}) collective-permute-start(f32[4,2,128,128]{3,2,1,0:T(8,128)S(1)} %get-tuple-element.44), channel_id=1, source_target_pairs={{0,8},{4,12},{8,0},{12,4},{16,24},{20,28},{24,16},{28,20},{1,9},{5... | collective-permute-start | bytes 1572872 | tf_op jit(solution)/shard_map/ppermute | solution.py:56
  26.7 2.9 %grads.3 = (bf16[512,256]{1,0:T(8,128)(2,1)S(1)}, bf16[2,512,1024]{2,1,0:T(8,128)(2,1)S(1)}, f32[2,2,64,256]{3,2,1,0:T(8,128)S(1)}, f32[2,2,64,256]{3,2,1,0:T(8,128)S(1)}) custom-call(bf16[512,256]{1,0:T(8,128)(2,1)S(1)} %get-tuple-element.31.after.refs_0_, bf16[512,512]{1,0:T(8,128)(2,1)S(1)} %copy-done.3, bf16[512,128]{1,0:T(8,128)(2,1)S(1)} %get-tuple-element.32.keys, ...), custom_call_target="tpu_custom_call" | custom-call | flops 1073741824 | bytes 4194304 | tf_op jit(solution)/shard_map/grads/pallas_call | solution.py:341
  29.6 1.4 %collective-permute-start.13 = (f32[2,2,64,256]{3,2,1,0:T(8,128)S(1)}, f32[2,2,64,256]{3,2,1,0:T(8,128)S(1)}, u32[]{:S(2)}, u32[]{:S(2)}) collective-permute-start(f32[2,2,64,256]{3,2,1,0:T(8,128)S(1)} %get-tuple-element.41), channel_id=1, source_target_pairs={{0,4},{4,0},{8,12},{12,8},{16,20},{20,16},{24,28},{28,24},{1,5},{5... | collective-permute-start | bytes 786440 | tf_op jit(solution)/shard_map/ppermute | solution.py:56
  31.1 1.1 %query.3 = (f32[4,2,128,128]{3,2,1,0:T(8,128)S(1)}, f32[4,2,128,128]{3,2,1,0:T(8,128)S(1)}) custom-call(bf16[512,256]{1,0:T(8,128)(2,1)S(1)} %get-tuple-element.35.refs_1_.after, bf16[2,512,1024]{2,1,0:T(8,128)(2,1)S(1)} %get-tuple-element.46.score_grads, bf16[512,128]{1,0:T(8,128)(2,1)S(1)} %get-tuple-element.32.keys), custom_call_target="tpu_custom_call" | custom-call | flops 1073741824 | bytes 4194304 | tf_op jit(solution)/shard_map/query/pallas_call | solution.py:341
  33.5 5.4 %collective-permute-done.13 = f32[2,2,64,256]{3,2,1,0:T(8,128)S(1)} collective-permute-done((f32[2,2,64,256]{3,2,1,0:T(8,128)S(1)}, f32[2,2,64,256]{3,2,1,0:T(8,128)S(1)}, u32[]{:S(2)}, u32[]{:S(2)}) %collective-permute-start.13) | collective-permute-done | bytes 262176 | tf_op jit(solution)/shard_map/ppermute | solution.py:56
  39.8 5.3 %collective-permute-start.8 = (f32[1,2,64,256]{3,2,1,0:T(8,128)S(1)}, f32[1,2,64,256]{3,2,1,0:T(8,128)S(1)}, u32[]{:S(2)}, u32[]{:S(2)}) collective-permute-start(f32[1,2,64,256]{3,2,1,0:T(8,128)S(1)} %fusion), channel_id=1, source_target_pairs={{0,24},{4,28},{8,16},{12,20},{16,8},{20,12},{24,0},{28,4},{1,25},{... | collective-permute-start | bytes 393224 | tf_op jit(solution)/shard_map/ppermute | solution.py:56
  45.7 2.4 %collective-permute-start.16 = (f32[1,2,64,256]{3,2,1,0:T(8,128)S(1)}, f32[1,2,64,256]{3,2,1,0:T(8,128)S(1)}, u32[]{:S(2)}, u32[]{:S(2)}) collective-permute-start(f32[1,2,64,256]{3,2,1,0:T(8,128)S(1)} %added.1), channel_id=1, source_target_pairs={{0,24},{4,28},{8,16},{12,20},{16,8},{20,12},{24,0},{28,4},{1,25},{... | collective-permute-start | bytes 393224 | tf_op jit(solution)/shard_map/ppermute | solution.py:56
  50.2 2.3 %collective-permute-start.9 = (f32[2,512,128]{2,1,0:T(8,128)S(1)}, f32[2,512,128]{2,1,0:T(8,128)S(1)}, u32[]{:S(2)}, u32[]{:S(2)}) collective-permute-start(f32[2,512,128]{2,1,0:T(8,128)S(1)} %get-tuple-element.39), channel_id=1, source_target_pairs={{0,2},{1,3},{2,0},{3,1},{4,6},{5,7},{6,4},{7,5},{8,10},{9,11},{10,... | collective-permute-start | bytes 1572872 | tf_op jit(solution)/shard_map/ppermute | solution.py:41
  52.6 2.1 %collective-permute-start.22 = (f32[2,2,128,128]{3,2,1,0:T(8,128)S(1)}, f32[2,2,128,128]{3,2,1,0:T(8,128)S(1)}, u32[]{:S(2)}, u32[]{:S(2)}) collective-permute-start(f32[2,2,128,128]{3,2,1,0:T(8,128)S(1)} %get-tuple-element.53), channel_id=1, source_target_pairs={{0,8},{4,12},{8,0},{12,4},{16,24},{20,28},{24,16},{28,20},{1,9},{5... | collective-permute-start | bytes 786440 | tf_op jit(solution)/shard_map/ppermute | solution.py:56
  54.7 1.4 %collective-permute-done.11 = f32[1,2,64,256]{3,2,1,0:T(8,128)S(1)} collective-permute-done((f32[1,2,64,256]{3,2,1,0:T(8,128)S(1)}, f32[1,2,64,256]{3,2,1,0:T(8,128)S(1)}, u32[]{:S(2)}, u32[]{:S(2)}) %collective-permute-start.11) | collective-permute-done | bytes 131104 | tf_op jit(solution)/shard_map/ppermute | solution.py:56
  56.9 3.6 %collective-permute-start.20 = (f32[1,2,128,128]{3,2,1,0:T(8,128)S(1)}, f32[1,2,128,128]{3,2,1,0:T(8,128)S(1)}, u32[]{:S(2)}, u32[]{:S(2)}) collective-permute-start(f32[1,2,128,128]{3,2,1,0:T(8,128)S(1)} %get-tuple-element.60), channel_id=1, source_target_pairs={{0,24},{4,28},{8,16},{12,20},{16,8},{20,12},{24,0},{28,4},{1,25},{... | collective-permute-start | bytes 393224 | tf_op jit(solution)/shard_map/ppermute | solution.py:56
  62.5 2.4 %collective-permute-start.23 = (f32[1,2,128,128]{3,2,1,0:T(8,128)S(1)}, f32[1,2,128,128]{3,2,1,0:T(8,128)S(1)}, u32[]{:S(2)}, u32[]{:S(2)}) collective-permute-start(f32[1,2,128,128]{3,2,1,0:T(8,128)S(1)} %get-tuple-element.58), channel_id=1, source_target_pairs={{0,24},{4,28},{8,16},{12,20},{16,8},{20,12},{24,0},{28,4},{1,25},{... | collective-permute-start | bytes 393224 | tf_op jit(solution)/shard_map/ppermute | solution.py:56
  64.9 3.0 %collective-permute-done.18.refs_5_ = f32[2,2,64,256]{3,2,1,0:T(8,128)S(1)} collective-permute-done((f32[2,2,64,256]{3,2,1,0:T(8,128)S(1)}, f32[2,2,64,256]{3,2,1,0:T(8,128)S(1)}, u32[]{:S(2)}, u32[]{:S(2)}) %collective-permute-start.18) | collective-permute-done | bytes 262176 | tf_op jit(solution)/shard_map/ppermute | solution.py:56
  67.9 1.2 %weights.1 = (f32[512,256]{1,0:T(8,128)}, f32[512,256]{1,0:T(8,128)}, f32[512,128]{1,0:T(8,128)}, f32[8,128]{1,0:T(8,128)S(1)}) custom-call(f32[1,512,128]{2,1,0:T(8,128)S(1)} %get-tuple-element.57.refs_0_, f32[1,512,128]{2,1,0:T(8,128)S(1)} %collective-permute-done.10.refs_1_, f32[2,2,64,256]{3,2,1,0:T(8,128)S(1)} %pad_maximum_fusion.refs_2_, ...), custom_call_target="tpu_custom_call" | custom-call | tf_op jit(solution)/shard_map/weights/pallas_call | solution.py:470
  69.1 1.2 %collective-permute-done.23.refs_3_ = f32[1,2,128,128]{3,2,1,0:T(8,128)S(1)} collective-permute-done((f32[1,2,128,128]{3,2,1,0:T(8,128)S(1)}, f32[1,2,128,128]{3,2,1,0:T(8,128)S(1)}, u32[]{:S(2)}, u32[]{:S(2)}) %collective-permute-start.23) | collective-permute-done | bytes 131104 | tf_op jit(solution)/shard_map/ppermute | solution.py:56
  (66 shorter events, 10.3 us)
Async XLA Ops:
  5.1 4.9 %collective-permute-start = (f32[4,1024]{1,0:T(4,128)}, f32[4,1024]{1,0:T(4,128)S(1)}, u32[]{:S(2)}, u32[]{:S(2)}) collective-permute-start(f32[4,1024]{1,0:T(4,128)} %get-tuple-element.28.mine), channel_id=1, source_target_pairs={{0,4},{4,0},{8,12},{12,8},{16,20},{20,16},{24,28},{28,24},{1,5},{5... | collective-permute-start | bytes 49160 | tf_op jit(solution)/shard_map/ppermute | solution.py:41
  10.0 3.8 %collective-permute-start.3 = (f32[4,1024]{1,0:T(4,128)S(1)}, f32[4,1024]{1,0:T(4,128)S(1)}, u32[]{:S(2)}, u32[]{:S(2)}) collective-permute-start(f32[4,1024]{1,0:T(4,128)S(1)} %get-tuple-element.34.mine), channel_id=1, source_target_pairs={{0,4},{4,0},{8,12},{12,8},{16,20},{20,16},{24,28},{28,24},{1,5},{5... | collective-permute-start | bytes 49160 | tf_op jit(solution)/shard_map/ppermute | solution.py:41
  10.1 5.3 %collective-permute-start.1 = (f32[4,1024]{1,0:T(4,128)S(1)}, f32[4,1024]{1,0:T(4,128)S(1)}, u32[]{:S(2)}, u32[]{:S(2)}) collective-permute-start(f32[4,1024]{1,0:T(4,128)S(1)} %merge.4.mine), channel_id=1, source_target_pairs={{0,8},{4,12},{8,0},{12,4},{16,24},{20,28},{24,16},{28,20},{1,9},{5... | collective-permute-start | bytes 49160 | tf_op jit(solution)/shard_map/ppermute | solution.py:41
  13.8 4.3 %collective-permute-start.4 = (f32[4,1024]{1,0:T(4,128)S(1)}, f32[4,1024]{1,0:T(4,128)S(1)}, u32[]{:S(2)}, u32[]{:S(2)}) collective-permute-start(f32[4,1024]{1,0:T(4,128)S(1)} %merge.6.mine), channel_id=1, source_target_pairs={{0,8},{4,12},{8,0},{12,4},{16,24},{20,28},{24,16},{28,20},{1,9},{5... | collective-permute-start | bytes 49160 | tf_op jit(solution)/shard_map/ppermute | solution.py:41
  15.5 4.9 %collective-permute-start.2 = (f32[4,1024]{1,0:T(4,128)S(1)}, f32[4,1024]{1,0:T(4,128)S(1)}, u32[]{:S(2)}, u32[]{:S(2)}) collective-permute-start(f32[4,1024]{1,0:T(4,128)S(1)} %merge.5.after.mine), channel_id=1, source_target_pairs={{0,16},{4,20},{8,24},{12,28},{16,0},{20,4},{24,8},{28,12},{1,17},{... | collective-permute-start | bytes 49160 | tf_op jit(solution)/shard_map/ppermute | solution.py:41
  18.2 8.6 %collective-permute-start.5 = (f32[4,1024]{1,0:T(4,128)S(1)}, f32[4,1024]{1,0:T(4,128)S(1)}, u32[]{:S(2)}, u32[]{:S(2)}) collective-permute-start(f32[4,1024]{1,0:T(4,128)S(1)} %merge.7.mine), channel_id=1, source_target_pairs={{0,16},{4,20},{8,24},{12,28},{16,0},{20,4},{24,8},{28,12},{1,17},{... | collective-permute-start | bytes 49160 | tf_op jit(solution)/shard_map/ppermute | solution.py:41
  23.3 9.6 %collective-permute-start.6 = (f32[2,2,64,256]{3,2,1,0:T(8,128)S(1)}, f32[2,2,64,256]{3,2,1,0:T(8,128)S(1)}, u32[]{:S(2)}, u32[]{:S(2)}) collective-permute-start(f32[2,2,64,256]{3,2,1,0:T(8,128)S(1)} %get-tuple-element.37), channel_id=1, source_target_pairs={{0,4},{4,0},{8,12},{12,8},{16,20},{20,16},{24,28},{28,24},{1,5},{5... | collective-permute-start | bytes 786440 | tf_op jit(solution)/shard_map/ppermute | solution.py:56
  24.9 20.2 %collective-permute-start.15 = (f32[4,2,128,128]{3,2,1,0:T(8,128)S(1)}, f32[4,2,128,128]{3,2,1,0:T(8,128)S(1)}, u32[]{:S(2)}, u32[]{:S(2)}) collective-permute-start(f32[4,2,128,128]{3,2,1,0:T(8,128)S(1)} %get-tuple-element.44), channel_id=1, source_target_pairs={{0,8},{4,12},{8,0},{12,4},{16,24},{20,28},{24,16},{28,20},{1,9},{5... | collective-permute-start | bytes 1572872 | tf_op jit(solution)/shard_map/ppermute | solution.py:56
  29.6 9.3 %collective-permute-start.13 = (f32[2,2,64,256]{3,2,1,0:T(8,128)S(1)}, f32[2,2,64,256]{3,2,1,0:T(8,128)S(1)}, u32[]{:S(2)}, u32[]{:S(2)}) collective-permute-start(f32[2,2,64,256]{3,2,1,0:T(8,128)S(1)} %get-tuple-element.41), channel_id=1, source_target_pairs={{0,4},{4,0},{8,12},{12,8},{16,20},{20,16},{24,28},{28,24},{1,5},{5... | collective-permute-start | bytes 786440 | tf_op jit(solution)/shard_map/ppermute | solution.py:56
  32.2 20.3 %collective-permute-start.21 = (f32[4,2,128,128]{3,2,1,0:T(8,128)S(1)}, f32[4,2,128,128]{3,2,1,0:T(8,128)S(1)}, u32[]{:S(2)}, u32[]{:S(2)}) collective-permute-start(f32[4,2,128,128]{3,2,1,0:T(8,128)S(1)} %get-tuple-element.48), channel_id=1, source_target_pairs={{0,4},{4,0},{8,12},{12,8},{16,20},{20,16},{24,28},{28,24},{1,5},{5... | collective-permute-start | bytes 1572872 | tf_op jit(solution)/shard_map/ppermute | solution.py:56
  33.0 6.8 %collective-permute-start.7 = (f32[1,2,64,256]{3,2,1,0:T(8,128)S(1)}, f32[1,2,64,256]{3,2,1,0:T(8,128)S(1)}, u32[]{:S(2)}, u32[]{:S(2)}) collective-permute-start(f32[1,2,64,256]{3,2,1,0:T(8,128)S(1)} %slice_add_fusion.12), channel_id=1, source_target_pairs={{0,8},{4,12},{8,0},{12,4},{16,24},{20,28},{24,16},{28,20},{1,9},{5... | collective-permute-start | bytes 393224 | tf_op jit(solution)/shard_map/ppermute | solution.py:56
  39.0 6.7 %collective-permute-start.14 = (f32[1,2,64,256]{3,2,1,0:T(8,128)S(1)}, f32[1,2,64,256]{3,2,1,0:T(8,128)S(1)}, u32[]{:S(2)}, u32[]{:S(2)}) collective-permute-start(f32[1,2,64,256]{3,2,1,0:T(8,128)S(1)} %get-tuple-element.62), channel_id=1, source_target_pairs={{0,8},{4,12},{8,0},{12,4},{16,24},{20,28},{24,16},{28,20},{1,9},{5... | collective-permute-start | bytes 393224 | tf_op jit(solution)/shard_map/ppermute | solution.py:56
  39.8 9.4 %collective-permute-start.8 = (f32[1,2,64,256]{3,2,1,0:T(8,128)S(1)}, f32[1,2,64,256]{3,2,1,0:T(8,128)S(1)}, u32[]{:S(2)}, u32[]{:S(2)}) collective-permute-start(f32[1,2,64,256]{3,2,1,0:T(8,128)S(1)} %fusion), channel_id=1, source_target_pairs={{0,24},{4,28},{8,16},{12,20},{16,8},{20,12},{24,0},{28,4},{1,25},{... | collective-permute-start | bytes 393224 | tf_op jit(solution)/shard_map/ppermute | solution.py:56
  45.2 11.6 %collective-permute-start.19 = (f32[2,2,128,128]{3,2,1,0:T(8,128)S(1)}, f32[2,2,128,128]{3,2,1,0:T(8,128)S(1)}, u32[]{:S(2)}, u32[]{:S(2)}) collective-permute-start(f32[2,2,128,128]{3,2,1,0:T(8,128)S(1)} %get-tuple-element.55.after), channel_id=1, source_target_pairs={{0,4},{4,0},{8,12},{12,8},{16,20},{20,16},{24,28},{28,24},{1,5},{5... | collective-permute-start | bytes 786440 | tf_op jit(solution)/shard_map/ppermute | solution.py:56
  45.7 9.0 %collective-permute-start.16 = (f32[1,2,64,256]{3,2,1,0:T(8,128)S(1)}, f32[1,2,64,256]{3,2,1,0:T(8,128)S(1)}, u32[]{:S(2)}, u32[]{:S(2)}) collective-permute-start(f32[1,2,64,256]{3,2,1,0:T(8,128)S(1)} %added.1), channel_id=1, source_target_pairs={{0,24},{4,28},{8,16},{12,20},{16,8},{20,12},{24,0},{28,4},{1,25},{... | collective-permute-start | bytes 393224 | tf_op jit(solution)/shard_map/ppermute | solution.py:56
  49.2 6.9 %collective-permute-start.11 = (f32[1,2,64,256]{3,2,1,0:T(8,128)S(1)}, f32[1,2,64,256]{3,2,1,0:T(8,128)S(1)}, u32[]{:S(2)}, u32[]{:S(2)}) collective-permute-start(f32[1,2,64,256]{3,2,1,0:T(8,128)S(1)} %add.54.refs_2_), channel_id=1, source_target_pairs={{0,8},{4,12},{8,0},{12,4},{16,24},{20,28},{24,16},{28,20},{1,9},{5... | collective-permute-start | bytes 393224 | tf_op jit(solution)/shard_map/ppermute | solution.py:56
  50.2 12.2 %collective-permute-start.9 = (f32[2,512,128]{2,1,0:T(8,128)S(1)}, f32[2,512,128]{2,1,0:T(8,128)S(1)}, u32[]{:S(2)}, u32[]{:S(2)}) collective-permute-start(f32[2,512,128]{2,1,0:T(8,128)S(1)} %get-tuple-element.39), channel_id=1, source_target_pairs={{0,2},{1,3},{2,0},{3,1},{4,6},{5,7},{6,4},{7,5},{8,10},{9,11},{10,... | collective-permute-start | bytes 1572872 | tf_op jit(solution)/shard_map/ppermute | solution.py:41
  52.6 9.9 %collective-permute-start.22 = (f32[2,2,128,128]{3,2,1,0:T(8,128)S(1)}, f32[2,2,128,128]{3,2,1,0:T(8,128)S(1)}, u32[]{:S(2)}, u32[]{:S(2)}) collective-permute-start(f32[2,2,128,128]{3,2,1,0:T(8,128)S(1)} %get-tuple-element.53), channel_id=1, source_target_pairs={{0,8},{4,12},{8,0},{12,4},{16,24},{20,28},{24,16},{28,20},{1,9},{5... | collective-permute-start | bytes 786440 | tf_op jit(solution)/shard_map/ppermute | solution.py:56
  54.7 6.8 %collective-permute-start.17 = (f32[1,2,64,256]{3,2,1,0:T(8,128)S(1)}, f32[1,2,64,256]{3,2,1,0:T(8,128)S(1)}, u32[]{:S(2)}, u32[]{:S(2)}) collective-permute-start(f32[1,2,64,256]{3,2,1,0:T(8,128)S(1)} %add.60), channel_id=1, source_target_pairs={{0,8},{4,12},{8,0},{12,4},{16,24},{20,28},{24,16},{28,20},{1,9},{5... | collective-permute-start | bytes 393224 | tf_op jit(solution)/shard_map/ppermute | solution.py:56
  56.1 8.8 %collective-permute-start.12 = (f32[2,2,64,256]{3,2,1,0:T(8,128)S(1)}, f32[2,2,64,256]{3,2,1,0:T(8,128)S(1)}, u32[]{:S(2)}, u32[]{:S(2)}) collective-permute-start(f32[2,2,64,256]{3,2,1,0:T(8,128)S(1)} %pad_maximum_fusion.refs_2_), channel_id=1, source_target_pairs={{0,4},{4,0},{8,12},{12,8},{16,20},{20,16},{24,28},{28,24},{1,5},{5... | collective-permute-start | bytes 786440 | tf_op jit(solution)/shard_map/ppermute | solution.py:56
  56.9 12.3 %collective-permute-start.20 = (f32[1,2,128,128]{3,2,1,0:T(8,128)S(1)}, f32[1,2,128,128]{3,2,1,0:T(8,128)S(1)}, u32[]{:S(2)}, u32[]{:S(2)}) collective-permute-start(f32[1,2,128,128]{3,2,1,0:T(8,128)S(1)} %get-tuple-element.60), channel_id=1, source_target_pairs={{0,24},{4,28},{8,16},{12,20},{16,8},{20,12},{24,0},{28,4},{1,25},{... | collective-permute-start | bytes 393224 | tf_op jit(solution)/shard_map/ppermute | solution.py:56
  61.5 6.4 %collective-permute-start.18 = (f32[2,2,64,256]{3,2,1,0:T(8,128)S(1)}, f32[2,2,64,256]{3,2,1,0:T(8,128)S(1)}, u32[]{:S(2)}, u32[]{:S(2)}) collective-permute-start(f32[2,2,64,256]{3,2,1,0:T(8,128)S(1)} %pad_maximum_fusion.1.refs_4_), channel_id=1, source_target_pairs={{0,4},{4,0},{8,12},{12,8},{16,20},{20,16},{24,28},{28,24},{1,5},{5... | collective-permute-start | bytes 786440 | tf_op jit(solution)/shard_map/ppermute | solution.py:56
  62.4 5.6 %collective-permute-start.10 = (f32[1,512,128]{2,1,0:T(8,128)S(1)}, f32[1,512,128]{2,1,0:T(8,128)S(1)}, u32[]{:S(2)}, u32[]{:S(2)}) collective-permute-start(f32[1,512,128]{2,1,0:T(8,128)S(1)} %get-tuple-element.56), channel_id=1, source_target_pairs={{0,1},{1,0},{2,3},{3,2},{4,5},{5,4},{6,7},{7,6},{8,9},{9,8},{10,11... | collective-permute-start | bytes 786440 | tf_op jit(solution)/shard_map/ppermute | solution.py:41
  62.5 7.9 %collective-permute-start.23 = (f32[1,2,128,128]{3,2,1,0:T(8,128)S(1)}, f32[1,2,128,128]{3,2,1,0:T(8,128)S(1)}, u32[]{:S(2)}, u32[]{:S(2)}) collective-permute-start(f32[1,2,128,128]{3,2,1,0:T(8,128)S(1)} %get-tuple-element.58), channel_id=1, source_target_pairs={{0,24},{4,28},{8,16},{12,20},{16,8},{20,12},{24,0},{28,4},{1,25},{... | collective-permute-start | bytes 393224 | tf_op jit(solution)/shard_map/ppermute | solution.py:56
  (8 other events, 73.0 us)

commit v20 on v18

--- a/solution.py
+++ b/solution.py
@@ -203,12 +203,16 @@
     me = lax.axis_index(row_axis) // low
     side = lax.rem(me, 2)
     for part, (begin, end, bits) in enumerate(parts):
+        for read_index in range(begin, end):
+            for pair in range(GROUPS // 2):
+                at = slice(pair * 2 * piece, (pair + 1) * 2 * piece)
+                tile_ref[pair * reads + read_index] = rows_contract(
+                    score_grads[read_index, :, at], keys[...]
+                )
         for upper in range(GROUPS // 2):
             pair = counted(counted(me) ^ (2 * upper)) // 2
-            at = pl.ds(pl.multiple_of(pair * 2 * piece, 2 * piece), 2 * piece)
             for read_index in range(begin, end):
-                slot = upper * reads + read_index
-                tile_ref[slot] = rows_contract(score_grads[read_index, :, at], keys[...])
+                slot = pair * reads + read_index
                 for flip in range(2):
                     half = pl.ds(pl.multiple_of((side ^ flip) * piece, piece), piece)
                     relative = 2 * upper + flip

time: 71.3 us -> 70.9 us (level)
    ppermute x16, waiting for transfers between devices: 14.1 us -> 14.8 us  [row_swap_of(): return lax.ppermute(array, 'rows', pairs)]
  transfers between devices with their start and end apart: 24 -> 24, of which waited for: 9 -> 9; matrix products, arithmetic and copies ran while one was open for 1% -> 1% of each run, Pallas kernels for 17% -> 16%
where the time goes in v20:
time: 70.9 us; the launch traced here: 70.8 us
  starting transfers between devices  36.6 us (52%)
  Pallas kernels  16.6 us (23%)
  waiting for transfers between devices  16.3 us (23%)
  between operations  0.89 us (1%)
    ppermute x16, starting transfers between devices, row_swap_of(): return lax.ppermute(array, 'rows', pairs)  22.5 us
    ppermute x16, waiting for transfers between devices, row_swap_of(): return lax.ppermute(array, 'rows', pairs)  14.8 us
    ppermute x8, starting transfers between devices, swap(): return lax.ppermute(array, axis, pairs)  14.1 us
    pallas_call x4, Pallas kernels, kernel_call(): pl.pallas_call(kernel, out_shape=[shape_of(*item) for item in shapes], in...  7.52 us
    pallas_call x2, Pallas kernels, on_device(): pl.pallas_call(functools.partial(first_kernel, tile) if first else functo...  6.2 us
    ppermute x8, waiting for transfers between devices, swap(): return lax.ppermute(array, axis, pairs)  1.51 us
  transfers between devices with their start and end apart: 24, of which 9 were waited for; matrix products, arithmetic and copies ran while one was open for 1% of the time, Pallas kernels for 16%

profile of v20, /device:TPU:0, one launch (start us, length us, event | category | flops | bytes accessed | tf_op | source)
XLA Modules:
  0.0 70.8 jit_solution(16544919084299109000)
XLA Ops:
  0.7 4.4 %project.2 = (bf16[512,128]{1,0:T(8,128)(2,1)}, bf16[512,128]{1,0:T(8,128)(2,1)}, f32[4,1024]{1,0:T(4,128)}) custom-call(bf16[512,512]{1,0:T(8,128)(2,1)} %inputs.3, bf16[512,256]{1,0:T(8,128)(2,1)} %key_weight.1, bf16[512,256]{1,0:T(8,128)(2,1)} %value_weight.1, bf16[2,1024,256]{2,1,0:T(8,128)(2,1)} %queries.4, bf16[2,1024,256]{2,1,0:T(8,128)(2,1)} %out_grad.3), custom_call_target="tpu_custom_call" | custom-call | flops 1073741824 | bytes 4194304 | tf_op jit(solution)/shard_map/project/pallas_call | solution.py:289
  5.1 3.0 %collective-permute-start = (f32[4,1024]{1,0:T(4,128)}, f32[4,1024]{1,0:T(4,128)S(1)}, u32[]{:S(2)}, u32[]{:S(2)}) collective-permute-start(f32[4,1024]{1,0:T(4,128)} %get-tuple-element.28.mine), channel_id=1, source_target_pairs={{0,4},{4,0},{8,12},{12,8},{16,20},{20,16},{24,28},{28,24},{1,5},{5... | collective-permute-start | bytes 49160 | tf_op jit(solution)/shard_map/ppermute | solution.py:41
  8.2 1.8 %project.3 = (bf16[512,128]{1,0:T(8,128)(2,1)S(1)}, bf16[512,128]{1,0:T(8,128)(2,1)S(1)}, f32[4,1024]{1,0:T(4,128)S(1)}) custom-call(bf16[512,512]{1,0:T(8,128)(2,1)S(1)} %copy-done.3, bf16[512,256]{1,0:T(8,128)(2,1)S(1)} %copy-done.4, bf16[512,256]{1,0:T(8,128)(2,1)S(1)} %copy-done.5, bf16[2,1024,256]{2,1,0:T(8,128)(2,1)S(1)} %copy-done.1, ...), custom_call_target="tpu_custom_call" | custom-call | flops 1073741824 | bytes 4194304 | tf_op jit(solution)/shard_map/project/pallas_call | solution.py:289
  10.1 2.2 %collective-permute-start.1 = (f32[4,1024]{1,0:T(4,128)S(1)}, f32[4,1024]{1,0:T(4,128)S(1)}, u32[]{:S(2)}, u32[]{:S(2)}) collective-permute-start(f32[4,1024]{1,0:T(4,128)S(1)} %merge.4.mine), channel_id=1, source_target_pairs={{0,8},{4,12},{8,0},{12,4},{16,24},{20,28},{24,16},{28,20},{1,9},{5... | collective-permute-start | bytes 49160 | tf_op jit(solution)/shard_map/ppermute | solution.py:41
  12.3 1.5 %collective-permute-done.3.theirs = f32[4,1024]{1,0:T(4,128)S(1)} collective-permute-done((f32[4,1024]{1,0:T(4,128)S(1)}, f32[4,1024]{1,0:T(4,128)S(1)}, u32[]{:S(2)}, u32[]{:S(2)}) %collective-permute-start.3) | collective-permute-done | bytes 16416 | tf_op jit(solution)/shard_map/ppermute | solution.py:41
  13.8 1.6 %collective-permute-start.4 = (f32[4,1024]{1,0:T(4,128)S(1)}, f32[4,1024]{1,0:T(4,128)S(1)}, u32[]{:S(2)}, u32[]{:S(2)}) collective-permute-start(f32[4,1024]{1,0:T(4,128)S(1)} %merge.6.mine), channel_id=1, source_target_pairs={{0,8},{4,12},{8,0},{12,4},{16,24},{20,28},{24,16},{28,20},{1,9},{5... | collective-permute-start | bytes 49160 | tf_op jit(solution)/shard_map/ppermute | solution.py:41
  15.5 2.7 %collective-permute-start.2 = (f32[4,1024]{1,0:T(4,128)S(1)}, f32[4,1024]{1,0:T(4,128)S(1)}, u32[]{:S(2)}, u32[]{:S(2)}) collective-permute-start(f32[4,1024]{1,0:T(4,128)S(1)} %merge.5.after.mine), channel_id=1, source_target_pairs={{0,16},{4,20},{8,24},{12,28},{16,0},{20,4},{24,8},{28,12},{1,17},{... | collective-permute-start | bytes 49160 | tf_op jit(solution)/shard_map/ppermute | solution.py:41
  18.1 2.2 %collective-permute-start.5 = (f32[4,1024]{1,0:T(4,128)S(1)}, f32[4,1024]{1,0:T(4,128)S(1)}, u32[]{:S(2)}, u32[]{:S(2)}) collective-permute-start(f32[4,1024]{1,0:T(4,128)S(1)} %merge.7.mine), channel_id=1, source_target_pairs={{0,16},{4,20},{8,24},{12,28},{16,0},{20,4},{24,8},{28,12},{1,17},{... | collective-permute-start | bytes 49160 | tf_op jit(solution)/shard_map/ppermute | solution.py:41
  20.4 2.9 %grads.2 = (bf16[512,256]{1,0:T(8,128)(2,1)S(1)}, bf16[2,512,1024]{2,1,0:T(8,128)(2,1)S(1)}, f32[2,2,64,256]{3,2,1,0:T(8,128)S(1)}, f32[2,2,64,256]{3,2,1,0:T(8,128)S(1)}) custom-call(f32[4,1024]{1,0:T(4,128)S(1)} %merge.5.after.mine, bf16[512,512]{1,0:T(8,128)(2,1)S(1)} %copy-done.3, bf16[512,128]{1,0:T(8,128)(2,1)S(1)} %copy-done.6, ...), custom_call_target="tpu_custom_call" | custom-call | flops 1073741824 | bytes 4194304 | tf_op jit(solution)/shard_map/grads/pallas_call | solution.py:345
  24.7 1.8 %collective-permute-start.15 = (f32[4,2,128,128]{3,2,1,0:T(8,128)S(1)}, f32[4,2,128,128]{3,2,1,0:T(8,128)S(1)}, u32[]{:S(2)}, u32[]{:S(2)}) collective-permute-start(f32[4,2,128,128]{3,2,1,0:T(8,128)S(1)} %get-tuple-element.44), channel_id=1, source_target_pairs={{0,8},{4,12},{8,0},{12,4},{16,24},{20,28},{24,16},{28,20},{1,9},{5... | collective-permute-start | bytes 1572872 | tf_op jit(solution)/shard_map/ppermute | solution.py:56
  26.5 2.9 %grads.3 = (bf16[512,256]{1,0:T(8,128)(2,1)S(1)}, bf16[2,512,1024]{2,1,0:T(8,128)(2,1)S(1)}, f32[2,2,64,256]{3,2,1,0:T(8,128)S(1)}, f32[2,2,64,256]{3,2,1,0:T(8,128)S(1)}) custom-call(bf16[512,256]{1,0:T(8,128)(2,1)S(1)} %get-tuple-element.31.after.refs_0_, bf16[512,512]{1,0:T(8,128)(2,1)S(1)} %copy-done.3, bf16[512,128]{1,0:T(8,128)(2,1)S(1)} %get-tuple-element.32.keys, ...), custom_call_target="tpu_custom_call" | custom-call | flops 1073741824 | bytes 4194304 | tf_op jit(solution)/shard_map/grads/pallas_call | solution.py:345
  29.4 1.4 %collective-permute-start.13 = (f32[2,2,64,256]{3,2,1,0:T(8,128)S(1)}, f32[2,2,64,256]{3,2,1,0:T(8,128)S(1)}, u32[]{:S(2)}, u32[]{:S(2)}) collective-permute-start(f32[2,2,64,256]{3,2,1,0:T(8,128)S(1)} %get-tuple-element.41), channel_id=1, source_target_pairs={{0,4},{4,0},{8,12},{12,8},{16,20},{20,16},{24,28},{28,24},{1,5},{5... | collective-permute-start | bytes 786440 | tf_op jit(solution)/shard_map/ppermute | solution.py:56
  32.4 1.4 %collective-permute-start.7 = (f32[1,2,64,256]{3,2,1,0:T(8,128)S(1)}, f32[1,2,64,256]{3,2,1,0:T(8,128)S(1)}, u32[]{:S(2)}, u32[]{:S(2)}) collective-permute-start(f32[1,2,64,256]{3,2,1,0:T(8,128)S(1)} %slice_add_fusion.12), channel_id=1, source_target_pairs={{0,8},{4,12},{8,0},{12,4},{16,24},{20,28},{24,16},{28,20},{1,9},{5... | collective-permute-start | bytes 393224 | tf_op jit(solution)/shard_map/ppermute | solution.py:56
  33.8 4.9 %collective-permute-done.13 = f32[2,2,64,256]{3,2,1,0:T(8,128)S(1)} collective-permute-done((f32[2,2,64,256]{3,2,1,0:T(8,128)S(1)}, f32[2,2,64,256]{3,2,1,0:T(8,128)S(1)}, u32[]{:S(2)}, u32[]{:S(2)}) %collective-permute-start.13) | collective-permute-done | bytes 262176 | tf_op jit(solution)/shard_map/ppermute | solution.py:56
  39.5 5.3 %collective-permute-start.8 = (f32[1,2,64,256]{3,2,1,0:T(8,128)S(1)}, f32[1,2,64,256]{3,2,1,0:T(8,128)S(1)}, u32[]{:S(2)}, u32[]{:S(2)}) collective-permute-start(f32[1,2,64,256]{3,2,1,0:T(8,128)S(1)} %fusion), channel_id=1, source_target_pairs={{0,24},{4,28},{8,16},{12,20},{16,8},{20,12},{24,0},{28,4},{1,25},{... | collective-permute-start | bytes 393224 | tf_op jit(solution)/shard_map/ppermute | solution.py:56
  45.4 1.7 %collective-permute-start.16 = (f32[1,2,64,256]{3,2,1,0:T(8,128)S(1)}, f32[1,2,64,256]{3,2,1,0:T(8,128)S(1)}, u32[]{:S(2)}, u32[]{:S(2)}) collective-permute-start(f32[1,2,64,256]{3,2,1,0:T(8,128)S(1)} %added.1), channel_id=1, source_target_pairs={{0,24},{4,28},{8,16},{12,20},{16,8},{20,12},{24,0},{28,4},{1,25},{... | collective-permute-start | bytes 393224 | tf_op jit(solution)/shard_map/ppermute | solution.py:56
  47.1 1.8 %collective-permute-done.8 = f32[1,2,64,256]{3,2,1,0:T(8,128)S(1)} collective-permute-done((f32[1,2,64,256]{3,2,1,0:T(8,128)S(1)}, f32[1,2,64,256]{3,2,1,0:T(8,128)S(1)}, u32[]{:S(2)}, u32[]{:S(2)}) %collective-permute-start.8) | collective-permute-done | bytes 131104 | tf_op jit(solution)/shard_map/ppermute | solution.py:56
  49.9 2.3 %collective-permute-start.9 = (f32[2,512,128]{2,1,0:T(8,128)S(1)}, f32[2,512,128]{2,1,0:T(8,128)S(1)}, u32[]{:S(2)}, u32[]{:S(2)}) collective-permute-start(f32[2,512,128]{2,1,0:T(8,128)S(1)} %get-tuple-element.39), channel_id=1, source_target_pairs={{0,2},{1,3},{2,0},{3,1},{4,6},{5,7},{6,4},{7,5},{8,10},{9,11},{10,... | collective-permute-start | bytes 1572872 | tf_op jit(solution)/shard_map/ppermute | solution.py:41
  52.2 2.1 %collective-permute-start.22 = (f32[2,2,128,128]{3,2,1,0:T(8,128)S(1)}, f32[2,2,128,128]{3,2,1,0:T(8,128)S(1)}, u32[]{:S(2)}, u32[]{:S(2)}) collective-permute-start(f32[2,2,128,128]{3,2,1,0:T(8,128)S(1)} %get-tuple-element.53), channel_id=1, source_target_pairs={{0,8},{4,12},{8,0},{12,4},{16,24},{20,28},{24,16},{28,20},{1,9},{5... | collective-permute-start | bytes 786440 | tf_op jit(solution)/shard_map/ppermute | solution.py:56
  54.4 1.3 %collective-permute-done.11 = f32[1,2,64,256]{3,2,1,0:T(8,128)S(1)} collective-permute-done((f32[1,2,64,256]{3,2,1,0:T(8,128)S(1)}, f32[1,2,64,256]{3,2,1,0:T(8,128)S(1)}, u32[]{:S(2)}, u32[]{:S(2)}) %collective-permute-start.11) | collective-permute-done | bytes 131104 | tf_op jit(solution)/shard_map/ppermute | solution.py:56
  56.6 2.7 %collective-permute-start.20 = (f32[1,2,128,128]{3,2,1,0:T(8,128)S(1)}, f32[1,2,128,128]{3,2,1,0:T(8,128)S(1)}, u32[]{:S(2)}, u32[]{:S(2)}) collective-permute-start(f32[1,2,128,128]{3,2,1,0:T(8,128)S(1)} %get-tuple-element.60), channel_id=1, source_target_pairs={{0,24},{4,28},{8,16},{12,20},{16,8},{20,12},{24,0},{28,4},{1,25},{... | collective-permute-start | bytes 393224 | tf_op jit(solution)/shard_map/ppermute | solution.py:56
  59.3 2.1 %collective-permute-done.17 = f32[1,2,64,256]{3,2,1,0:T(8,128)S(1)} collective-permute-done((f32[1,2,64,256]{3,2,1,0:T(8,128)S(1)}, f32[1,2,64,256]{3,2,1,0:T(8,128)S(1)}, u32[]{:S(2)}, u32[]{:S(2)}) %collective-permute-start.17) | collective-permute-done | bytes 131104 | tf_op jit(solution)/shard_map/ppermute | solution.py:56
  62.2 2.4 %collective-permute-start.23 = (f32[1,2,128,128]{3,2,1,0:T(8,128)S(1)}, f32[1,2,128,128]{3,2,1,0:T(8,128)S(1)}, u32[]{:S(2)}, u32[]{:S(2)}) collective-permute-start(f32[1,2,128,128]{3,2,1,0:T(8,128)S(1)} %get-tuple-element.58), channel_id=1, source_target_pairs={{0,24},{4,28},{8,16},{12,20},{16,8},{20,12},{24,0},{28,4},{1,25},{... | collective-permute-start | bytes 393224 | tf_op jit(solution)/shard_map/ppermute | solution.py:56
  64.6 3.2 %collective-permute-done.18.refs_5_ = f32[2,2,64,256]{3,2,1,0:T(8,128)S(1)} collective-permute-done((f32[2,2,64,256]{3,2,1,0:T(8,128)S(1)}, f32[2,2,64,256]{3,2,1,0:T(8,128)S(1)}, u32[]{:S(2)}, u32[]{:S(2)}) %collective-permute-start.18) | collective-permute-done | bytes 262176 | tf_op jit(solution)/shard_map/ppermute | solution.py:56
  (66 shorter events, 10.5 us)
Async XLA Ops:
  5.1 4.9 %collective-permute-start = (f32[4,1024]{1,0:T(4,128)}, f32[4,1024]{1,0:T(4,128)S(1)}, u32[]{:S(2)}, u32[]{:S(2)}) collective-permute-start(f32[4,1024]{1,0:T(4,128)} %get-tuple-element.28.mine), channel_id=1, source_target_pairs={{0,4},{4,0},{8,12},{12,8},{16,20},{20,16},{24,28},{28,24},{1,5},{5... | collective-permute-start | bytes 49160 | tf_op jit(solution)/shard_map/ppermute | solution.py:41
  10.0 3.8 %collective-permute-start.3 = (f32[4,1024]{1,0:T(4,128)S(1)}, f32[4,1024]{1,0:T(4,128)S(1)}, u32[]{:S(2)}, u32[]{:S(2)}) collective-permute-start(f32[4,1024]{1,0:T(4,128)S(1)} %get-tuple-element.34.mine), channel_id=1, source_target_pairs={{0,4},{4,0},{8,12},{12,8},{16,20},{20,16},{24,28},{28,24},{1,5},{5... | collective-permute-start | bytes 49160 | tf_op jit(solution)/shard_map/ppermute | solution.py:41
  10.1 5.3 %collective-permute-start.1 = (f32[4,1024]{1,0:T(4,128)S(1)}, f32[4,1024]{1,0:T(4,128)S(1)}, u32[]{:S(2)}, u32[]{:S(2)}) collective-permute-start(f32[4,1024]{1,0:T(4,128)S(1)} %merge.4.mine), channel_id=1, source_target_pairs={{0,8},{4,12},{8,0},{12,4},{16,24},{20,28},{24,16},{28,20},{1,9},{5... | collective-permute-start | bytes 49160 | tf_op jit(solution)/shard_map/ppermute | solution.py:41
  13.8 4.3 %collective-permute-start.4 = (f32[4,1024]{1,0:T(4,128)S(1)}, f32[4,1024]{1,0:T(4,128)S(1)}, u32[]{:S(2)}, u32[]{:S(2)}) collective-permute-start(f32[4,1024]{1,0:T(4,128)S(1)} %merge.6.mine), channel_id=1, source_target_pairs={{0,8},{4,12},{8,0},{12,4},{16,24},{20,28},{24,16},{28,20},{1,9},{5... | collective-permute-start | bytes 49160 | tf_op jit(solution)/shard_map/ppermute | solution.py:41
  15.5 4.9 %collective-permute-start.2 = (f32[4,1024]{1,0:T(4,128)S(1)}, f32[4,1024]{1,0:T(4,128)S(1)}, u32[]{:S(2)}, u32[]{:S(2)}) collective-permute-start(f32[4,1024]{1,0:T(4,128)S(1)} %merge.5.after.mine), channel_id=1, source_target_pairs={{0,16},{4,20},{8,24},{12,28},{16,0},{20,4},{24,8},{28,12},{1,17},{... | collective-permute-start | bytes 49160 | tf_op jit(solution)/shard_map/ppermute | solution.py:41
  18.1 8.3 %collective-permute-start.5 = (f32[4,1024]{1,0:T(4,128)S(1)}, f32[4,1024]{1,0:T(4,128)S(1)}, u32[]{:S(2)}, u32[]{:S(2)}) collective-permute-start(f32[4,1024]{1,0:T(4,128)S(1)} %merge.7.mine), channel_id=1, source_target_pairs={{0,16},{4,20},{8,24},{12,28},{16,0},{20,4},{24,8},{28,12},{1,17},{... | collective-permute-start | bytes 49160 | tf_op jit(solution)/shard_map/ppermute | solution.py:41
  23.3 9.1 %collective-permute-start.6 = (f32[2,2,64,256]{3,2,1,0:T(8,128)S(1)}, f32[2,2,64,256]{3,2,1,0:T(8,128)S(1)}, u32[]{:S(2)}, u32[]{:S(2)}) collective-permute-start(f32[2,2,64,256]{3,2,1,0:T(8,128)S(1)} %get-tuple-element.37), channel_id=1, source_target_pairs={{0,4},{4,0},{8,12},{12,8},{16,20},{20,16},{24,28},{28,24},{1,5},{5... | collective-permute-start | bytes 786440 | tf_op jit(solution)/shard_map/ppermute | solution.py:56
  24.7 20.2 %collective-permute-start.15 = (f32[4,2,128,128]{3,2,1,0:T(8,128)S(1)}, f32[4,2,128,128]{3,2,1,0:T(8,128)S(1)}, u32[]{:S(2)}, u32[]{:S(2)}) collective-permute-start(f32[4,2,128,128]{3,2,1,0:T(8,128)S(1)} %get-tuple-element.44), channel_id=1, source_target_pairs={{0,8},{4,12},{8,0},{12,4},{16,24},{20,28},{24,16},{28,20},{1,9},{5... | collective-permute-start | bytes 1572872 | tf_op jit(solution)/shard_map/ppermute | solution.py:56
  29.4 9.3 %collective-permute-start.13 = (f32[2,2,64,256]{3,2,1,0:T(8,128)S(1)}, f32[2,2,64,256]{3,2,1,0:T(8,128)S(1)}, u32[]{:S(2)}, u32[]{:S(2)}) collective-permute-start(f32[2,2,64,256]{3,2,1,0:T(8,128)S(1)} %get-tuple-element.41), channel_id=1, source_target_pairs={{0,4},{4,0},{8,12},{12,8},{16,20},{20,16},{24,28},{28,24},{1,5},{5... | collective-permute-start | bytes 786440 | tf_op jit(solution)/shard_map/ppermute | solution.py:56
  31.6 20.5 %collective-permute-start.21 = (f32[4,2,128,128]{3,2,1,0:T(8,128)S(1)}, f32[4,2,128,128]{3,2,1,0:T(8,128)S(1)}, u32[]{:S(2)}, u32[]{:S(2)}) collective-permute-start(f32[4,2,128,128]{3,2,1,0:T(8,128)S(1)} %get-tuple-element.48), channel_id=1, source_target_pairs={{0,4},{4,0},{8,12},{12,8},{16,20},{20,16},{24,28},{28,24},{1,5},{5... | collective-permute-start | bytes 1572872 | tf_op jit(solution)/shard_map/ppermute | solution.py:56
  32.4 7.1 %collective-permute-start.7 = (f32[1,2,64,256]{3,2,1,0:T(8,128)S(1)}, f32[1,2,64,256]{3,2,1,0:T(8,128)S(1)}, u32[]{:S(2)}, u32[]{:S(2)}) collective-permute-start(f32[1,2,64,256]{3,2,1,0:T(8,128)S(1)} %slice_add_fusion.12), channel_id=1, source_target_pairs={{0,8},{4,12},{8,0},{12,4},{16,24},{20,28},{24,16},{28,20},{1,9},{5... | collective-permute-start | bytes 393224 | tf_op jit(solution)/shard_map/ppermute | solution.py:56
  38.7 6.7 %collective-permute-start.14 = (f32[1,2,64,256]{3,2,1,0:T(8,128)S(1)}, f32[1,2,64,256]{3,2,1,0:T(8,128)S(1)}, u32[]{:S(2)}, u32[]{:S(2)}) collective-permute-start(f32[1,2,64,256]{3,2,1,0:T(8,128)S(1)} %get-tuple-element.62), channel_id=1, source_target_pairs={{0,8},{4,12},{8,0},{12,4},{16,24},{20,28},{24,16},{28,20},{1,9},{5... | collective-permute-start | bytes 393224 | tf_op jit(solution)/shard_map/ppermute | solution.py:56
  39.5 9.4 %collective-permute-start.8 = (f32[1,2,64,256]{3,2,1,0:T(8,128)S(1)}, f32[1,2,64,256]{3,2,1,0:T(8,128)S(1)}, u32[]{:S(2)}, u32[]{:S(2)}) collective-permute-start(f32[1,2,64,256]{3,2,1,0:T(8,128)S(1)} %fusion), channel_id=1, source_target_pairs={{0,24},{4,28},{8,16},{12,20},{16,8},{20,12},{24,0},{28,4},{1,25},{... | collective-permute-start | bytes 393224 | tf_op jit(solution)/shard_map/ppermute | solution.py:56
  44.9 11.6 %collective-permute-start.19 = (f32[2,2,128,128]{3,2,1,0:T(8,128)S(1)}, f32[2,2,128,128]{3,2,1,0:T(8,128)S(1)}, u32[]{:S(2)}, u32[]{:S(2)}) collective-permute-start(f32[2,2,128,128]{3,2,1,0:T(8,128)S(1)} %get-tuple-element.55.after), channel_id=1, source_target_pairs={{0,4},{4,0},{8,12},{12,8},{16,20},{20,16},{24,28},{28,24},{1,5},{5... | collective-permute-start | bytes 786440 | tf_op jit(solution)/shard_map/ppermute | solution.py:56
  45.4 8.9 %collective-permute-start.16 = (f32[1,2,64,256]{3,2,1,0:T(8,128)S(1)}, f32[1,2,64,256]{3,2,1,0:T(8,128)S(1)}, u32[]{:S(2)}, u32[]{:S(2)}) collective-permute-start(f32[1,2,64,256]{3,2,1,0:T(8,128)S(1)} %added.1), channel_id=1, source_target_pairs={{0,24},{4,28},{8,16},{12,20},{16,8},{20,12},{24,0},{28,4},{1,25},{... | collective-permute-start | bytes 393224 | tf_op jit(solution)/shard_map/ppermute | solution.py:56
  49.0 6.7 %collective-permute-start.11 = (f32[1,2,64,256]{3,2,1,0:T(8,128)S(1)}, f32[1,2,64,256]{3,2,1,0:T(8,128)S(1)}, u32[]{:S(2)}, u32[]{:S(2)}) collective-permute-start(f32[1,2,64,256]{3,2,1,0:T(8,128)S(1)} %add.54.refs_2_), channel_id=1, source_target_pairs={{0,8},{4,12},{8,0},{12,4},{16,24},{20,28},{24,16},{28,20},{1,9},{5... | collective-permute-start | bytes 393224 | tf_op jit(solution)/shard_map/ppermute | solution.py:56
  49.9 12.1 %collective-permute-start.9 = (f32[2,512,128]{2,1,0:T(8,128)S(1)}, f32[2,512,128]{2,1,0:T(8,128)S(1)}, u32[]{:S(2)}, u32[]{:S(2)}) collective-permute-start(f32[2,512,128]{2,1,0:T(8,128)S(1)} %get-tuple-element.39), channel_id=1, source_target_pairs={{0,2},{1,3},{2,0},{3,1},{4,6},{5,7},{6,4},{7,5},{8,10},{9,11},{10,... | collective-permute-start | bytes 1572872 | tf_op jit(solution)/shard_map/ppermute | solution.py:41
  52.2 10.0 %collective-permute-start.22 = (f32[2,2,128,128]{3,2,1,0:T(8,128)S(1)}, f32[2,2,128,128]{3,2,1,0:T(8,128)S(1)}, u32[]{:S(2)}, u32[]{:S(2)}) collective-permute-start(f32[2,2,128,128]{3,2,1,0:T(8,128)S(1)} %get-tuple-element.53), channel_id=1, source_target_pairs={{0,8},{4,12},{8,0},{12,4},{16,24},{20,28},{24,16},{28,20},{1,9},{5... | collective-permute-start | bytes 786440 | tf_op jit(solution)/shard_map/ppermute | solution.py:56
  54.3 7.0 %collective-permute-start.17 = (f32[1,2,64,256]{3,2,1,0:T(8,128)S(1)}, f32[1,2,64,256]{3,2,1,0:T(8,128)S(1)}, u32[]{:S(2)}, u32[]{:S(2)}) collective-permute-start(f32[1,2,64,256]{3,2,1,0:T(8,128)S(1)} %add.60), channel_id=1, source_target_pairs={{0,8},{4,12},{8,0},{12,4},{16,24},{20,28},{24,16},{28,20},{1,9},{5... | collective-permute-start | bytes 393224 | tf_op jit(solution)/shard_map/ppermute | solution.py:56
  55.7 8.9 %collective-permute-start.12 = (f32[2,2,64,256]{3,2,1,0:T(8,128)S(1)}, f32[2,2,64,256]{3,2,1,0:T(8,128)S(1)}, u32[]{:S(2)}, u32[]{:S(2)}) collective-permute-start(f32[2,2,64,256]{3,2,1,0:T(8,128)S(1)} %pad_maximum_fusion.refs_2_), channel_id=1, source_target_pairs={{0,4},{4,0},{8,12},{12,8},{16,20},{20,16},{24,28},{28,24},{1,5},{5... | collective-permute-start | bytes 786440 | tf_op jit(solution)/shard_map/ppermute | solution.py:56
  56.6 12.5 %collective-permute-start.20 = (f32[1,2,128,128]{3,2,1,0:T(8,128)S(1)}, f32[1,2,128,128]{3,2,1,0:T(8,128)S(1)}, u32[]{:S(2)}, u32[]{:S(2)}) collective-permute-start(f32[1,2,128,128]{3,2,1,0:T(8,128)S(1)} %get-tuple-element.60), channel_id=1, source_target_pairs={{0,24},{4,28},{8,16},{12,20},{16,8},{20,12},{24,0},{28,4},{1,25},{... | collective-permute-start | bytes 393224 | tf_op jit(solution)/shard_map/ppermute | solution.py:56
  61.4 6.4 %collective-permute-start.18 = (f32[2,2,64,256]{3,2,1,0:T(8,128)S(1)}, f32[2,2,64,256]{3,2,1,0:T(8,128)S(1)}, u32[]{:S(2)}, u32[]{:S(2)}) collective-permute-start(f32[2,2,64,256]{3,2,1,0:T(8,128)S(1)} %pad_maximum_fusion.1.refs_4_), channel_id=1, source_target_pairs={{0,4},{4,0},{8,12},{12,8},{16,20},{20,16},{24,28},{28,24},{1,5},{5... | collective-permute-start | bytes 786440 | tf_op jit(solution)/shard_map/ppermute | solution.py:56
  62.1 5.7 %collective-permute-start.10 = (f32[1,512,128]{2,1,0:T(8,128)S(1)}, f32[1,512,128]{2,1,0:T(8,128)S(1)}, u32[]{:S(2)}, u32[]{:S(2)}) collective-permute-start(f32[1,512,128]{2,1,0:T(8,128)S(1)} %get-tuple-element.56), channel_id=1, source_target_pairs={{0,1},{1,0},{2,3},{3,2},{4,5},{5,4},{6,7},{7,6},{8,9},{9,8},{10,11... | collective-permute-start | bytes 786440 | tf_op jit(solution)/shard_map/ppermute | solution.py:41
  62.2 7.9 %collective-permute-start.23 = (f32[1,2,128,128]{3,2,1,0:T(8,128)S(1)}, f32[1,2,128,128]{3,2,1,0:T(8,128)S(1)}, u32[]{:S(2)}, u32[]{:S(2)}) collective-permute-start(f32[1,2,128,128]{3,2,1,0:T(8,128)S(1)} %get-tuple-element.58), channel_id=1, source_target_pairs={{0,24},{4,28},{8,16},{12,20},{16,8},{20,12},{24,0},{28,4},{1,25},{... | collective-permute-start | bytes 393224 | tf_op jit(solution)/shard_map/ppermute | solution.py:56
  (8 other events, 73.0 us)
